TPU v7x, 32 devices: a whole 2x2x4 slice. The times are simulated.
32 devices in a mesh: tm: 8 (over z, x), seq: 2 (over y), mp: 2 (over core).
Axes of the slice: x: 2, y: 2, z: 4, core: 2. Of those that a mesh axis runs over, the one named last changes fastest.
Arguments:
- student_q: bfloat16 [2, 1024, 5120], P('seq', 'tm', 'mp'), may hold values from -110 to 110
- student_k: bfloat16 [2, 1024, 5120], P('seq', 'tm', 'mp'), may hold values from -6 to 6
- student_v: bfloat16 [2, 1024, 5120], P('seq', 'tm', 'mp'), may hold values from -6 to 6
- teacher_q: bfloat16 [2, 1024, 5120], P('seq', 'tm', 'mp'), may hold values from -110 to 110
- teacher_k: bfloat16 [2, 1024, 5120], P('seq', 'tm', 'mp'), may hold values from -6 to 6
- stagger: int32 [2], P('seq'), may hold values from 0 to 4, as said below
- clip_lengths: int32 [2, 3], P('seq'), may hold values from 1 to 5, 8 in all within a row
Outputs:
- generated: bfloat16 [2, 1024, 5120], P('seq', 'tm', 'mp')
- score_rows: bfloat16 [2, 1024, 5120], P('seq', 'tm', 'mp')
Inputs may be any that keep to these rules, and one draw needn't show every extreme that they name: `clip_lengths`: the lengths of each video sum to 8, and some clip has 5 blocks. `stagger`: some video has the value 8 // 2.
All inputs are finite; a program needn't handle non-finite values.
Results may differ from a plain program's by a relative error of at most 0.007.
Values may be sent and summed in bfloat16 or wider, within the bound.
No kernel may reach another device: no remote copies, remote signals or barrier semaphores. Data moves between devices by JAX's collectives and lax.ppermute only.
A program may use at most 64 MiB of HBM per device.

v0:
```python
import functools
import math

import jax
import jax.numpy as jnp
from jax import lax
from jax.experimental import pallas as pl
from jax.experimental.pallas import tpu as pltpu
from jax.sharding import PartitionSpec as P

HD = 128
TOK = 128
NEG = -1e30
RATE = math.log2(math.e) / math.sqrt(HD)
MIB = 2**20
VMEM = pl.BlockSpec(memory_space=pltpu.VMEM)
SMEM = pl.BlockSpec(memory_space=pltpu.SMEM)
WHOLE = pltpu.CompilerParams(vmem_limit_bytes=60 * MIB)
LOCAL = pltpu.CompilerParams(vmem_limit_bytes=24 * MIB)


def attend(q, k, v, bias):
    g = q.shape[0]
    scores = lax.dot_general(
        q.reshape(g * TOK, HD), k, (((1,), (1,)), ((), ())), preferred_element_type=jnp.float32
    )
    scores = scores.reshape(g, TOK, -1)
    if bias is not None:
        scores = scores + bias
    top = jnp.max(scores, axis=-1, keepdims=True)
    weights = jnp.exp2((scores - top) * RATE)
    total = jnp.sum(weights, axis=-1, keepdims=True)
    weights = weights.astype(jnp.bfloat16).reshape(g * TOK, -1)
    mixed = jnp.dot(weights, v, preferred_element_type=jnp.float32)
    return mixed.reshape(g, TOK, HD) / total


def student_head(pairs, first, sources, o_ref, o_at):
    (q_ref, q_at), (k_ref, k_at), (v_ref, v_at) = sources
    for i in pairs:
        width = (i + 2) * TOK
        block = lax.broadcasted_iota(jnp.int32, (2, 1, width), 2) // TOK
        own = lax.broadcasted_iota(jnp.int32, (2, 1, width), 0) + i
        bias = jnp.where((block == own) | (block >= first) & (block < own), 0.0, NEG)
        k = k_ref[0 : i + 2, k_at].reshape(width, HD)
        v = v_ref[0 : i + 2, v_at].reshape(width, HD)
        o_ref[i : i + 2, o_at] = attend(q_ref[i : i + 2, q_at], k, v, bias).astype(jnp.bfloat16)


def teacher_head(blocks, rows, clip_ref, sources, gen, o_ref, o_at):
    (q_ref, q_at), (k_ref, k_at) = sources
    reach = blocks // 2 + 1
    width = reach * TOK
    offset = lax.broadcasted_iota(jnp.int32, (1, 1, width), 2) // TOK
    for i in rows:
        low = clip_ref[0, i]
        high = clip_ref[1, i]
        start = jnp.minimum(low, blocks - reach)
        block = offset + start
        bias = jnp.where((block >= low) & (block < high), 0.0, NEG)
        k = k_ref[pl.ds(start, reach), k_at].reshape(width, HD)
        v = gen(pl.ds(start, reach)).reshape(width, HD)
        out = attend(q_ref[pl.ds(i, 1), q_at], k, v, bias)
        score = (out[0] - gen(i).astype(jnp.float32)).astype(jnp.bfloat16)
        if o_at is None:
            o_ref[1] = score
        else:
            o_ref[i, o_at] = score


def teacher_whole_head(blocks, clip_ref, sources, gen, o_ref, o_at):
    (q_ref, q_at), (k_ref, k_at) = sources
    reach = blocks // 2 + 1

    def put(at, out):
        score = out - gen(at).astype(jnp.float32)
        o_ref[at, o_at] = score.astype(jnp.bfloat16)

    large = clip_ref[2, 0]
    k = k_ref[pl.ds(large, reach), k_at].reshape(reach * TOK, HD)
    v = gen(pl.ds(large, reach)).reshape(reach * TOK, HD)
    for i in range(0, reach, 2):
        at = pl.ds(large + i, min(2, reach - i))
        put(at, attend(q_ref[at, q_at], k, v, None))
    span = blocks - reach - 1
    offset = lax.broadcasted_iota(jnp.int32, (1, 1, span * TOK), 2) // TOK
    for j in range(blocks - reach):
        i = jnp.where(j < large, j, j + reach)
        low, high = clip_ref[0, i], clip_ref[1, i]
        start = jnp.minimum(low, blocks - span)
        block = offset + start
        bias = jnp.where((block >= low) & (block < high), 0.0, NEG)
        k = k_ref[pl.ds(start, span), k_at].reshape(span * TOK, HD)
        v = gen(pl.ds(start, span)).reshape(span * TOK, HD)
        put(pl.ds(i, 1), attend(q_ref[pl.ds(i, 1), q_at], k, v, bias))


def cost(heads, blocks, units):
    return pl.CostEstimate(
        flops=heads * blocks * blocks * 4 * TOK * TOK * HD,
        bytes_accessed=units * blocks * TOK * HD * 2,
        transcendentals=heads * blocks * blocks * TOK * TOK,
    )


def pack(plan, ranges, tensors):
    peers, units = len(plan), len(plan[0])
    widths = [count * HD for _, count in ranges]
    starts = [sum(widths[:r]) for r in range(len(ranges))]

    def place(h):
        for r, (head, count) in enumerate(ranges):
            if head <= h < head + count:
                return r, starts[r] + (h - head) * HD

    need = []
    for u in range(units):
        need.append(list(dict.fromkeys((plan[p][u][0], place(plan[p][u][1])[0]) for p in range(peers))))
    order = sorted(range(units), key=lambda u: (len(need[u]), u))
    fetch = list(dict.fromkeys(piece for u in order for piece in need[u]))

    def body(*refs):
        o_ref, rows, tiles, in_sem, out_sem = refs[len(tensors) :]
        copies = {}
        for n, (t, r) in enumerate(fetch):
            source = refs[t].at[0, :, pl.ds(ranges[r][0] * HD, widths[r])]
            target = rows.at[t, :, pl.ds(starts[r], widths[r])]
            copies[t, r] = pltpu.make_async_copy(source, target, in_sem.at[n])
            copies[t, r].start()
        sent = []
        for u in order:
            for piece in need[u]:
                if piece in copies:
                    copies.pop(piece).wait()
            for p in range(peers):
                t, h = plan[p][u]
                at = place(h)[1]
                tiles[p, u] = rows[t, :, at : at + HD]
            sent.append(pltpu.make_async_copy(tiles.at[:, u], o_ref.at[:, u], out_sem.at[u]))
            sent[-1].start()
        for copy in sent:
            copy.wait()

    return pl.pallas_call(
        body,
        in_specs=[pl.BlockSpec(memory_space=pl.ANY)] * len(tensors),
        out_specs=pl.BlockSpec(memory_space=pl.ANY),
        out_shape=jax.ShapeDtypeStruct((peers, units, TOK, HD), jnp.bfloat16),
        scratch_shapes=[
            pltpu.VMEM((len(tensors), TOK, sum(widths)), jnp.bfloat16),
            pltpu.VMEM((peers, units, TOK, HD), jnp.bfloat16),
            pltpu.SemaphoreType.DMA((len(fetch),)),
            pltpu.SemaphoreType.DMA((units,)),
        ],
        compiler_params=WHOLE,
        cost_estimate=cost(0, peers, 2 * units),
    )(*tensors)


def unpack(places, back):
    def body(x_ref, *o_refs):
        for o_ref, place in zip(o_refs, places):
            for h, (p, u) in enumerate(place):
                o_ref[0, :, h * HD : (h + 1) * HD] = x_ref[p, u]

    width = len(places[0]) * HD
    return pl.pallas_call(
        body,
        out_shape=[jax.ShapeDtypeStruct((1, TOK, width), jnp.bfloat16) for _ in places],
        compiler_params=LOCAL,
        cost_estimate=cost(0, 1, 4 * len(places[0])),
    )(back)


def student_kernel(blocks, first, role, arrived):
    def body(first_ref, role_ref, x_ref, o_ref):
        @pl.when(role_ref[0] == 1)
        def _():
            sources = [(x_ref, t) for t in range(3)]
            student_head(range(0, blocks, 2), first_ref[0], sources, o_ref, 0)

    return pl.pallas_call(
        body,
        in_specs=[SMEM, SMEM, VMEM],
        out_specs=VMEM,
        out_shape=jax.ShapeDtypeStruct((blocks, 1, TOK, HD), jnp.bfloat16),
        compiler_params=LOCAL,
        cost_estimate=cost(1, blocks, 4),
    )(first, role, arrived)


def rest_teacher(blocks, clips, role, arrived, offset, gen, shared):
    def body(clip_ref, role_ref, x_ref, gen_ref, shared_ref, o_ref):
        @pl.when(role_ref[0] == 1)
        def _():
            o_ref[...] = gen_ref[...]

        @pl.when(role_ref[0] == 2)
        def _():
            sources = [(x_ref, offset + t) for t in range(2)]
            teacher_head(
                blocks, range(blocks), clip_ref, sources, lambda at: shared_ref[at, 0], o_ref, 0
            )

    return pl.pallas_call(
        body,
        in_specs=[SMEM, SMEM, VMEM, VMEM, VMEM],
        out_specs=VMEM,
        out_shape=jax.ShapeDtypeStruct((blocks, 1, TOK, HD), jnp.bfloat16),
        compiler_params=LOCAL,
        cost_estimate=cost(1, blocks, 5),
    )(clips, role, arrived, gen, shared)


def slots_kernel(full, order, first, clips, where, arrived):
    blocks = len(order)

    def body(first_ref, clip_ref, where_ref, *refs):
        x_refs, o_refs, (x, y) = refs[:blocks], refs[blocks : 2 * blocks], refs[2 * blocks :]
        at = [where_ref[2] ^ d for d in order]
        for i in range(blocks):
            x[at[i]] = x_refs[i][...]

        def head(s, carry):
            sources = [(x, 5 * s + t) for t in range(5)]
            student_head(range(0, blocks, 2), first_ref[0], sources[:3], y, 2 * s)
            gen = lambda at: y[at, 2 * s]
            teacher_whole_head(blocks, clip_ref, sources[3:], gen, y, 2 * s + 1)

        lax.fori_loop(0, full, head, None)
        for i in range(blocks):
            o_refs[i][...] = y[at[i]]

    return pl.pallas_call(
        body,
        in_specs=[SMEM] * 3 + [VMEM] * blocks,
        out_specs=[VMEM] * blocks,
        out_shape=[jax.ShapeDtypeStruct((2 * full, TOK, HD), jnp.bfloat16)] * blocks,
        scratch_shapes=[
            pltpu.VMEM((blocks, 5 * full, TOK, HD), jnp.bfloat16),
            pltpu.VMEM((blocks, 2 * full, TOK, HD), jnp.bfloat16),
        ],
        compiler_params=LOCAL,
        cost_estimate=cost(2 * full, blocks, 7 * full),
    )(first, clips, where, *arrived)


def slots_pack(full, order, where, tensors):
    peers = len(order)

    def body(where_ref, *refs):
        o_refs, (rows, sems) = refs[5 : 5 + peers], refs[5 + peers :]
        copies = []
        for t in range(5):
            source = refs[t].at[0, :, pl.ds(0, full * peers * HD)]
            copies.append(pltpu.make_async_copy(source, rows.at[t], sems.at[t]))
            copies[-1].start()
        for t in range(5):
            copies[t].wait()
            for s in range(full):
                for i, d in enumerate(order):
                    at = pl.multiple_of((s * peers + (where_ref[2] ^ d)) * HD, HD)
                    o_refs[i][5 * s + t] = rows[t, :, pl.ds(at, HD)]

    return pl.pallas_call(
        body,
        in_specs=[SMEM] + [pl.BlockSpec(memory_space=pl.ANY)] * 5,
        out_specs=[VMEM] * peers,
        out_shape=[jax.ShapeDtypeStruct((5 * full, TOK, HD), jnp.bfloat16)] * peers,
        scratch_shapes=[
            pltpu.VMEM((5, TOK, full * peers * HD), jnp.bfloat16),
            pltpu.SemaphoreType.DMA((5,)),
        ],
        compiler_params=WHOLE,
        cost_estimate=cost(0, peers, 10 * full),
    )(where, *tensors)


def rest_pack(base, columns, column, tensors):
    def body(column_ref, *refs):
        rows, sems = refs[-2:]
        copies = []
        for t in range(5):
            source = refs[t].at[0, :, pl.ds(base * HD, columns * HD)]
            copies.append(pltpu.make_async_copy(source, rows.at[t], sems.at[t]))
            copies[-1].start()
        for t in range(5):
            copies[t].wait()
            for s in range(columns):
                at = pl.multiple_of((column_ref[0] ^ s) * HD, HD)
                refs[5 + s][t] = rows[t, :, pl.ds(at, HD)]

    return pl.pallas_call(
        body,
        in_specs=[SMEM] + [pl.BlockSpec(memory_space=pl.ANY)] * 5,
        out_specs=[VMEM] * columns,
        out_shape=[jax.ShapeDtypeStruct((5, TOK, HD), jnp.bfloat16)] * columns,
        scratch_shapes=[
            pltpu.VMEM((5, TOK, columns * HD), jnp.bfloat16),
            pltpu.SemaphoreType.DMA((5,)),
        ],
        compiler_params=WHOLE,
        cost_estimate=cost(0, 1, 10 * columns),
    )(column, *tensors)


def rest_kernel(columns, first, clips, where, own, other):
    blocks = 2 * columns

    def body(first_ref, clip_ref, where_ref, *refs):
        x, gen = refs[-2:]
        column, side = where_ref[0], where_ref[1]
        mine = [2 * (column ^ s) + side for s in range(columns)]
        for s in range(columns):
            x[mine[s]] = refs[s][...]
            x[mine[s] ^ 1] = refs[columns + s][...]
        sources = [(x, t) for t in range(5)]
        student_head(range(0, blocks, 2), first_ref[0], sources[:3], gen, 0)
        at_gen = lambda at: gen[at, 0]
        for s in range(columns):
            o_ref = refs[2 * columns + s]
            o_ref[0:1] = gen[mine[s]]
            teacher_head(blocks, [mine[s]], clip_ref, sources[3:], at_gen, o_ref, None)

    return pl.pallas_call(
        body,
        in_specs=[SMEM] * 3 + [VMEM] * (2 * columns),
        out_specs=[VMEM] * columns,
        out_shape=[jax.ShapeDtypeStruct((2, TOK, HD), jnp.bfloat16)] * columns,
        scratch_shapes=[
            pltpu.VMEM((blocks, 5, TOK, HD), jnp.bfloat16),
            pltpu.VMEM((blocks, 1, TOK, HD), jnp.bfloat16),
        ],
        compiler_params=LOCAL,
        cost_estimate=cost(0, 1, 1),
    )(first, clips, where, *own, *other)


def join(full, order, columns, where, slots, rests):
    peers = len(order)

    def body(where_ref, *refs):
        for i, o_ref in enumerate(refs[peers + columns :]):

            def put(h, tile):
                o_ref[0, :, pl.ds(pl.multiple_of(h * HD, HD), HD)] = tile

            for n, d in enumerate(order):
                for s in range(full):
                    put(s * peers + (where_ref[2] ^ d), refs[n][2 * s + i])
            for s in range(columns):
                put(full * peers + (where_ref[0] ^ s), refs[peers + s][i])

    width = (full * peers + columns) * HD
    return pl.pallas_call(
        body,
        in_specs=[SMEM] + [VMEM] * (peers + columns),
        out_specs=[VMEM] * 2,
        out_shape=[jax.ShapeDtypeStruct((1, TOK, width), jnp.bfloat16)] * 2,
        compiler_params=LOCAL,
        cost_estimate=cost(0, 1, 4 * width // HD),
    )(where, *slots, *rests)


def by_slots_and_columns(tensors, peers, full, rest, first, clips):
    here = lax.axis_index("tm")
    where = jnp.stack([here // 2, here % 2, here]).astype(jnp.int32)

    def swapped(x, by):
        return lax.ppermute(x, "tm", [(i, i ^ by) for i in range(peers)]) if by else x

    order = sorted(range(peers), key=lambda d: (-(d // rest), d % 2, d))

    pieces = rest_pack(full * peers, rest, where[:1], tensors)
    own = [swapped(x, 2 * s) for s, x in enumerate(pieces)]
    packed = slots_pack(full, order, where, tensors)
    packed, own = lax.optimization_barrier((packed, own))
    arrived = [swapped(x, d) for x, d in zip(packed, order)]
    other = [swapped(x, 1) for x in own]
    pieces = rest_kernel(rest, first, clips, where, own, other)
    arrived, pieces = lax.optimization_barrier((arrived, pieces))
    rests = [swapped(x, 2 * s) for s, x in enumerate(pieces)]
    results = slots_kernel(full, order, first, clips, where, arrived)
    results, rests = lax.optimization_barrier((results, rests))
    slots = [swapped(x, d) for x, d in zip(results, order)]
    return tuple(join(full, order, rest, where, slots, rests))


def by_roles(tensors, peers, heads, first, clips):
    here = lax.axis_index("tm")
    role = jnp.where(here < 2 * heads, 1 + here % 2, 0).astype(jnp.int32)[None]
    plan = [
        [(t, min(p // 2, heads - 1)) for t in ((3, 4, 4) if p % 2 else (0, 1, 2))]
        for p in range(peers)
    ]
    arrived = lax.all_to_all(pack(plan, [(0, heads)], tensors), "tm", 0, 0)
    gen = student_kernel(peers, first, role, arrived)
    shared = lax.ppermute(gen, "tm", [(2 * r, 2 * r + 1) for r in range(heads)])
    results = rest_teacher(peers, clips, role, arrived, 0, gen, shared)
    back = lax.all_to_all(results, "tm", 0, 0)
    return tuple(unpack([[(2 * r + i, 0) for r in range(heads)] for i in (0, 1)], back))


def per_device(student_q, student_k, student_v, teacher_q, teacher_k, stagger, clip_lengths):
    heads = student_q.shape[2] // HD
    peers = lax.axis_size("tm")
    full, rest = divmod(heads, peers)
    running = jnp.cumsum(clip_lengths[0])
    block = jnp.arange(peers, dtype=jnp.int32)
    before = running[None, :] <= block[:, None]
    low = jnp.max(jnp.where(before, running[None, :], 0), axis=1)
    high = jnp.min(jnp.where(before, peers, running[None, :]), axis=1)
    large = jnp.where(clip_lengths[0] == peers // 2 + 1, running - clip_lengths[0], 0)
    large = jnp.broadcast_to(jnp.max(large), (peers,))
    clips = jnp.stack([low, high, large]).astype(jnp.int32)
    tensors = (student_q, student_k, student_v, teacher_q, teacher_k)
    if full == 0:
        assert 2 * rest <= peers
        return by_roles(tensors, peers, rest, stagger, clips)
    assert peers == 2 * rest and rest & (rest - 1) == 0
    return by_slots_and_columns(tensors, peers, full, rest, stagger, clips)


def solution(mesh):
    spec = P("seq", "tm", "mp")
    return jax.shard_map(
        per_device,
        mesh=mesh,
        in_specs=(spec,) * 5 + (P("seq"), P("seq", None)),
        out_specs=(spec, spec),
        check_vma=False,
    )
```

profile of v0, /device:TPU:0, one launch (start us, length us, event | category | flops | bytes accessed | tf_op | source)
XLA Modules:
  0.0 124.3 jit_solution(16403319431541958256)
XLA Ops:
  0.6 2.1 %shard_map.87 = (bf16[5,128,128]{2,1,0:T(8,128)(2,1)}, bf16[5,128,128]{2,1,0:T(8,128)(2,1)}, bf16[5,128,128]{2,1,0:T(8,128)(2,1)}, bf16[5,128,128]{2,1,0:T(8,128)(2,1)}) custom-call(s32[1]{0:T(128)} %bitcast.column_ref, bf16[1,128,2560]{2,1,0:T(8,128)(2,1)} %refs_0_.3, bf16[1,128,2560]{2,1,0:T(8,128)(2,1)} %refs_1_.3, bf16[1,128,2560]{2,1,0:T(8,128)(2,1)} %refs_2_.3, ...), custom_call_target="tpu_custom_call" | custom-call | bytes 1310720 | tf_op jit(solution)/shard_map/pallas_call | solution.py:293
  2.7 3.1 %collective-permute-start = (bf16[5,128,128]{2,1,0:T(8,128)(2,1)}, bf16[5,128,128]{2,1,0:T(8,128)(2,1)S(1)}, u32[]{:S(2)}, u32[]{:S(2)}) collective-permute-start(bf16[5,128,128]{2,1,0:T(8,128)(2,1)} %get-tuple-element.71), channel_id=1, source_target_pairs={{0,8},{4,12},{8,0},{12,4},{16,24},{20,28},{24,16},{28,20},{1,9},{5... | collective-permute-start | bytes 491528 | tf_op jit(solution)/shard_map/ppermute | solution.py:370
  5.8 2.6 %collective-permute-start.1 = (bf16[5,128,128]{2,1,0:T(8,128)(2,1)}, bf16[5,128,128]{2,1,0:T(8,128)(2,1)S(1)}, u32[]{:S(2)}, u32[]{:S(2)}) collective-permute-start(bf16[5,128,128]{2,1,0:T(8,128)(2,1)} %get-tuple-element.72), channel_id=1, source_target_pairs={{0,16},{4,20},{8,24},{12,28},{16,0},{20,4},{24,8},{28,12},{1,17},{... | collective-permute-start | bytes 491528 | tf_op jit(solution)/shard_map/ppermute | solution.py:370
  8.4 0.0 collective-permute-start.2
  8.4 0.6 pad_add_fusion.where_ref
  9.0 4.1 %shard_map.86 = (bf16[10,128,128]{2,1,0:T(8,128)(2,1)}, bf16[10,128,128]{2,1,0:T(8,128)(2,1)}, bf16[10,128,128]{2,1,0:T(8,128)(2,1)}, bf16[10,128,128]{2,1,0:T(8...) custom-call(s32[3]{0:T(128)} %pad_add_fusion.where_ref, ...), custom_call_target="tpu_custom_call" | custom-call | bytes 5242880 | tf_op jit(solution)/shard_map/pallas_call | solution.py:265
  13.1 0.0 collective-permute-done.refs_1_
  13.1 7.9 %collective-permute-done.1.refs_2_ = bf16[5,128,128]{2,1,0:T(8,128)(2,1)S(1)} collective-permute-done((bf16[5,128,128]{2,1,0:T(8,128)(2,1)}, bf16[5,128,128]{2,1,0:T(8,128)(2,1)S(1)}, u32[]{:S(2)}, u32[]{:S(2)}) %collective-permute-start.1) | collective-permute-done | bytes 163872 | tf_op jit(solution)/shard_map/ppermute | solution.py:370
  21.1 0.0 collective-permute-done.2.refs_3_
  21.1 0.0 copy-done
  21.1 1.5 %collective-permute-start.10 = (bf16[5,128,128]{2,1,0:T(8,128)(2,1)S(1)}, bf16[5,128,128]{2,1,0:T(8,128)(2,1)S(1)}, u32[]{:S(2)}, u32[]{:S(2)}) collective-permute-start(bf16[5,128,128]{2,1,0:T(8,128)(2,1)S(1)} %copy-done), channel_id=1, source_target_pairs={{0,4},{4,0},{8,12},{12,8},{16,20},{20,16},{24,28},{28,24},{1,5},{5... | collective-permute-start | bytes 491528 | tf_op jit(solution)/shard_map/ppermute | solution.py:370
  22.6 3.7 %collective-permute-start.3 = (bf16[10,128,128]{2,1,0:T(8,128)(2,1)}, bf16[10,128,128]{2,1,0:T(8,128)(2,1)S(1)}, u32[]{:S(2)}, u32[]{:S(2)}) collective-permute-start(bf16[10,128,128]{2,1,0:T(8,128)(2,1)} %get-tuple-element.74), channel_id=1, source_target_pairs={{0,16},{4,20},{8,24},{12,28},{16,0},{20,4},{24,8},{28,12},{1,17},{... | collective-permute-start | bytes 983048 | tf_op jit(solution)/shard_map/ppermute | solution.py:370
  26.2 1.4 %collective-permute-start.4 = (bf16[10,128,128]{2,1,0:T(8,128)(2,1)}, bf16[10,128,128]{2,1,0:T(8,128)(2,1)S(1)}, u32[]{:S(2)}, u32[]{:S(2)}) collective-permute-start(bf16[10,128,128]{2,1,0:T(8,128)(2,1)} %get-tuple-element.75), channel_id=1, source_target_pairs={{0,24},{4,28},{8,16},{12,20},{16,8},{20,12},{24,0},{28,4},{1,25},{... | collective-permute-start | bytes 983048 | tf_op jit(solution)/shard_map/ppermute | solution.py:370
  27.6 0.5 collective-permute-start.11
  28.1 1.5 %collective-permute-start.12 = (bf16[5,128,128]{2,1,0:T(8,128)(2,1)S(1)}, bf16[5,128,128]{2,1,0:T(8,128)(2,1)S(1)}, u32[]{:S(2)}, u32[]{:S(2)}) collective-permute-start(bf16[5,128,128]{2,1,0:T(8,128)(2,1)S(1)} %collective-permute-done.1.refs_2_), channel_id=1, source_target_pairs={{0,4},{4,0},{8,12},{12,8},{16,20},{20,16},{24,28},{28,24},{1,5},{5... | collective-permute-start | bytes 491528 | tf_op jit(solution)/shard_map/ppermute | solution.py:370
  29.6 0.0 collective-permute-done.10.refs_4_
  29.6 0.5 collective-permute-start.13
  30.8 0.0 copy-start.3
  30.8 0.6 copy-done.3
  31.5 0.2 reduce-window.8
  31.6 0.7 fusion
  32.3 0.7 pad.2.clone
  33.0 1.7 %collective-permute-done.11.refs_5_ = bf16[5,128,128]{2,1,0:T(8,128)(2,1)S(1)} collective-permute-done((bf16[5,128,128]{2,1,0:T(8,128)(2,1)S(1)}, bf16[5,128,128]{2,1,0:T(8,128)(2,1)S(1)}, u32[]{:S(2)}, u32[]{:S(2)}) %collective-permute-start.11) | collective-permute-done | bytes 163872 | tf_op jit(solution)/shard_map/ppermute | solution.py:370
  34.7 1.6 %collective-permute-start.5 = (bf16[10,128,128]{2,1,0:T(8,128)(2,1)}, bf16[10,128,128]{2,1,0:T(8,128)(2,1)S(1)}, u32[]{:S(2)}, u32[]{:S(2)}) collective-permute-start(bf16[10,128,128]{2,1,0:T(8,128)(2,1)} %get-tuple-element.76), channel_id=1, source_target_pairs={{0,20},{4,16},{8,28},{12,24},{16,4},{20,0},{24,12},{28,8},{1,21},{... | collective-permute-start | bytes 983048 | tf_op jit(solution)/shard_map/ppermute | solution.py:370
  36.3 0.5 collective-permute-done.12.refs_6_
  36.8 2.6 %collective-permute-start.6 = (bf16[10,128,128]{2,1,0:T(8,128)(2,1)}, bf16[10,128,128]{2,1,0:T(8,128)(2,1)S(1)}, u32[]{:S(2)}, u32[]{:S(2)}) collective-permute-start(bf16[10,128,128]{2,1,0:T(8,128)(2,1)} %get-tuple-element.77), channel_id=1, source_target_pairs={{0,28},{4,24},{8,20},{12,16},{16,12},{20,8},{24,4},{28,0},{1,29},{... | collective-permute-start | bytes 983048 | tf_op jit(solution)/shard_map/ppermute | solution.py:370
  39.4 0.0 collective-permute-done.13.refs_7_
  39.4 0.9 collective-permute-start.7
  40.3 21.8 %collective-permute-done.3.refs_0_ = bf16[10,128,128]{2,1,0:T(8,128)(2,1)S(1)} collective-permute-done((bf16[10,128,128]{2,1,0:T(8,128)(2,1)}, bf16[10,128,128]{2,1,0:T(8,128)(2,1)S(1)}, u32[]{:S(2)}, u32[]{:S(2)}) %collective-permute-start.3) | collective-permute-done | bytes 327712 | tf_op jit(solution)/shard_map/ppermute | solution.py:370
  62.1 0.5 collective-permute-start.8
  62.6 0.0 collective-permute-done.4.refs_1_
  62.6 7.0 %collective-permute-start.9 = (bf16[10,128,128]{2,1,0:T(8,128)(2,1)}, bf16[10,128,128]{2,1,0:T(8,128)(2,1)S(1)}, u32[]{:S(2)}, u32[]{:S(2)}) collective-permute-start(bf16[10,128,128]{2,1,0:T(8,128)(2,1)} %get-tuple-element.81), channel_id=1, source_target_pairs={{0,12},{4,8},{8,4},{12,0},{16,28},{20,24},{24,20},{28,16},{1,13},{... | collective-permute-start | bytes 983048 | tf_op jit(solution)/shard_map/ppermute | solution.py:370
  69.7 0.1 select_reduce_fusion.1
  69.7 0.1 add_add_fusion.clip_ref
  69.8 0.5 copy-done.1
  70.3 3.6 %shard_map.88 = (bf16[2,128,128]{2,1,0:T(8,128)(2,1)S(1)}, bf16[2,128,128]{2,1,0:T(8,128)(2,1)S(1)}, bf16[2,128,128]{2,1,0:T(8,128)(2,1)S(1)}, bf16[2,128,128]{2,1,0:T(8,128)(2,1)S(1)}) custom-call(s32[1]{0:T(128)S(6)} %copy.9.first_ref, s32[3,8]{1,0:T(4,128)S(1)} %add_add_fusion.clip_ref, s32[3]{0:T(128)S(1)} %copy-done.1, ...), custom_call_target="tpu_custom_call" | custom-call | bytes 32768 | tf_op jit(solution)/shard_map/pallas_call | solution.py:325
  73.9 2.3 %collective-permute-done.5.refs_2_ = bf16[10,128,128]{2,1,0:T(8,128)(2,1)S(1)} collective-permute-done((bf16[10,128,128]{2,1,0:T(8,128)(2,1)}, bf16[10,128,128]{2,1,0:T(8,128)(2,1)S(1)}, u32[]{:S(2)}, u32[]{:S(2)}) %collective-permute-start.5) | collective-permute-done | bytes 327712 | tf_op jit(solution)/shard_map/ppermute | solution.py:370
  76.3 0.0 collective-permute-done.6.refs_3_
  76.3 0.0 collective-permute-done.7.refs_5_
  76.3 7.7 %collective-permute-done.8.refs_6_ = bf16[10,128,128]{2,1,0:T(8,128)(2,1)S(1)} collective-permute-done((bf16[10,128,128]{2,1,0:T(8,128)(2,1)}, bf16[10,128,128]{2,1,0:T(8,128)(2,1)S(1)}, u32[]{:S(2)}, u32[]{:S(2)}) %collective-permute-start.8) | collective-permute-done | bytes 327712 | tf_op jit(solution)/shard_map/ppermute | solution.py:370
  84.0 0.0 collective-permute-done.9.refs_7_
  84.0 1.5 %collective-permute-start.14 = (bf16[2,128,128]{2,1,0:T(8,128)(2,1)S(1)}, bf16[2,128,128]{2,1,0:T(8,128)(2,1)S(1)}, u32[]{:S(2)}, u32[]{:S(2)}) collective-permute-start(bf16[2,128,128]{2,1,0:T(8,128)(2,1)S(1)} %get-tuple-element.107), channel_id=1, source_target_pairs={{0,8},{4,12},{8,0},{12,4},{16,24},{20,28},{24,16},{28,20},{1,9},{5... | collective-permute-start | bytes 196616 | tf_op jit(solution)/shard_map/ppermute | solution.py:370
  85.5 0.2 collective-permute-start.15
  85.7 2.7 %collective-permute-start.16 = (bf16[2,128,128]{2,1,0:T(8,128)(2,1)S(1)}, bf16[2,128,128]{2,1,0:T(8,128)(2,1)S(1)}, u32[]{:S(2)}, u32[]{:S(2)}) collective-permute-start(bf16[2,128,128]{2,1,0:T(8,128)(2,1)S(1)} %get-tuple-element.109), channel_id=1, source_target_pairs={{0,24},{4,28},{8,16},{12,20},{16,8},{20,12},{24,0},{28,4},{1,25},{... | collective-permute-start | bytes 196616 | tf_op jit(solution)/shard_map/ppermute | solution.py:370
  88.4 0.0 copy-done.2
  88.4 7.5 %shard_map.89 = (bf16[4,128,128]{2,1,0:T(8,128)(2,1)S(1)}, bf16[4,128,128]{2,1,0:T(8,128)(2,1)S(1)}, bf16[4,128,128]{2,1,0:T(8,128)(2,1)S(1)}, bf16[4,128,128]{2...) custom-call(s32[1]{0:T(128)S(6)} %copy.9.first_ref, ...), custom_call_target="tpu_custom_call" | custom-call | flops 2147483648 | bytes 3670016 | tf_op jit(solution)/shard_map/pallas_call | solution.py:234
  95.9 0.0 collective-permute-done.14.refs_9_
  95.9 0.0 collective-permute-done.15.refs_10_
  95.9 0.0 collective-permute-done.16.refs_11_
  95.9 0.1 collective-permute-start.17
  96.1 2.9 %collective-permute-start.18 = (bf16[4,128,128]{2,1,0:T(8,128)(2,1)S(1)}, bf16[4,128,128]{2,1,0:T(8,128)(2,1)S(1)}, u32[]{:S(2)}, u32[]{:S(2)}) collective-permute-start(bf16[4,128,128]{2,1,0:T(8,128)(2,1)S(1)} %get-tuple-element.111), channel_id=1, source_target_pairs={{0,24},{4,28},{8,16},{12,20},{16,8},{20,12},{24,0},{28,4},{1,25},{... | collective-permute-start | bytes 393224 | tf_op jit(solution)/shard_map/ppermute | solution.py:370
  99.0 0.7 collective-permute-start.19
  99.7 3.1 %collective-permute-start.20 = (bf16[4,128,128]{2,1,0:T(8,128)(2,1)S(1)}, bf16[4,128,128]{2,1,0:T(8,128)(2,1)S(1)}, u32[]{:S(2)}, u32[]{:S(2)}) collective-permute-start(bf16[4,128,128]{2,1,0:T(8,128)(2,1)S(1)} %get-tuple-element.113), channel_id=1, source_target_pairs={{0,28},{4,24},{8,20},{12,16},{16,12},{20,8},{24,4},{28,0},{1,29},{... | collective-permute-start | bytes 393224 | tf_op jit(solution)/shard_map/ppermute | solution.py:370
  102.8 0.6 collective-permute-start.21
  103.4 8.5 %collective-permute-done.17.refs_0_ = bf16[4,128,128]{2,1,0:T(8,128)(2,1)S(1)} collective-permute-done((bf16[4,128,128]{2,1,0:T(8,128)(2,1)S(1)}, bf16[4,128,128]{2,1,0:T(8,128)(2,1)S(1)}, u32[]{:S(2)}, u32[]{:S(2)}) %collective-permute-start.17) | collective-permute-done | bytes 131104 | tf_op jit(solution)/shard_map/ppermute | solution.py:370
  111.9 0.5 collective-permute-start.22
  112.5 0.0 collective-permute-done.18.refs_1_
  112.5 2.8 %collective-permute-start.23 = (bf16[4,128,128]{2,1,0:T(8,128)(2,1)S(1)}, bf16[4,128,128]{2,1,0:T(8,128)(2,1)S(1)}, u32[]{:S(2)}, u32[]{:S(2)}) collective-permute-start(bf16[4,128,128]{2,1,0:T(8,128)(2,1)S(1)} %get-tuple-element.117), channel_id=1, source_target_pairs={{0,12},{4,8},{8,4},{12,0},{16,28},{20,24},{24,20},{28,16},{1,13},{... | collective-permute-start | bytes 393224 | tf_op jit(solution)/shard_map/ppermute | solution.py:370
  115.3 2.3 %collective-permute-done.19.refs_2_ = bf16[4,128,128]{2,1,0:T(8,128)(2,1)S(1)} collective-permute-done((bf16[4,128,128]{2,1,0:T(8,128)(2,1)S(1)}, bf16[4,128,128]{2,1,0:T(8,128)(2,1)S(1)}, u32[]{:S(2)}, u32[]{:S(2)}) %collective-permute-start.19) | collective-permute-done | bytes 131104 | tf_op jit(solution)/shard_map/ppermute | solution.py:370
  117.6 0.0 collective-permute-done.20.refs_3_
  117.6 0.0 collective-permute-done.21.refs_5_
  117.6 4.8 %collective-permute-done.22.refs_6_ = bf16[4,128,128]{2,1,0:T(8,128)(2,1)S(1)} collective-permute-done((bf16[4,128,128]{2,1,0:T(8,128)(2,1)S(1)}, bf16[4,128,128]{2,1,0:T(8,128)(2,1)S(1)}, u32[]{:S(2)}, u32[]{:S(2)}) %collective-permute-start.22) | collective-permute-done | bytes 131104 | tf_op jit(solution)/shard_map/ppermute | solution.py:370
  122.4 0.0 collective-permute-done.23.refs_7_
  122.4 1.8 %shard_map.90 = (bf16[1,128,2560]{2,1,0:T(8,128)(2,1)}, bf16[1,128,2560]{2,1,0:T(8,128)(2,1)}) custom-call(s32[3]{0:T(128)S(1)} %copy-done.1, bf16[4,128,128]{2,1,0:T(8,128)(2,1)S(1)} %collective-permute-done.17.refs_0_, bf16[4,128,128]{2,1,0:T(8,128)(2,1)S(1)} %collective-permute-done.18.refs_1_, bf16[4,128,128]{2,1,0:T(8,128)(2,1)S(1)} %collective-permute-done.19.refs_2_, ...), custom_call_target="tpu_custom_call" | custom-call | bytes 2621440 | tf_op jit(solution)/shard_map/pallas_call | solution.py:355
  (3 shorter events, 0.0 us)
Async XLA Ops:
  2.7 10.4 %collective-permute-start = (bf16[5,128,128]{2,1,0:T(8,128)(2,1)}, bf16[5,128,128]{2,1,0:T(8,128)(2,1)S(1)}, u32[]{:S(2)}, u32[]{:S(2)}) collective-permute-start(bf16[5,128,128]{2,1,0:T(8,128)(2,1)} %get-tuple-element.71), channel_id=1, source_target_pairs={{0,8},{4,12},{8,0},{12,4},{16,24},{20,28},{24,16},{28,20},{1,9},{5... | collective-permute-start | bytes 491528 | tf_op jit(solution)/shard_map/ppermute | solution.py:370
  5.8 15.3 %collective-permute-start.1 = (bf16[5,128,128]{2,1,0:T(8,128)(2,1)}, bf16[5,128,128]{2,1,0:T(8,128)(2,1)S(1)}, u32[]{:S(2)}, u32[]{:S(2)}) collective-permute-start(bf16[5,128,128]{2,1,0:T(8,128)(2,1)} %get-tuple-element.72), channel_id=1, source_target_pairs={{0,16},{4,20},{8,24},{12,28},{16,0},{20,4},{24,8},{28,12},{1,17},{... | collective-permute-start | bytes 491528 | tf_op jit(solution)/shard_map/ppermute | solution.py:370
  8.4 12.7 %collective-permute-start.2 = (bf16[5,128,128]{2,1,0:T(8,128)(2,1)}, bf16[5,128,128]{2,1,0:T(8,128)(2,1)S(1)}, u32[]{:S(2)}, u32[]{:S(2)}) collective-permute-start(bf16[5,128,128]{2,1,0:T(8,128)(2,1)} %get-tuple-element.73), channel_id=1, source_target_pairs={{0,24},{4,28},{8,16},{12,20},{16,8},{20,12},{24,0},{28,4},{1,25},{... | collective-permute-start | bytes 491528 | tf_op jit(solution)/shard_map/ppermute | solution.py:370
  9.0 12.1 %copy-start = (bf16[5,128,128]{2,1,0:T(8,128)(2,1)S(1)}, bf16[5,128,128]{2,1,0:T(8,128)(2,1)}, u32[]{:S(2)}) copy-start(bf16[5,128,128]{2,1,0:T(8,128)(2,1)} %get-tuple-element.82.refs_0_) | copy-start | bytes 491524
  21.1 8.5 %collective-permute-start.10 = (bf16[5,128,128]{2,1,0:T(8,128)(2,1)S(1)}, bf16[5,128,128]{2,1,0:T(8,128)(2,1)S(1)}, u32[]{:S(2)}, u32[]{:S(2)}) collective-permute-start(bf16[5,128,128]{2,1,0:T(8,128)(2,1)S(1)} %copy-done), channel_id=1, source_target_pairs={{0,4},{4,0},{8,12},{12,8},{16,20},{20,16},{24,28},{28,24},{1,5},{5... | collective-permute-start | bytes 491528 | tf_op jit(solution)/shard_map/ppermute | solution.py:370
  22.6 39.5 %collective-permute-start.3 = (bf16[10,128,128]{2,1,0:T(8,128)(2,1)}, bf16[10,128,128]{2,1,0:T(8,128)(2,1)S(1)}, u32[]{:S(2)}, u32[]{:S(2)}) collective-permute-start(bf16[10,128,128]{2,1,0:T(8,128)(2,1)} %get-tuple-element.74), channel_id=1, source_target_pairs={{0,16},{4,20},{8,24},{12,28},{16,0},{20,4},{24,8},{28,12},{1,17},{... | collective-permute-start | bytes 983048 | tf_op jit(solution)/shard_map/ppermute | solution.py:370
  26.2 36.4 %collective-permute-start.4 = (bf16[10,128,128]{2,1,0:T(8,128)(2,1)}, bf16[10,128,128]{2,1,0:T(8,128)(2,1)S(1)}, u32[]{:S(2)}, u32[]{:S(2)}) collective-permute-start(bf16[10,128,128]{2,1,0:T(8,128)(2,1)} %get-tuple-element.75), channel_id=1, source_target_pairs={{0,24},{4,28},{8,16},{12,20},{16,8},{20,12},{24,0},{28,4},{1,25},{... | collective-permute-start | bytes 983048 | tf_op jit(solution)/shard_map/ppermute | solution.py:370
  27.6 7.1 %collective-permute-start.11 = (bf16[5,128,128]{2,1,0:T(8,128)(2,1)S(1)}, bf16[5,128,128]{2,1,0:T(8,128)(2,1)S(1)}, u32[]{:S(2)}, u32[]{:S(2)}) collective-permute-start(bf16[5,128,128]{2,1,0:T(8,128)(2,1)S(1)} %collective-permute-done.refs_1_), channel_id=1, source_target_pairs={{0,4},{4,0},{8,12},{12,8},{16,20},{20,16},{24,28},{28,24},{1,5},{5... | collective-permute-start | bytes 491528 | tf_op jit(solution)/shard_map/ppermute | solution.py:370
  28.1 8.7 %collective-permute-start.12 = (bf16[5,128,128]{2,1,0:T(8,128)(2,1)S(1)}, bf16[5,128,128]{2,1,0:T(8,128)(2,1)S(1)}, u32[]{:S(2)}, u32[]{:S(2)}) collective-permute-start(bf16[5,128,128]{2,1,0:T(8,128)(2,1)S(1)} %collective-permute-done.1.refs_2_), channel_id=1, source_target_pairs={{0,4},{4,0},{8,12},{12,8},{16,20},{20,16},{24,28},{28,24},{1,5},{5... | collective-permute-start | bytes 491528 | tf_op jit(solution)/shard_map/ppermute | solution.py:370
  29.6 9.8 %collective-permute-start.13 = (bf16[5,128,128]{2,1,0:T(8,128)(2,1)S(1)}, bf16[5,128,128]{2,1,0:T(8,128)(2,1)S(1)}, u32[]{:S(2)}, u32[]{:S(2)}) collective-permute-start(bf16[5,128,128]{2,1,0:T(8,128)(2,1)S(1)} %collective-permute-done.2.refs_3_), channel_id=1, source_target_pairs={{0,4},{4,0},{8,12},{12,8},{16,20},{20,16},{24,28},{28,24},{1,5},{5... | collective-permute-start | bytes 491528 | tf_op jit(solution)/shard_map/ppermute | solution.py:370
  30.8 0.7 copy-start.3
  34.7 41.5 %collective-permute-start.5 = (bf16[10,128,128]{2,1,0:T(8,128)(2,1)}, bf16[10,128,128]{2,1,0:T(8,128)(2,1)S(1)}, u32[]{:S(2)}, u32[]{:S(2)}) collective-permute-start(bf16[10,128,128]{2,1,0:T(8,128)(2,1)} %get-tuple-element.76), channel_id=1, source_target_pairs={{0,20},{4,16},{8,28},{12,24},{16,4},{20,0},{24,12},{28,8},{1,21},{... | collective-permute-start | bytes 983048 | tf_op jit(solution)/shard_map/ppermute | solution.py:370
  36.8 39.4 %collective-permute-start.6 = (bf16[10,128,128]{2,1,0:T(8,128)(2,1)}, bf16[10,128,128]{2,1,0:T(8,128)(2,1)S(1)}, u32[]{:S(2)}, u32[]{:S(2)}) collective-permute-start(bf16[10,128,128]{2,1,0:T(8,128)(2,1)} %get-tuple-element.77), channel_id=1, source_target_pairs={{0,28},{4,24},{8,20},{12,16},{16,12},{20,8},{24,4},{28,0},{1,29},{... | collective-permute-start | bytes 983048 | tf_op jit(solution)/shard_map/ppermute | solution.py:370
  39.4 36.8 %collective-permute-start.7 = (bf16[10,128,128]{2,1,0:T(8,128)(2,1)}, bf16[10,128,128]{2,1,0:T(8,128)(2,1)S(1)}, u32[]{:S(2)}, u32[]{:S(2)}) collective-permute-start(bf16[10,128,128]{2,1,0:T(8,128)(2,1)} %get-tuple-element.79), channel_id=1, source_target_pairs={{0,8},{4,12},{8,0},{12,4},{16,24},{20,28},{24,16},{28,20},{1,9},{5... | collective-permute-start | bytes 983048 | tf_op jit(solution)/shard_map/ppermute | solution.py:370
  62.1 21.9 %collective-permute-start.8 = (bf16[10,128,128]{2,1,0:T(8,128)(2,1)}, bf16[10,128,128]{2,1,0:T(8,128)(2,1)S(1)}, u32[]{:S(2)}, u32[]{:S(2)}) collective-permute-start(bf16[10,128,128]{2,1,0:T(8,128)(2,1)} %get-tuple-element.80), channel_id=1, source_target_pairs={{0,4},{4,0},{8,12},{12,8},{16,20},{20,16},{24,28},{28,24},{1,5},{5... | collective-permute-start | bytes 983048 | tf_op jit(solution)/shard_map/ppermute | solution.py:370
  62.6 21.3 %collective-permute-start.9 = (bf16[10,128,128]{2,1,0:T(8,128)(2,1)}, bf16[10,128,128]{2,1,0:T(8,128)(2,1)S(1)}, u32[]{:S(2)}, u32[]{:S(2)}) collective-permute-start(bf16[10,128,128]{2,1,0:T(8,128)(2,1)} %get-tuple-element.81), channel_id=1, source_target_pairs={{0,12},{4,8},{8,4},{12,0},{16,28},{20,24},{24,20},{28,16},{1,13},{... | collective-permute-start | bytes 983048 | tf_op jit(solution)/shard_map/ppermute | solution.py:370
  69.7 0.6 copy-start.1
  70.3 18.1 %copy-start.2 = (bf16[10,128,128]{2,1,0:T(8,128)(2,1)S(1)}, bf16[10,128,128]{2,1,0:T(8,128)(2,1)}, u32[]{:S(2)}) copy-start(bf16[10,128,128]{2,1,0:T(8,128)(2,1)} %get-tuple-element.94.refs_4_) | copy-start | bytes 983044
  84.0 11.9 %collective-permute-start.14 = (bf16[2,128,128]{2,1,0:T(8,128)(2,1)S(1)}, bf16[2,128,128]{2,1,0:T(8,128)(2,1)S(1)}, u32[]{:S(2)}, u32[]{:S(2)}) collective-permute-start(bf16[2,128,128]{2,1,0:T(8,128)(2,1)S(1)} %get-tuple-element.107), channel_id=1, source_target_pairs={{0,8},{4,12},{8,0},{12,4},{16,24},{20,28},{24,16},{28,20},{1,9},{5... | collective-permute-start | bytes 196616 | tf_op jit(solution)/shard_map/ppermute | solution.py:370
  85.5 10.4 %collective-permute-start.15 = (bf16[2,128,128]{2,1,0:T(8,128)(2,1)S(1)}, bf16[2,128,128]{2,1,0:T(8,128)(2,1)S(1)}, u32[]{:S(2)}, u32[]{:S(2)}) collective-permute-start(bf16[2,128,128]{2,1,0:T(8,128)(2,1)S(1)} %get-tuple-element.108), channel_id=1, source_target_pairs={{0,16},{4,20},{8,24},{12,28},{16,0},{20,4},{24,8},{28,12},{1,17},{... | collective-permute-start | bytes 196616 | tf_op jit(solution)/shard_map/ppermute | solution.py:370
  85.7 10.2 %collective-permute-start.16 = (bf16[2,128,128]{2,1,0:T(8,128)(2,1)S(1)}, bf16[2,128,128]{2,1,0:T(8,128)(2,1)S(1)}, u32[]{:S(2)}, u32[]{:S(2)}) collective-permute-start(bf16[2,128,128]{2,1,0:T(8,128)(2,1)S(1)} %get-tuple-element.109), channel_id=1, source_target_pairs={{0,24},{4,28},{8,16},{12,20},{16,8},{20,12},{24,0},{28,4},{1,25},{... | collective-permute-start | bytes 196616 | tf_op jit(solution)/shard_map/ppermute | solution.py:370
  95.9 16.0 %collective-permute-start.17 = (bf16[4,128,128]{2,1,0:T(8,128)(2,1)S(1)}, bf16[4,128,128]{2,1,0:T(8,128)(2,1)S(1)}, u32[]{:S(2)}, u32[]{:S(2)}) collective-permute-start(bf16[4,128,128]{2,1,0:T(8,128)(2,1)S(1)} %get-tuple-element.110), channel_id=1, source_target_pairs={{0,16},{4,20},{8,24},{12,28},{16,0},{20,4},{24,8},{28,12},{1,17},{... | collective-permute-start | bytes 393224 | tf_op jit(solution)/shard_map/ppermute | solution.py:370
  96.1 16.4 %collective-permute-start.18 = (bf16[4,128,128]{2,1,0:T(8,128)(2,1)S(1)}, bf16[4,128,128]{2,1,0:T(8,128)(2,1)S(1)}, u32[]{:S(2)}, u32[]{:S(2)}) collective-permute-start(bf16[4,128,128]{2,1,0:T(8,128)(2,1)S(1)} %get-tuple-element.111), channel_id=1, source_target_pairs={{0,24},{4,28},{8,16},{12,20},{16,8},{20,12},{24,0},{28,4},{1,25},{... | collective-permute-start | bytes 393224 | tf_op jit(solution)/shard_map/ppermute | solution.py:370
  99.0 18.6 %collective-permute-start.19 = (bf16[4,128,128]{2,1,0:T(8,128)(2,1)S(1)}, bf16[4,128,128]{2,1,0:T(8,128)(2,1)S(1)}, u32[]{:S(2)}, u32[]{:S(2)}) collective-permute-start(bf16[4,128,128]{2,1,0:T(8,128)(2,1)S(1)} %get-tuple-element.112), channel_id=1, source_target_pairs={{0,20},{4,16},{8,28},{12,24},{16,4},{20,0},{24,12},{28,8},{1,21},{... | collective-permute-start | bytes 393224 | tf_op jit(solution)/shard_map/ppermute | solution.py:370
  99.7 17.9 %collective-permute-start.20 = (bf16[4,128,128]{2,1,0:T(8,128)(2,1)S(1)}, bf16[4,128,128]{2,1,0:T(8,128)(2,1)S(1)}, u32[]{:S(2)}, u32[]{:S(2)}) collective-permute-start(bf16[4,128,128]{2,1,0:T(8,128)(2,1)S(1)} %get-tuple-element.113), channel_id=1, source_target_pairs={{0,28},{4,24},{8,20},{12,16},{16,12},{20,8},{24,4},{28,0},{1,29},{... | collective-permute-start | bytes 393224 | tf_op jit(solution)/shard_map/ppermute | solution.py:370
  102.8 14.8 %collective-permute-start.21 = (bf16[4,128,128]{2,1,0:T(8,128)(2,1)S(1)}, bf16[4,128,128]{2,1,0:T(8,128)(2,1)S(1)}, u32[]{:S(2)}, u32[]{:S(2)}) collective-permute-start(bf16[4,128,128]{2,1,0:T(8,128)(2,1)S(1)} %get-tuple-element.115), channel_id=1, source_target_pairs={{0,8},{4,12},{8,0},{12,4},{16,24},{20,28},{24,16},{28,20},{1,9},{5... | collective-permute-start | bytes 393224 | tf_op jit(solution)/shard_map/ppermute | solution.py:370
  111.9 10.5 %collective-permute-start.22 = (bf16[4,128,128]{2,1,0:T(8,128)(2,1)S(1)}, bf16[4,128,128]{2,1,0:T(8,128)(2,1)S(1)}, u32[]{:S(2)}, u32[]{:S(2)}) collective-permute-start(bf16[4,128,128]{2,1,0:T(8,128)(2,1)S(1)} %get-tuple-element.116), channel_id=1, source_target_pairs={{0,4},{4,0},{8,12},{12,8},{16,20},{20,16},{24,28},{28,24},{1,5},{5... | collective-permute-start | bytes 393224 | tf_op jit(solution)/shard_map/ppermute | solution.py:370
  112.5 10.0 %collective-permute-start.23 = (bf16[4,128,128]{2,1,0:T(8,128)(2,1)S(1)}, bf16[4,128,128]{2,1,0:T(8,128)(2,1)S(1)}, u32[]{:S(2)}, u32[]{:S(2)}) collective-permute-start(bf16[4,128,128]{2,1,0:T(8,128)(2,1)S(1)} %get-tuple-element.117), channel_id=1, source_target_pairs={{0,12},{4,8},{8,4},{12,0},{16,28},{20,24},{24,20},{28,16},{1,13},{... | collective-permute-start | bytes 393224 | tf_op jit(solution)/shard_map/ppermute | solution.py:370
where the time goes:
time: 124 us
  waiting for transfers between devices  57.7 us (47%)
  starting transfers between devices  42.6 us (34%)
  Pallas kernels  19.2 us (15%)
  local copies, waits for them, and re-layouts  1.86 us (2%)
  other arithmetic  1.55 us (1%)
  between operations  1.4 us (1%)
    ppermute x24, waiting for transfers between devices, swapped(): lax.ppermute(x, 'tm', [(i, i ^ by) for i in range(peers)])  57.7 us
    ppermute x24, starting transfers between devices, swapped(): lax.ppermute(x, 'tm', [(i, i ^ by) for i in range(peers)])  42.6 us
    pallas_call x1, Pallas kernels, slots_kernel(): pl.pallas_call(body, in_specs=[SMEM] * 3 + [VMEM] * blocks, out_specs=[VM...  7.54 us
    pallas_call x1, Pallas kernels, slots_pack(): pl.pallas_call(body, in_specs=[SMEM] + [pl.BlockSpec(memory_space=pl.ANY)...  4.14 us
    pallas_call x1, Pallas kernels, rest_kernel(): pl.pallas_call(body, in_specs=[SMEM] * 3 + [VMEM] * (2 * columns), out_sp...  3.59 us
  transfers between devices with their start and end apart: 24, of which 9 were waited for; matrix products, arithmetic and copies ran while one was open for 2% of the time, Pallas kernels for 12%

commit v1 on v0

--- a/solution.py
+++ b/solution.py
@@ -369,7 +369,9 @@
     def swapped(x, by):
         return lax.ppermute(x, "tm", [(i, i ^ by) for i in range(peers)]) if by else x
 
-    order = sorted(range(peers), key=lambda d: (-(d // rest), d % 2, d))
+    far = sorted(range(rest, peers), key=lambda d: (d % 2, d))
+    near = sorted(range(1, rest), key=lambda d: (d % 2, d))
+    order = [far[0], near[0], far[1], *near[1:], *far[2:], 0]
 
     pieces = rest_pack(full * peers, rest, where[:1], tensors)
     own = [swapped(x, 2 * s) for s, x in enumerate(pieces)]

time: 124 us -> 118 us (0.952)
  starting transfers between devices: 42.6 us -> 38.7 us
  waiting for transfers between devices: 57.7 us -> 55.5 us
    ppermute x24, starting transfers between devices: 42.6 us -> 38.7 us  [swapped(): lax.ppermute(x, 'tm', [(i, i ^ by) for i in range(peers)])]
    ppermute x24, waiting for transfers between devices: 57.7 us -> 55.5 us  [swapped(): lax.ppermute(x, 'tm', [(i, i ^ by) for i in range(peers)])]
  transfers between devices with their start and end apart: 24 -> 24, of which waited for: 9 -> 10; matrix products, arithmetic and copies ran while one was open for 2% -> 2% of each run, Pallas kernels for 12% -> 13%
where the time goes in v1:
time: 118 us
  waiting for transfers between devices  55.5 us (47%)
  starting transfers between devices  38.7 us (33%)
  Pallas kernels  19.2 us (16%)
  local copies, waits for them, and re-layouts  1.86 us (2%)
  other arithmetic  1.55 us (1%)
  between operations  1.42 us (1%)
    ppermute x24, waiting for transfers between devices, swapped(): lax.ppermute(x, 'tm', [(i, i ^ by) for i in range(peers)])  55.5 us
    ppermute x24, starting transfers between devices, swapped(): lax.ppermute(x, 'tm', [(i, i ^ by) for i in range(peers)])  38.7 us
    pallas_call x1, Pallas kernels, slots_kernel(): pl.pallas_call(body, in_specs=[SMEM] * 3 + [VMEM] * blocks, out_specs=[VM...  7.55 us
    pallas_call x1, Pallas kernels, slots_pack(): pl.pallas_call(body, in_specs=[SMEM] + [pl.BlockSpec(memory_space=pl.ANY)...  4.14 us
    pallas_call x1, Pallas kernels, rest_kernel(): pl.pallas_call(body, in_specs=[SMEM] * 3 + [VMEM] * (2 * columns), out_sp...  3.56 us
  transfers between devices with their start and end apart: 24, of which 10 were waited for; matrix products, arithmetic and copies ran while one was open for 2% of the time, Pallas kernels for 13%

profile of v1, /device:TPU:0, one launch (start us, length us, event | category | flops | bytes accessed | tf_op | source)
XLA Modules:
  0.0 118.2 jit_solution(13907341296730609087)
XLA Ops:
  0.6 2.1 %shard_map.87 = (bf16[5,128,128]{2,1,0:T(8,128)(2,1)}, bf16[5,128,128]{2,1,0:T(8,128)(2,1)}, bf16[5,128,128]{2,1,0:T(8,128)(2,1)}, bf16[5,128,128]{2,1,0:T(8,128)(2,1)}) custom-call(s32[1]{0:T(128)} %bitcast.column_ref, bf16[1,128,2560]{2,1,0:T(8,128)(2,1)} %refs_0_.3, bf16[1,128,2560]{2,1,0:T(8,128)(2,1)} %refs_1_.3, bf16[1,128,2560]{2,1,0:T(8,128)(2,1)} %refs_2_.3, ...), custom_call_target="tpu_custom_call" | custom-call | bytes 1310720 | tf_op jit(solution)/shard_map/pallas_call | solution.py:293
  2.7 3.1 %collective-permute-start = (bf16[5,128,128]{2,1,0:T(8,128)(2,1)}, bf16[5,128,128]{2,1,0:T(8,128)(2,1)S(1)}, u32[]{:S(2)}, u32[]{:S(2)}) collective-permute-start(bf16[5,128,128]{2,1,0:T(8,128)(2,1)} %get-tuple-element.71), channel_id=1, source_target_pairs={{0,8},{4,12},{8,0},{12,4},{16,24},{20,28},{24,16},{28,20},{1,9},{5... | collective-permute-start | bytes 491528 | tf_op jit(solution)/shard_map/ppermute | solution.py:370
  5.8 2.6 %collective-permute-start.1 = (bf16[5,128,128]{2,1,0:T(8,128)(2,1)}, bf16[5,128,128]{2,1,0:T(8,128)(2,1)S(1)}, u32[]{:S(2)}, u32[]{:S(2)}) collective-permute-start(bf16[5,128,128]{2,1,0:T(8,128)(2,1)} %get-tuple-element.72), channel_id=1, source_target_pairs={{0,16},{4,20},{8,24},{12,28},{16,0},{20,4},{24,8},{28,12},{1,17},{... | collective-permute-start | bytes 491528 | tf_op jit(solution)/shard_map/ppermute | solution.py:370
  8.4 0.0 collective-permute-start.2
  8.4 0.6 pad_add_fusion.where_ref
  9.0 4.1 %shard_map.86 = (bf16[10,128,128]{2,1,0:T(8,128)(2,1)}, bf16[10,128,128]{2,1,0:T(8,128)(2,1)}, bf16[10,128,128]{2,1,0:T(8,128)(2,1)}, bf16[10,128,128]{2,1,0:T(8...) custom-call(s32[3]{0:T(128)} %pad_add_fusion.where_ref, ...), custom_call_target="tpu_custom_call" | custom-call | bytes 5242880 | tf_op jit(solution)/shard_map/pallas_call | solution.py:265
  13.1 0.0 collective-permute-done.refs_1_
  13.1 7.9 %collective-permute-done.1.refs_2_ = bf16[5,128,128]{2,1,0:T(8,128)(2,1)S(1)} collective-permute-done((bf16[5,128,128]{2,1,0:T(8,128)(2,1)}, bf16[5,128,128]{2,1,0:T(8,128)(2,1)S(1)}, u32[]{:S(2)}, u32[]{:S(2)}) %collective-permute-start.1) | collective-permute-done | bytes 163872 | tf_op jit(solution)/shard_map/ppermute | solution.py:370
  21.1 0.0 collective-permute-done.2.refs_3_
  21.1 0.0 copy-done
  21.1 1.5 %collective-permute-start.10 = (bf16[5,128,128]{2,1,0:T(8,128)(2,1)S(1)}, bf16[5,128,128]{2,1,0:T(8,128)(2,1)S(1)}, u32[]{:S(2)}, u32[]{:S(2)}) collective-permute-start(bf16[5,128,128]{2,1,0:T(8,128)(2,1)S(1)} %copy-done), channel_id=1, source_target_pairs={{0,4},{4,0},{8,12},{12,8},{16,20},{20,16},{24,28},{28,24},{1,5},{5... | collective-permute-start | bytes 491528 | tf_op jit(solution)/shard_map/ppermute | solution.py:370
  22.6 3.7 %collective-permute-start.3 = (bf16[10,128,128]{2,1,0:T(8,128)(2,1)}, bf16[10,128,128]{2,1,0:T(8,128)(2,1)S(1)}, u32[]{:S(2)}, u32[]{:S(2)}) collective-permute-start(bf16[10,128,128]{2,1,0:T(8,128)(2,1)} %get-tuple-element.74), channel_id=1, source_target_pairs={{0,16},{4,20},{8,24},{12,28},{16,0},{20,4},{24,8},{28,12},{1,17},{... | collective-permute-start | bytes 983048 | tf_op jit(solution)/shard_map/ppermute | solution.py:370
  26.2 0.0 collective-permute-start.4
  26.2 0.5 collective-permute-start.11
  26.8 1.5 %collective-permute-start.12 = (bf16[5,128,128]{2,1,0:T(8,128)(2,1)S(1)}, bf16[5,128,128]{2,1,0:T(8,128)(2,1)S(1)}, u32[]{:S(2)}, u32[]{:S(2)}) collective-permute-start(bf16[5,128,128]{2,1,0:T(8,128)(2,1)S(1)} %collective-permute-done.1.refs_2_), channel_id=1, source_target_pairs={{0,4},{4,0},{8,12},{12,8},{16,20},{20,16},{24,28},{28,24},{1,5},{5... | collective-permute-start | bytes 491528 | tf_op jit(solution)/shard_map/ppermute | solution.py:370
  28.3 0.0 collective-permute-done.10.refs_4_
  28.3 0.5 collective-permute-start.13
  29.5 0.0 copy-start.3
  29.5 0.6 copy-done.3
  30.1 0.2 reduce-window.8
  30.3 0.7 fusion
  31.0 0.7 pad.2.clone
  31.7 1.7 %collective-permute-done.11.refs_5_ = bf16[5,128,128]{2,1,0:T(8,128)(2,1)S(1)} collective-permute-done((bf16[5,128,128]{2,1,0:T(8,128)(2,1)S(1)}, bf16[5,128,128]{2,1,0:T(8,128)(2,1)S(1)}, u32[]{:S(2)}, u32[]{:S(2)}) %collective-permute-start.11) | collective-permute-done | bytes 163872 | tf_op jit(solution)/shard_map/ppermute | solution.py:370
  33.4 1.5 %collective-permute-start.5 = (bf16[10,128,128]{2,1,0:T(8,128)(2,1)}, bf16[10,128,128]{2,1,0:T(8,128)(2,1)S(1)}, u32[]{:S(2)}, u32[]{:S(2)}) collective-permute-start(bf16[10,128,128]{2,1,0:T(8,128)(2,1)} %get-tuple-element.76), channel_id=1, source_target_pairs={{0,24},{4,28},{8,16},{12,20},{16,8},{20,12},{24,0},{28,4},{1,25},{... | collective-permute-start | bytes 983048 | tf_op jit(solution)/shard_map/ppermute | solution.py:370
  34.8 2.0 %collective-permute-done.12.refs_6_ = bf16[5,128,128]{2,1,0:T(8,128)(2,1)S(1)} collective-permute-done((bf16[5,128,128]{2,1,0:T(8,128)(2,1)S(1)}, bf16[5,128,128]{2,1,0:T(8,128)(2,1)S(1)}, u32[]{:S(2)}, u32[]{:S(2)}) %collective-permute-start.12) | collective-permute-done | bytes 163872 | tf_op jit(solution)/shard_map/ppermute | solution.py:370
  36.9 0.5 collective-permute-start.6
  37.4 3.0 %collective-permute-done.13.refs_7_ = bf16[5,128,128]{2,1,0:T(8,128)(2,1)S(1)} collective-permute-done((bf16[5,128,128]{2,1,0:T(8,128)(2,1)S(1)}, bf16[5,128,128]{2,1,0:T(8,128)(2,1)S(1)}, u32[]{:S(2)}, u32[]{:S(2)}) %collective-permute-start.13) | collective-permute-done | bytes 163872 | tf_op jit(solution)/shard_map/ppermute | solution.py:370
  40.4 1.9 %collective-permute-start.7 = (bf16[10,128,128]{2,1,0:T(8,128)(2,1)}, bf16[10,128,128]{2,1,0:T(8,128)(2,1)S(1)}, u32[]{:S(2)}, u32[]{:S(2)}) collective-permute-start(bf16[10,128,128]{2,1,0:T(8,128)(2,1)} %get-tuple-element.78), channel_id=1, source_target_pairs={{0,12},{4,8},{8,4},{12,0},{16,28},{20,24},{24,20},{28,16},{1,13},{... | collective-permute-start | bytes 983048 | tf_op jit(solution)/shard_map/ppermute | solution.py:370
  42.4 3.2 %collective-permute-done.3.refs_0_ = bf16[10,128,128]{2,1,0:T(8,128)(2,1)S(1)} collective-permute-done((bf16[10,128,128]{2,1,0:T(8,128)(2,1)}, bf16[10,128,128]{2,1,0:T(8,128)(2,1)S(1)}, u32[]{:S(2)}, u32[]{:S(2)}) %collective-permute-start.3) | collective-permute-done | bytes 327712 | tf_op jit(solution)/shard_map/ppermute | solution.py:370
  45.6 0.0 collective-permute-start.8
  45.6 0.0 collective-permute-done.4.refs_1_
  45.6 2.7 %collective-permute-start.9 = (bf16[10,128,128]{2,1,0:T(8,128)(2,1)}, bf16[10,128,128]{2,1,0:T(8,128)(2,1)S(1)}, u32[]{:S(2)}, u32[]{:S(2)}) collective-permute-start(bf16[10,128,128]{2,1,0:T(8,128)(2,1)} %get-tuple-element.80), channel_id=1, source_target_pairs={{0,28},{4,24},{8,20},{12,16},{16,12},{20,8},{24,4},{28,0},{1,29},{... | collective-permute-start | bytes 983048 | tf_op jit(solution)/shard_map/ppermute | solution.py:370
  48.3 0.1 select_reduce_fusion.1
  48.4 0.1 add_add_fusion.clip_ref
  48.5 0.5 copy-done.1
  49.0 3.6 %shard_map.88 = (bf16[2,128,128]{2,1,0:T(8,128)(2,1)S(1)}, bf16[2,128,128]{2,1,0:T(8,128)(2,1)S(1)}, bf16[2,128,128]{2,1,0:T(8,128)(2,1)S(1)}, bf16[2,128,128]{2,1,0:T(8,128)(2,1)S(1)}) custom-call(s32[1]{0:T(128)S(6)} %copy.9.first_ref, s32[3,8]{1,0:T(4,128)S(1)} %add_add_fusion.clip_ref, s32[3]{0:T(128)S(1)} %copy-done.1, ...), custom_call_target="tpu_custom_call" | custom-call | bytes 32768 | tf_op jit(solution)/shard_map/pallas_call | solution.py:325
  52.5 0.0 collective-permute-done.5.refs_2_
  52.5 0.0 collective-permute-done.6.refs_3_
  52.5 3.3 %collective-permute-done.7.refs_4_ = bf16[10,128,128]{2,1,0:T(8,128)(2,1)S(1)} collective-permute-done((bf16[10,128,128]{2,1,0:T(8,128)(2,1)}, bf16[10,128,128]{2,1,0:T(8,128)(2,1)S(1)}, u32[]{:S(2)}, u32[]{:S(2)}) %collective-permute-start.7) | collective-permute-done | bytes 327712 | tf_op jit(solution)/shard_map/ppermute | solution.py:370
  55.8 20.3 %collective-permute-done.8.refs_5_ = bf16[10,128,128]{2,1,0:T(8,128)(2,1)S(1)} collective-permute-done((bf16[10,128,128]{2,1,0:T(8,128)(2,1)}, bf16[10,128,128]{2,1,0:T(8,128)(2,1)S(1)}, u32[]{:S(2)}, u32[]{:S(2)}) %collective-permute-start.8) | collective-permute-done | bytes 327712 | tf_op jit(solution)/shard_map/ppermute | solution.py:370
  76.1 0.0 collective-permute-done.9.refs_6_
  76.1 6.5 %collective-permute-start.14 = (bf16[2,128,128]{2,1,0:T(8,128)(2,1)S(1)}, bf16[2,128,128]{2,1,0:T(8,128)(2,1)S(1)}, u32[]{:S(2)}, u32[]{:S(2)}) collective-permute-start(bf16[2,128,128]{2,1,0:T(8,128)(2,1)S(1)} %get-tuple-element.107), channel_id=1, source_target_pairs={{0,8},{4,12},{8,0},{12,4},{16,24},{20,28},{24,16},{28,20},{1,9},{5... | collective-permute-start | bytes 196616 | tf_op jit(solution)/shard_map/ppermute | solution.py:370
  82.6 0.0 collective-permute-start.15
  82.7 2.4 %collective-permute-start.16 = (bf16[2,128,128]{2,1,0:T(8,128)(2,1)S(1)}, bf16[2,128,128]{2,1,0:T(8,128)(2,1)S(1)}, u32[]{:S(2)}, u32[]{:S(2)}) collective-permute-start(bf16[2,128,128]{2,1,0:T(8,128)(2,1)S(1)} %get-tuple-element.109), channel_id=1, source_target_pairs={{0,24},{4,28},{8,16},{12,20},{16,8},{20,12},{24,0},{28,4},{1,25},{... | collective-permute-start | bytes 196616 | tf_op jit(solution)/shard_map/ppermute | solution.py:370
  85.0 0.0 copy-done.2
  85.0 7.5 %shard_map.89 = (bf16[4,128,128]{2,1,0:T(8,128)(2,1)S(1)}, bf16[4,128,128]{2,1,0:T(8,128)(2,1)S(1)}, bf16[4,128,128]{2,1,0:T(8,128)(2,1)S(1)}, bf16[4,128,128]{2...) custom-call(s32[1]{0:T(128)S(6)} %copy.9.first_ref, ...), custom_call_target="tpu_custom_call" | custom-call | flops 2147483648 | bytes 3670016 | tf_op jit(solution)/shard_map/pallas_call | solution.py:234
  92.6 0.0 collective-permute-done.14.refs_9_
  92.6 0.0 collective-permute-done.15.refs_10_
  92.6 0.0 collective-permute-done.16.refs_11_
  92.6 0.8 collective-permute-start.17
  93.4 1.2 %collective-permute-start.18 = (bf16[4,128,128]{2,1,0:T(8,128)(2,1)S(1)}, bf16[4,128,128]{2,1,0:T(8,128)(2,1)S(1)}, u32[]{:S(2)}, u32[]{:S(2)}) collective-permute-start(bf16[4,128,128]{2,1,0:T(8,128)(2,1)S(1)} %get-tuple-element.111), channel_id=1, source_target_pairs={{0,8},{4,12},{8,0},{12,4},{16,24},{20,28},{24,16},{28,20},{1,9},{5... | collective-permute-start | bytes 393224 | tf_op jit(solution)/shard_map/ppermute | solution.py:370
  94.7 2.4 %collective-permute-start.19 = (bf16[4,128,128]{2,1,0:T(8,128)(2,1)S(1)}, bf16[4,128,128]{2,1,0:T(8,128)(2,1)S(1)}, u32[]{:S(2)}, u32[]{:S(2)}) collective-permute-start(bf16[4,128,128]{2,1,0:T(8,128)(2,1)S(1)} %get-tuple-element.112), channel_id=1, source_target_pairs={{0,24},{4,28},{8,16},{12,20},{16,8},{20,12},{24,0},{28,4},{1,25},{... | collective-permute-start | bytes 393224 | tf_op jit(solution)/shard_map/ppermute | solution.py:370
  97.1 1.5 %collective-permute-start.20 = (bf16[4,128,128]{2,1,0:T(8,128)(2,1)S(1)}, bf16[4,128,128]{2,1,0:T(8,128)(2,1)S(1)}, u32[]{:S(2)}, u32[]{:S(2)}) collective-permute-start(bf16[4,128,128]{2,1,0:T(8,128)(2,1)S(1)} %get-tuple-element.113), channel_id=1, source_target_pairs={{0,4},{4,0},{8,12},{12,8},{16,20},{20,16},{24,28},{28,24},{1,5},{5... | collective-permute-start | bytes 393224 | tf_op jit(solution)/shard_map/ppermute | solution.py:370
  98.5 0.2 collective-permute-start.21
  98.7 4.1 %collective-permute-done.17.refs_0_ = bf16[4,128,128]{2,1,0:T(8,128)(2,1)S(1)} collective-permute-done((bf16[4,128,128]{2,1,0:T(8,128)(2,1)S(1)}, bf16[4,128,128]{2,1,0:T(8,128)(2,1)S(1)}, u32[]{:S(2)}, u32[]{:S(2)}) %collective-permute-start.17) | collective-permute-done | bytes 131104 | tf_op jit(solution)/shard_map/ppermute | solution.py:370
  102.8 0.5 collective-permute-start.22
  103.3 0.0 collective-permute-done.18.refs_1_
  103.3 3.1 %collective-permute-start.23 = (bf16[4,128,128]{2,1,0:T(8,128)(2,1)S(1)}, bf16[4,128,128]{2,1,0:T(8,128)(2,1)S(1)}, u32[]{:S(2)}, u32[]{:S(2)}) collective-permute-start(bf16[4,128,128]{2,1,0:T(8,128)(2,1)S(1)} %get-tuple-element.116), channel_id=1, source_target_pairs={{0,28},{4,24},{8,20},{12,16},{16,12},{20,8},{24,4},{28,0},{1,29},{... | collective-permute-start | bytes 393224 | tf_op jit(solution)/shard_map/ppermute | solution.py:370
  106.4 0.0 collective-permute-done.19.refs_2_
  106.4 0.0 collective-permute-done.20.refs_3_
  106.4 0.1 collective-permute-done.21.refs_4_
  106.6 9.8 %collective-permute-done.22.refs_5_ = bf16[4,128,128]{2,1,0:T(8,128)(2,1)S(1)} collective-permute-done((bf16[4,128,128]{2,1,0:T(8,128)(2,1)S(1)}, bf16[4,128,128]{2,1,0:T(8,128)(2,1)S(1)}, u32[]{:S(2)}, u32[]{:S(2)}) %collective-permute-start.22) | collective-permute-done | bytes 131104 | tf_op jit(solution)/shard_map/ppermute | solution.py:370
  116.4 0.0 collective-permute-done.23.refs_6_
  116.4 1.8 %shard_map.90 = (bf16[1,128,2560]{2,1,0:T(8,128)(2,1)}, bf16[1,128,2560]{2,1,0:T(8,128)(2,1)}) custom-call(s32[3]{0:T(128)S(1)} %copy-done.1, bf16[4,128,128]{2,1,0:T(8,128)(2,1)S(1)} %collective-permute-done.17.refs_0_, bf16[4,128,128]{2,1,0:T(8,128)(2,1)S(1)} %collective-permute-done.18.refs_1_, bf16[4,128,128]{2,1,0:T(8,128)(2,1)S(1)} %collective-permute-done.19.refs_2_, ...), custom_call_target="tpu_custom_call" | custom-call | bytes 2621440 | tf_op jit(solution)/shard_map/pallas_call | solution.py:355
  (3 shorter events, 0.0 us)
Async XLA Ops:
  2.7 10.4 %collective-permute-start = (bf16[5,128,128]{2,1,0:T(8,128)(2,1)}, bf16[5,128,128]{2,1,0:T(8,128)(2,1)S(1)}, u32[]{:S(2)}, u32[]{:S(2)}) collective-permute-start(bf16[5,128,128]{2,1,0:T(8,128)(2,1)} %get-tuple-element.71), channel_id=1, source_target_pairs={{0,8},{4,12},{8,0},{12,4},{16,24},{20,28},{24,16},{28,20},{1,9},{5... | collective-permute-start | bytes 491528 | tf_op jit(solution)/shard_map/ppermute | solution.py:370
  5.8 15.3 %collective-permute-start.1 = (bf16[5,128,128]{2,1,0:T(8,128)(2,1)}, bf16[5,128,128]{2,1,0:T(8,128)(2,1)S(1)}, u32[]{:S(2)}, u32[]{:S(2)}) collective-permute-start(bf16[5,128,128]{2,1,0:T(8,128)(2,1)} %get-tuple-element.72), channel_id=1, source_target_pairs={{0,16},{4,20},{8,24},{12,28},{16,0},{20,4},{24,8},{28,12},{1,17},{... | collective-permute-start | bytes 491528 | tf_op jit(solution)/shard_map/ppermute | solution.py:370
  8.4 12.7 %collective-permute-start.2 = (bf16[5,128,128]{2,1,0:T(8,128)(2,1)}, bf16[5,128,128]{2,1,0:T(8,128)(2,1)S(1)}, u32[]{:S(2)}, u32[]{:S(2)}) collective-permute-start(bf16[5,128,128]{2,1,0:T(8,128)(2,1)} %get-tuple-element.73), channel_id=1, source_target_pairs={{0,24},{4,28},{8,16},{12,20},{16,8},{20,12},{24,0},{28,4},{1,25},{... | collective-permute-start | bytes 491528 | tf_op jit(solution)/shard_map/ppermute | solution.py:370
  9.0 12.1 %copy-start = (bf16[5,128,128]{2,1,0:T(8,128)(2,1)S(1)}, bf16[5,128,128]{2,1,0:T(8,128)(2,1)}, u32[]{:S(2)}) copy-start(bf16[5,128,128]{2,1,0:T(8,128)(2,1)} %get-tuple-element.82.refs_0_) | copy-start | bytes 491524
  21.1 7.2 %collective-permute-start.10 = (bf16[5,128,128]{2,1,0:T(8,128)(2,1)S(1)}, bf16[5,128,128]{2,1,0:T(8,128)(2,1)S(1)}, u32[]{:S(2)}, u32[]{:S(2)}) collective-permute-start(bf16[5,128,128]{2,1,0:T(8,128)(2,1)S(1)} %copy-done), channel_id=1, source_target_pairs={{0,4},{4,0},{8,12},{12,8},{16,20},{20,16},{24,28},{28,24},{1,5},{5... | collective-permute-start | bytes 491528 | tf_op jit(solution)/shard_map/ppermute | solution.py:370
  22.6 23.0 %collective-permute-start.3 = (bf16[10,128,128]{2,1,0:T(8,128)(2,1)}, bf16[10,128,128]{2,1,0:T(8,128)(2,1)S(1)}, u32[]{:S(2)}, u32[]{:S(2)}) collective-permute-start(bf16[10,128,128]{2,1,0:T(8,128)(2,1)} %get-tuple-element.74), channel_id=1, source_target_pairs={{0,16},{4,20},{8,24},{12,28},{16,0},{20,4},{24,8},{28,12},{1,17},{... | collective-permute-start | bytes 983048 | tf_op jit(solution)/shard_map/ppermute | solution.py:370
  26.2 19.4 %collective-permute-start.4 = (bf16[10,128,128]{2,1,0:T(8,128)(2,1)}, bf16[10,128,128]{2,1,0:T(8,128)(2,1)S(1)}, u32[]{:S(2)}, u32[]{:S(2)}) collective-permute-start(bf16[10,128,128]{2,1,0:T(8,128)(2,1)} %get-tuple-element.75), channel_id=1, source_target_pairs={{0,8},{4,12},{8,0},{12,4},{16,24},{20,28},{24,16},{28,20},{1,9},{5... | collective-permute-start | bytes 983048 | tf_op jit(solution)/shard_map/ppermute | solution.py:370
  26.2 7.1 %collective-permute-start.11 = (bf16[5,128,128]{2,1,0:T(8,128)(2,1)S(1)}, bf16[5,128,128]{2,1,0:T(8,128)(2,1)S(1)}, u32[]{:S(2)}, u32[]{:S(2)}) collective-permute-start(bf16[5,128,128]{2,1,0:T(8,128)(2,1)S(1)} %collective-permute-done.refs_1_), channel_id=1, source_target_pairs={{0,4},{4,0},{8,12},{12,8},{16,20},{20,16},{24,28},{28,24},{1,5},{5... | collective-permute-start | bytes 491528 | tf_op jit(solution)/shard_map/ppermute | solution.py:370
  26.8 10.1 %collective-permute-start.12 = (bf16[5,128,128]{2,1,0:T(8,128)(2,1)S(1)}, bf16[5,128,128]{2,1,0:T(8,128)(2,1)S(1)}, u32[]{:S(2)}, u32[]{:S(2)}) collective-permute-start(bf16[5,128,128]{2,1,0:T(8,128)(2,1)S(1)} %collective-permute-done.1.refs_2_), channel_id=1, source_target_pairs={{0,4},{4,0},{8,12},{12,8},{16,20},{20,16},{24,28},{28,24},{1,5},{5... | collective-permute-start | bytes 491528 | tf_op jit(solution)/shard_map/ppermute | solution.py:370
  28.3 12.2 %collective-permute-start.13 = (bf16[5,128,128]{2,1,0:T(8,128)(2,1)S(1)}, bf16[5,128,128]{2,1,0:T(8,128)(2,1)S(1)}, u32[]{:S(2)}, u32[]{:S(2)}) collective-permute-start(bf16[5,128,128]{2,1,0:T(8,128)(2,1)S(1)} %collective-permute-done.2.refs_3_), channel_id=1, source_target_pairs={{0,4},{4,0},{8,12},{12,8},{16,20},{20,16},{24,28},{28,24},{1,5},{5... | collective-permute-start | bytes 491528 | tf_op jit(solution)/shard_map/ppermute | solution.py:370
  29.5 0.7 copy-start.3
  33.4 19.1 %collective-permute-start.5 = (bf16[10,128,128]{2,1,0:T(8,128)(2,1)}, bf16[10,128,128]{2,1,0:T(8,128)(2,1)S(1)}, u32[]{:S(2)}, u32[]{:S(2)}) collective-permute-start(bf16[10,128,128]{2,1,0:T(8,128)(2,1)} %get-tuple-element.76), channel_id=1, source_target_pairs={{0,24},{4,28},{8,16},{12,20},{16,8},{20,12},{24,0},{28,4},{1,25},{... | collective-permute-start | bytes 983048 | tf_op jit(solution)/shard_map/ppermute | solution.py:370
  36.9 15.6 %collective-permute-start.6 = (bf16[10,128,128]{2,1,0:T(8,128)(2,1)}, bf16[10,128,128]{2,1,0:T(8,128)(2,1)S(1)}, u32[]{:S(2)}, u32[]{:S(2)}) collective-permute-start(bf16[10,128,128]{2,1,0:T(8,128)(2,1)} %get-tuple-element.77), channel_id=1, source_target_pairs={{0,4},{4,0},{8,12},{12,8},{16,20},{20,16},{24,28},{28,24},{1,5},{5... | collective-permute-start | bytes 983048 | tf_op jit(solution)/shard_map/ppermute | solution.py:370
  40.4 15.4 %collective-permute-start.7 = (bf16[10,128,128]{2,1,0:T(8,128)(2,1)}, bf16[10,128,128]{2,1,0:T(8,128)(2,1)S(1)}, u32[]{:S(2)}, u32[]{:S(2)}) collective-permute-start(bf16[10,128,128]{2,1,0:T(8,128)(2,1)} %get-tuple-element.78), channel_id=1, source_target_pairs={{0,12},{4,8},{8,4},{12,0},{16,28},{20,24},{24,20},{28,16},{1,13},{... | collective-permute-start | bytes 983048 | tf_op jit(solution)/shard_map/ppermute | solution.py:370
  45.6 30.5 %collective-permute-start.8 = (bf16[10,128,128]{2,1,0:T(8,128)(2,1)}, bf16[10,128,128]{2,1,0:T(8,128)(2,1)S(1)}, u32[]{:S(2)}, u32[]{:S(2)}) collective-permute-start(bf16[10,128,128]{2,1,0:T(8,128)(2,1)} %get-tuple-element.79), channel_id=1, source_target_pairs={{0,20},{4,16},{8,28},{12,24},{16,4},{20,0},{24,12},{28,8},{1,21},{... | collective-permute-start | bytes 983048 | tf_op jit(solution)/shard_map/ppermute | solution.py:370
  45.6 30.5 %collective-permute-start.9 = (bf16[10,128,128]{2,1,0:T(8,128)(2,1)}, bf16[10,128,128]{2,1,0:T(8,128)(2,1)S(1)}, u32[]{:S(2)}, u32[]{:S(2)}) collective-permute-start(bf16[10,128,128]{2,1,0:T(8,128)(2,1)} %get-tuple-element.80), channel_id=1, source_target_pairs={{0,28},{4,24},{8,20},{12,16},{16,12},{20,8},{24,4},{28,0},{1,29},{... | collective-permute-start | bytes 983048 | tf_op jit(solution)/shard_map/ppermute | solution.py:370
  48.4 0.6 copy-start.1
  49.0 36.1 %copy-start.2 = (bf16[10,128,128]{2,1,0:T(8,128)(2,1)S(1)}, bf16[10,128,128]{2,1,0:T(8,128)(2,1)}, u32[]{:S(2)}) copy-start(bf16[10,128,128]{2,1,0:T(8,128)(2,1)} %get-tuple-element.97.refs_7_) | copy-start | bytes 983044
  76.1 16.5 %collective-permute-start.14 = (bf16[2,128,128]{2,1,0:T(8,128)(2,1)S(1)}, bf16[2,128,128]{2,1,0:T(8,128)(2,1)S(1)}, u32[]{:S(2)}, u32[]{:S(2)}) collective-permute-start(bf16[2,128,128]{2,1,0:T(8,128)(2,1)S(1)} %get-tuple-element.107), channel_id=1, source_target_pairs={{0,8},{4,12},{8,0},{12,4},{16,24},{20,28},{24,16},{28,20},{1,9},{5... | collective-permute-start | bytes 196616 | tf_op jit(solution)/shard_map/ppermute | solution.py:370
  82.6 9.9 %collective-permute-start.15 = (bf16[2,128,128]{2,1,0:T(8,128)(2,1)S(1)}, bf16[2,128,128]{2,1,0:T(8,128)(2,1)S(1)}, u32[]{:S(2)}, u32[]{:S(2)}) collective-permute-start(bf16[2,128,128]{2,1,0:T(8,128)(2,1)S(1)} %get-tuple-element.108), channel_id=1, source_target_pairs={{0,16},{4,20},{8,24},{12,28},{16,0},{20,4},{24,8},{28,12},{1,17},{... | collective-permute-start | bytes 196616 | tf_op jit(solution)/shard_map/ppermute | solution.py:370
  82.7 9.9 %collective-permute-start.16 = (bf16[2,128,128]{2,1,0:T(8,128)(2,1)S(1)}, bf16[2,128,128]{2,1,0:T(8,128)(2,1)S(1)}, u32[]{:S(2)}, u32[]{:S(2)}) collective-permute-start(bf16[2,128,128]{2,1,0:T(8,128)(2,1)S(1)} %get-tuple-element.109), channel_id=1, source_target_pairs={{0,24},{4,28},{8,16},{12,20},{16,8},{20,12},{24,0},{28,4},{1,25},{... | collective-permute-start | bytes 196616 | tf_op jit(solution)/shard_map/ppermute | solution.py:370
  92.6 10.2 %collective-permute-start.17 = (bf16[4,128,128]{2,1,0:T(8,128)(2,1)S(1)}, bf16[4,128,128]{2,1,0:T(8,128)(2,1)S(1)}, u32[]{:S(2)}, u32[]{:S(2)}) collective-permute-start(bf16[4,128,128]{2,1,0:T(8,128)(2,1)S(1)} %get-tuple-element.110), channel_id=1, source_target_pairs={{0,16},{4,20},{8,24},{12,28},{16,0},{20,4},{24,8},{28,12},{1,17},{... | collective-permute-start | bytes 393224 | tf_op jit(solution)/shard_map/ppermute | solution.py:370
  93.4 9.8 %collective-permute-start.18 = (bf16[4,128,128]{2,1,0:T(8,128)(2,1)S(1)}, bf16[4,128,128]{2,1,0:T(8,128)(2,1)S(1)}, u32[]{:S(2)}, u32[]{:S(2)}) collective-permute-start(bf16[4,128,128]{2,1,0:T(8,128)(2,1)S(1)} %get-tuple-element.111), channel_id=1, source_target_pairs={{0,8},{4,12},{8,0},{12,4},{16,24},{20,28},{24,16},{28,20},{1,9},{5... | collective-permute-start | bytes 393224 | tf_op jit(solution)/shard_map/ppermute | solution.py:370
  94.7 11.7 %collective-permute-start.19 = (bf16[4,128,128]{2,1,0:T(8,128)(2,1)S(1)}, bf16[4,128,128]{2,1,0:T(8,128)(2,1)S(1)}, u32[]{:S(2)}, u32[]{:S(2)}) collective-permute-start(bf16[4,128,128]{2,1,0:T(8,128)(2,1)S(1)} %get-tuple-element.112), channel_id=1, source_target_pairs={{0,24},{4,28},{8,16},{12,20},{16,8},{20,12},{24,0},{28,4},{1,25},{... | collective-permute-start | bytes 393224 | tf_op jit(solution)/shard_map/ppermute | solution.py:370
  97.1 9.4 %collective-permute-start.20 = (bf16[4,128,128]{2,1,0:T(8,128)(2,1)S(1)}, bf16[4,128,128]{2,1,0:T(8,128)(2,1)S(1)}, u32[]{:S(2)}, u32[]{:S(2)}) collective-permute-start(bf16[4,128,128]{2,1,0:T(8,128)(2,1)S(1)} %get-tuple-element.113), channel_id=1, source_target_pairs={{0,4},{4,0},{8,12},{12,8},{16,20},{20,16},{24,28},{28,24},{1,5},{5... | collective-permute-start | bytes 393224 | tf_op jit(solution)/shard_map/ppermute | solution.py:370
  98.5 8.0 %collective-permute-start.21 = (bf16[4,128,128]{2,1,0:T(8,128)(2,1)S(1)}, bf16[4,128,128]{2,1,0:T(8,128)(2,1)S(1)}, u32[]{:S(2)}, u32[]{:S(2)}) collective-permute-start(bf16[4,128,128]{2,1,0:T(8,128)(2,1)S(1)} %get-tuple-element.114), channel_id=1, source_target_pairs={{0,12},{4,8},{8,4},{12,0},{16,28},{20,24},{24,20},{28,16},{1,13},{... | collective-permute-start | bytes 393224 | tf_op jit(solution)/shard_map/ppermute | solution.py:370
  102.8 13.6 %collective-permute-start.22 = (bf16[4,128,128]{2,1,0:T(8,128)(2,1)S(1)}, bf16[4,128,128]{2,1,0:T(8,128)(2,1)S(1)}, u32[]{:S(2)}, u32[]{:S(2)}) collective-permute-start(bf16[4,128,128]{2,1,0:T(8,128)(2,1)S(1)} %get-tuple-element.115), channel_id=1, source_target_pairs={{0,20},{4,16},{8,28},{12,24},{16,4},{20,0},{24,12},{28,8},{1,21},{... | collective-permute-start | bytes 393224 | tf_op jit(solution)/shard_map/ppermute | solution.py:370
  103.3 13.1 %collective-permute-start.23 = (bf16[4,128,128]{2,1,0:T(8,128)(2,1)S(1)}, bf16[4,128,128]{2,1,0:T(8,128)(2,1)S(1)}, u32[]{:S(2)}, u32[]{:S(2)}) collective-permute-start(bf16[4,128,128]{2,1,0:T(8,128)(2,1)S(1)} %get-tuple-element.116), channel_id=1, source_target_pairs={{0,28},{4,24},{8,20},{12,16},{16,12},{20,8},{24,4},{28,0},{1,29},{... | collective-permute-start | bytes 393224 | tf_op jit(solution)/shard_map/ppermute | solution.py:370

commit v2 on v1

--- a/solution.py
+++ b/solution.py
@@ -212,14 +212,14 @@
     )(clips, role, arrived, gen, shared)
 
 
-def slots_kernel(full, order, first, clips, where, arrived):
+def slots_kernel(full, order, home, first, clips, where, arrived):
     blocks = len(order)
 
     def body(first_ref, clip_ref, where_ref, *refs):
         x_refs, o_refs, (x, y) = refs[:blocks], refs[blocks : 2 * blocks], refs[2 * blocks :]
         at = [where_ref[2] ^ d for d in order]
         for i in range(blocks):
-            x[at[i]] = x_refs[i][...]
+            x[at[i]] = x_refs[i][0 : 5 * full]
 
         def head(s, carry):
             sources = [(x, 5 * s + t) for t in range(5)]
@@ -228,8 +228,8 @@
             teacher_whole_head(blocks, clip_ref, sources[3:], gen, y, 2 * s + 1)
 
         lax.fori_loop(0, full, head, None)
-        for i in range(blocks):
-            o_refs[i][...] = y[at[i]]
+        for i, d in enumerate(home):
+            o_refs[i][...] = y[where_ref[2] ^ d]
 
     return pl.pallas_call(
         body,
@@ -304,7 +304,7 @@
     )(column, *tensors)
 
 
-def rest_kernel(columns, first, clips, where, own, other):
+def rest_kernel(columns, offset, first, clips, where, own, across):
     blocks = 2 * columns
 
     def body(first_ref, clip_ref, where_ref, *refs):
@@ -313,18 +313,18 @@
         mine = [2 * (column ^ s) + side for s in range(columns)]
         for s in range(columns):
             x[mine[s]] = refs[s][...]
-            x[mine[s] ^ 1] = refs[columns + s][...]
+            x[mine[s] ^ 1] = refs[columns][offset + 5 * s : offset + 5 * s + 5]
         sources = [(x, t) for t in range(5)]
         student_head(range(0, blocks, 2), first_ref[0], sources[:3], gen, 0)
         at_gen = lambda at: gen[at, 0]
         for s in range(columns):
-            o_ref = refs[2 * columns + s]
+            o_ref = refs[columns + 1 + s]
             o_ref[0:1] = gen[mine[s]]
             teacher_head(blocks, [mine[s]], clip_ref, sources[3:], at_gen, o_ref, None)
 
     return pl.pallas_call(
         body,
-        in_specs=[SMEM] * 3 + [VMEM] * (2 * columns),
+        in_specs=[SMEM] * 3 + [VMEM] * (columns + 1),
         out_specs=[VMEM] * columns,
         out_shape=[jax.ShapeDtypeStruct((2, TOK, HD), jnp.bfloat16)] * columns,
         scratch_shapes=[
@@ -333,7 +333,7 @@
         ],
         compiler_params=LOCAL,
         cost_estimate=cost(0, 1, 1),
-    )(first, clips, where, *own, *other)
+    )(first, clips, where, *own, across)
 
 
 def join(full, order, columns, where, slots, rests):
@@ -371,21 +371,23 @@
 
     far = sorted(range(rest, peers), key=lambda d: (d % 2, d))
     near = sorted(range(1, rest), key=lambda d: (d % 2, d))
-    order = [far[0], near[0], far[1], *near[1:], *far[2:], 0]
+    there = [d for d in near if d != 1] + far + [1, 0]
+    home = near[:2] + far + near[2:] + [0]
 
     pieces = rest_pack(full * peers, rest, where[:1], tensors)
     own = [swapped(x, 2 * s) for s, x in enumerate(pieces)]
-    packed = slots_pack(full, order, where, tensors)
-    packed, own = lax.optimization_barrier((packed, own))
-    arrived = [swapped(x, d) for x, d in zip(packed, order)]
-    other = [swapped(x, 1) for x in own]
-    pieces = rest_kernel(rest, first, clips, where, own, other)
-    arrived, pieces = lax.optimization_barrier((arrived, pieces))
+    packed = dict(zip(there, slots_pack(full, there, where, tensors)))
+    arrived = {d: swapped(packed[d], d) for d in there if d != 1}
+    across = jnp.concatenate([packed[1], *own])
+    across, _ = lax.optimization_barrier((across, [arrived[d] for d in near if d != 1]))
+    arrived[1] = swapped(across, 1)
+    pieces = rest_kernel(rest, 5 * full, first, clips, where, own, arrived[1])
+    arrived, pieces = lax.optimization_barrier(([arrived[d] for d in there], pieces))
     rests = [swapped(x, 2 * s) for s, x in enumerate(pieces)]
-    results = slots_kernel(full, order, first, clips, where, arrived)
+    results = slots_kernel(full, there, home, first, clips, where, arrived)
     results, rests = lax.optimization_barrier((results, rests))
-    slots = [swapped(x, d) for x, d in zip(results, order)]
-    return tuple(join(full, order, rest, where, slots, rests))
+    slots = [swapped(x, d) for x, d in zip(results, home)]
+    return tuple(join(full, home, rest, where, slots, rests))
 
 
 def by_roles(tensors, peers, heads, first, clips):

time: 118 us -> 133 us (1.13)
  waiting for transfers between devices: 55.5 us -> 69.2 us
  local copies, waits for them, and re-layouts: 1.86 us -> 5.18 us
  starting transfers between devices: 38.7 us -> 35.4 us
    ppermute x24 -> x20, waiting for transfers between devices: 55.5 us -> 69.2 us  [swapped(): lax.ppermute(x, 'tm', [(i, i ^ by) for i in range(peers)])]
    ppermute x24 -> x20, starting transfers between devices: 38.7 us -> 35.4 us  [swapped(): lax.ppermute(x, 'tm', [(i, i ^ by) for i in range(peers)])]
    unnamed x8 -> x12, local copies, waits for them, and re-layouts: 1.15 us -> 3.79 us
  transfers between devices with their start and end apart: 24 -> 20, of which waited for: 10 -> 8; matrix products, arithmetic and copies ran while one was open for 2% -> 5% of each run, Pallas kernels for 13% -> 12%
where the time goes in v2:
time: 133 us; the launch traced here: 132 us
  waiting for transfers between devices  69.2 us (52%)
  starting transfers between devices  35.4 us (27%)
  Pallas kernels  19.5 us (15%)
  local copies, waits for them, and re-layouts  5.18 us (4%)
  other arithmetic  1.62 us (1%)
  between operations  1.39 us (1%)
    ppermute x20, waiting for transfers between devices, swapped(): lax.ppermute(x, 'tm', [(i, i ^ by) for i in range(peers)])  69.2 us
    ppermute x20, starting transfers between devices, swapped(): lax.ppermute(x, 'tm', [(i, i ^ by) for i in range(peers)])  35.4 us
    pallas_call x1, Pallas kernels, slots_kernel(): pl.pallas_call(body, in_specs=[SMEM] * 3 + [VMEM] * blocks, out_specs=[VM...  7.96 us
    pallas_call x1, Pallas kernels, slots_pack(): pl.pallas_call(body, in_specs=[SMEM] + [pl.BlockSpec(memory_space=pl.ANY)...  4 us
    unnamed x12, local copies, waits for them, and re-layouts  3.79 us
    pallas_call x1, Pallas kernels, rest_kernel(): pl.pallas_call(body, in_specs=[SMEM] * 3 + [VMEM] * (columns + 1), out_sp...  3.59 us
  transfers between devices with their start and end apart: 20, of which 8 were waited for; matrix products, arithmetic and copies ran while one was open for 5% of the time, Pallas kernels for 12%

profile of v2, /device:TPU:0, one launch (start us, length us, event | category | flops | bytes accessed | tf_op | source)
XLA Modules:
  0.0 132.3 jit_solution(17153850871464297990)
XLA Ops:
  0.6 2.1 %shard_map.87 = (bf16[5,128,128]{2,1,0:T(8,128)(2,1)}, bf16[5,128,128]{2,1,0:T(8,128)(2,1)}, bf16[5,128,128]{2,1,0:T(8,128)(2,1)}, bf16[5,128,128]{2,1,0:T(8,128)(2,1)}) custom-call(s32[1]{0:T(128)} %bitcast.column_ref, bf16[1,128,2560]{2,1,0:T(8,128)(2,1)} %refs_0_.3, bf16[1,128,2560]{2,1,0:T(8,128)(2,1)} %refs_1_.3, bf16[1,128,2560]{2,1,0:T(8,128)(2,1)} %refs_2_.3, ...), custom_call_target="tpu_custom_call" | custom-call | bytes 1310720 | tf_op jit(solution)/shard_map/pallas_call | solution.py:293
  2.7 3.1 %collective-permute-start.6 = (bf16[5,128,128]{2,1,0:T(8,128)(2,1)}, bf16[5,128,128]{2,1,0:T(8,128)(2,1)S(1)}, u32[]{:S(2)}, u32[]{:S(2)}) collective-permute-start(bf16[5,128,128]{2,1,0:T(8,128)(2,1)} %get-tuple-element.59), channel_id=1, source_target_pairs={{0,8},{4,12},{8,0},{12,4},{16,24},{20,28},{24,16},{28,20},{1,9},{5... | collective-permute-start | bytes 491528 | tf_op jit(solution)/shard_map/ppermute | solution.py:370
  5.8 2.6 %collective-permute-start.7 = (bf16[5,128,128]{2,1,0:T(8,128)(2,1)}, bf16[5,128,128]{2,1,0:T(8,128)(2,1)S(1)}, u32[]{:S(2)}, u32[]{:S(2)}) collective-permute-start(bf16[5,128,128]{2,1,0:T(8,128)(2,1)} %get-tuple-element.60), channel_id=1, source_target_pairs={{0,16},{4,20},{8,24},{12,28},{16,0},{20,4},{24,8},{28,12},{1,17},{... | collective-permute-start | bytes 491528 | tf_op jit(solution)/shard_map/ppermute | solution.py:370
  8.4 0.0 collective-permute-start.8
  8.4 0.6 pad_add_fusion.where_ref
  9.1 4.0 %shard_map.86 = (bf16[10,128,128]{2,1,0:T(8,128)(2,1)}, bf16[10,128,128]{2,1,0:T(8,128)(2,1)}, bf16[10,128,128]{2,1,0:T(8,128)(2,1)}, bf16[10,128,128]{2,1,0:T(8...) custom-call(s32[3]{0:T(128)} %pad_add_fusion.where_ref, ...), custom_call_target="tpu_custom_call" | custom-call | bytes 5242880 | tf_op jit(solution)/shard_map/pallas_call | solution.py:265
  13.1 1.0 collective-permute-start
  14.0 2.3 %collective-permute-start.1 = (bf16[10,128,128]{2,1,0:T(8,128)(2,1)}, bf16[10,128,128]{2,1,0:T(8,128)(2,1)S(1)}, u32[]{:S(2)}, u32[]{:S(2)}) collective-permute-start(bf16[10,128,128]{2,1,0:T(8,128)(2,1)} %get-tuple-element.52), channel_id=1, source_target_pairs={{0,12},{4,8},{8,4},{12,0},{16,28},{20,24},{24,20},{28,16},{1,13},{... | collective-permute-start | bytes 983048 | tf_op jit(solution)/shard_map/ppermute | solution.py:370
  16.3 0.0 copy-start
  16.3 1.8 %constant_dynamic-update-slice_fusion.4 = bf16[30,128,128]{2,1,0:T(8,128)(2,1)} fusion(bf16[10,128,128]{2,1,0:T(8,128)(2,1)} %get-tuple-element.57), kind=kLoop, calls=%fused_computation.4 | loop fusion | bytes 655360
  18.1 0.0 copy-done
  18.1 0.7 constant_dynamic-update-slice_fusion.3
  18.7 0.0 collective-permute-done.6.refs_1_
  18.7 0.7 constant_dynamic-update-slice_fusion.2
  19.4 1.7 %collective-permute-done.7.refs_2_ = bf16[5,128,128]{2,1,0:T(8,128)(2,1)S(1)} collective-permute-done((bf16[5,128,128]{2,1,0:T(8,128)(2,1)}, bf16[5,128,128]{2,1,0:T(8,128)(2,1)S(1)}, u32[]{:S(2)}, u32[]{:S(2)}) %collective-permute-start.7) | collective-permute-done | bytes 163872 | tf_op jit(solution)/shard_map/ppermute | solution.py:370
  21.1 0.7 constant_dynamic-update-slice_fusion.1
  21.8 0.0 collective-permute-done.8.refs_3_
  21.8 0.7 constant_dynamic-update-slice_fusion
  22.5 4.8 %collective-permute-done.refs_0_ = bf16[10,128,128]{2,1,0:T(8,128)(2,1)S(1)} collective-permute-done((bf16[10,128,128]{2,1,0:T(8,128)(2,1)}, bf16[10,128,128]{2,1,0:T(8,128)(2,1)S(1)}, u32[]{:S(2)}, u32[]{:S(2)}) %collective-permute-start) | collective-permute-done | bytes 327712 | tf_op jit(solution)/shard_map/ppermute | solution.py:370
  27.3 7.0 %collective-permute-done.1.refs_1_ = bf16[10,128,128]{2,1,0:T(8,128)(2,1)S(1)} collective-permute-done((bf16[10,128,128]{2,1,0:T(8,128)(2,1)}, bf16[10,128,128]{2,1,0:T(8,128)(2,1)S(1)}, u32[]{:S(2)}, u32[]{:S(2)}) %collective-permute-start.1) | collective-permute-done | bytes 327712 | tf_op jit(solution)/shard_map/ppermute | solution.py:370
  34.3 0.5 collective-permute-start.9
  34.8 1.0 collective-permute-start.2
  35.9 1.8 %collective-permute-start.3 = (bf16[10,128,128]{2,1,0:T(8,128)(2,1)}, bf16[10,128,128]{2,1,0:T(8,128)(2,1)S(1)}, u32[]{:S(2)}, u32[]{:S(2)}) collective-permute-start(bf16[10,128,128]{2,1,0:T(8,128)(2,1)} %get-tuple-element.54), channel_id=1, source_target_pairs={{0,24},{4,28},{8,16},{12,20},{16,8},{20,12},{24,0},{28,4},{1,25},{... | collective-permute-start | bytes 983048 | tf_op jit(solution)/shard_map/ppermute | solution.py:370
  37.6 3.0 %collective-permute-start.4 = (bf16[10,128,128]{2,1,0:T(8,128)(2,1)}, bf16[10,128,128]{2,1,0:T(8,128)(2,1)S(1)}, u32[]{:S(2)}, u32[]{:S(2)}) collective-permute-start(bf16[10,128,128]{2,1,0:T(8,128)(2,1)} %get-tuple-element.55), channel_id=1, source_target_pairs={{0,20},{4,16},{8,28},{12,24},{16,4},{20,0},{24,12},{28,8},{1,21},{... | collective-permute-start | bytes 983048 | tf_op jit(solution)/shard_map/ppermute | solution.py:370
  40.6 0.0 copy-start.3
  40.6 1.0 collective-permute-start.5
  41.6 0.0 copy-done.3
  41.6 0.2 reduce-window.8
  41.8 0.6 fusion
  42.4 0.7 pad.2.clone
  43.8 0.1 select_reduce_fusion.1
  43.9 0.0 copy-start.1
  43.9 0.1 add_add_fusion.clip_ref
  43.9 0.0 copy-start.2
  43.9 13.3 %collective-permute-done.9.refs_4_.refs_6_ = bf16[30,128,128]{2,1,0:T(8,128)(2,1)S(1)} collective-permute-done((bf16[30,128,128]{2,1,0:T(8,128)(2,1)}, bf16[30,128,128]{2,1,0:T(8,128)(2,1)S(1)}, u32[]{:S(2)}, u32[]{:S(2)}) %collective-permute-start.9) | collective-permute-done | bytes 983072 | tf_op jit(solution)/shard_map/ppermute | solution.py:370
  57.3 0.0 copy-done.1
  57.3 3.6 %shard_map.88 = (bf16[2,128,128]{2,1,0:T(8,128)(2,1)S(1)}, bf16[2,128,128]{2,1,0:T(8,128)(2,1)S(1)}, bf16[2,128,128]{2,1,0:T(8,128)(2,1)S(1)}, bf16[2,128,128]{2,1,0:T(8,128)(2,1)S(1)}) custom-call(s32[1]{0:T(128)S(6)} %copy.13.first_ref, s32[3,8]{1,0:T(4,128)S(1)} %add_add_fusion.clip_ref, s32[3]{0:T(128)S(1)} %copy-done.1, ...), custom_call_target="tpu_custom_call" | custom-call | bytes 32768 | tf_op jit(solution)/shard_map/pallas_call | solution.py:325
  60.9 12.7 %collective-permute-done.2.refs_2_ = bf16[10,128,128]{2,1,0:T(8,128)(2,1)S(1)} collective-permute-done((bf16[10,128,128]{2,1,0:T(8,128)(2,1)}, bf16[10,128,128]{2,1,0:T(8,128)(2,1)S(1)}, u32[]{:S(2)}, u32[]{:S(2)}) %collective-permute-start.2) | collective-permute-done | bytes 327712 | tf_op jit(solution)/shard_map/ppermute | solution.py:370
  73.6 0.0 collective-permute-done.3.refs_3_
  73.6 15.0 %collective-permute-done.4.refs_4_ = bf16[10,128,128]{2,1,0:T(8,128)(2,1)S(1)} collective-permute-done((bf16[10,128,128]{2,1,0:T(8,128)(2,1)}, bf16[10,128,128]{2,1,0:T(8,128)(2,1)S(1)}, u32[]{:S(2)}, u32[]{:S(2)}) %collective-permute-start.4) | collective-permute-done | bytes 327712 | tf_op jit(solution)/shard_map/ppermute | solution.py:370
  88.6 0.0 collective-permute-done.5.refs_5_
  88.6 6.6 %collective-permute-start.10 = (bf16[2,128,128]{2,1,0:T(8,128)(2,1)S(1)}, bf16[2,128,128]{2,1,0:T(8,128)(2,1)S(1)}, u32[]{:S(2)}, u32[]{:S(2)}) collective-permute-start(bf16[2,128,128]{2,1,0:T(8,128)(2,1)S(1)} %get-tuple-element.85), channel_id=1, source_target_pairs={{0,8},{4,12},{8,0},{12,4},{16,24},{20,28},{24,16},{28,20},{1,9},{5... | collective-permute-start | bytes 196616 | tf_op jit(solution)/shard_map/ppermute | solution.py:370
  95.1 0.3 collective-permute-start.11
  95.4 2.1 %collective-permute-start.12 = (bf16[2,128,128]{2,1,0:T(8,128)(2,1)S(1)}, bf16[2,128,128]{2,1,0:T(8,128)(2,1)S(1)}, u32[]{:S(2)}, u32[]{:S(2)}) collective-permute-start(bf16[2,128,128]{2,1,0:T(8,128)(2,1)S(1)} %get-tuple-element.87), channel_id=1, source_target_pairs={{0,24},{4,28},{8,16},{12,20},{16,8},{20,12},{24,0},{28,4},{1,25},{... | collective-permute-start | bytes 196616 | tf_op jit(solution)/shard_map/ppermute | solution.py:370
  97.5 0.0 copy-done.2
  97.5 8.0 %shard_map.89 = (bf16[4,128,128]{2,1,0:T(8,128)(2,1)S(1)}, bf16[4,128,128]{2,1,0:T(8,128)(2,1)S(1)}, bf16[4,128,128]{2,1,0:T(8,128)(2,1)S(1)}, bf16[4,128,128]{2...) custom-call(s32[1]{0:T(128)S(6)} %copy.13.first_ref, ...), custom_call_target="tpu_custom_call" | custom-call | flops 2147483648 | bytes 3670016 | tf_op jit(solution)/shard_map/pallas_call | solution.py:234
  105.5 0.0 collective-permute-done.10.refs_9_
  105.5 0.0 collective-permute-done.11.refs_10_
  105.5 0.0 collective-permute-done.12.refs_11_
  105.5 1.2 collective-permute-start.13
  106.7 0.7 collective-permute-start.14
  107.3 2.0 %collective-permute-start.15 = (bf16[4,128,128]{2,1,0:T(8,128)(2,1)S(1)}, bf16[4,128,128]{2,1,0:T(8,128)(2,1)S(1)}, u32[]{:S(2)}, u32[]{:S(2)}) collective-permute-start(bf16[4,128,128]{2,1,0:T(8,128)(2,1)S(1)} %get-tuple-element.90), channel_id=1, source_target_pairs={{0,16},{4,20},{8,24},{12,28},{16,0},{20,4},{24,8},{28,12},{1,17},{... | collective-permute-start | bytes 393224 | tf_op jit(solution)/shard_map/ppermute | solution.py:370
  109.4 1.5 %collective-permute-start.16 = (bf16[4,128,128]{2,1,0:T(8,128)(2,1)S(1)}, bf16[4,128,128]{2,1,0:T(8,128)(2,1)S(1)}, u32[]{:S(2)}, u32[]{:S(2)}) collective-permute-start(bf16[4,128,128]{2,1,0:T(8,128)(2,1)S(1)} %get-tuple-element.91), channel_id=1, source_target_pairs={{0,24},{4,28},{8,16},{12,20},{16,8},{20,12},{24,0},{28,4},{1,25},{... | collective-permute-start | bytes 393224 | tf_op jit(solution)/shard_map/ppermute | solution.py:370
  110.8 1.1 collective-permute-start.17
  111.9 0.0 collective-permute-done.13.refs_0_
  111.9 2.7 %collective-permute-start.18 = (bf16[4,128,128]{2,1,0:T(8,128)(2,1)S(1)}, bf16[4,128,128]{2,1,0:T(8,128)(2,1)S(1)}, u32[]{:S(2)}, u32[]{:S(2)}) collective-permute-start(bf16[4,128,128]{2,1,0:T(8,128)(2,1)S(1)} %get-tuple-element.93), channel_id=1, source_target_pairs={{0,28},{4,24},{8,20},{12,16},{16,12},{20,8},{24,4},{28,0},{1,29},{... | collective-permute-start | bytes 393224 | tf_op jit(solution)/shard_map/ppermute | solution.py:370
  114.6 0.0 collective-permute-done.14.refs_1_
  114.6 1.2 collective-permute-start.19
  115.8 9.3 %collective-permute-done.15.refs_2_ = bf16[4,128,128]{2,1,0:T(8,128)(2,1)S(1)} collective-permute-done((bf16[4,128,128]{2,1,0:T(8,128)(2,1)S(1)}, bf16[4,128,128]{2,1,0:T(8,128)(2,1)S(1)}, u32[]{:S(2)}, u32[]{:S(2)}) %collective-permute-start.15) | collective-permute-done | bytes 131104 | tf_op jit(solution)/shard_map/ppermute | solution.py:370
  125.1 0.0 collective-permute-done.16.refs_3_
  125.1 5.3 %collective-permute-done.17.refs_4_ = bf16[4,128,128]{2,1,0:T(8,128)(2,1)S(1)} collective-permute-done((bf16[4,128,128]{2,1,0:T(8,128)(2,1)S(1)}, bf16[4,128,128]{2,1,0:T(8,128)(2,1)S(1)}, u32[]{:S(2)}, u32[]{:S(2)}) %collective-permute-start.17) | collective-permute-done | bytes 131104 | tf_op jit(solution)/shard_map/ppermute | solution.py:370
  130.4 0.0 collective-permute-done.18.refs_5_
  130.4 0.0 collective-permute-done.19.refs_6_
  130.4 1.8 %shard_map.90 = (bf16[1,128,2560]{2,1,0:T(8,128)(2,1)}, bf16[1,128,2560]{2,1,0:T(8,128)(2,1)}) custom-call(s32[3]{0:T(128)S(1)} %copy-done.1, bf16[4,128,128]{2,1,0:T(8,128)(2,1)S(1)} %collective-permute-done.13.refs_0_, bf16[4,128,128]{2,1,0:T(8,128)(2,1)S(1)} %collective-permute-done.14.refs_1_, bf16[4,128,128]{2,1,0:T(8,128)(2,1)S(1)} %collective-permute-done.15.refs_2_, ...), custom_call_target="tpu_custom_call" | custom-call | bytes 2621440 | tf_op jit(solution)/shard_map/pallas_call | solution.py:355
Async XLA Ops:
  2.7 16.0 %collective-permute-start.6 = (bf16[5,128,128]{2,1,0:T(8,128)(2,1)}, bf16[5,128,128]{2,1,0:T(8,128)(2,1)S(1)}, u32[]{:S(2)}, u32[]{:S(2)}) collective-permute-start(bf16[5,128,128]{2,1,0:T(8,128)(2,1)} %get-tuple-element.59), channel_id=1, source_target_pairs={{0,8},{4,12},{8,0},{12,4},{16,24},{20,28},{24,16},{28,20},{1,9},{5... | collective-permute-start | bytes 491528 | tf_op jit(solution)/shard_map/ppermute | solution.py:370
  5.8 15.3 %collective-permute-start.7 = (bf16[5,128,128]{2,1,0:T(8,128)(2,1)}, bf16[5,128,128]{2,1,0:T(8,128)(2,1)S(1)}, u32[]{:S(2)}, u32[]{:S(2)}) collective-permute-start(bf16[5,128,128]{2,1,0:T(8,128)(2,1)} %get-tuple-element.60), channel_id=1, source_target_pairs={{0,16},{4,20},{8,24},{12,28},{16,0},{20,4},{24,8},{28,12},{1,17},{... | collective-permute-start | bytes 491528 | tf_op jit(solution)/shard_map/ppermute | solution.py:370
  8.4 13.4 %collective-permute-start.8 = (bf16[5,128,128]{2,1,0:T(8,128)(2,1)}, bf16[5,128,128]{2,1,0:T(8,128)(2,1)S(1)}, u32[]{:S(2)}, u32[]{:S(2)}) collective-permute-start(bf16[5,128,128]{2,1,0:T(8,128)(2,1)} %get-tuple-element.61), channel_id=1, source_target_pairs={{0,24},{4,28},{8,16},{12,20},{16,8},{20,12},{24,0},{28,4},{1,25},{... | collective-permute-start | bytes 491528 | tf_op jit(solution)/shard_map/ppermute | solution.py:370
  13.1 14.2 %collective-permute-start = (bf16[10,128,128]{2,1,0:T(8,128)(2,1)}, bf16[10,128,128]{2,1,0:T(8,128)(2,1)S(1)}, u32[]{:S(2)}, u32[]{:S(2)}) collective-permute-start(bf16[10,128,128]{2,1,0:T(8,128)(2,1)} %get-tuple-element.51), channel_id=1, source_target_pairs={{0,8},{4,12},{8,0},{12,4},{16,24},{20,28},{24,16},{28,20},{1,9},{5... | collective-permute-start | bytes 983048 | tf_op jit(solution)/shard_map/ppermute | solution.py:370
  14.0 20.3 %collective-permute-start.1 = (bf16[10,128,128]{2,1,0:T(8,128)(2,1)}, bf16[10,128,128]{2,1,0:T(8,128)(2,1)S(1)}, u32[]{:S(2)}, u32[]{:S(2)}) collective-permute-start(bf16[10,128,128]{2,1,0:T(8,128)(2,1)} %get-tuple-element.52), channel_id=1, source_target_pairs={{0,12},{4,8},{8,4},{12,0},{16,28},{20,24},{24,20},{28,16},{1,13},{... | collective-permute-start | bytes 983048 | tf_op jit(solution)/shard_map/ppermute | solution.py:370
  16.3 1.8 %copy-start = (bf16[5,128,128]{2,1,0:T(8,128)(2,1)S(1)}, bf16[5,128,128]{2,1,0:T(8,128)(2,1)}, u32[]{:S(2)}) copy-start(bf16[5,128,128]{2,1,0:T(8,128)(2,1)} %get-tuple-element.58.refs_0_) | copy-start | bytes 491524
  34.3 23.0 %collective-permute-start.9 = (bf16[30,128,128]{2,1,0:T(8,128)(2,1)}, bf16[30,128,128]{2,1,0:T(8,128)(2,1)S(1)}, u32[]{:S(2)}, u32[]{:S(2)}) collective-permute-start(bf16[30,128,128]{2,1,0:T(8,128)(2,1)} %constant_dynamic-update-slice_fusion), channel_id=1, source_target_pairs={{0,4},{4,0},{8,12},{12,8},{16,20},{20,16},{24,28},{28,24},{1,5},{5... | collective-permute-start | bytes 2949128 | tf_op jit(solution)/shard_map/ppermute | solution.py:370
  34.8 38.7 %collective-permute-start.2 = (bf16[10,128,128]{2,1,0:T(8,128)(2,1)}, bf16[10,128,128]{2,1,0:T(8,128)(2,1)S(1)}, u32[]{:S(2)}, u32[]{:S(2)}) collective-permute-start(bf16[10,128,128]{2,1,0:T(8,128)(2,1)} %get-tuple-element.53), channel_id=1, source_target_pairs={{0,16},{4,20},{8,24},{12,28},{16,0},{20,4},{24,8},{28,12},{1,17},{... | collective-permute-start | bytes 983048 | tf_op jit(solution)/shard_map/ppermute | solution.py:370
  35.9 37.7 %collective-permute-start.3 = (bf16[10,128,128]{2,1,0:T(8,128)(2,1)}, bf16[10,128,128]{2,1,0:T(8,128)(2,1)S(1)}, u32[]{:S(2)}, u32[]{:S(2)}) collective-permute-start(bf16[10,128,128]{2,1,0:T(8,128)(2,1)} %get-tuple-element.54), channel_id=1, source_target_pairs={{0,24},{4,28},{8,16},{12,20},{16,8},{20,12},{24,0},{28,4},{1,25},{... | collective-permute-start | bytes 983048 | tf_op jit(solution)/shard_map/ppermute | solution.py:370
  37.6 50.9 %collective-permute-start.4 = (bf16[10,128,128]{2,1,0:T(8,128)(2,1)}, bf16[10,128,128]{2,1,0:T(8,128)(2,1)S(1)}, u32[]{:S(2)}, u32[]{:S(2)}) collective-permute-start(bf16[10,128,128]{2,1,0:T(8,128)(2,1)} %get-tuple-element.55), channel_id=1, source_target_pairs={{0,20},{4,16},{8,28},{12,24},{16,4},{20,0},{24,12},{28,8},{1,21},{... | collective-permute-start | bytes 983048 | tf_op jit(solution)/shard_map/ppermute | solution.py:370
  40.6 1.0 copy-start.3
  40.6 48.0 %collective-permute-start.5 = (bf16[10,128,128]{2,1,0:T(8,128)(2,1)}, bf16[10,128,128]{2,1,0:T(8,128)(2,1)}, u32[]{:S(2)}, u32[]{:S(2)}) collective-permute-start(bf16[10,128,128]{2,1,0:T(8,128)(2,1)} %get-tuple-element.56), channel_id=1, source_target_pairs={{0,28},{4,24},{8,20},{12,16},{16,12},{20,8},{24,4},{28,0},{1,29},{... | collective-permute-start | bytes 983048 | tf_op jit(solution)/shard_map/ppermute | solution.py:370
  43.9 13.4 %copy-start.1 = (s32[3]{0:T(128)S(1)}, s32[3]{0:T(128)}, u32[]{:S(2)}) copy-start(s32[3]{0:T(128)} %pad_add_fusion.where_ref) | copy-start | bytes 40
  43.9 53.6 %copy-start.2 = (bf16[10,128,128]{2,1,0:T(8,128)(2,1)S(1)}, bf16[10,128,128]{2,1,0:T(8,128)(2,1)}, u32[]{:S(2)}) copy-start(bf16[10,128,128]{2,1,0:T(8,128)(2,1)} %get-tuple-element.75.refs_7_) | copy-start | bytes 983044
  88.6 16.9 %collective-permute-start.10 = (bf16[2,128,128]{2,1,0:T(8,128)(2,1)S(1)}, bf16[2,128,128]{2,1,0:T(8,128)(2,1)S(1)}, u32[]{:S(2)}, u32[]{:S(2)}) collective-permute-start(bf16[2,128,128]{2,1,0:T(8,128)(2,1)S(1)} %get-tuple-element.85), channel_id=1, source_target_pairs={{0,8},{4,12},{8,0},{12,4},{16,24},{20,28},{24,16},{28,20},{1,9},{5... | collective-permute-start | bytes 196616 | tf_op jit(solution)/shard_map/ppermute | solution.py:370
  95.1 10.3 %collective-permute-start.11 = (bf16[2,128,128]{2,1,0:T(8,128)(2,1)S(1)}, bf16[2,128,128]{2,1,0:T(8,128)(2,1)S(1)}, u32[]{:S(2)}, u32[]{:S(2)}) collective-permute-start(bf16[2,128,128]{2,1,0:T(8,128)(2,1)S(1)} %get-tuple-element.86), channel_id=1, source_target_pairs={{0,16},{4,20},{8,24},{12,28},{16,0},{20,4},{24,8},{28,12},{1,17},{... | collective-permute-start | bytes 196616 | tf_op jit(solution)/shard_map/ppermute | solution.py:370
  95.4 10.1 %collective-permute-start.12 = (bf16[2,128,128]{2,1,0:T(8,128)(2,1)S(1)}, bf16[2,128,128]{2,1,0:T(8,128)(2,1)S(1)}, u32[]{:S(2)}, u32[]{:S(2)}) collective-permute-start(bf16[2,128,128]{2,1,0:T(8,128)(2,1)S(1)} %get-tuple-element.87), channel_id=1, source_target_pairs={{0,24},{4,28},{8,16},{12,20},{16,8},{20,12},{24,0},{28,4},{1,25},{... | collective-permute-start | bytes 196616 | tf_op jit(solution)/shard_map/ppermute | solution.py:370
  105.5 6.4 %collective-permute-start.13 = (bf16[4,128,128]{2,1,0:T(8,128)(2,1)S(1)}, bf16[4,128,128]{2,1,0:T(8,128)(2,1)S(1)}, u32[]{:S(2)}, u32[]{:S(2)}) collective-permute-start(bf16[4,128,128]{2,1,0:T(8,128)(2,1)S(1)} %get-tuple-element.88), channel_id=1, source_target_pairs={{0,8},{4,12},{8,0},{12,4},{16,24},{20,28},{24,16},{28,20},{1,9},{5... | collective-permute-start | bytes 393224 | tf_op jit(solution)/shard_map/ppermute | solution.py:370
  106.7 7.9 %collective-permute-start.14 = (bf16[4,128,128]{2,1,0:T(8,128)(2,1)S(1)}, bf16[4,128,128]{2,1,0:T(8,128)(2,1)S(1)}, u32[]{:S(2)}, u32[]{:S(2)}) collective-permute-start(bf16[4,128,128]{2,1,0:T(8,128)(2,1)S(1)} %get-tuple-element.89), channel_id=1, source_target_pairs={{0,4},{4,0},{8,12},{12,8},{16,20},{20,16},{24,28},{28,24},{1,5},{5... | collective-permute-start | bytes 393224 | tf_op jit(solution)/shard_map/ppermute | solution.py:370
  107.3 17.8 %collective-permute-start.15 = (bf16[4,128,128]{2,1,0:T(8,128)(2,1)S(1)}, bf16[4,128,128]{2,1,0:T(8,128)(2,1)S(1)}, u32[]{:S(2)}, u32[]{:S(2)}) collective-permute-start(bf16[4,128,128]{2,1,0:T(8,128)(2,1)S(1)} %get-tuple-element.90), channel_id=1, source_target_pairs={{0,16},{4,20},{8,24},{12,28},{16,0},{20,4},{24,8},{28,12},{1,17},{... | collective-permute-start | bytes 393224 | tf_op jit(solution)/shard_map/ppermute | solution.py:370
  109.4 15.8 %collective-permute-start.16 = (bf16[4,128,128]{2,1,0:T(8,128)(2,1)S(1)}, bf16[4,128,128]{2,1,0:T(8,128)(2,1)S(1)}, u32[]{:S(2)}, u32[]{:S(2)}) collective-permute-start(bf16[4,128,128]{2,1,0:T(8,128)(2,1)S(1)} %get-tuple-element.91), channel_id=1, source_target_pairs={{0,24},{4,28},{8,16},{12,20},{16,8},{20,12},{24,0},{28,4},{1,25},{... | collective-permute-start | bytes 393224 | tf_op jit(solution)/shard_map/ppermute | solution.py:370
  110.8 19.6 %collective-permute-start.17 = (bf16[4,128,128]{2,1,0:T(8,128)(2,1)S(1)}, bf16[4,128,128]{2,1,0:T(8,128)(2,1)S(1)}, u32[]{:S(2)}, u32[]{:S(2)}) collective-permute-start(bf16[4,128,128]{2,1,0:T(8,128)(2,1)S(1)} %get-tuple-element.92), channel_id=1, source_target_pairs={{0,20},{4,16},{8,28},{12,24},{16,4},{20,0},{24,12},{28,8},{1,21},{... | collective-permute-start | bytes 393224 | tf_op jit(solution)/shard_map/ppermute | solution.py:370
  111.9 18.5 %collective-permute-start.18 = (bf16[4,128,128]{2,1,0:T(8,128)(2,1)S(1)}, bf16[4,128,128]{2,1,0:T(8,128)(2,1)S(1)}, u32[]{:S(2)}, u32[]{:S(2)}) collective-permute-start(bf16[4,128,128]{2,1,0:T(8,128)(2,1)S(1)} %get-tuple-element.93), channel_id=1, source_target_pairs={{0,28},{4,24},{8,20},{12,16},{16,12},{20,8},{24,4},{28,0},{1,29},{... | collective-permute-start | bytes 393224 | tf_op jit(solution)/shard_map/ppermute | solution.py:370
  114.6 15.8 %collective-permute-start.19 = (bf16[4,128,128]{2,1,0:T(8,128)(2,1)S(1)}, bf16[4,128,128]{2,1,0:T(8,128)(2,1)S(1)}, u32[]{:S(2)}, u32[]{:S(2)}) collective-permute-start(bf16[4,128,128]{2,1,0:T(8,128)(2,1)S(1)} %get-tuple-element.94), channel_id=1, source_target_pairs={{0,12},{4,8},{8,4},{12,0},{16,28},{20,24},{24,20},{28,16},{1,13},{... | collective-permute-start | bytes 393224 | tf_op jit(solution)/shard_map/ppermute | solution.py:370

commit v3 on v1

--- a/solution.py
+++ b/solution.py
@@ -212,7 +212,7 @@
     )(clips, role, arrived, gen, shared)
 
 
-def slots_kernel(full, order, first, clips, where, arrived):
+def slots_kernel(full, order, home, first, clips, where, arrived):
     blocks = len(order)
 
     def body(first_ref, clip_ref, where_ref, *refs):
@@ -228,8 +228,8 @@
             teacher_whole_head(blocks, clip_ref, sources[3:], gen, y, 2 * s + 1)
 
         lax.fori_loop(0, full, head, None)
-        for i in range(blocks):
-            o_refs[i][...] = y[at[i]]
+        for i, d in enumerate(home):
+            o_refs[i][...] = y[where_ref[2] ^ d]
 
     return pl.pallas_call(
         body,
@@ -369,23 +369,23 @@
     def swapped(x, by):
         return lax.ppermute(x, "tm", [(i, i ^ by) for i in range(peers)]) if by else x
 
-    far = sorted(range(rest, peers), key=lambda d: (d % 2, d))
+    far = list(range(rest, peers))
     near = sorted(range(1, rest), key=lambda d: (d % 2, d))
-    order = [far[0], near[0], far[1], *near[1:], *far[2:], 0]
+    there = [far[0], near[0], far[1], *near[1:], *far[2:], 0]
+    home = [*range(1, peers), 0]
 
     pieces = rest_pack(full * peers, rest, where[:1], tensors)
     own = [swapped(x, 2 * s) for s, x in enumerate(pieces)]
-    packed = slots_pack(full, order, where, tensors)
-    packed, own = lax.optimization_barrier((packed, own))
-    arrived = [swapped(x, d) for x, d in zip(packed, order)]
+    packed = slots_pack(full, there, where, tensors)
+    arrived = [swapped(x, d) for x, d in zip(packed, there)]
     other = [swapped(x, 1) for x in own]
     pieces = rest_kernel(rest, first, clips, where, own, other)
     arrived, pieces = lax.optimization_barrier((arrived, pieces))
     rests = [swapped(x, 2 * s) for s, x in enumerate(pieces)]
-    results = slots_kernel(full, order, first, clips, where, arrived)
+    results = slots_kernel(full, there, home, first, clips, where, arrived)
     results, rests = lax.optimization_barrier((results, rests))
-    slots = [swapped(x, d) for x, d in zip(results, order)]
-    return tuple(join(full, order, rest, where, slots, rests))
+    slots = [swapped(x, d) for x, d in zip(results, home)]
+    return tuple(join(full, home, rest, where, slots, rests))
 
 
 def by_roles(tensors, peers, heads, first, clips):

time: 118 us -> 118 us (level); the launches traced: 118 us -> 116 us
  waiting for transfers between devices: 55.5 us -> 29.2 us
  starting transfers between devices: 38.7 us -> 63.3 us
    ppermute x24, waiting for transfers between devices: 55.5 us -> 29.2 us  [swapped(): lax.ppermute(x, 'tm', [(i, i ^ by) for i in range(peers)])]
    ppermute x24, starting transfers between devices: 38.7 us -> 63.3 us  [swapped(): lax.ppermute(x, 'tm', [(i, i ^ by) for i in range(peers)])]
  transfers between devices with their start and end apart: 24 -> 24, of which waited for: 10 -> 5; matrix products, arithmetic and copies ran while one was open for 2% -> 2% of each run, Pallas kernels for 13% -> 13%
where the time goes in v3:
time: 118 us; the launch traced here: 116 us
  starting transfers between devices  63.3 us (54%)
  waiting for transfers between devices  29.2 us (25%)
  Pallas kernels  19.2 us (16%)
  local copies, waits for them, and re-layouts  1.85 us (2%)
  other arithmetic  1.57 us (1%)
  between operations  1.41 us (1%)
    ppermute x24, starting transfers between devices, swapped(): lax.ppermute(x, 'tm', [(i, i ^ by) for i in range(peers)])  63.3 us
    ppermute x24, waiting for transfers between devices, swapped(): lax.ppermute(x, 'tm', [(i, i ^ by) for i in range(peers)])  29.2 us
    pallas_call x1, Pallas kernels, slots_kernel(): pl.pallas_call(body, in_specs=[SMEM] * 3 + [VMEM] * blocks, out_specs=[VM...  7.54 us
    pallas_call x1, Pallas kernels, slots_pack(): pl.pallas_call(body, in_specs=[SMEM] + [pl.BlockSpec(memory_space=pl.ANY)...  4.14 us
    pallas_call x1, Pallas kernels, rest_kernel(): pl.pallas_call(body, in_specs=[SMEM] * 3 + [VMEM] * (2 * columns), out_sp...  3.58 us
  transfers between devices with their start and end apart: 24, of which 5 were waited for; matrix products, arithmetic and copies ran while one was open for 2% of the time, Pallas kernels for 13%

profile of v3, /device:TPU:0, one launch (start us, length us, event | category | flops | bytes accessed | tf_op | source)
XLA Modules:
  0.0 116.4 jit_solution(1918822683179952912)
XLA Ops:
  0.6 2.1 %shard_map.87 = (bf16[5,128,128]{2,1,0:T(8,128)(2,1)}, bf16[5,128,128]{2,1,0:T(8,128)(2,1)}, bf16[5,128,128]{2,1,0:T(8,128)(2,1)}, bf16[5,128,128]{2,1,0:T(8,128)(2,1)}) custom-call(s32[1]{0:T(128)} %bitcast.column_ref, bf16[1,128,2560]{2,1,0:T(8,128)(2,1)} %refs_0_.3, bf16[1,128,2560]{2,1,0:T(8,128)(2,1)} %refs_1_.3, bf16[1,128,2560]{2,1,0:T(8,128)(2,1)} %refs_2_.3, ...), custom_call_target="tpu_custom_call" | custom-call | bytes 1310720 | tf_op jit(solution)/shard_map/pallas_call | solution.py:293
  2.7 3.1 %collective-permute-start.7 = (bf16[5,128,128]{2,1,0:T(8,128)(2,1)}, bf16[5,128,128]{2,1,0:T(8,128)(2,1)S(1)}, u32[]{:S(2)}, u32[]{:S(2)}) collective-permute-start(bf16[5,128,128]{2,1,0:T(8,128)(2,1)} %get-tuple-element.59), channel_id=1, source_target_pairs={{0,8},{4,12},{8,0},{12,4},{16,24},{20,28},{24,16},{28,20},{1,9},{5... | collective-permute-start | bytes 491528 | tf_op jit(solution)/shard_map/ppermute | solution.py:370
  5.8 2.6 %collective-permute-start.8 = (bf16[5,128,128]{2,1,0:T(8,128)(2,1)}, bf16[5,128,128]{2,1,0:T(8,128)(2,1)S(1)}, u32[]{:S(2)}, u32[]{:S(2)}) collective-permute-start(bf16[5,128,128]{2,1,0:T(8,128)(2,1)} %get-tuple-element.60), channel_id=1, source_target_pairs={{0,16},{4,20},{8,24},{12,28},{16,0},{20,4},{24,8},{28,12},{1,17},{... | collective-permute-start | bytes 491528 | tf_op jit(solution)/shard_map/ppermute | solution.py:370
  8.4 0.0 collective-permute-start.9
  8.4 1.7 %collective-permute-start.10 = (bf16[5,128,128]{2,1,0:T(8,128)(2,1)}, bf16[5,128,128]{2,1,0:T(8,128)(2,1)S(1)}, u32[]{:S(2)}, u32[]{:S(2)}) collective-permute-start(bf16[5,128,128]{2,1,0:T(8,128)(2,1)} %get-tuple-element.58.refs_0_), channel_id=1, source_target_pairs={{0,4},{4,0},{8,12},{12,8},{16,20},{20,16},{24,28},{28,24},{1,5},{5... | collective-permute-start | bytes 491528 | tf_op jit(solution)/shard_map/ppermute | solution.py:370
  10.1 0.6 pad_add_fusion.where_ref
  10.7 4.1 %shard_map.86 = (bf16[10,128,128]{2,1,0:T(8,128)(2,1)}, bf16[10,128,128]{2,1,0:T(8,128)(2,1)}, bf16[10,128,128]{2,1,0:T(8,128)(2,1)}, bf16[10,128,128]{2,1,0:T(8...) custom-call(s32[3]{0:T(128)} %pad_add_fusion.where_ref, ...), custom_call_target="tpu_custom_call" | custom-call | bytes 5242880 | tf_op jit(solution)/shard_map/pallas_call | solution.py:265
  14.8 1.8 %collective-permute-start = (bf16[10,128,128]{2,1,0:T(8,128)(2,1)}, bf16[10,128,128]{2,1,0:T(8,128)(2,1)S(1)}, u32[]{:S(2)}, u32[]{:S(2)}) collective-permute-start(bf16[10,128,128]{2,1,0:T(8,128)(2,1)} %get-tuple-element.50), channel_id=1, source_target_pairs={{0,16},{4,20},{8,24},{12,28},{16,0},{20,4},{24,8},{28,12},{1,17},{... | collective-permute-start | bytes 983048 | tf_op jit(solution)/shard_map/ppermute | solution.py:370
  16.6 0.0 collective-permute-done.7.refs_1_
  16.6 2.5 %collective-permute-start.1 = (bf16[10,128,128]{2,1,0:T(8,128)(2,1)}, bf16[10,128,128]{2,1,0:T(8,128)(2,1)S(1)}, u32[]{:S(2)}, u32[]{:S(2)}) collective-permute-start(bf16[10,128,128]{2,1,0:T(8,128)(2,1)} %get-tuple-element.51), channel_id=1, source_target_pairs={{0,8},{4,12},{8,0},{12,4},{16,24},{20,28},{24,16},{28,20},{1,9},{5... | collective-permute-start | bytes 983048 | tf_op jit(solution)/shard_map/ppermute | solution.py:370
  19.1 9.0 %collective-permute-done.8.refs_2_ = bf16[5,128,128]{2,1,0:T(8,128)(2,1)S(1)} collective-permute-done((bf16[5,128,128]{2,1,0:T(8,128)(2,1)}, bf16[5,128,128]{2,1,0:T(8,128)(2,1)S(1)}, u32[]{:S(2)}, u32[]{:S(2)}) %collective-permute-start.8) | collective-permute-done | bytes 163872 | tf_op jit(solution)/shard_map/ppermute | solution.py:370
  28.1 1.5 %collective-permute-start.11 = (bf16[5,128,128]{2,1,0:T(8,128)(2,1)S(1)}, bf16[5,128,128]{2,1,0:T(8,128)(2,1)S(1)}, u32[]{:S(2)}, u32[]{:S(2)}) collective-permute-start(bf16[5,128,128]{2,1,0:T(8,128)(2,1)S(1)} %collective-permute-done.7.refs_1_), channel_id=1, source_target_pairs={{0,4},{4,0},{8,12},{12,8},{16,20},{20,16},{24,28},{28,24},{1,5},{5... | collective-permute-start | bytes 491528 | tf_op jit(solution)/shard_map/ppermute | solution.py:370
  29.6 0.0 collective-permute-done.9.refs_3_
  29.6 0.5 collective-permute-start.12
  30.1 0.0 collective-permute-done.10.refs_4_
  30.1 1.5 %collective-permute-start.13 = (bf16[5,128,128]{2,1,0:T(8,128)(2,1)S(1)}, bf16[5,128,128]{2,1,0:T(8,128)(2,1)S(1)}, u32[]{:S(2)}, u32[]{:S(2)}) collective-permute-start(bf16[5,128,128]{2,1,0:T(8,128)(2,1)S(1)} %collective-permute-done.9.refs_3_), channel_id=1, source_target_pairs={{0,4},{4,0},{8,12},{12,8},{16,20},{20,16},{24,28},{28,24},{1,5},{5... | collective-permute-start | bytes 491528 | tf_op jit(solution)/shard_map/ppermute | solution.py:370
  32.3 0.0 copy-start.3
  32.3 0.6 copy-done.3
  32.9 0.2 reduce-window.8
  33.1 0.7 fusion
  33.8 0.7 pad.2.clone
  34.5 0.0 collective-permute-done.11.refs_5_
  34.5 4.4 %collective-permute-start.2 = (bf16[10,128,128]{2,1,0:T(8,128)(2,1)}, bf16[10,128,128]{2,1,0:T(8,128)(2,1)S(1)}, u32[]{:S(2)}, u32[]{:S(2)}) collective-permute-start(bf16[10,128,128]{2,1,0:T(8,128)(2,1)} %get-tuple-element.52), channel_id=1, source_target_pairs={{0,20},{4,16},{8,28},{12,24},{16,4},{20,0},{24,12},{28,8},{1,21},{... | collective-permute-start | bytes 983048 | tf_op jit(solution)/shard_map/ppermute | solution.py:370
  38.9 0.0 collective-permute-done.12.refs_6_
  38.9 0.5 collective-permute-start.3
  39.4 0.0 collective-permute-done.13.refs_7_
  39.4 14.7 %collective-permute-start.4 = (bf16[10,128,128]{2,1,0:T(8,128)(2,1)}, bf16[10,128,128]{2,1,0:T(8,128)(2,1)S(1)}, u32[]{:S(2)}, u32[]{:S(2)}) collective-permute-start(bf16[10,128,128]{2,1,0:T(8,128)(2,1)} %get-tuple-element.54), channel_id=1, source_target_pairs={{0,12},{4,8},{8,4},{12,0},{16,28},{20,24},{24,20},{28,16},{1,13},{... | collective-permute-start | bytes 983048 | tf_op jit(solution)/shard_map/ppermute | solution.py:370
  54.1 0.0 collective-permute-done.refs_0_
  54.1 1.4 %collective-permute-start.5 = (bf16[10,128,128]{2,1,0:T(8,128)(2,1)}, bf16[10,128,128]{2,1,0:T(8,128)(2,1)S(1)}, u32[]{:S(2)}, u32[]{:S(2)}) collective-permute-start(bf16[10,128,128]{2,1,0:T(8,128)(2,1)} %get-tuple-element.55), channel_id=1, source_target_pairs={{0,24},{4,28},{8,16},{12,20},{16,8},{20,12},{24,0},{28,4},{1,25},{... | collective-permute-start | bytes 983048 | tf_op jit(solution)/shard_map/ppermute | solution.py:370
  55.5 0.0 collective-permute-done.1.refs_1_
  55.5 2.4 %collective-permute-start.6 = (bf16[10,128,128]{2,1,0:T(8,128)(2,1)}, bf16[10,128,128]{2,1,0:T(8,128)(2,1)S(1)}, u32[]{:S(2)}, u32[]{:S(2)}) collective-permute-start(bf16[10,128,128]{2,1,0:T(8,128)(2,1)} %get-tuple-element.56), channel_id=1, source_target_pairs={{0,28},{4,24},{8,20},{12,16},{16,12},{20,8},{24,4},{28,0},{1,29},{... | collective-permute-start | bytes 983048 | tf_op jit(solution)/shard_map/ppermute | solution.py:370
  57.9 0.1 select_reduce_fusion.1
  58.0 0.1 add_add_fusion.clip_ref
  58.0 0.0 copy-done
  58.0 0.5 copy-done.1
  58.5 3.6 %shard_map.88 = (bf16[2,128,128]{2,1,0:T(8,128)(2,1)S(1)}, bf16[2,128,128]{2,1,0:T(8,128)(2,1)S(1)}, bf16[2,128,128]{2,1,0:T(8,128)(2,1)S(1)}, bf16[2,128,128]{2,1,0:T(8,128)(2,1)S(1)}) custom-call(s32[1]{0:T(128)S(6)} %copy.9.first_ref, s32[3,8]{1,0:T(4,128)S(1)} %add_add_fusion.clip_ref, s32[3]{0:T(128)S(1)} %copy-done.1, ...), custom_call_target="tpu_custom_call" | custom-call | bytes 32768 | tf_op jit(solution)/shard_map/pallas_call | solution.py:325
  62.1 0.0 collective-permute-done.2.refs_2_
  62.1 0.0 collective-permute-done.3.refs_3_
  62.1 7.6 %collective-permute-done.4.refs_4_ = bf16[10,128,128]{2,1,0:T(8,128)(2,1)S(1)} collective-permute-done((bf16[10,128,128]{2,1,0:T(8,128)(2,1)}, bf16[10,128,128]{2,1,0:T(8,128)(2,1)S(1)}, u32[]{:S(2)}, u32[]{:S(2)}) %collective-permute-start.4) | collective-permute-done | bytes 327712 | tf_op jit(solution)/shard_map/ppermute | solution.py:370
  69.7 0.0 collective-permute-done.5.refs_5_
  69.7 0.0 collective-permute-done.6.refs_6_
  69.8 11.1 %collective-permute-start.14 = (bf16[2,128,128]{2,1,0:T(8,128)(2,1)S(1)}, bf16[2,128,128]{2,1,0:T(8,128)(2,1)S(1)}, u32[]{:S(2)}, u32[]{:S(2)}) collective-permute-start(bf16[2,128,128]{2,1,0:T(8,128)(2,1)S(1)} %get-tuple-element.83), channel_id=1, source_target_pairs={{0,8},{4,12},{8,0},{12,4},{16,24},{20,28},{24,16},{28,20},{1,9},{5... | collective-permute-start | bytes 196616 | tf_op jit(solution)/shard_map/ppermute | solution.py:370
  80.8 1.0 collective-permute-start.15
  81.9 1.5 %collective-permute-start.16 = (bf16[2,128,128]{2,1,0:T(8,128)(2,1)S(1)}, bf16[2,128,128]{2,1,0:T(8,128)(2,1)S(1)}, u32[]{:S(2)}, u32[]{:S(2)}) collective-permute-start(bf16[2,128,128]{2,1,0:T(8,128)(2,1)S(1)} %get-tuple-element.85), channel_id=1, source_target_pairs={{0,24},{4,28},{8,16},{12,20},{16,8},{20,12},{24,0},{28,4},{1,25},{... | collective-permute-start | bytes 196616 | tf_op jit(solution)/shard_map/ppermute | solution.py:370
  83.3 0.0 copy-done.2
  83.3 7.5 %shard_map.89 = (bf16[4,128,128]{2,1,0:T(8,128)(2,1)S(1)}, bf16[4,128,128]{2,1,0:T(8,128)(2,1)S(1)}, bf16[4,128,128]{2,1,0:T(8,128)(2,1)S(1)}, bf16[4,128,128]{2...) custom-call(s32[1]{0:T(128)S(6)} %copy.9.first_ref, ...), custom_call_target="tpu_custom_call" | custom-call | flops 2147483648 | bytes 3670016 | tf_op jit(solution)/shard_map/pallas_call | solution.py:234
  90.9 0.0 collective-permute-done.14.refs_9_
  90.9 0.0 collective-permute-done.15.refs_10_
  90.9 0.0 collective-permute-done.16.refs_11_
  90.9 0.6 collective-permute-start.17
  91.5 1.0 collective-permute-start.18
  92.5 1.9 %collective-permute-start.19 = (bf16[4,128,128]{2,1,0:T(8,128)(2,1)S(1)}, bf16[4,128,128]{2,1,0:T(8,128)(2,1)S(1)}, u32[]{:S(2)}, u32[]{:S(2)}) collective-permute-start(bf16[4,128,128]{2,1,0:T(8,128)(2,1)S(1)} %get-tuple-element.88), channel_id=1, source_target_pairs={{0,12},{4,8},{8,4},{12,0},{16,28},{20,24},{24,20},{28,16},{1,13},{... | collective-permute-start | bytes 393224 | tf_op jit(solution)/shard_map/ppermute | solution.py:370
  94.4 2.0 %collective-permute-start.20 = (bf16[4,128,128]{2,1,0:T(8,128)(2,1)S(1)}, bf16[4,128,128]{2,1,0:T(8,128)(2,1)S(1)}, u32[]{:S(2)}, u32[]{:S(2)}) collective-permute-start(bf16[4,128,128]{2,1,0:T(8,128)(2,1)S(1)} %get-tuple-element.89), channel_id=1, source_target_pairs={{0,16},{4,20},{8,24},{12,28},{16,0},{20,4},{24,8},{28,12},{1,17},{... | collective-permute-start | bytes 393224 | tf_op jit(solution)/shard_map/ppermute | solution.py:370
  96.5 0.9 collective-permute-start.21
  97.4 0.0 collective-permute-done.17.refs_0_
  97.4 2.4 %collective-permute-start.22 = (bf16[4,128,128]{2,1,0:T(8,128)(2,1)S(1)}, bf16[4,128,128]{2,1,0:T(8,128)(2,1)S(1)}, u32[]{:S(2)}, u32[]{:S(2)}) collective-permute-start(bf16[4,128,128]{2,1,0:T(8,128)(2,1)S(1)} %get-tuple-element.91), channel_id=1, source_target_pairs={{0,24},{4,28},{8,16},{12,20},{16,8},{20,12},{24,0},{28,4},{1,25},{... | collective-permute-start | bytes 393224 | tf_op jit(solution)/shard_map/ppermute | solution.py:370
  99.7 0.0 collective-permute-done.18.refs_1_
  99.7 2.4 %collective-permute-start.23 = (bf16[4,128,128]{2,1,0:T(8,128)(2,1)S(1)}, bf16[4,128,128]{2,1,0:T(8,128)(2,1)S(1)}, u32[]{:S(2)}, u32[]{:S(2)}) collective-permute-start(bf16[4,128,128]{2,1,0:T(8,128)(2,1)S(1)} %get-tuple-element.92), channel_id=1, source_target_pairs={{0,28},{4,24},{8,20},{12,16},{16,12},{20,8},{24,4},{28,0},{1,29},{... | collective-permute-start | bytes 393224 | tf_op jit(solution)/shard_map/ppermute | solution.py:370
  102.1 0.6 collective-permute-done.19.refs_2_
  102.7 9.1 %collective-permute-done.20.refs_3_ = bf16[4,128,128]{2,1,0:T(8,128)(2,1)S(1)} collective-permute-done((bf16[4,128,128]{2,1,0:T(8,128)(2,1)S(1)}, bf16[4,128,128]{2,1,0:T(8,128)(2,1)S(1)}, u32[]{:S(2)}, u32[]{:S(2)}) %collective-permute-start.20) | collective-permute-done | bytes 131104 | tf_op jit(solution)/shard_map/ppermute | solution.py:370
  111.8 2.8 %collective-permute-done.21.refs_4_ = bf16[4,128,128]{2,1,0:T(8,128)(2,1)S(1)} collective-permute-done((bf16[4,128,128]{2,1,0:T(8,128)(2,1)S(1)}, bf16[4,128,128]{2,1,0:T(8,128)(2,1)S(1)}, u32[]{:S(2)}, u32[]{:S(2)}) %collective-permute-start.21) | collective-permute-done | bytes 131104 | tf_op jit(solution)/shard_map/ppermute | solution.py:370
  114.6 0.0 collective-permute-done.22.refs_5_
  114.6 0.0 collective-permute-done.23.refs_6_
  114.6 1.8 %shard_map.90 = (bf16[1,128,2560]{2,1,0:T(8,128)(2,1)}, bf16[1,128,2560]{2,1,0:T(8,128)(2,1)}) custom-call(s32[3]{0:T(128)S(1)} %copy-done.1, bf16[4,128,128]{2,1,0:T(8,128)(2,1)S(1)} %collective-permute-done.17.refs_0_, bf16[4,128,128]{2,1,0:T(8,128)(2,1)S(1)} %collective-permute-done.18.refs_1_, bf16[4,128,128]{2,1,0:T(8,128)(2,1)S(1)} %collective-permute-done.19.refs_2_, ...), custom_call_target="tpu_custom_call" | custom-call | bytes 2621440 | tf_op jit(solution)/shard_map/pallas_call | solution.py:355
  (3 shorter events, 0.0 us)
Async XLA Ops:
  2.7 13.9 %collective-permute-start.7 = (bf16[5,128,128]{2,1,0:T(8,128)(2,1)}, bf16[5,128,128]{2,1,0:T(8,128)(2,1)S(1)}, u32[]{:S(2)}, u32[]{:S(2)}) collective-permute-start(bf16[5,128,128]{2,1,0:T(8,128)(2,1)} %get-tuple-element.59), channel_id=1, source_target_pairs={{0,8},{4,12},{8,0},{12,4},{16,24},{20,28},{24,16},{28,20},{1,9},{5... | collective-permute-start | bytes 491528 | tf_op jit(solution)/shard_map/ppermute | solution.py:370
  5.8 22.3 %collective-permute-start.8 = (bf16[5,128,128]{2,1,0:T(8,128)(2,1)}, bf16[5,128,128]{2,1,0:T(8,128)(2,1)S(1)}, u32[]{:S(2)}, u32[]{:S(2)}) collective-permute-start(bf16[5,128,128]{2,1,0:T(8,128)(2,1)} %get-tuple-element.60), channel_id=1, source_target_pairs={{0,16},{4,20},{8,24},{12,28},{16,0},{20,4},{24,8},{28,12},{1,17},{... | collective-permute-start | bytes 491528 | tf_op jit(solution)/shard_map/ppermute | solution.py:370
  8.4 21.2 %collective-permute-start.9 = (bf16[5,128,128]{2,1,0:T(8,128)(2,1)}, bf16[5,128,128]{2,1,0:T(8,128)(2,1)S(1)}, u32[]{:S(2)}, u32[]{:S(2)}) collective-permute-start(bf16[5,128,128]{2,1,0:T(8,128)(2,1)} %get-tuple-element.61), channel_id=1, source_target_pairs={{0,24},{4,28},{8,16},{12,20},{16,8},{20,12},{24,0},{28,4},{1,25},{... | collective-permute-start | bytes 491528 | tf_op jit(solution)/shard_map/ppermute | solution.py:370
  8.4 21.7 %collective-permute-start.10 = (bf16[5,128,128]{2,1,0:T(8,128)(2,1)}, bf16[5,128,128]{2,1,0:T(8,128)(2,1)S(1)}, u32[]{:S(2)}, u32[]{:S(2)}) collective-permute-start(bf16[5,128,128]{2,1,0:T(8,128)(2,1)} %get-tuple-element.58.refs_0_), channel_id=1, source_target_pairs={{0,4},{4,0},{8,12},{12,8},{16,20},{20,16},{24,28},{28,24},{1,5},{5... | collective-permute-start | bytes 491528 | tf_op jit(solution)/shard_map/ppermute | solution.py:370
  10.7 47.4 %copy-start = (bf16[5,128,128]{2,1,0:T(8,128)(2,1)S(1)}, bf16[5,128,128]{2,1,0:T(8,128)(2,1)}, u32[]{:S(2)}) copy-start(bf16[5,128,128]{2,1,0:T(8,128)(2,1)} %get-tuple-element.58.refs_0_) | copy-start | bytes 491524
  14.8 39.2 %collective-permute-start = (bf16[10,128,128]{2,1,0:T(8,128)(2,1)}, bf16[10,128,128]{2,1,0:T(8,128)(2,1)S(1)}, u32[]{:S(2)}, u32[]{:S(2)}) collective-permute-start(bf16[10,128,128]{2,1,0:T(8,128)(2,1)} %get-tuple-element.50), channel_id=1, source_target_pairs={{0,16},{4,20},{8,24},{12,28},{16,0},{20,4},{24,8},{28,12},{1,17},{... | collective-permute-start | bytes 983048 | tf_op jit(solution)/shard_map/ppermute | solution.py:370
  16.6 38.9 %collective-permute-start.1 = (bf16[10,128,128]{2,1,0:T(8,128)(2,1)}, bf16[10,128,128]{2,1,0:T(8,128)(2,1)S(1)}, u32[]{:S(2)}, u32[]{:S(2)}) collective-permute-start(bf16[10,128,128]{2,1,0:T(8,128)(2,1)} %get-tuple-element.51), channel_id=1, source_target_pairs={{0,8},{4,12},{8,0},{12,4},{16,24},{20,28},{24,16},{28,20},{1,9},{5... | collective-permute-start | bytes 983048 | tf_op jit(solution)/shard_map/ppermute | solution.py:370
  28.1 6.4 %collective-permute-start.11 = (bf16[5,128,128]{2,1,0:T(8,128)(2,1)S(1)}, bf16[5,128,128]{2,1,0:T(8,128)(2,1)S(1)}, u32[]{:S(2)}, u32[]{:S(2)}) collective-permute-start(bf16[5,128,128]{2,1,0:T(8,128)(2,1)S(1)} %collective-permute-done.7.refs_1_), channel_id=1, source_target_pairs={{0,4},{4,0},{8,12},{12,8},{16,20},{20,16},{24,28},{28,24},{1,5},{5... | collective-permute-start | bytes 491528 | tf_op jit(solution)/shard_map/ppermute | solution.py:370
  29.6 9.3 %collective-permute-start.12 = (bf16[5,128,128]{2,1,0:T(8,128)(2,1)S(1)}, bf16[5,128,128]{2,1,0:T(8,128)(2,1)S(1)}, u32[]{:S(2)}, u32[]{:S(2)}) collective-permute-start(bf16[5,128,128]{2,1,0:T(8,128)(2,1)S(1)} %collective-permute-done.8.refs_2_), channel_id=1, source_target_pairs={{0,4},{4,0},{8,12},{12,8},{16,20},{20,16},{24,28},{28,24},{1,5},{5... | collective-permute-start | bytes 491528 | tf_op jit(solution)/shard_map/ppermute | solution.py:370
  30.1 9.3 %collective-permute-start.13 = (bf16[5,128,128]{2,1,0:T(8,128)(2,1)S(1)}, bf16[5,128,128]{2,1,0:T(8,128)(2,1)S(1)}, u32[]{:S(2)}, u32[]{:S(2)}) collective-permute-start(bf16[5,128,128]{2,1,0:T(8,128)(2,1)S(1)} %collective-permute-done.9.refs_3_), channel_id=1, source_target_pairs={{0,4},{4,0},{8,12},{12,8},{16,20},{20,16},{24,28},{28,24},{1,5},{5... | collective-permute-start | bytes 491528 | tf_op jit(solution)/shard_map/ppermute | solution.py:370
  32.3 0.7 copy-start.3
  34.5 27.6 %collective-permute-start.2 = (bf16[10,128,128]{2,1,0:T(8,128)(2,1)}, bf16[10,128,128]{2,1,0:T(8,128)(2,1)S(1)}, u32[]{:S(2)}, u32[]{:S(2)}) collective-permute-start(bf16[10,128,128]{2,1,0:T(8,128)(2,1)} %get-tuple-element.52), channel_id=1, source_target_pairs={{0,20},{4,16},{8,28},{12,24},{16,4},{20,0},{24,12},{28,8},{1,21},{... | collective-permute-start | bytes 983048 | tf_op jit(solution)/shard_map/ppermute | solution.py:370
  38.9 23.3 %collective-permute-start.3 = (bf16[10,128,128]{2,1,0:T(8,128)(2,1)}, bf16[10,128,128]{2,1,0:T(8,128)(2,1)S(1)}, u32[]{:S(2)}, u32[]{:S(2)}) collective-permute-start(bf16[10,128,128]{2,1,0:T(8,128)(2,1)} %get-tuple-element.53), channel_id=1, source_target_pairs={{0,4},{4,0},{8,12},{12,8},{16,20},{20,16},{24,28},{28,24},{1,5},{5... | collective-permute-start | bytes 983048 | tf_op jit(solution)/shard_map/ppermute | solution.py:370
  39.4 30.3 %collective-permute-start.4 = (bf16[10,128,128]{2,1,0:T(8,128)(2,1)}, bf16[10,128,128]{2,1,0:T(8,128)(2,1)S(1)}, u32[]{:S(2)}, u32[]{:S(2)}) collective-permute-start(bf16[10,128,128]{2,1,0:T(8,128)(2,1)} %get-tuple-element.54), channel_id=1, source_target_pairs={{0,12},{4,8},{8,4},{12,0},{16,28},{20,24},{24,20},{28,16},{1,13},{... | collective-permute-start | bytes 983048 | tf_op jit(solution)/shard_map/ppermute | solution.py:370
  54.1 15.7 %collective-permute-start.5 = (bf16[10,128,128]{2,1,0:T(8,128)(2,1)}, bf16[10,128,128]{2,1,0:T(8,128)(2,1)S(1)}, u32[]{:S(2)}, u32[]{:S(2)}) collective-permute-start(bf16[10,128,128]{2,1,0:T(8,128)(2,1)} %get-tuple-element.55), channel_id=1, source_target_pairs={{0,24},{4,28},{8,16},{12,20},{16,8},{20,12},{24,0},{28,4},{1,25},{... | collective-permute-start | bytes 983048 | tf_op jit(solution)/shard_map/ppermute | solution.py:370
  55.5 14.2 %collective-permute-start.6 = (bf16[10,128,128]{2,1,0:T(8,128)(2,1)}, bf16[10,128,128]{2,1,0:T(8,128)(2,1)S(1)}, u32[]{:S(2)}, u32[]{:S(2)}) collective-permute-start(bf16[10,128,128]{2,1,0:T(8,128)(2,1)} %get-tuple-element.56), channel_id=1, source_target_pairs={{0,28},{4,24},{8,20},{12,16},{16,12},{20,8},{24,4},{28,0},{1,29},{... | collective-permute-start | bytes 983048 | tf_op jit(solution)/shard_map/ppermute | solution.py:370
  58.0 0.6 copy-start.1
  58.5 24.8 %copy-start.2 = (bf16[10,128,128]{2,1,0:T(8,128)(2,1)S(1)}, bf16[10,128,128]{2,1,0:T(8,128)(2,1)}, u32[]{:S(2)}) copy-start(bf16[10,128,128]{2,1,0:T(8,128)(2,1)} %get-tuple-element.73.refs_7_) | copy-start | bytes 983044
  69.8 21.1 %collective-permute-start.14 = (bf16[2,128,128]{2,1,0:T(8,128)(2,1)S(1)}, bf16[2,128,128]{2,1,0:T(8,128)(2,1)S(1)}, u32[]{:S(2)}, u32[]{:S(2)}) collective-permute-start(bf16[2,128,128]{2,1,0:T(8,128)(2,1)S(1)} %get-tuple-element.83), channel_id=1, source_target_pairs={{0,8},{4,12},{8,0},{12,4},{16,24},{20,28},{24,16},{28,20},{1,9},{5... | collective-permute-start | bytes 196616 | tf_op jit(solution)/shard_map/ppermute | solution.py:370
  80.8 10.0 %collective-permute-start.15 = (bf16[2,128,128]{2,1,0:T(8,128)(2,1)S(1)}, bf16[2,128,128]{2,1,0:T(8,128)(2,1)S(1)}, u32[]{:S(2)}, u32[]{:S(2)}) collective-permute-start(bf16[2,128,128]{2,1,0:T(8,128)(2,1)S(1)} %get-tuple-element.84), channel_id=1, source_target_pairs={{0,16},{4,20},{8,24},{12,28},{16,0},{20,4},{24,8},{28,12},{1,17},{... | collective-permute-start | bytes 196616 | tf_op jit(solution)/shard_map/ppermute | solution.py:370
  81.9 9.0 %collective-permute-start.16 = (bf16[2,128,128]{2,1,0:T(8,128)(2,1)S(1)}, bf16[2,128,128]{2,1,0:T(8,128)(2,1)S(1)}, u32[]{:S(2)}, u32[]{:S(2)}) collective-permute-start(bf16[2,128,128]{2,1,0:T(8,128)(2,1)S(1)} %get-tuple-element.85), channel_id=1, source_target_pairs={{0,24},{4,28},{8,16},{12,20},{16,8},{20,12},{24,0},{28,4},{1,25},{... | collective-permute-start | bytes 196616 | tf_op jit(solution)/shard_map/ppermute | solution.py:370
  90.9 6.5 %collective-permute-start.17 = (bf16[4,128,128]{2,1,0:T(8,128)(2,1)S(1)}, bf16[4,128,128]{2,1,0:T(8,128)(2,1)S(1)}, u32[]{:S(2)}, u32[]{:S(2)}) collective-permute-start(bf16[4,128,128]{2,1,0:T(8,128)(2,1)S(1)} %get-tuple-element.86), channel_id=1, source_target_pairs={{0,4},{4,0},{8,12},{12,8},{16,20},{20,16},{24,28},{28,24},{1,5},{5... | collective-permute-start | bytes 393224 | tf_op jit(solution)/shard_map/ppermute | solution.py:370
  91.5 8.2 %collective-permute-start.18 = (bf16[4,128,128]{2,1,0:T(8,128)(2,1)S(1)}, bf16[4,128,128]{2,1,0:T(8,128)(2,1)S(1)}, u32[]{:S(2)}, u32[]{:S(2)}) collective-permute-start(bf16[4,128,128]{2,1,0:T(8,128)(2,1)S(1)} %get-tuple-element.87), channel_id=1, source_target_pairs={{0,8},{4,12},{8,0},{12,4},{16,24},{20,28},{24,16},{28,20},{1,9},{5... | collective-permute-start | bytes 393224 | tf_op jit(solution)/shard_map/ppermute | solution.py:370
  92.5 10.2 %collective-permute-start.19 = (bf16[4,128,128]{2,1,0:T(8,128)(2,1)S(1)}, bf16[4,128,128]{2,1,0:T(8,128)(2,1)S(1)}, u32[]{:S(2)}, u32[]{:S(2)}) collective-permute-start(bf16[4,128,128]{2,1,0:T(8,128)(2,1)S(1)} %get-tuple-element.88), channel_id=1, source_target_pairs={{0,12},{4,8},{8,4},{12,0},{16,28},{20,24},{24,20},{28,16},{1,13},{... | collective-permute-start | bytes 393224 | tf_op jit(solution)/shard_map/ppermute | solution.py:370
  94.4 17.4 %collective-permute-start.20 = (bf16[4,128,128]{2,1,0:T(8,128)(2,1)S(1)}, bf16[4,128,128]{2,1,0:T(8,128)(2,1)S(1)}, u32[]{:S(2)}, u32[]{:S(2)}) collective-permute-start(bf16[4,128,128]{2,1,0:T(8,128)(2,1)S(1)} %get-tuple-element.89), channel_id=1, source_target_pairs={{0,16},{4,20},{8,24},{12,28},{16,0},{20,4},{24,8},{28,12},{1,17},{... | collective-permute-start | bytes 393224 | tf_op jit(solution)/shard_map/ppermute | solution.py:370
  96.5 18.1 %collective-permute-start.21 = (bf16[4,128,128]{2,1,0:T(8,128)(2,1)S(1)}, bf16[4,128,128]{2,1,0:T(8,128)(2,1)S(1)}, u32[]{:S(2)}, u32[]{:S(2)}) collective-permute-start(bf16[4,128,128]{2,1,0:T(8,128)(2,1)S(1)} %get-tuple-element.90), channel_id=1, source_target_pairs={{0,20},{4,16},{8,28},{12,24},{16,4},{20,0},{24,12},{28,8},{1,21},{... | collective-permute-start | bytes 393224 | tf_op jit(solution)/shard_map/ppermute | solution.py:370
  97.4 17.2 %collective-permute-start.22 = (bf16[4,128,128]{2,1,0:T(8,128)(2,1)S(1)}, bf16[4,128,128]{2,1,0:T(8,128)(2,1)S(1)}, u32[]{:S(2)}, u32[]{:S(2)}) collective-permute-start(bf16[4,128,128]{2,1,0:T(8,128)(2,1)S(1)} %get-tuple-element.91), channel_id=1, source_target_pairs={{0,24},{4,28},{8,16},{12,20},{16,8},{20,12},{24,0},{28,4},{1,25},{... | collective-permute-start | bytes 393224 | tf_op jit(solution)/shard_map/ppermute | solution.py:370
  99.7 14.9 %collective-permute-start.23 = (bf16[4,128,128]{2,1,0:T(8,128)(2,1)S(1)}, bf16[4,128,128]{2,1,0:T(8,128)(2,1)S(1)}, u32[]{:S(2)}, u32[]{:S(2)}) collective-permute-start(bf16[4,128,128]{2,1,0:T(8,128)(2,1)S(1)} %get-tuple-element.92), channel_id=1, source_target_pairs={{0,28},{4,24},{8,20},{12,16},{16,12},{20,8},{24,4},{28,0},{1,29},{... | collective-permute-start | bytes 393224 | tf_op jit(solution)/shard_map/ppermute | solution.py:370

commit v4 on v3

--- a/solution.py
+++ b/solution.py
@@ -212,11 +212,13 @@
     )(clips, role, arrived, gen, shared)
 
 
-def slots_kernel(full, order, home, first, clips, where, arrived):
+def slots_kernel(full, order, home, first, clips, where, arrived, pieces):
     blocks = len(order)
 
     def body(first_ref, clip_ref, where_ref, *refs):
-        x_refs, o_refs, (x, y) = refs[:blocks], refs[blocks : 2 * blocks], refs[2 * blocks :]
+        x_refs, refs = refs[:blocks], refs[blocks:]
+        piece_refs, refs = refs[: len(pieces)], refs[len(pieces) :]
+        o_refs, (x, y) = refs[:blocks], refs[blocks:]
         at = [where_ref[2] ^ d for d in order]
         for i in range(blocks):
             x[at[i]] = x_refs[i][...]
@@ -229,20 +231,25 @@
 
         lax.fori_loop(0, full, head, None)
         for i, d in enumerate(home):
-            o_refs[i][...] = y[where_ref[2] ^ d]
-
-    return pl.pallas_call(
-        body,
-        in_specs=[SMEM] * 3 + [VMEM] * blocks,
+            o_refs[i][0 : 2 * full] = y[where_ref[2] ^ d]
+            if d % 2 == 0:
+                o_refs[i][2 * full : 2 * full + 2] = piece_refs[d // 2][...]
+
+    return pl.pallas_call(
+        body,
+        in_specs=[SMEM] * 3 + [VMEM] * (blocks + len(pieces)),
         out_specs=[VMEM] * blocks,
-        out_shape=[jax.ShapeDtypeStruct((2 * full, TOK, HD), jnp.bfloat16)] * blocks,
+        out_shape=[
+            jax.ShapeDtypeStruct((2 * full + 2 * (d % 2 == 0), TOK, HD), jnp.bfloat16)
+            for d in home
+        ],
         scratch_shapes=[
             pltpu.VMEM((blocks, 5 * full, TOK, HD), jnp.bfloat16),
             pltpu.VMEM((blocks, 2 * full, TOK, HD), jnp.bfloat16),
         ],
         compiler_params=LOCAL,
         cost_estimate=cost(2 * full, blocks, 7 * full),
-    )(first, clips, where, *arrived)
+    )(first, clips, where, *arrived, *pieces)
 
 
 def slots_pack(full, order, where, tensors):
@@ -304,16 +311,16 @@
     )(column, *tensors)
 
 
-def rest_kernel(columns, first, clips, where, own, other):
+def rest_kernel(columns, order, first, clips, where, own, other):
     blocks = 2 * columns
 
     def body(first_ref, clip_ref, where_ref, *refs):
         x, gen = refs[-2:]
         column, side = where_ref[0], where_ref[1]
         mine = [2 * (column ^ s) + side for s in range(columns)]
-        for s in range(columns):
-            x[mine[s]] = refs[s][...]
-            x[mine[s] ^ 1] = refs[columns + s][...]
+        for n, s in enumerate(order):
+            x[mine[s]] = refs[n][...]
+            x[mine[s] ^ 1] = refs[columns + n][...]
         sources = [(x, t) for t in range(5)]
         student_head(range(0, blocks, 2), first_ref[0], sources[:3], gen, 0)
         at_gen = lambda at: gen[at, 0]
@@ -336,11 +343,11 @@
     )(first, clips, where, *own, *other)
 
 
-def join(full, order, columns, where, slots, rests):
+def join(full, order, columns, where, slots):
     peers = len(order)
 
     def body(where_ref, *refs):
-        for i, o_ref in enumerate(refs[peers + columns :]):
+        for i, o_ref in enumerate(refs[peers:]):
 
             def put(h, tile):
                 o_ref[0, :, pl.ds(pl.multiple_of(h * HD, HD), HD)] = tile
@@ -349,17 +356,18 @@
                 for s in range(full):
                     put(s * peers + (where_ref[2] ^ d), refs[n][2 * s + i])
             for s in range(columns):
-                put(full * peers + (where_ref[0] ^ s), refs[peers + s][i])
+                ref = refs[order.index(2 * s)]
+                put(full * peers + (where_ref[0] ^ s), ref[2 * full + i])
 
     width = (full * peers + columns) * HD
     return pl.pallas_call(
         body,
-        in_specs=[SMEM] + [VMEM] * (peers + columns),
+        in_specs=[SMEM] + [VMEM] * peers,
         out_specs=[VMEM] * 2,
         out_shape=[jax.ShapeDtypeStruct((1, TOK, width), jnp.bfloat16)] * 2,
         compiler_params=LOCAL,
         cost_estimate=cost(0, 1, 4 * width // HD),
-    )(where, *slots, *rests)
+    )(where, *slots)
 
 
 def by_slots_and_columns(tensors, peers, full, rest, first, clips):
@@ -372,20 +380,19 @@
     far = list(range(rest, peers))
     near = sorted(range(1, rest), key=lambda d: (d % 2, d))
     there = [far[0], near[0], far[1], *near[1:], *far[2:], 0]
-    home = [*range(1, peers), 0]
+    home = [far[0]] + [d for pair in zip(range(1, rest), far[1:]) for d in pair] + [0]
+    across = [*range(rest // 2, rest), *range(1, rest // 2), 0]
 
     pieces = rest_pack(full * peers, rest, where[:1], tensors)
-    own = [swapped(x, 2 * s) for s, x in enumerate(pieces)]
+    own = [swapped(pieces[s], 2 * s) for s in across]
     packed = slots_pack(full, there, where, tensors)
     arrived = [swapped(x, d) for x, d in zip(packed, there)]
     other = [swapped(x, 1) for x in own]
-    pieces = rest_kernel(rest, first, clips, where, own, other)
+    pieces = rest_kernel(rest, across, first, clips, where, own, other)
     arrived, pieces = lax.optimization_barrier((arrived, pieces))
-    rests = [swapped(x, 2 * s) for s, x in enumerate(pieces)]
-    results = slots_kernel(full, there, home, first, clips, where, arrived)
-    results, rests = lax.optimization_barrier((results, rests))
+    results = slots_kernel(full, there, home, first, clips, where, arrived, pieces)
     slots = [swapped(x, d) for x, d in zip(results, home)]
-    return tuple(join(full, home, rest, where, slots, rests))
+    return tuple(join(full, home, rest, where, slots))
 
 
 def by_roles(tensors, peers, heads, first, clips):

time: 118 us -> 118 us (level)
  the two profiles are of different devices: /device:TPU:0 before, /device:TPU:12 now
where the time goes in v4:
time: 118 us
  waiting for transfers between devices  61.1 us (52%)
  starting transfers between devices  32.6 us (28%)
  Pallas kernels  19.2 us (16%)
  local copies, waits for them, and re-layouts  1.83 us (2%)
  other arithmetic  1.56 us (1%)
  between operations  1.38 us (1%)
    ppermute x21, waiting for transfers between devices, swapped(): lax.ppermute(x, 'tm', [(i, i ^ by) for i in range(peers)])  61.1 us
    ppermute x21, starting transfers between devices, swapped(): lax.ppermute(x, 'tm', [(i, i ^ by) for i in range(peers)])  32.6 us
    pallas_call x1, Pallas kernels, slots_kernel(): pl.pallas_call(body, in_specs=[SMEM] * 3 + [VMEM] * (blocks + len(pieces)...  7.55 us
    pallas_call x1, Pallas kernels, slots_pack(): pl.pallas_call(body, in_specs=[SMEM] + [pl.BlockSpec(memory_space=pl.ANY)...  4.14 us
    pallas_call x1, Pallas kernels, rest_kernel(): pl.pallas_call(body, in_specs=[SMEM] * 3 + [VMEM] * (2 * columns), out_sp...  3.58 us
  transfers between devices with their start and end apart: 21, of which 11 were waited for; matrix products, arithmetic and copies ran while one was open for 2% of the time, Pallas kernels for 7%

profile of v4, /device:TPU:12, one launch (start us, length us, event | category | flops | bytes accessed | tf_op | source)
XLA Modules:
  0.0 117.6 jit_solution(6750519036219050237)
XLA Ops:
  0.6 2.1 %shard_map.87 = (bf16[5,128,128]{2,1,0:T(8,128)(2,1)}, bf16[5,128,128]{2,1,0:T(8,128)(2,1)}, bf16[5,128,128]{2,1,0:T(8,128)(2,1)}, bf16[5,128,128]{2,1,0:T(8,128)(2,1)}) custom-call(s32[1]{0:T(128)} %bitcast.column_ref, bf16[1,128,2560]{2,1,0:T(8,128)(2,1)} %refs_0_.3, bf16[1,128,2560]{2,1,0:T(8,128)(2,1)} %refs_1_.3, bf16[1,128,2560]{2,1,0:T(8,128)(2,1)} %refs_2_.3, ...), custom_call_target="tpu_custom_call" | custom-call | bytes 1310720 | tf_op jit(solution)/shard_map/pallas_call | solution.py:300
  2.7 2.7 %collective-permute-start.7 = (bf16[5,128,128]{2,1,0:T(8,128)(2,1)}, bf16[5,128,128]{2,1,0:T(8,128)(2,1)S(1)}, u32[]{:S(2)}, u32[]{:S(2)}) collective-permute-start(bf16[5,128,128]{2,1,0:T(8,128)(2,1)} %get-tuple-element.46), channel_id=1, source_target_pairs={{0,16},{4,20},{8,24},{12,28},{16,0},{20,4},{24,8},{28,12},{1,17},{... | collective-permute-start | bytes 491528 | tf_op jit(solution)/shard_map/ppermute | solution.py:378
  5.4 0.0 collective-permute-start.8
  5.4 1.8 %collective-permute-start.9 = (bf16[5,128,128]{2,1,0:T(8,128)(2,1)}, bf16[5,128,128]{2,1,0:T(8,128)(2,1)S(1)}, u32[]{:S(2)}, u32[]{:S(2)}) collective-permute-start(bf16[5,128,128]{2,1,0:T(8,128)(2,1)} %get-tuple-element.48), channel_id=1, source_target_pairs={{0,8},{4,12},{8,0},{12,4},{16,24},{20,28},{24,16},{28,20},{1,9},{5... | collective-permute-start | bytes 491528 | tf_op jit(solution)/shard_map/ppermute | solution.py:378
  7.2 1.5 %collective-permute-start.13 = (bf16[5,128,128]{2,1,0:T(8,128)(2,1)}, bf16[5,128,128]{2,1,0:T(8,128)(2,1)S(1)}, u32[]{:S(2)}, u32[]{:S(2)}) collective-permute-start(bf16[5,128,128]{2,1,0:T(8,128)(2,1)} %get-tuple-element.49.refs_3_), channel_id=1, source_target_pairs={{0,4},{4,0},{8,12},{12,8},{16,20},{20,16},{24,28},{28,24},{1,5},{5... | collective-permute-start | bytes 491528 | tf_op jit(solution)/shard_map/ppermute | solution.py:378
  8.7 0.6 pad_add_fusion.where_ref
  9.3 0.0 copy-start
  9.3 4.1 %shard_map.86 = (bf16[10,128,128]{2,1,0:T(8,128)(2,1)}, bf16[10,128,128]{2,1,0:T(8,128)(2,1)}, bf16[10,128,128]{2,1,0:T(8,128)(2,1)}, bf16[10,128,128]{2,1,0:T(8...) custom-call(s32[3]{0:T(128)} %pad_add_fusion.where_ref, ...), custom_call_target="tpu_custom_call" | custom-call | bytes 5242880 | tf_op jit(solution)/shard_map/pallas_call | solution.py:272
  13.4 1.8 %collective-permute-start = (bf16[10,128,128]{2,1,0:T(8,128)(2,1)}, bf16[10,128,128]{2,1,0:T(8,128)(2,1)S(1)}, u32[]{:S(2)}, u32[]{:S(2)}) collective-permute-start(bf16[10,128,128]{2,1,0:T(8,128)(2,1)} %get-tuple-element.38), channel_id=1, source_target_pairs={{0,16},{4,20},{8,24},{12,28},{16,0},{20,4},{24,8},{28,12},{1,17},{... | collective-permute-start | bytes 983048 | tf_op jit(solution)/shard_map/ppermute | solution.py:378
  15.2 1.7 %collective-permute-done.7.refs_0_ = bf16[5,128,128]{2,1,0:T(8,128)(2,1)S(1)} collective-permute-done((bf16[5,128,128]{2,1,0:T(8,128)(2,1)}, bf16[5,128,128]{2,1,0:T(8,128)(2,1)S(1)}, u32[]{:S(2)}, u32[]{:S(2)}) %collective-permute-start.7) | collective-permute-done | bytes 163872 | tf_op jit(solution)/shard_map/ppermute | solution.py:378
  16.9 7.4 %collective-permute-start.1 = (bf16[10,128,128]{2,1,0:T(8,128)(2,1)}, bf16[10,128,128]{2,1,0:T(8,128)(2,1)S(1)}, u32[]{:S(2)}, u32[]{:S(2)}) collective-permute-start(bf16[10,128,128]{2,1,0:T(8,128)(2,1)} %get-tuple-element.39), channel_id=1, source_target_pairs={{0,8},{4,12},{8,0},{12,4},{16,24},{20,28},{24,16},{28,20},{1,9},{5... | collective-permute-start | bytes 983048 | tf_op jit(solution)/shard_map/ppermute | solution.py:378
  24.3 3.3 %collective-permute-done.8.refs_1_ = bf16[5,128,128]{2,1,0:T(8,128)(2,1)S(1)} collective-permute-done((bf16[5,128,128]{2,1,0:T(8,128)(2,1)}, bf16[5,128,128]{2,1,0:T(8,128)(2,1)S(1)}, u32[]{:S(2)}, u32[]{:S(2)}) %collective-permute-start.8) | collective-permute-done | bytes 163872 | tf_op jit(solution)/shard_map/ppermute | solution.py:378
  27.6 1.5 %collective-permute-start.10 = (bf16[5,128,128]{2,1,0:T(8,128)(2,1)S(1)}, bf16[5,128,128]{2,1,0:T(8,128)(2,1)S(1)}, u32[]{:S(2)}, u32[]{:S(2)}) collective-permute-start(bf16[5,128,128]{2,1,0:T(8,128)(2,1)S(1)} %collective-permute-done.7.refs_0_), channel_id=1, source_target_pairs={{0,4},{4,0},{8,12},{12,8},{16,20},{20,16},{24,28},{28,24},{1,5},{5... | collective-permute-start | bytes 491528 | tf_op jit(solution)/shard_map/ppermute | solution.py:378
  29.1 0.0 collective-permute-done.9.refs_2_
  29.1 0.5 collective-permute-start.11
  29.6 0.0 collective-permute-done.13.refs_7_
  29.6 1.5 %collective-permute-start.12 = (bf16[5,128,128]{2,1,0:T(8,128)(2,1)S(1)}, bf16[5,128,128]{2,1,0:T(8,128)(2,1)S(1)}, u32[]{:S(2)}, u32[]{:S(2)}) collective-permute-start(bf16[5,128,128]{2,1,0:T(8,128)(2,1)S(1)} %collective-permute-done.9.refs_2_), channel_id=1, source_target_pairs={{0,4},{4,0},{8,12},{12,8},{16,20},{20,16},{24,28},{28,24},{1,5},{5... | collective-permute-start | bytes 491528 | tf_op jit(solution)/shard_map/ppermute | solution.py:378
  31.7 0.0 copy-start.3
  31.8 0.6 copy-done.3
  32.4 0.2 reduce-window.8
  32.6 0.6 fusion
  33.2 0.6 pad.2.clone
  33.8 0.9 collective-permute-done.10.refs_4_
  34.7 0.0 collective-permute-start.2
  34.7 10.5 %collective-permute-done.11.refs_5_ = bf16[5,128,128]{2,1,0:T(8,128)(2,1)S(1)} collective-permute-done((bf16[5,128,128]{2,1,0:T(8,128)(2,1)S(1)}, bf16[5,128,128]{2,1,0:T(8,128)(2,1)S(1)}, u32[]{:S(2)}, u32[]{:S(2)}) %collective-permute-start.11) | collective-permute-done | bytes 163872 | tf_op jit(solution)/shard_map/ppermute | solution.py:378
  45.2 1.5 %collective-permute-start.3 = (bf16[10,128,128]{2,1,0:T(8,128)(2,1)}, bf16[10,128,128]{2,1,0:T(8,128)(2,1)S(1)}, u32[]{:S(2)}, u32[]{:S(2)}) collective-permute-start(bf16[10,128,128]{2,1,0:T(8,128)(2,1)} %get-tuple-element.41), channel_id=1, source_target_pairs={{0,4},{4,0},{8,12},{12,8},{16,20},{20,16},{24,28},{28,24},{1,5},{5... | collective-permute-start | bytes 983048 | tf_op jit(solution)/shard_map/ppermute | solution.py:378
  46.7 2.0 %collective-permute-done.12.refs_6_ = bf16[5,128,128]{2,1,0:T(8,128)(2,1)S(1)} collective-permute-done((bf16[5,128,128]{2,1,0:T(8,128)(2,1)S(1)}, bf16[5,128,128]{2,1,0:T(8,128)(2,1)S(1)}, u32[]{:S(2)}, u32[]{:S(2)}) %collective-permute-start.12) | collective-permute-done | bytes 163872 | tf_op jit(solution)/shard_map/ppermute | solution.py:378
  48.8 0.0 collective-permute-start.4
  48.8 0.0 collective-permute-done.refs_0_
  48.8 1.5 %collective-permute-start.5 = (bf16[10,128,128]{2,1,0:T(8,128)(2,1)}, bf16[10,128,128]{2,1,0:T(8,128)(2,1)S(1)}, u32[]{:S(2)}, u32[]{:S(2)}) collective-permute-start(bf16[10,128,128]{2,1,0:T(8,128)(2,1)} %get-tuple-element.43), channel_id=1, source_target_pairs={{0,24},{4,28},{8,16},{12,20},{16,8},{20,12},{24,0},{28,4},{1,25},{... | collective-permute-start | bytes 983048 | tf_op jit(solution)/shard_map/ppermute | solution.py:378
  50.3 0.0 collective-permute-done.1.refs_1_
  50.3 1.5 %collective-permute-start.6 = (bf16[10,128,128]{2,1,0:T(8,128)(2,1)}, bf16[10,128,128]{2,1,0:T(8,128)(2,1)S(1)}, u32[]{:S(2)}, u32[]{:S(2)}) collective-permute-start(bf16[10,128,128]{2,1,0:T(8,128)(2,1)} %get-tuple-element.44), channel_id=1, source_target_pairs={{0,28},{4,24},{8,20},{12,16},{16,12},{20,8},{24,4},{28,0},{1,29},{... | collective-permute-start | bytes 983048 | tf_op jit(solution)/shard_map/ppermute | solution.py:378
  51.7 0.1 select_reduce_fusion.1
  51.8 0.0 copy-start.1
  51.8 0.1 add_add_fusion.clip_ref
  51.9 0.0 copy-done
  51.9 0.5 copy-done.1
  52.4 0.0 copy-start.2
  52.4 3.6 %shard_map.88 = (bf16[2,128,128]{2,1,0:T(8,128)(2,1)S(1)}, bf16[2,128,128]{2,1,0:T(8,128)(2,1)S(1)}, bf16[2,128,128]{2,1,0:T(8,128)(2,1)S(1)}, bf16[2,128,128]{2,1,0:T(8,128)(2,1)S(1)}) custom-call(s32[1]{0:T(128)S(6)} %copy.9.first_ref, s32[3,8]{1,0:T(4,128)S(1)} %add_add_fusion.clip_ref, s32[3]{0:T(128)S(1)} %copy-done.1, ...), custom_call_target="tpu_custom_call" | custom-call | bytes 32768 | tf_op jit(solution)/shard_map/pallas_call | solution.py:332
  56.0 0.0 collective-permute-done.2.refs_2_
  56.0 7.0 %collective-permute-done.3.refs_3_ = bf16[10,128,128]{2,1,0:T(8,128)(2,1)S(1)} collective-permute-done((bf16[10,128,128]{2,1,0:T(8,128)(2,1)}, bf16[10,128,128]{2,1,0:T(8,128)(2,1)S(1)}, u32[]{:S(2)}, u32[]{:S(2)}) %collective-permute-start.3) | collective-permute-done | bytes 327712 | tf_op jit(solution)/shard_map/ppermute | solution.py:378
  63.1 0.0 collective-permute-done.4.refs_4_
  63.1 10.6 %collective-permute-done.5.refs_5_ = bf16[10,128,128]{2,1,0:T(8,128)(2,1)S(1)} collective-permute-done((bf16[10,128,128]{2,1,0:T(8,128)(2,1)}, bf16[10,128,128]{2,1,0:T(8,128)(2,1)S(1)}, u32[]{:S(2)}, u32[]{:S(2)}) %collective-permute-start.5) | collective-permute-done | bytes 327712 | tf_op jit(solution)/shard_map/ppermute | solution.py:378
  73.7 4.7 %collective-permute-done.6.refs_6_ = bf16[10,128,128]{2,1,0:T(8,128)(2,1)S(1)} collective-permute-done((bf16[10,128,128]{2,1,0:T(8,128)(2,1)}, bf16[10,128,128]{2,1,0:T(8,128)(2,1)S(1)}, u32[]{:S(2)}, u32[]{:S(2)}) %collective-permute-start.6) | collective-permute-done | bytes 327712 | tf_op jit(solution)/shard_map/ppermute | solution.py:378
  78.4 0.0 copy-done.2
  78.4 7.5 %shard_map.89 = (bf16[6,128,128]{2,1,0:T(8,128)(2,1)S(1)}, bf16[4,128,128]{2,1,0:T(8,128)(2,1)S(1)}, bf16[4,128,128]{2,1,0:T(8,128)(2,1)S(1)}, bf16[6,128,128]{2...) custom-call(s32[1]{0:T(128)S(6)} %copy.9.first_ref, ...), custom_call_target="tpu_custom_call" | custom-call | flops 2147483648 | bytes 3670016 | tf_op jit(solution)/shard_map/pallas_call | solution.py:238
  86.0 0.9 collective-permute-start.15
  86.9 0.0 collective-permute-start.16
  86.9 3.6 %collective-permute-start.14 = (bf16[6,128,128]{2,1,0:T(8,128)(2,1)S(1)}, bf16[6,128,128]{2,1,0:T(8,128)(2,1)S(1)}, u32[]{:S(2)}, u32[]{:S(2)}) collective-permute-start(bf16[6,128,128]{2,1,0:T(8,128)(2,1)S(1)} %get-tuple-element.66), channel_id=1, source_target_pairs={{0,16},{4,20},{8,24},{12,28},{16,0},{20,4},{24,8},{28,12},{1,17},{... | collective-permute-start | bytes 589832 | tf_op jit(solution)/shard_map/ppermute | solution.py:378
  90.4 0.2 collective-permute-start.17
  90.6 1.5 %collective-permute-start.18 = (bf16[6,128,128]{2,1,0:T(8,128)(2,1)S(1)}, bf16[6,128,128]{2,1,0:T(8,128)(2,1)S(1)}, u32[]{:S(2)}, u32[]{:S(2)}) collective-permute-start(bf16[6,128,128]{2,1,0:T(8,128)(2,1)S(1)} %get-tuple-element.70), channel_id=1, source_target_pairs={{0,24},{4,28},{8,16},{12,20},{16,8},{20,12},{24,0},{28,4},{1,25},{... | collective-permute-start | bytes 589832 | tf_op jit(solution)/shard_map/ppermute | solution.py:378
  92.1 0.0 collective-permute-done.15.refs_1_
  92.1 2.9 %collective-permute-start.19 = (bf16[4,128,128]{2,1,0:T(8,128)(2,1)S(1)}, bf16[4,128,128]{2,1,0:T(8,128)(2,1)S(1)}, u32[]{:S(2)}, u32[]{:S(2)}) collective-permute-start(bf16[4,128,128]{2,1,0:T(8,128)(2,1)S(1)} %get-tuple-element.71), channel_id=1, source_target_pairs={{0,12},{4,8},{8,4},{12,0},{16,28},{20,24},{24,20},{28,16},{1,13},{... | collective-permute-start | bytes 393224 | tf_op jit(solution)/shard_map/ppermute | solution.py:378
  95.0 4.2 %collective-permute-done.16.refs_2_ = bf16[4,128,128]{2,1,0:T(8,128)(2,1)S(1)} collective-permute-done((bf16[4,128,128]{2,1,0:T(8,128)(2,1)S(1)}, bf16[4,128,128]{2,1,0:T(8,128)(2,1)S(1)}, u32[]{:S(2)}, u32[]{:S(2)}) %collective-permute-start.16) | collective-permute-done | bytes 131104 | tf_op jit(solution)/shard_map/ppermute | solution.py:378
  99.2 0.5 collective-permute-start.20
  99.7 8.7 %collective-permute-done.19.refs_5_ = bf16[4,128,128]{2,1,0:T(8,128)(2,1)S(1)} collective-permute-done((bf16[4,128,128]{2,1,0:T(8,128)(2,1)S(1)}, bf16[4,128,128]{2,1,0:T(8,128)(2,1)S(1)}, u32[]{:S(2)}, u32[]{:S(2)}) %collective-permute-start.19) | collective-permute-done | bytes 131104 | tf_op jit(solution)/shard_map/ppermute | solution.py:378
  108.4 7.4 %collective-permute-done.20.refs_6_ = bf16[4,128,128]{2,1,0:T(8,128)(2,1)S(1)} collective-permute-done((bf16[4,128,128]{2,1,0:T(8,128)(2,1)S(1)}, bf16[4,128,128]{2,1,0:T(8,128)(2,1)S(1)}, u32[]{:S(2)}, u32[]{:S(2)}) %collective-permute-start.20) | collective-permute-done | bytes 131104 | tf_op jit(solution)/shard_map/ppermute | solution.py:378
  115.7 0.0 collective-permute-done.14.refs_0_
  115.7 0.0 collective-permute-done.17.refs_3_
  115.7 0.0 collective-permute-done.18.refs_4_
  115.7 1.8 %shard_map.90 = (bf16[1,128,2560]{2,1,0:T(8,128)(2,1)}, bf16[1,128,2560]{2,1,0:T(8,128)(2,1)}) custom-call(s32[3]{0:T(128)S(1)} %copy-done.1, bf16[6,128,128]{2,1,0:T(8,128)(2,1)S(1)} %collective-permute-done.14.refs_0_, bf16[4,128,128]{2,1,0:T(8,128)(2,1)S(1)} %collective-permute-done.15.refs_1_, bf16[4,128,128]{2,1,0:T(8,128)(2,1)S(1)} %collective-permute-done.16.refs_2_, ...), custom_call_target="tpu_custom_call" | custom-call | bytes 2621440 | tf_op jit(solution)/shard_map/pallas_call | solution.py:363
Async XLA Ops:
  2.7 14.2 %collective-permute-start.7 = (bf16[5,128,128]{2,1,0:T(8,128)(2,1)}, bf16[5,128,128]{2,1,0:T(8,128)(2,1)S(1)}, u32[]{:S(2)}, u32[]{:S(2)}) collective-permute-start(bf16[5,128,128]{2,1,0:T(8,128)(2,1)} %get-tuple-element.46), channel_id=1, source_target_pairs={{0,16},{4,20},{8,24},{12,28},{16,0},{20,4},{24,8},{28,12},{1,17},{... | collective-permute-start | bytes 491528 | tf_op jit(solution)/shard_map/ppermute | solution.py:378
  5.4 22.2 %collective-permute-start.8 = (bf16[5,128,128]{2,1,0:T(8,128)(2,1)}, bf16[5,128,128]{2,1,0:T(8,128)(2,1)S(1)}, u32[]{:S(2)}, u32[]{:S(2)}) collective-permute-start(bf16[5,128,128]{2,1,0:T(8,128)(2,1)} %get-tuple-element.47), channel_id=1, source_target_pairs={{0,24},{4,28},{8,16},{12,20},{16,8},{20,12},{24,0},{28,4},{1,25},{... | collective-permute-start | bytes 491528 | tf_op jit(solution)/shard_map/ppermute | solution.py:378
  5.4 23.7 %collective-permute-start.9 = (bf16[5,128,128]{2,1,0:T(8,128)(2,1)}, bf16[5,128,128]{2,1,0:T(8,128)(2,1)S(1)}, u32[]{:S(2)}, u32[]{:S(2)}) collective-permute-start(bf16[5,128,128]{2,1,0:T(8,128)(2,1)} %get-tuple-element.48), channel_id=1, source_target_pairs={{0,8},{4,12},{8,0},{12,4},{16,24},{20,28},{24,16},{28,20},{1,9},{5... | collective-permute-start | bytes 491528 | tf_op jit(solution)/shard_map/ppermute | solution.py:378
  7.2 22.4 %collective-permute-start.13 = (bf16[5,128,128]{2,1,0:T(8,128)(2,1)}, bf16[5,128,128]{2,1,0:T(8,128)(2,1)S(1)}, u32[]{:S(2)}, u32[]{:S(2)}) collective-permute-start(bf16[5,128,128]{2,1,0:T(8,128)(2,1)} %get-tuple-element.49.refs_3_), channel_id=1, source_target_pairs={{0,4},{4,0},{8,12},{12,8},{16,20},{20,16},{24,28},{28,24},{1,5},{5... | collective-permute-start | bytes 491528 | tf_op jit(solution)/shard_map/ppermute | solution.py:378
  9.3 42.6 %copy-start = (bf16[5,128,128]{2,1,0:T(8,128)(2,1)S(1)}, bf16[5,128,128]{2,1,0:T(8,128)(2,1)}, u32[]{:S(2)}) copy-start(bf16[5,128,128]{2,1,0:T(8,128)(2,1)} %get-tuple-element.49.refs_3_) | copy-start | bytes 491524
  13.4 35.3 %collective-permute-start = (bf16[10,128,128]{2,1,0:T(8,128)(2,1)}, bf16[10,128,128]{2,1,0:T(8,128)(2,1)S(1)}, u32[]{:S(2)}, u32[]{:S(2)}) collective-permute-start(bf16[10,128,128]{2,1,0:T(8,128)(2,1)} %get-tuple-element.38), channel_id=1, source_target_pairs={{0,16},{4,20},{8,24},{12,28},{16,0},{20,4},{24,8},{28,12},{1,17},{... | collective-permute-start | bytes 983048 | tf_op jit(solution)/shard_map/ppermute | solution.py:378
  16.9 33.3 %collective-permute-start.1 = (bf16[10,128,128]{2,1,0:T(8,128)(2,1)}, bf16[10,128,128]{2,1,0:T(8,128)(2,1)S(1)}, u32[]{:S(2)}, u32[]{:S(2)}) collective-permute-start(bf16[10,128,128]{2,1,0:T(8,128)(2,1)} %get-tuple-element.39), channel_id=1, source_target_pairs={{0,8},{4,12},{8,0},{12,4},{16,24},{20,28},{24,16},{28,20},{1,9},{5... | collective-permute-start | bytes 983048 | tf_op jit(solution)/shard_map/ppermute | solution.py:378
  27.6 7.1 %collective-permute-start.10 = (bf16[5,128,128]{2,1,0:T(8,128)(2,1)S(1)}, bf16[5,128,128]{2,1,0:T(8,128)(2,1)S(1)}, u32[]{:S(2)}, u32[]{:S(2)}) collective-permute-start(bf16[5,128,128]{2,1,0:T(8,128)(2,1)S(1)} %collective-permute-done.7.refs_0_), channel_id=1, source_target_pairs={{0,4},{4,0},{8,12},{12,8},{16,20},{20,16},{24,28},{28,24},{1,5},{5... | collective-permute-start | bytes 491528 | tf_op jit(solution)/shard_map/ppermute | solution.py:378
  29.1 16.2 %collective-permute-start.11 = (bf16[5,128,128]{2,1,0:T(8,128)(2,1)S(1)}, bf16[5,128,128]{2,1,0:T(8,128)(2,1)S(1)}, u32[]{:S(2)}, u32[]{:S(2)}) collective-permute-start(bf16[5,128,128]{2,1,0:T(8,128)(2,1)S(1)} %collective-permute-done.8.refs_1_), channel_id=1, source_target_pairs={{0,4},{4,0},{8,12},{12,8},{16,20},{20,16},{24,28},{28,24},{1,5},{5... | collective-permute-start | bytes 491528 | tf_op jit(solution)/shard_map/ppermute | solution.py:378
  29.6 19.2 %collective-permute-start.12 = (bf16[5,128,128]{2,1,0:T(8,128)(2,1)S(1)}, bf16[5,128,128]{2,1,0:T(8,128)(2,1)S(1)}, u32[]{:S(2)}, u32[]{:S(2)}) collective-permute-start(bf16[5,128,128]{2,1,0:T(8,128)(2,1)S(1)} %collective-permute-done.9.refs_2_), channel_id=1, source_target_pairs={{0,4},{4,0},{8,12},{12,8},{16,20},{20,16},{24,28},{28,24},{1,5},{5... | collective-permute-start | bytes 491528 | tf_op jit(solution)/shard_map/ppermute | solution.py:378
  31.7 0.7 copy-start.3
  34.7 21.3 %collective-permute-start.2 = (bf16[10,128,128]{2,1,0:T(8,128)(2,1)}, bf16[10,128,128]{2,1,0:T(8,128)(2,1)S(1)}, u32[]{:S(2)}, u32[]{:S(2)}) collective-permute-start(bf16[10,128,128]{2,1,0:T(8,128)(2,1)} %get-tuple-element.40), channel_id=1, source_target_pairs={{0,20},{4,16},{8,28},{12,24},{16,4},{20,0},{24,12},{28,8},{1,21},{... | collective-permute-start | bytes 983048 | tf_op jit(solution)/shard_map/ppermute | solution.py:378
  45.2 17.8 %collective-permute-start.3 = (bf16[10,128,128]{2,1,0:T(8,128)(2,1)}, bf16[10,128,128]{2,1,0:T(8,128)(2,1)S(1)}, u32[]{:S(2)}, u32[]{:S(2)}) collective-permute-start(bf16[10,128,128]{2,1,0:T(8,128)(2,1)} %get-tuple-element.41), channel_id=1, source_target_pairs={{0,4},{4,0},{8,12},{12,8},{16,20},{20,16},{24,28},{28,24},{1,5},{5... | collective-permute-start | bytes 983048 | tf_op jit(solution)/shard_map/ppermute | solution.py:378
  48.8 14.3 %collective-permute-start.4 = (bf16[10,128,128]{2,1,0:T(8,128)(2,1)}, bf16[10,128,128]{2,1,0:T(8,128)(2,1)S(1)}, u32[]{:S(2)}, u32[]{:S(2)}) collective-permute-start(bf16[10,128,128]{2,1,0:T(8,128)(2,1)} %get-tuple-element.42), channel_id=1, source_target_pairs={{0,12},{4,8},{8,4},{12,0},{16,28},{20,24},{24,20},{28,16},{1,13},{... | collective-permute-start | bytes 983048 | tf_op jit(solution)/shard_map/ppermute | solution.py:378
  48.8 24.9 %collective-permute-start.5 = (bf16[10,128,128]{2,1,0:T(8,128)(2,1)}, bf16[10,128,128]{2,1,0:T(8,128)(2,1)S(1)}, u32[]{:S(2)}, u32[]{:S(2)}) collective-permute-start(bf16[10,128,128]{2,1,0:T(8,128)(2,1)} %get-tuple-element.43), channel_id=1, source_target_pairs={{0,24},{4,28},{8,16},{12,20},{16,8},{20,12},{24,0},{28,4},{1,25},{... | collective-permute-start | bytes 983048 | tf_op jit(solution)/shard_map/ppermute | solution.py:378
  50.3 28.2 %collective-permute-start.6 = (bf16[10,128,128]{2,1,0:T(8,128)(2,1)}, bf16[10,128,128]{2,1,0:T(8,128)(2,1)S(1)}, u32[]{:S(2)}, u32[]{:S(2)}) collective-permute-start(bf16[10,128,128]{2,1,0:T(8,128)(2,1)} %get-tuple-element.44), channel_id=1, source_target_pairs={{0,28},{4,24},{8,20},{12,16},{16,12},{20,8},{24,4},{28,0},{1,29},{... | collective-permute-start | bytes 983048 | tf_op jit(solution)/shard_map/ppermute | solution.py:378
  51.8 0.6 copy-start.1
  52.4 26.0 %copy-start.2 = (bf16[10,128,128]{2,1,0:T(8,128)(2,1)S(1)}, bf16[10,128,128]{2,1,0:T(8,128)(2,1)}, u32[]{:S(2)}) copy-start(bf16[10,128,128]{2,1,0:T(8,128)(2,1)} %get-tuple-element.61.refs_7_) | copy-start | bytes 983044
  86.0 6.1 %collective-permute-start.15 = (bf16[4,128,128]{2,1,0:T(8,128)(2,1)S(1)}, bf16[4,128,128]{2,1,0:T(8,128)(2,1)S(1)}, u32[]{:S(2)}, u32[]{:S(2)}) collective-permute-start(bf16[4,128,128]{2,1,0:T(8,128)(2,1)S(1)} %get-tuple-element.67), channel_id=1, source_target_pairs={{0,4},{4,0},{8,12},{12,8},{16,20},{20,16},{24,28},{28,24},{1,5},{5... | collective-permute-start | bytes 393224 | tf_op jit(solution)/shard_map/ppermute | solution.py:378
  86.9 12.3 %collective-permute-start.16 = (bf16[4,128,128]{2,1,0:T(8,128)(2,1)S(1)}, bf16[4,128,128]{2,1,0:T(8,128)(2,1)S(1)}, u32[]{:S(2)}, u32[]{:S(2)}) collective-permute-start(bf16[4,128,128]{2,1,0:T(8,128)(2,1)S(1)} %get-tuple-element.68), channel_id=1, source_target_pairs={{0,20},{4,16},{8,28},{12,24},{16,4},{20,0},{24,12},{28,8},{1,21},{... | collective-permute-start | bytes 393224 | tf_op jit(solution)/shard_map/ppermute | solution.py:378
  86.9 28.9 %collective-permute-start.14 = (bf16[6,128,128]{2,1,0:T(8,128)(2,1)S(1)}, bf16[6,128,128]{2,1,0:T(8,128)(2,1)S(1)}, u32[]{:S(2)}, u32[]{:S(2)}) collective-permute-start(bf16[6,128,128]{2,1,0:T(8,128)(2,1)S(1)} %get-tuple-element.66), channel_id=1, source_target_pairs={{0,16},{4,20},{8,24},{12,28},{16,0},{20,4},{24,8},{28,12},{1,17},{... | collective-permute-start | bytes 589832 | tf_op jit(solution)/shard_map/ppermute | solution.py:378
  90.4 25.3 %collective-permute-start.17 = (bf16[6,128,128]{2,1,0:T(8,128)(2,1)S(1)}, bf16[6,128,128]{2,1,0:T(8,128)(2,1)S(1)}, u32[]{:S(2)}, u32[]{:S(2)}) collective-permute-start(bf16[6,128,128]{2,1,0:T(8,128)(2,1)S(1)} %get-tuple-element.69), channel_id=1, source_target_pairs={{0,8},{4,12},{8,0},{12,4},{16,24},{20,28},{24,16},{28,20},{1,9},{5... | collective-permute-start | bytes 589832 | tf_op jit(solution)/shard_map/ppermute | solution.py:378
  90.6 25.1 %collective-permute-start.18 = (bf16[6,128,128]{2,1,0:T(8,128)(2,1)S(1)}, bf16[6,128,128]{2,1,0:T(8,128)(2,1)S(1)}, u32[]{:S(2)}, u32[]{:S(2)}) collective-permute-start(bf16[6,128,128]{2,1,0:T(8,128)(2,1)S(1)} %get-tuple-element.70), channel_id=1, source_target_pairs={{0,24},{4,28},{8,16},{12,20},{16,8},{20,12},{24,0},{28,4},{1,25},{... | collective-permute-start | bytes 589832 | tf_op jit(solution)/shard_map/ppermute | solution.py:378
  92.1 16.3 %collective-permute-start.19 = (bf16[4,128,128]{2,1,0:T(8,128)(2,1)S(1)}, bf16[4,128,128]{2,1,0:T(8,128)(2,1)S(1)}, u32[]{:S(2)}, u32[]{:S(2)}) collective-permute-start(bf16[4,128,128]{2,1,0:T(8,128)(2,1)S(1)} %get-tuple-element.71), channel_id=1, source_target_pairs={{0,12},{4,8},{8,4},{12,0},{16,28},{20,24},{24,20},{28,16},{1,13},{... | collective-permute-start | bytes 393224 | tf_op jit(solution)/shard_map/ppermute | solution.py:378
  99.2 16.6 %collective-permute-start.20 = (bf16[4,128,128]{2,1,0:T(8,128)(2,1)S(1)}, bf16[4,128,128]{2,1,0:T(8,128)(2,1)S(1)}, u32[]{:S(2)}, u32[]{:S(2)}) collective-permute-start(bf16[4,128,128]{2,1,0:T(8,128)(2,1)S(1)} %get-tuple-element.72), channel_id=1, source_target_pairs={{0,28},{4,24},{8,20},{12,16},{16,12},{20,8},{24,4},{28,0},{1,29},{... | collective-permute-start | bytes 393224 | tf_op jit(solution)/shard_map/ppermute | solution.py:378

commit v5 on v4

--- a/solution.py
+++ b/solution.py
@@ -379,7 +379,7 @@
 
     far = list(range(rest, peers))
     near = sorted(range(1, rest), key=lambda d: (d % 2, d))
-    there = [far[0], near[0], far[1], *near[1:], *far[2:], 0]
+    there = [far[0]] + [d for pair in zip(far[1:], near) for d in pair] + [0]
     home = [far[0]] + [d for pair in zip(range(1, rest), far[1:]) for d in pair] + [0]
     across = [*range(rest // 2, rest), *range(1, rest // 2), 0]
 

time: 118 us -> 122 us (1.034)
  the two profiles are of different devices: /device:TPU:12 before, /device:TPU:10 now
where the time goes in v5:
time: 122 us; the launch traced here: 121 us
  waiting for transfers between devices  62.2 us (51%)
  starting transfers between devices  35.2 us (29%)
  Pallas kernels  19.2 us (16%)
  local copies, waits for them, and re-layouts  1.83 us (2%)
  other arithmetic  1.56 us (1%)
  between operations  1.37 us (1%)
    ppermute x21, waiting for transfers between devices, swapped(): lax.ppermute(x, 'tm', [(i, i ^ by) for i in range(peers)])  62.2 us
    ppermute x21, starting transfers between devices, swapped(): lax.ppermute(x, 'tm', [(i, i ^ by) for i in range(peers)])  35.2 us
    pallas_call x1, Pallas kernels, slots_kernel(): pl.pallas_call(body, in_specs=[SMEM] * 3 + [VMEM] * (blocks + len(pieces)...  7.54 us
    pallas_call x1, Pallas kernels, slots_pack(): pl.pallas_call(body, in_specs=[SMEM] + [pl.BlockSpec(memory_space=pl.ANY)...  4.14 us
    pallas_call x1, Pallas kernels, rest_kernel(): pl.pallas_call(body, in_specs=[SMEM] * 3 + [VMEM] * (2 * columns), out_sp...  3.56 us
  transfers between devices with their start and end apart: 21, of which 11 were waited for; matrix products, arithmetic and copies ran while one was open for 2% of the time, Pallas kernels for 6%

profile of v5, /device:TPU:10, one launch (start us, length us, event | category | flops | bytes accessed | tf_op | source)
XLA Modules:
  0.0 121.4 jit_solution(134617761383103621)
XLA Ops:
  0.6 2.1 %shard_map.87 = (bf16[5,128,128]{2,1,0:T(8,128)(2,1)}, bf16[5,128,128]{2,1,0:T(8,128)(2,1)}, bf16[5,128,128]{2,1,0:T(8,128)(2,1)}, bf16[5,128,128]{2,1,0:T(8,128)(2,1)}) custom-call(s32[1]{0:T(128)} %bitcast.column_ref, bf16[1,128,2560]{2,1,0:T(8,128)(2,1)} %refs_0_.3, bf16[1,128,2560]{2,1,0:T(8,128)(2,1)} %refs_1_.3, bf16[1,128,2560]{2,1,0:T(8,128)(2,1)} %refs_2_.3, ...), custom_call_target="tpu_custom_call" | custom-call | bytes 1310720 | tf_op jit(solution)/shard_map/pallas_call | solution.py:300
  2.7 2.7 %collective-permute-start.7 = (bf16[5,128,128]{2,1,0:T(8,128)(2,1)}, bf16[5,128,128]{2,1,0:T(8,128)(2,1)S(1)}, u32[]{:S(2)}, u32[]{:S(2)}) collective-permute-start(bf16[5,128,128]{2,1,0:T(8,128)(2,1)} %get-tuple-element.46), channel_id=1, source_target_pairs={{0,16},{4,20},{8,24},{12,28},{16,0},{20,4},{24,8},{28,12},{1,17},{... | collective-permute-start | bytes 491528 | tf_op jit(solution)/shard_map/ppermute | solution.py:378
  5.4 0.0 collective-permute-start.8
  5.4 1.8 %collective-permute-start.9 = (bf16[5,128,128]{2,1,0:T(8,128)(2,1)}, bf16[5,128,128]{2,1,0:T(8,128)(2,1)S(1)}, u32[]{:S(2)}, u32[]{:S(2)}) collective-permute-start(bf16[5,128,128]{2,1,0:T(8,128)(2,1)} %get-tuple-element.48), channel_id=1, source_target_pairs={{0,8},{4,12},{8,0},{12,4},{16,24},{20,28},{24,16},{28,20},{1,9},{5... | collective-permute-start | bytes 491528 | tf_op jit(solution)/shard_map/ppermute | solution.py:378
  7.2 0.5 collective-permute-start.13
  7.7 0.6 pad_add_fusion.where_ref
  8.3 0.0 copy-start
  8.3 4.1 %shard_map.86 = (bf16[10,128,128]{2,1,0:T(8,128)(2,1)}, bf16[10,128,128]{2,1,0:T(8,128)(2,1)}, bf16[10,128,128]{2,1,0:T(8,128)(2,1)}, bf16[10,128,128]{2,1,0:T(8...) custom-call(s32[3]{0:T(128)} %pad_add_fusion.where_ref, ...), custom_call_target="tpu_custom_call" | custom-call | bytes 5242880 | tf_op jit(solution)/shard_map/pallas_call | solution.py:272
  12.5 1.8 %collective-permute-start = (bf16[10,128,128]{2,1,0:T(8,128)(2,1)}, bf16[10,128,128]{2,1,0:T(8,128)(2,1)S(1)}, u32[]{:S(2)}, u32[]{:S(2)}) collective-permute-start(bf16[10,128,128]{2,1,0:T(8,128)(2,1)} %get-tuple-element.38), channel_id=1, source_target_pairs={{0,16},{4,20},{8,24},{12,28},{16,0},{20,4},{24,8},{28,12},{1,17},{... | collective-permute-start | bytes 983048 | tf_op jit(solution)/shard_map/ppermute | solution.py:378
  14.2 2.9 %collective-permute-done.7.refs_0_ = bf16[5,128,128]{2,1,0:T(8,128)(2,1)S(1)} collective-permute-done((bf16[5,128,128]{2,1,0:T(8,128)(2,1)}, bf16[5,128,128]{2,1,0:T(8,128)(2,1)S(1)}, u32[]{:S(2)}, u32[]{:S(2)}) %collective-permute-start.7) | collective-permute-done | bytes 163872 | tf_op jit(solution)/shard_map/ppermute | solution.py:378
  17.1 3.3 %collective-permute-start.1 = (bf16[10,128,128]{2,1,0:T(8,128)(2,1)}, bf16[10,128,128]{2,1,0:T(8,128)(2,1)S(1)}, u32[]{:S(2)}, u32[]{:S(2)}) collective-permute-start(bf16[10,128,128]{2,1,0:T(8,128)(2,1)} %get-tuple-element.39), channel_id=1, source_target_pairs={{0,20},{4,16},{8,28},{12,24},{16,4},{20,0},{24,12},{28,8},{1,21},{... | collective-permute-start | bytes 983048 | tf_op jit(solution)/shard_map/ppermute | solution.py:378
  20.4 14.2 %collective-permute-done.8.refs_1_ = bf16[5,128,128]{2,1,0:T(8,128)(2,1)S(1)} collective-permute-done((bf16[5,128,128]{2,1,0:T(8,128)(2,1)}, bf16[5,128,128]{2,1,0:T(8,128)(2,1)S(1)}, u32[]{:S(2)}, u32[]{:S(2)}) %collective-permute-start.8) | collective-permute-done | bytes 163872 | tf_op jit(solution)/shard_map/ppermute | solution.py:378
  34.6 0.2 collective-permute-start.10
  34.8 0.0 collective-permute-done.9.refs_2_
  34.8 1.8 %collective-permute-start.11 = (bf16[5,128,128]{2,1,0:T(8,128)(2,1)S(1)}, bf16[5,128,128]{2,1,0:T(8,128)(2,1)S(1)}, u32[]{:S(2)}, u32[]{:S(2)}) collective-permute-start(bf16[5,128,128]{2,1,0:T(8,128)(2,1)S(1)} %collective-permute-done.8.refs_1_), channel_id=1, source_target_pairs={{0,4},{4,0},{8,12},{12,8},{16,20},{20,16},{24,28},{28,24},{1,5},{5... | collective-permute-start | bytes 491528 | tf_op jit(solution)/shard_map/ppermute | solution.py:378
  36.6 0.0 collective-permute-done.13.refs_7_
  36.6 0.2 collective-permute-start.12
  37.5 0.0 copy-start.3
  37.5 0.6 copy-done.3
  38.1 0.2 reduce-window.8
  38.3 0.6 fusion
  38.9 0.6 pad.2.clone
  39.6 2.2 %collective-permute-done.10.refs_4_ = bf16[5,128,128]{2,1,0:T(8,128)(2,1)S(1)} collective-permute-done((bf16[5,128,128]{2,1,0:T(8,128)(2,1)S(1)}, bf16[5,128,128]{2,1,0:T(8,128)(2,1)S(1)}, u32[]{:S(2)}, u32[]{:S(2)}) %collective-permute-start.10) | collective-permute-done | bytes 163872 | tf_op jit(solution)/shard_map/ppermute | solution.py:378
  41.7 0.0 collective-permute-start.2
  41.7 2.1 %collective-permute-done.11.refs_5_ = bf16[5,128,128]{2,1,0:T(8,128)(2,1)S(1)} collective-permute-done((bf16[5,128,128]{2,1,0:T(8,128)(2,1)S(1)}, bf16[5,128,128]{2,1,0:T(8,128)(2,1)S(1)}, u32[]{:S(2)}, u32[]{:S(2)}) %collective-permute-start.11) | collective-permute-done | bytes 163872 | tf_op jit(solution)/shard_map/ppermute | solution.py:378
  43.9 1.6 %collective-permute-start.3 = (bf16[10,128,128]{2,1,0:T(8,128)(2,1)}, bf16[10,128,128]{2,1,0:T(8,128)(2,1)S(1)}, u32[]{:S(2)}, u32[]{:S(2)}) collective-permute-start(bf16[10,128,128]{2,1,0:T(8,128)(2,1)} %get-tuple-element.41), channel_id=1, source_target_pairs={{0,24},{4,28},{8,16},{12,20},{16,8},{20,12},{24,0},{28,4},{1,25},{... | collective-permute-start | bytes 983048 | tf_op jit(solution)/shard_map/ppermute | solution.py:378
  45.5 0.1 collective-permute-done.12.refs_6_
  45.6 2.3 %collective-permute-start.4 = (bf16[10,128,128]{2,1,0:T(8,128)(2,1)}, bf16[10,128,128]{2,1,0:T(8,128)(2,1)S(1)}, u32[]{:S(2)}, u32[]{:S(2)}) collective-permute-start(bf16[10,128,128]{2,1,0:T(8,128)(2,1)} %get-tuple-element.42), channel_id=1, source_target_pairs={{0,4},{4,0},{8,12},{12,8},{16,20},{20,16},{24,28},{28,24},{1,5},{5... | collective-permute-start | bytes 983048 | tf_op jit(solution)/shard_map/ppermute | solution.py:378
  48.0 0.0 collective-permute-done.refs_0_
  48.0 2.9 %collective-permute-start.5 = (bf16[10,128,128]{2,1,0:T(8,128)(2,1)}, bf16[10,128,128]{2,1,0:T(8,128)(2,1)S(1)}, u32[]{:S(2)}, u32[]{:S(2)}) collective-permute-start(bf16[10,128,128]{2,1,0:T(8,128)(2,1)} %get-tuple-element.43), channel_id=1, source_target_pairs={{0,28},{4,24},{8,20},{12,16},{16,12},{20,8},{24,4},{28,0},{1,29},{... | collective-permute-start | bytes 983048 | tf_op jit(solution)/shard_map/ppermute | solution.py:378
  50.8 0.4 collective-permute-done.1.refs_1_
  51.2 0.0 collective-permute-start.6
  51.2 0.1 select_reduce_fusion.1
  51.3 0.0 copy-start.1
  51.3 0.1 add_add_fusion.clip_ref
  51.3 0.0 copy-done
  51.3 0.5 copy-done.1
  51.9 0.0 copy-start.2
  51.9 3.6 %shard_map.88 = (bf16[2,128,128]{2,1,0:T(8,128)(2,1)S(1)}, bf16[2,128,128]{2,1,0:T(8,128)(2,1)S(1)}, bf16[2,128,128]{2,1,0:T(8,128)(2,1)S(1)}, bf16[2,128,128]{2,1,0:T(8,128)(2,1)S(1)}) custom-call(s32[1]{0:T(128)S(6)} %copy.9.first_ref, s32[3,8]{1,0:T(4,128)S(1)} %add_add_fusion.clip_ref, s32[3]{0:T(128)S(1)} %copy-done.1, ...), custom_call_target="tpu_custom_call" | custom-call | bytes 32768 | tf_op jit(solution)/shard_map/pallas_call | solution.py:332
  55.5 12.3 %collective-permute-done.2.refs_2_ = bf16[10,128,128]{2,1,0:T(8,128)(2,1)S(1)} collective-permute-done((bf16[10,128,128]{2,1,0:T(8,128)(2,1)}, bf16[10,128,128]{2,1,0:T(8,128)(2,1)S(1)}, u32[]{:S(2)}, u32[]{:S(2)}) %collective-permute-start.2) | collective-permute-done | bytes 327712 | tf_op jit(solution)/shard_map/ppermute | solution.py:378
  67.8 1.9 %collective-permute-done.3.refs_3_ = bf16[10,128,128]{2,1,0:T(8,128)(2,1)S(1)} collective-permute-done((bf16[10,128,128]{2,1,0:T(8,128)(2,1)}, bf16[10,128,128]{2,1,0:T(8,128)(2,1)S(1)}, u32[]{:S(2)}, u32[]{:S(2)}) %collective-permute-start.3) | collective-permute-done | bytes 327712 | tf_op jit(solution)/shard_map/ppermute | solution.py:378
  69.7 0.0 collective-permute-done.4.refs_4_
  69.7 7.8 %collective-permute-done.5.refs_5_ = bf16[10,128,128]{2,1,0:T(8,128)(2,1)S(1)} collective-permute-done((bf16[10,128,128]{2,1,0:T(8,128)(2,1)}, bf16[10,128,128]{2,1,0:T(8,128)(2,1)S(1)}, u32[]{:S(2)}, u32[]{:S(2)}) %collective-permute-start.5) | collective-permute-done | bytes 327712 | tf_op jit(solution)/shard_map/ppermute | solution.py:378
  77.4 0.0 collective-permute-done.6.refs_6_
  77.4 0.0 copy-done.2
  77.4 7.5 %shard_map.89 = (bf16[6,128,128]{2,1,0:T(8,128)(2,1)S(1)}, bf16[4,128,128]{2,1,0:T(8,128)(2,1)S(1)}, bf16[4,128,128]{2,1,0:T(8,128)(2,1)S(1)}, bf16[6,128,128]{2...) custom-call(s32[1]{0:T(128)S(6)} %copy.9.first_ref, ...), custom_call_target="tpu_custom_call" | custom-call | flops 2147483648 | bytes 3670016 | tf_op jit(solution)/shard_map/pallas_call | solution.py:238
  85.0 2.6 %collective-permute-start.15 = (bf16[4,128,128]{2,1,0:T(8,128)(2,1)S(1)}, bf16[4,128,128]{2,1,0:T(8,128)(2,1)S(1)}, u32[]{:S(2)}, u32[]{:S(2)}) collective-permute-start(bf16[4,128,128]{2,1,0:T(8,128)(2,1)S(1)} %get-tuple-element.67), channel_id=1, source_target_pairs={{0,4},{4,0},{8,12},{12,8},{16,20},{20,16},{24,28},{28,24},{1,5},{5... | collective-permute-start | bytes 393224 | tf_op jit(solution)/shard_map/ppermute | solution.py:378
  87.5 0.6 collective-permute-start.16
  88.1 1.8 %collective-permute-start.14 = (bf16[6,128,128]{2,1,0:T(8,128)(2,1)S(1)}, bf16[6,128,128]{2,1,0:T(8,128)(2,1)S(1)}, u32[]{:S(2)}, u32[]{:S(2)}) collective-permute-start(bf16[6,128,128]{2,1,0:T(8,128)(2,1)S(1)} %get-tuple-element.66), channel_id=1, source_target_pairs={{0,16},{4,20},{8,24},{12,28},{16,0},{20,4},{24,8},{28,12},{1,17},{... | collective-permute-start | bytes 589832 | tf_op jit(solution)/shard_map/ppermute | solution.py:378
  90.0 2.4 %collective-permute-start.17 = (bf16[6,128,128]{2,1,0:T(8,128)(2,1)S(1)}, bf16[6,128,128]{2,1,0:T(8,128)(2,1)S(1)}, u32[]{:S(2)}, u32[]{:S(2)}) collective-permute-start(bf16[6,128,128]{2,1,0:T(8,128)(2,1)S(1)} %get-tuple-element.69), channel_id=1, source_target_pairs={{0,8},{4,12},{8,0},{12,4},{16,24},{20,28},{24,16},{28,20},{1,9},{5... | collective-permute-start | bytes 589832 | tf_op jit(solution)/shard_map/ppermute | solution.py:378
  92.3 1.5 %collective-permute-start.18 = (bf16[6,128,128]{2,1,0:T(8,128)(2,1)S(1)}, bf16[6,128,128]{2,1,0:T(8,128)(2,1)S(1)}, u32[]{:S(2)}, u32[]{:S(2)}) collective-permute-start(bf16[6,128,128]{2,1,0:T(8,128)(2,1)S(1)} %get-tuple-element.70), channel_id=1, source_target_pairs={{0,24},{4,28},{8,16},{12,20},{16,8},{20,12},{24,0},{28,4},{1,25},{... | collective-permute-start | bytes 589832 | tf_op jit(solution)/shard_map/ppermute | solution.py:378
  93.8 0.0 collective-permute-done.15.refs_1_
  93.8 2.4 %collective-permute-start.19 = (bf16[4,128,128]{2,1,0:T(8,128)(2,1)S(1)}, bf16[4,128,128]{2,1,0:T(8,128)(2,1)S(1)}, u32[]{:S(2)}, u32[]{:S(2)}) collective-permute-start(bf16[4,128,128]{2,1,0:T(8,128)(2,1)S(1)} %get-tuple-element.71), channel_id=1, source_target_pairs={{0,12},{4,8},{8,4},{12,0},{16,28},{20,24},{24,20},{28,16},{1,13},{... | collective-permute-start | bytes 393224 | tf_op jit(solution)/shard_map/ppermute | solution.py:378
  96.2 0.0 collective-permute-done.16.refs_2_
  96.2 4.9 %collective-permute-start.20 = (bf16[4,128,128]{2,1,0:T(8,128)(2,1)S(1)}, bf16[4,128,128]{2,1,0:T(8,128)(2,1)S(1)}, u32[]{:S(2)}, u32[]{:S(2)}) collective-permute-start(bf16[4,128,128]{2,1,0:T(8,128)(2,1)S(1)} %get-tuple-element.72), channel_id=1, source_target_pairs={{0,28},{4,24},{8,20},{12,16},{16,12},{20,8},{24,4},{28,0},{1,29},{... | collective-permute-start | bytes 393224 | tf_op jit(solution)/shard_map/ppermute | solution.py:378
  101.2 11.4 %collective-permute-done.19.refs_5_ = bf16[4,128,128]{2,1,0:T(8,128)(2,1)S(1)} collective-permute-done((bf16[4,128,128]{2,1,0:T(8,128)(2,1)S(1)}, bf16[4,128,128]{2,1,0:T(8,128)(2,1)S(1)}, u32[]{:S(2)}, u32[]{:S(2)}) %collective-permute-start.19) | collective-permute-done | bytes 131104 | tf_op jit(solution)/shard_map/ppermute | solution.py:378
  112.5 7.0 %collective-permute-done.20.refs_6_ = bf16[4,128,128]{2,1,0:T(8,128)(2,1)S(1)} collective-permute-done((bf16[4,128,128]{2,1,0:T(8,128)(2,1)S(1)}, bf16[4,128,128]{2,1,0:T(8,128)(2,1)S(1)}, u32[]{:S(2)}, u32[]{:S(2)}) %collective-permute-start.20) | collective-permute-done | bytes 131104 | tf_op jit(solution)/shard_map/ppermute | solution.py:378
  119.5 0.0 collective-permute-done.14.refs_0_
  119.5 0.0 collective-permute-done.17.refs_3_
  119.5 0.0 collective-permute-done.18.refs_4_
  119.5 1.8 %shard_map.90 = (bf16[1,128,2560]{2,1,0:T(8,128)(2,1)}, bf16[1,128,2560]{2,1,0:T(8,128)(2,1)}) custom-call(s32[3]{0:T(128)S(1)} %copy-done.1, bf16[6,128,128]{2,1,0:T(8,128)(2,1)S(1)} %collective-permute-done.14.refs_0_, bf16[4,128,128]{2,1,0:T(8,128)(2,1)S(1)} %collective-permute-done.15.refs_1_, bf16[4,128,128]{2,1,0:T(8,128)(2,1)S(1)} %collective-permute-done.16.refs_2_, ...), custom_call_target="tpu_custom_call" | custom-call | bytes 2621440 | tf_op jit(solution)/shard_map/pallas_call | solution.py:363
Async XLA Ops:
  2.7 14.4 %collective-permute-start.7 = (bf16[5,128,128]{2,1,0:T(8,128)(2,1)}, bf16[5,128,128]{2,1,0:T(8,128)(2,1)S(1)}, u32[]{:S(2)}, u32[]{:S(2)}) collective-permute-start(bf16[5,128,128]{2,1,0:T(8,128)(2,1)} %get-tuple-element.46), channel_id=1, source_target_pairs={{0,16},{4,20},{8,24},{12,28},{16,0},{20,4},{24,8},{28,12},{1,17},{... | collective-permute-start | bytes 491528 | tf_op jit(solution)/shard_map/ppermute | solution.py:378
  5.4 29.2 %collective-permute-start.8 = (bf16[5,128,128]{2,1,0:T(8,128)(2,1)}, bf16[5,128,128]{2,1,0:T(8,128)(2,1)S(1)}, u32[]{:S(2)}, u32[]{:S(2)}) collective-permute-start(bf16[5,128,128]{2,1,0:T(8,128)(2,1)} %get-tuple-element.47), channel_id=1, source_target_pairs={{0,24},{4,28},{8,16},{12,20},{16,8},{20,12},{24,0},{28,4},{1,25},{... | collective-permute-start | bytes 491528 | tf_op jit(solution)/shard_map/ppermute | solution.py:378
  5.4 29.4 %collective-permute-start.9 = (bf16[5,128,128]{2,1,0:T(8,128)(2,1)}, bf16[5,128,128]{2,1,0:T(8,128)(2,1)S(1)}, u32[]{:S(2)}, u32[]{:S(2)}) collective-permute-start(bf16[5,128,128]{2,1,0:T(8,128)(2,1)} %get-tuple-element.48), channel_id=1, source_target_pairs={{0,8},{4,12},{8,0},{12,4},{16,24},{20,28},{24,16},{28,20},{1,9},{5... | collective-permute-start | bytes 491528 | tf_op jit(solution)/shard_map/ppermute | solution.py:378
  7.2 29.4 %collective-permute-start.13 = (bf16[5,128,128]{2,1,0:T(8,128)(2,1)}, bf16[5,128,128]{2,1,0:T(8,128)(2,1)S(1)}, u32[]{:S(2)}, u32[]{:S(2)}) collective-permute-start(bf16[5,128,128]{2,1,0:T(8,128)(2,1)} %get-tuple-element.49.refs_3_), channel_id=1, source_target_pairs={{0,4},{4,0},{8,12},{12,8},{16,20},{20,16},{24,28},{28,24},{1,5},{5... | collective-permute-start | bytes 491528 | tf_op jit(solution)/shard_map/ppermute | solution.py:378
  8.3 43.0 %copy-start = (bf16[5,128,128]{2,1,0:T(8,128)(2,1)S(1)}, bf16[5,128,128]{2,1,0:T(8,128)(2,1)}, u32[]{:S(2)}) copy-start(bf16[5,128,128]{2,1,0:T(8,128)(2,1)} %get-tuple-element.49.refs_3_) | copy-start | bytes 491524
  12.5 35.5 %collective-permute-start = (bf16[10,128,128]{2,1,0:T(8,128)(2,1)}, bf16[10,128,128]{2,1,0:T(8,128)(2,1)S(1)}, u32[]{:S(2)}, u32[]{:S(2)}) collective-permute-start(bf16[10,128,128]{2,1,0:T(8,128)(2,1)} %get-tuple-element.38), channel_id=1, source_target_pairs={{0,16},{4,20},{8,24},{12,28},{16,0},{20,4},{24,8},{28,12},{1,17},{... | collective-permute-start | bytes 983048 | tf_op jit(solution)/shard_map/ppermute | solution.py:378
  17.1 34.1 %collective-permute-start.1 = (bf16[10,128,128]{2,1,0:T(8,128)(2,1)}, bf16[10,128,128]{2,1,0:T(8,128)(2,1)S(1)}, u32[]{:S(2)}, u32[]{:S(2)}) collective-permute-start(bf16[10,128,128]{2,1,0:T(8,128)(2,1)} %get-tuple-element.39), channel_id=1, source_target_pairs={{0,20},{4,16},{8,28},{12,24},{16,4},{20,0},{24,12},{28,8},{1,21},{... | collective-permute-start | bytes 983048 | tf_op jit(solution)/shard_map/ppermute | solution.py:378
  34.6 7.1 %collective-permute-start.10 = (bf16[5,128,128]{2,1,0:T(8,128)(2,1)S(1)}, bf16[5,128,128]{2,1,0:T(8,128)(2,1)S(1)}, u32[]{:S(2)}, u32[]{:S(2)}) collective-permute-start(bf16[5,128,128]{2,1,0:T(8,128)(2,1)S(1)} %collective-permute-done.7.refs_0_), channel_id=1, source_target_pairs={{0,4},{4,0},{8,12},{12,8},{16,20},{20,16},{24,28},{28,24},{1,5},{5... | collective-permute-start | bytes 491528 | tf_op jit(solution)/shard_map/ppermute | solution.py:378
  34.8 9.1 %collective-permute-start.11 = (bf16[5,128,128]{2,1,0:T(8,128)(2,1)S(1)}, bf16[5,128,128]{2,1,0:T(8,128)(2,1)S(1)}, u32[]{:S(2)}, u32[]{:S(2)}) collective-permute-start(bf16[5,128,128]{2,1,0:T(8,128)(2,1)S(1)} %collective-permute-done.8.refs_1_), channel_id=1, source_target_pairs={{0,4},{4,0},{8,12},{12,8},{16,20},{20,16},{24,28},{28,24},{1,5},{5... | collective-permute-start | bytes 491528 | tf_op jit(solution)/shard_map/ppermute | solution.py:378
  36.6 9.0 %collective-permute-start.12 = (bf16[5,128,128]{2,1,0:T(8,128)(2,1)S(1)}, bf16[5,128,128]{2,1,0:T(8,128)(2,1)S(1)}, u32[]{:S(2)}, u32[]{:S(2)}) collective-permute-start(bf16[5,128,128]{2,1,0:T(8,128)(2,1)S(1)} %collective-permute-done.9.refs_2_), channel_id=1, source_target_pairs={{0,4},{4,0},{8,12},{12,8},{16,20},{20,16},{24,28},{28,24},{1,5},{5... | collective-permute-start | bytes 491528 | tf_op jit(solution)/shard_map/ppermute | solution.py:378
  37.5 0.7 copy-start.3
  41.7 26.0 %collective-permute-start.2 = (bf16[10,128,128]{2,1,0:T(8,128)(2,1)}, bf16[10,128,128]{2,1,0:T(8,128)(2,1)S(1)}, u32[]{:S(2)}, u32[]{:S(2)}) collective-permute-start(bf16[10,128,128]{2,1,0:T(8,128)(2,1)} %get-tuple-element.40), channel_id=1, source_target_pairs={{0,8},{4,12},{8,0},{12,4},{16,24},{20,28},{24,16},{28,20},{1,9},{5... | collective-permute-start | bytes 983048 | tf_op jit(solution)/shard_map/ppermute | solution.py:378
  43.9 25.8 %collective-permute-start.3 = (bf16[10,128,128]{2,1,0:T(8,128)(2,1)}, bf16[10,128,128]{2,1,0:T(8,128)(2,1)S(1)}, u32[]{:S(2)}, u32[]{:S(2)}) collective-permute-start(bf16[10,128,128]{2,1,0:T(8,128)(2,1)} %get-tuple-element.41), channel_id=1, source_target_pairs={{0,24},{4,28},{8,16},{12,20},{16,8},{20,12},{24,0},{28,4},{1,25},{... | collective-permute-start | bytes 983048 | tf_op jit(solution)/shard_map/ppermute | solution.py:378
  45.6 24.0 %collective-permute-start.4 = (bf16[10,128,128]{2,1,0:T(8,128)(2,1)}, bf16[10,128,128]{2,1,0:T(8,128)(2,1)S(1)}, u32[]{:S(2)}, u32[]{:S(2)}) collective-permute-start(bf16[10,128,128]{2,1,0:T(8,128)(2,1)} %get-tuple-element.42), channel_id=1, source_target_pairs={{0,4},{4,0},{8,12},{12,8},{16,20},{20,16},{24,28},{28,24},{1,5},{5... | collective-permute-start | bytes 983048 | tf_op jit(solution)/shard_map/ppermute | solution.py:378
  48.0 29.5 %collective-permute-start.5 = (bf16[10,128,128]{2,1,0:T(8,128)(2,1)}, bf16[10,128,128]{2,1,0:T(8,128)(2,1)S(1)}, u32[]{:S(2)}, u32[]{:S(2)}) collective-permute-start(bf16[10,128,128]{2,1,0:T(8,128)(2,1)} %get-tuple-element.43), channel_id=1, source_target_pairs={{0,28},{4,24},{8,20},{12,16},{16,12},{20,8},{24,4},{28,0},{1,29},{... | collective-permute-start | bytes 983048 | tf_op jit(solution)/shard_map/ppermute | solution.py:378
  51.2 26.2 %collective-permute-start.6 = (bf16[10,128,128]{2,1,0:T(8,128)(2,1)}, bf16[10,128,128]{2,1,0:T(8,128)(2,1)S(1)}, u32[]{:S(2)}, u32[]{:S(2)}) collective-permute-start(bf16[10,128,128]{2,1,0:T(8,128)(2,1)} %get-tuple-element.44), channel_id=1, source_target_pairs={{0,12},{4,8},{8,4},{12,0},{16,28},{20,24},{24,20},{28,16},{1,13},{... | collective-permute-start | bytes 983048 | tf_op jit(solution)/shard_map/ppermute | solution.py:378
  51.3 0.6 copy-start.1
  51.9 25.5 %copy-start.2 = (bf16[10,128,128]{2,1,0:T(8,128)(2,1)S(1)}, bf16[10,128,128]{2,1,0:T(8,128)(2,1)}, u32[]{:S(2)}) copy-start(bf16[10,128,128]{2,1,0:T(8,128)(2,1)} %get-tuple-element.61.refs_7_) | copy-start | bytes 983044
  85.0 8.8 %collective-permute-start.15 = (bf16[4,128,128]{2,1,0:T(8,128)(2,1)S(1)}, bf16[4,128,128]{2,1,0:T(8,128)(2,1)S(1)}, u32[]{:S(2)}, u32[]{:S(2)}) collective-permute-start(bf16[4,128,128]{2,1,0:T(8,128)(2,1)S(1)} %get-tuple-element.67), channel_id=1, source_target_pairs={{0,4},{4,0},{8,12},{12,8},{16,20},{20,16},{24,28},{28,24},{1,5},{5... | collective-permute-start | bytes 393224 | tf_op jit(solution)/shard_map/ppermute | solution.py:378
  87.5 8.7 %collective-permute-start.16 = (bf16[4,128,128]{2,1,0:T(8,128)(2,1)S(1)}, bf16[4,128,128]{2,1,0:T(8,128)(2,1)S(1)}, u32[]{:S(2)}, u32[]{:S(2)}) collective-permute-start(bf16[4,128,128]{2,1,0:T(8,128)(2,1)S(1)} %get-tuple-element.68), channel_id=1, source_target_pairs={{0,20},{4,16},{8,28},{12,24},{16,4},{20,0},{24,12},{28,8},{1,21},{... | collective-permute-start | bytes 393224 | tf_op jit(solution)/shard_map/ppermute | solution.py:378
  88.1 31.4 %collective-permute-start.14 = (bf16[6,128,128]{2,1,0:T(8,128)(2,1)S(1)}, bf16[6,128,128]{2,1,0:T(8,128)(2,1)S(1)}, u32[]{:S(2)}, u32[]{:S(2)}) collective-permute-start(bf16[6,128,128]{2,1,0:T(8,128)(2,1)S(1)} %get-tuple-element.66), channel_id=1, source_target_pairs={{0,16},{4,20},{8,24},{12,28},{16,0},{20,4},{24,8},{28,12},{1,17},{... | collective-permute-start | bytes 589832 | tf_op jit(solution)/shard_map/ppermute | solution.py:378
  90.0 29.6 %collective-permute-start.17 = (bf16[6,128,128]{2,1,0:T(8,128)(2,1)S(1)}, bf16[6,128,128]{2,1,0:T(8,128)(2,1)S(1)}, u32[]{:S(2)}, u32[]{:S(2)}) collective-permute-start(bf16[6,128,128]{2,1,0:T(8,128)(2,1)S(1)} %get-tuple-element.69), channel_id=1, source_target_pairs={{0,8},{4,12},{8,0},{12,4},{16,24},{20,28},{24,16},{28,20},{1,9},{5... | collective-permute-start | bytes 589832 | tf_op jit(solution)/shard_map/ppermute | solution.py:378
  92.3 27.2 %collective-permute-start.18 = (bf16[6,128,128]{2,1,0:T(8,128)(2,1)S(1)}, bf16[6,128,128]{2,1,0:T(8,128)(2,1)S(1)}, u32[]{:S(2)}, u32[]{:S(2)}) collective-permute-start(bf16[6,128,128]{2,1,0:T(8,128)(2,1)S(1)} %get-tuple-element.70), channel_id=1, source_target_pairs={{0,24},{4,28},{8,16},{12,20},{16,8},{20,12},{24,0},{28,4},{1,25},{... | collective-permute-start | bytes 589832 | tf_op jit(solution)/shard_map/ppermute | solution.py:378
  93.8 18.8 %collective-permute-start.19 = (bf16[4,128,128]{2,1,0:T(8,128)(2,1)S(1)}, bf16[4,128,128]{2,1,0:T(8,128)(2,1)S(1)}, u32[]{:S(2)}, u32[]{:S(2)}) collective-permute-start(bf16[4,128,128]{2,1,0:T(8,128)(2,1)S(1)} %get-tuple-element.71), channel_id=1, source_target_pairs={{0,12},{4,8},{8,4},{12,0},{16,28},{20,24},{24,20},{28,16},{1,13},{... | collective-permute-start | bytes 393224 | tf_op jit(solution)/shard_map/ppermute | solution.py:378
  96.2 23.3 %collective-permute-start.20 = (bf16[4,128,128]{2,1,0:T(8,128)(2,1)S(1)}, bf16[4,128,128]{2,1,0:T(8,128)(2,1)S(1)}, u32[]{:S(2)}, u32[]{:S(2)}) collective-permute-start(bf16[4,128,128]{2,1,0:T(8,128)(2,1)S(1)} %get-tuple-element.72), channel_id=1, source_target_pairs={{0,28},{4,24},{8,20},{12,16},{16,12},{20,8},{24,4},{28,0},{1,29},{... | collective-permute-start | bytes 393224 | tf_op jit(solution)/shard_map/ppermute | solution.py:378

commit v6 on v4

--- a/solution.py
+++ b/solution.py
@@ -212,7 +212,7 @@
     )(clips, role, arrived, gen, shared)
 
 
-def slots_kernel(full, order, home, first, clips, where, arrived, pieces):
+def slot_kernel(order, home, first, clips, where, arrived, pieces):
     blocks = len(order)
 
     def body(first_ref, clip_ref, where_ref, *refs):
@@ -223,32 +223,29 @@
         for i in range(blocks):
             x[at[i]] = x_refs[i][...]
 
-        def head(s, carry):
-            sources = [(x, 5 * s + t) for t in range(5)]
-            student_head(range(0, blocks, 2), first_ref[0], sources[:3], y, 2 * s)
-            gen = lambda at: y[at, 2 * s]
-            teacher_whole_head(blocks, clip_ref, sources[3:], gen, y, 2 * s + 1)
-
-        lax.fori_loop(0, full, head, None)
+        sources = [(x, t) for t in range(5)]
+        student_head(range(0, blocks, 2), first_ref[0], sources[:3], y, 0)
+        gen = lambda at: y[at, 0]
+        teacher_whole_head(blocks, clip_ref, sources[3:], gen, y, 1)
         for i, d in enumerate(home):
-            o_refs[i][0 : 2 * full] = y[where_ref[2] ^ d]
-            if d % 2 == 0:
-                o_refs[i][2 * full : 2 * full + 2] = piece_refs[d // 2][...]
+            o_refs[i][0:2] = y[where_ref[2] ^ d]
+            if pieces and d % 2 == 0:
+                o_refs[i][2:4] = piece_refs[d // 2][...]
 
     return pl.pallas_call(
         body,
         in_specs=[SMEM] * 3 + [VMEM] * (blocks + len(pieces)),
         out_specs=[VMEM] * blocks,
         out_shape=[
-            jax.ShapeDtypeStruct((2 * full + 2 * (d % 2 == 0), TOK, HD), jnp.bfloat16)
+            jax.ShapeDtypeStruct((4 if pieces and d % 2 == 0 else 2, TOK, HD), jnp.bfloat16)
             for d in home
         ],
         scratch_shapes=[
-            pltpu.VMEM((blocks, 5 * full, TOK, HD), jnp.bfloat16),
-            pltpu.VMEM((blocks, 2 * full, TOK, HD), jnp.bfloat16),
-        ],
-        compiler_params=LOCAL,
-        cost_estimate=cost(2 * full, blocks, 7 * full),
+            pltpu.VMEM((blocks, 5, TOK, HD), jnp.bfloat16),
+            pltpu.VMEM((blocks, 2, TOK, HD), jnp.bfloat16),
+        ],
+        compiler_params=LOCAL,
+        cost_estimate=cost(2, blocks, 7),
     )(first, clips, where, *arrived, *pieces)
 
 
@@ -256,7 +253,7 @@
     peers = len(order)
 
     def body(where_ref, *refs):
-        o_refs, (rows, sems) = refs[5 : 5 + peers], refs[5 + peers :]
+        o_refs, (rows, sems) = refs[5 : 5 + full * peers], refs[5 + full * peers :]
         copies = []
         for t in range(5):
             source = refs[t].at[0, :, pl.ds(0, full * peers * HD)]
@@ -267,13 +264,13 @@
             for s in range(full):
                 for i, d in enumerate(order):
                     at = pl.multiple_of((s * peers + (where_ref[2] ^ d)) * HD, HD)
-                    o_refs[i][5 * s + t] = rows[t, :, pl.ds(at, HD)]
-
-    return pl.pallas_call(
+                    o_refs[s * peers + i][t] = rows[t, :, pl.ds(at, HD)]
+
+    packed = pl.pallas_call(
         body,
         in_specs=[SMEM] + [pl.BlockSpec(memory_space=pl.ANY)] * 5,
-        out_specs=[VMEM] * peers,
-        out_shape=[jax.ShapeDtypeStruct((5 * full, TOK, HD), jnp.bfloat16)] * peers,
+        out_specs=[VMEM] * (full * peers),
+        out_shape=[jax.ShapeDtypeStruct((5, TOK, HD), jnp.bfloat16)] * (full * peers),
         scratch_shapes=[
             pltpu.VMEM((5, TOK, full * peers * HD), jnp.bfloat16),
             pltpu.SemaphoreType.DMA((5,)),
@@ -281,6 +278,7 @@
         compiler_params=WHOLE,
         cost_estimate=cost(0, peers, 10 * full),
     )(where, *tensors)
+    return [packed[s * peers : (s + 1) * peers] for s in range(full)]
 
 
 def rest_pack(base, columns, column, tensors):
@@ -347,22 +345,22 @@
     peers = len(order)
 
     def body(where_ref, *refs):
-        for i, o_ref in enumerate(refs[peers:]):
+        for i, o_ref in enumerate(refs[full * peers :]):
 
             def put(h, tile):
                 o_ref[0, :, pl.ds(pl.multiple_of(h * HD, HD), HD)] = tile
 
             for n, d in enumerate(order):
                 for s in range(full):
-                    put(s * peers + (where_ref[2] ^ d), refs[n][2 * s + i])
+                    put(s * peers + (where_ref[2] ^ d), refs[s * peers + n][i])
             for s in range(columns):
                 ref = refs[order.index(2 * s)]
-                put(full * peers + (where_ref[0] ^ s), ref[2 * full + i])
+                put(full * peers + (where_ref[0] ^ s), ref[2 + i])
 
     width = (full * peers + columns) * HD
     return pl.pallas_call(
         body,
-        in_specs=[SMEM] + [VMEM] * peers,
+        in_specs=[SMEM] + [VMEM] * (full * peers),
         out_specs=[VMEM] * 2,
         out_shape=[jax.ShapeDtypeStruct((1, TOK, width), jnp.bfloat16)] * 2,
         compiler_params=LOCAL,
@@ -386,12 +384,14 @@
     pieces = rest_pack(full * peers, rest, where[:1], tensors)
     own = [swapped(pieces[s], 2 * s) for s in across]
     packed = slots_pack(full, there, where, tensors)
-    arrived = [swapped(x, d) for x, d in zip(packed, there)]
+    arrived = [[swapped(x, d) for x, d in zip(xs, there)] for xs in packed]
     other = [swapped(x, 1) for x in own]
     pieces = rest_kernel(rest, across, first, clips, where, own, other)
-    arrived, pieces = lax.optimization_barrier((arrived, pieces))
-    results = slots_kernel(full, there, home, first, clips, where, arrived, pieces)
-    slots = [swapped(x, d) for x, d in zip(results, home)]
+    slots = []
+    for xs in arrived:
+        results = slot_kernel(there, home, first, clips, where, xs, pieces)
+        slots += [swapped(x, d) for x, d in zip(results, home)]
+        pieces = ()
     return tuple(join(full, home, rest, where, slots))
 
 

time: 118 us -> 125 us (1.059)
  the two profiles are of different devices: /device:TPU:12 before, /device:TPU:0 now
where the time goes in v6:
time: 125 us
  starting transfers between devices  66.4 us (53%)
  waiting for transfers between devices  33.7 us (27%)
  Pallas kernels  19.6 us (16%)
  local copies, waits for them, and re-layouts  2 us (2%)
  other arithmetic  1.55 us (1%)
  between operations  1.49 us (1%)
    ppermute x35, starting transfers between devices, swapped(): lax.ppermute(x, 'tm', [(i, i ^ by) for i in range(peers)])  66.4 us
    ppermute x35, waiting for transfers between devices, swapped(): lax.ppermute(x, 'tm', [(i, i ^ by) for i in range(peers)])  33.7 us
    pallas_call x2, Pallas kernels, slot_kernel(): pl.pallas_call(body, in_specs=[SMEM] * 3 + [VMEM] * (blocks + len(pieces)...  8.1 us
    pallas_call x1, Pallas kernels, slots_pack(): pl.pallas_call(body, in_specs=[SMEM] + [pl.BlockSpec(memory_space=pl.ANY)...  3.98 us
    pallas_call x1, Pallas kernels, rest_kernel(): pl.pallas_call(body, in_specs=[SMEM] * 3 + [VMEM] * (2 * columns), out_sp...  3.6 us
  transfers between devices with their start and end apart: 35, of which 11 were waited for; matrix products, arithmetic and copies ran while one was open for 1% of the time, Pallas kernels for 11%

profile of v6, /device:TPU:0, one launch (start us, length us, event | category | flops | bytes accessed | tf_op | source)
XLA Modules:
  0.0 124.7 jit_solution(12554695758864908023)
XLA Ops:
  0.6 0.6 pad_add_fusion.where_ref
  1.2 4.0 %shard_map.86 = (bf16[5,128,128]{2,1,0:T(8,128)(2,1)}, bf16[5,128,128]{2,1,0:T(8,128)(2,1)}, bf16[5,128,128]{2,1,0:T(8,128)(2,1)}, bf16[5,128,128]{2,1,0:T(8,128...) custom-call(s32[3]{0:T(128)} %pad_add_fusion.where_ref, ...), custom_call_target="tpu_custom_call" | custom-call | bytes 5242880 | tf_op jit(solution)/shard_map/pallas_call | solution.py:269
  5.2 4.1 %collective-permute-start.21 = (bf16[5,128,128]{2,1,0:T(8,128)(2,1)}, bf16[5,128,128]{2,1,0:T(8,128)(2,1)S(1)}, u32[]{:S(2)}, u32[]{:S(2)}) collective-permute-start(bf16[5,128,128]{2,1,0:T(8,128)(2,1)} %get-tuple-element.66), channel_id=1, source_target_pairs={{0,16},{4,20},{8,24},{12,28},{16,0},{20,4},{24,8},{28,12},{1,17},{... | collective-permute-start | bytes 491528 | tf_op jit(solution)/shard_map/ppermute | solution.py:376
  9.3 1.6 %collective-permute-start.22 = (bf16[5,128,128]{2,1,0:T(8,128)(2,1)}, bf16[5,128,128]{2,1,0:T(8,128)(2,1)S(1)}, u32[]{:S(2)}, u32[]{:S(2)}) collective-permute-start(bf16[5,128,128]{2,1,0:T(8,128)(2,1)} %get-tuple-element.67), channel_id=1, source_target_pairs={{0,8},{4,12},{8,0},{12,4},{16,24},{20,28},{24,16},{28,20},{1,9},{5... | collective-permute-start | bytes 491528 | tf_op jit(solution)/shard_map/ppermute | solution.py:376
  10.9 1.3 %collective-permute-start.23 = (bf16[5,128,128]{2,1,0:T(8,128)(2,1)}, bf16[5,128,128]{2,1,0:T(8,128)(2,1)S(1)}, u32[]{:S(2)}, u32[]{:S(2)}) collective-permute-start(bf16[5,128,128]{2,1,0:T(8,128)(2,1)} %get-tuple-element.68), channel_id=1, source_target_pairs={{0,20},{4,16},{8,28},{12,24},{16,4},{20,0},{24,12},{28,8},{1,21},{... | collective-permute-start | bytes 491528 | tf_op jit(solution)/shard_map/ppermute | solution.py:376
  12.2 0.5 collective-permute-start.24
  12.8 1.4 %collective-permute-start.25 = (bf16[5,128,128]{2,1,0:T(8,128)(2,1)}, bf16[5,128,128]{2,1,0:T(8,128)(2,1)S(1)}, u32[]{:S(2)}, u32[]{:S(2)}) collective-permute-start(bf16[5,128,128]{2,1,0:T(8,128)(2,1)} %get-tuple-element.70), channel_id=1, source_target_pairs={{0,12},{4,8},{8,4},{12,0},{16,28},{20,24},{24,20},{28,16},{1,13},{... | collective-permute-start | bytes 491528 | tf_op jit(solution)/shard_map/ppermute | solution.py:376
  14.2 2.1 %shard_map.87 = (bf16[5,128,128]{2,1,0:T(8,128)(2,1)}, bf16[5,128,128]{2,1,0:T(8,128)(2,1)}, bf16[5,128,128]{2,1,0:T(8,128)(2,1)}, bf16[5,128,128]{2,1,0:T(8,128)(2,1)}) custom-call(s32[1]{0:T(128)} %bitcast.column_ref, bf16[1,128,2560]{2,1,0:T(8,128)(2,1)} %refs_0_.3, bf16[1,128,2560]{2,1,0:T(8,128)(2,1)} %refs_1_.3, bf16[1,128,2560]{2,1,0:T(8,128)(2,1)} %refs_2_.3, ...), custom_call_target="tpu_custom_call" | custom-call | bytes 1310720 | tf_op jit(solution)/shard_map/pallas_call | solution.py:298
  16.3 2.7 %collective-permute-done.21.refs_0_ = bf16[5,128,128]{2,1,0:T(8,128)(2,1)S(1)} collective-permute-done((bf16[5,128,128]{2,1,0:T(8,128)(2,1)}, bf16[5,128,128]{2,1,0:T(8,128)(2,1)S(1)}, u32[]{:S(2)}, u32[]{:S(2)}) %collective-permute-start.21) | collective-permute-done | bytes 163872 | tf_op jit(solution)/shard_map/ppermute | solution.py:376
  19.0 3.1 %collective-permute-start.26 = (bf16[5,128,128]{2,1,0:T(8,128)(2,1)S(1)}, bf16[5,128,128]{2,1,0:T(8,128)(2,1)S(1)}, u32[]{:S(2)}, u32[]{:S(2)}) collective-permute-start(bf16[5,128,128]{2,1,0:T(8,128)(2,1)S(1)} %copy-done.12), channel_id=1, source_target_pairs={{0,24},{4,28},{8,16},{12,20},{16,8},{20,12},{24,0},{28,4},{1,25},{... | collective-permute-start | bytes 491528 | tf_op jit(solution)/shard_map/ppermute | solution.py:376
  22.1 3.6 %collective-permute-start.27 = (bf16[5,128,128]{2,1,0:T(8,128)(2,1)S(1)}, bf16[5,128,128]{2,1,0:T(8,128)(2,1)S(1)}, u32[]{:S(2)}, u32[]{:S(2)}) collective-permute-start(bf16[5,128,128]{2,1,0:T(8,128)(2,1)S(1)} %copy-done.11), channel_id=1, source_target_pairs={{0,28},{4,24},{8,20},{12,16},{16,12},{20,8},{24,4},{28,0},{1,29},{... | collective-permute-start | bytes 491528 | tf_op jit(solution)/shard_map/ppermute | solution.py:376
  25.7 1.2 collective-permute-done.23.refs_2_
  26.9 0.0 collective-permute-start.7
  26.9 0.7 copy-done.13
  27.6 0.2 reduce-window.8
  27.8 3.1 %collective-permute-start.8 = (bf16[5,128,128]{2,1,0:T(8,128)(2,1)}, bf16[5,128,128]{2,1,0:T(8,128)(2,1)S(1)}, u32[]{:S(2)}, u32[]{:S(2)}) collective-permute-start(bf16[5,128,128]{2,1,0:T(8,128)(2,1)} %get-tuple-element.51), channel_id=1, source_target_pairs={{0,24},{4,28},{8,16},{12,20},{16,8},{20,12},{24,0},{28,4},{1,25},{... | collective-permute-start | bytes 491528 | tf_op jit(solution)/shard_map/ppermute | solution.py:376
  30.9 0.0 collective-permute-start.9
  30.9 0.0 collective-permute-done.26.refs_5_
  30.9 1.4 %collective-permute-start.13 = (bf16[5,128,128]{2,1,0:T(8,128)(2,1)}, bf16[5,128,128]{2,1,0:T(8,128)(2,1)S(1)}, u32[]{:S(2)}, u32[]{:S(2)}) collective-permute-start(bf16[5,128,128]{2,1,0:T(8,128)(2,1)} %get-tuple-element.53.refs_3_), channel_id=1, source_target_pairs={{0,4},{4,0},{8,12},{12,8},{16,20},{20,16},{24,28},{28,24},{1,5},{5... | collective-permute-start | bytes 491528 | tf_op jit(solution)/shard_map/ppermute | solution.py:376
  32.3 3.0 %collective-permute-done.27.refs_6_ = bf16[5,128,128]{2,1,0:T(8,128)(2,1)S(1)} collective-permute-done((bf16[5,128,128]{2,1,0:T(8,128)(2,1)S(1)}, bf16[5,128,128]{2,1,0:T(8,128)(2,1)S(1)}, u32[]{:S(2)}, u32[]{:S(2)}) %collective-permute-start.27) | collective-permute-done | bytes 163872 | tf_op jit(solution)/shard_map/ppermute | solution.py:376
  35.2 13.8 %collective-permute-start = (bf16[5,128,128]{2,1,0:T(8,128)(2,1)S(1)}, bf16[5,128,128]{2,1,0:T(8,128)(2,1)S(1)}, u32[]{:S(2)}, u32[]{:S(2)}) collective-permute-start(bf16[5,128,128]{2,1,0:T(8,128)(2,1)S(1)} %copy-done.10), channel_id=1, source_target_pairs={{0,16},{4,20},{8,24},{12,28},{16,0},{20,4},{24,8},{28,12},{1,17},{... | collective-permute-start | bytes 491528 | tf_op jit(solution)/shard_map/ppermute | solution.py:376
  49.1 2.4 %collective-permute-done.7.refs_0_ = bf16[5,128,128]{2,1,0:T(8,128)(2,1)S(1)} collective-permute-done((bf16[5,128,128]{2,1,0:T(8,128)(2,1)}, bf16[5,128,128]{2,1,0:T(8,128)(2,1)S(1)}, u32[]{:S(2)}, u32[]{:S(2)}) %collective-permute-start.7) | collective-permute-done | bytes 163872 | tf_op jit(solution)/shard_map/ppermute | solution.py:376
  51.5 0.0 collective-permute-start.1
  51.5 0.6 fusion
  52.1 0.7 pad.2.clone
  52.8 0.1 select_reduce_fusion.1
  52.9 0.0 collective-permute-done.8.refs_1_
  52.9 6.6 %collective-permute-start.2 = (bf16[5,128,128]{2,1,0:T(8,128)(2,1)S(1)}, bf16[5,128,128]{2,1,0:T(8,128)(2,1)S(1)}, u32[]{:S(2)}, u32[]{:S(2)}) collective-permute-start(bf16[5,128,128]{2,1,0:T(8,128)(2,1)S(1)} %copy-done.8), channel_id=1, source_target_pairs={{0,20},{4,16},{8,28},{12,24},{16,4},{20,0},{24,12},{28,8},{1,21},{... | collective-permute-start | bytes 491528 | tf_op jit(solution)/shard_map/ppermute | solution.py:376
  59.6 0.0 collective-permute-done.9.refs_2_
  59.6 0.5 collective-permute-start.3
  60.1 0.0 collective-permute-done.13.refs_7_
  60.1 1.5 %collective-permute-start.10 = (bf16[5,128,128]{2,1,0:T(8,128)(2,1)S(1)}, bf16[5,128,128]{2,1,0:T(8,128)(2,1)S(1)}, u32[]{:S(2)}, u32[]{:S(2)}) collective-permute-start(bf16[5,128,128]{2,1,0:T(8,128)(2,1)S(1)} %collective-permute-done.7.refs_0_), channel_id=1, source_target_pairs={{0,4},{4,0},{8,12},{12,8},{16,20},{20,16},{24,28},{28,24},{1,5},{5... | collective-permute-start | bytes 491528 | tf_op jit(solution)/shard_map/ppermute | solution.py:376
  61.6 0.5 collective-permute-start.11
  62.2 1.5 %collective-permute-start.12 = (bf16[5,128,128]{2,1,0:T(8,128)(2,1)S(1)}, bf16[5,128,128]{2,1,0:T(8,128)(2,1)S(1)}, u32[]{:S(2)}, u32[]{:S(2)}) collective-permute-start(bf16[5,128,128]{2,1,0:T(8,128)(2,1)S(1)} %collective-permute-done.9.refs_2_), channel_id=1, source_target_pairs={{0,4},{4,0},{8,12},{12,8},{16,20},{20,16},{24,28},{28,24},{1,5},{5... | collective-permute-start | bytes 491528 | tf_op jit(solution)/shard_map/ppermute | solution.py:376
  63.7 0.1 add_add_fusion.clip_ref
  64.4 3.2 %collective-permute-done.2.refs_2_ = bf16[5,128,128]{2,1,0:T(8,128)(2,1)S(1)} collective-permute-done((bf16[5,128,128]{2,1,0:T(8,128)(2,1)S(1)}, bf16[5,128,128]{2,1,0:T(8,128)(2,1)S(1)}, u32[]{:S(2)}, u32[]{:S(2)}) %collective-permute-start.2) | collective-permute-done | bytes 163872 | tf_op jit(solution)/shard_map/ppermute | solution.py:376
  67.6 0.6 collective-permute-start.4
  68.2 1.8 %collective-permute-done.3.refs_3_ = bf16[5,128,128]{2,1,0:T(8,128)(2,1)S(1)} collective-permute-done((bf16[5,128,128]{2,1,0:T(8,128)(2,1)S(1)}, bf16[5,128,128]{2,1,0:T(8,128)(2,1)S(1)}, u32[]{:S(2)}, u32[]{:S(2)}) %collective-permute-start.3) | collective-permute-done | bytes 163872 | tf_op jit(solution)/shard_map/ppermute | solution.py:376
  70.0 1.6 %collective-permute-start.5 = (bf16[5,128,128]{2,1,0:T(8,128)(2,1)S(1)}, bf16[5,128,128]{2,1,0:T(8,128)(2,1)S(1)}, u32[]{:S(2)}, u32[]{:S(2)}) collective-permute-start(bf16[5,128,128]{2,1,0:T(8,128)(2,1)S(1)} %copy-done.5), channel_id=1, source_target_pairs={{0,24},{4,28},{8,16},{12,20},{16,8},{20,12},{24,0},{28,4},{1,25},{... | collective-permute-start | bytes 491528 | tf_op jit(solution)/shard_map/ppermute | solution.py:376
  71.5 5.4 %collective-permute-done.10.refs_4_ = bf16[5,128,128]{2,1,0:T(8,128)(2,1)S(1)} collective-permute-done((bf16[5,128,128]{2,1,0:T(8,128)(2,1)S(1)}, bf16[5,128,128]{2,1,0:T(8,128)(2,1)S(1)}, u32[]{:S(2)}, u32[]{:S(2)}) %collective-permute-start.10) | collective-permute-done | bytes 163872 | tf_op jit(solution)/shard_map/ppermute | solution.py:376
  77.0 0.6 copy-done.1
  77.6 4.1 %shard_map.90 = (bf16[2,128,128]{2,1,0:T(8,128)(2,1)S(1)}, bf16[2,128,128]{2,1,0:T(8,128)(2,1)S(1)}, bf16[2,128,128]{2,1,0:T(8,128)(2,1)S(1)}, bf16[2,128,128]{2...) custom-call(s32[1]{0:T(128)S(6)} %copy.9.first_ref, ...), custom_call_target="tpu_custom_call" | custom-call | flops 1073741824 | bytes 1835008 | tf_op jit(solution)/shard_map/pallas_call | solution.py:235
  81.7 0.6 collective-permute-done.11.refs_5_
  82.3 4.2 %collective-permute-done.12.refs_6_ = bf16[5,128,128]{2,1,0:T(8,128)(2,1)S(1)} collective-permute-done((bf16[5,128,128]{2,1,0:T(8,128)(2,1)S(1)}, bf16[5,128,128]{2,1,0:T(8,128)(2,1)S(1)}, u32[]{:S(2)}, u32[]{:S(2)}) %collective-permute-start.12) | collective-permute-done | bytes 163872 | tf_op jit(solution)/shard_map/ppermute | solution.py:376
  86.5 3.6 %shard_map.88 = (bf16[2,128,128]{2,1,0:T(8,128)(2,1)S(1)}, bf16[2,128,128]{2,1,0:T(8,128)(2,1)S(1)}, bf16[2,128,128]{2,1,0:T(8,128)(2,1)S(1)}, bf16[2,128,128]{2,1,0:T(8,128)(2,1)S(1)}) custom-call(s32[1]{0:T(128)S(6)} %copy.9.first_ref, s32[3,8]{1,0:T(4,128)S(1)} %add_add_fusion.clip_ref, s32[3]{0:T(128)S(1)} %copy-done.1, ...), custom_call_target="tpu_custom_call" | custom-call | bytes 32768 | tf_op jit(solution)/shard_map/pallas_call | solution.py:330
  90.1 0.0 collective-permute-done.4.refs_4_
  90.1 0.2 collective-permute-start.30
  90.3 0.0 collective-permute-done.5.refs_5_
  90.3 3.0 %collective-permute-start.31 = (bf16[2,128,128]{2,1,0:T(8,128)(2,1)S(1)}, bf16[2,128,128]{2,1,0:T(8,128)(2,1)S(1)}, u32[]{:S(2)}, u32[]{:S(2)}) collective-permute-start(bf16[2,128,128]{2,1,0:T(8,128)(2,1)S(1)} %get-tuple-element.77), channel_id=1, source_target_pairs={{0,8},{4,12},{8,0},{12,4},{16,24},{20,28},{24,16},{28,20},{1,9},{5... | collective-permute-start | bytes 196616 | tf_op jit(solution)/shard_map/ppermute | solution.py:376
  93.4 0.0 collective-permute-done.6.refs_6_
  93.4 2.7 %collective-permute-start.32 = (bf16[2,128,128]{2,1,0:T(8,128)(2,1)S(1)}, bf16[2,128,128]{2,1,0:T(8,128)(2,1)S(1)}, u32[]{:S(2)}, u32[]{:S(2)}) collective-permute-start(bf16[2,128,128]{2,1,0:T(8,128)(2,1)S(1)} %get-tuple-element.78), channel_id=1, source_target_pairs={{0,24},{4,28},{8,16},{12,20},{16,8},{20,12},{24,0},{28,4},{1,25},{... | collective-permute-start | bytes 196616 | tf_op jit(solution)/shard_map/ppermute | solution.py:376
  96.0 0.0 collective-permute-done.28.refs_8_
  96.1 1.2 collective-permute-start.34
  97.3 4.0 %shard_map.89 = (bf16[4,128,128]{2,1,0:T(8,128)(2,1)S(1)}, bf16[2,128,128]{2,1,0:T(8,128)(2,1)S(1)}, bf16[2,128,128]{2,1,0:T(8,128)(2,1)S(1)}, bf16[4,128,128]{2...) custom-call(s32[1]{0:T(128)S(6)} %copy.9.first_ref, ...), custom_call_target="tpu_custom_call" | custom-call | flops 1073741824 | bytes 1835008 | tf_op jit(solution)/shard_map/pallas_call | solution.py:235
  101.3 3.2 %collective-permute-start.14 = (bf16[4,128,128]{2,1,0:T(8,128)(2,1)S(1)}, bf16[4,128,128]{2,1,0:T(8,128)(2,1)S(1)}, u32[]{:S(2)}, u32[]{:S(2)}) collective-permute-start(bf16[4,128,128]{2,1,0:T(8,128)(2,1)S(1)} %get-tuple-element.58), channel_id=1, source_target_pairs={{0,16},{4,20},{8,24},{12,28},{16,0},{20,4},{24,8},{28,12},{1,17},{... | collective-permute-start | bytes 393224 | tf_op jit(solution)/shard_map/ppermute | solution.py:376
  104.6 0.0 collective-permute-start.15
  104.6 1.5 %collective-permute-start.16 = (bf16[2,128,128]{2,1,0:T(8,128)(2,1)S(1)}, bf16[2,128,128]{2,1,0:T(8,128)(2,1)S(1)}, u32[]{:S(2)}, u32[]{:S(2)}) collective-permute-start(bf16[2,128,128]{2,1,0:T(8,128)(2,1)S(1)} %get-tuple-element.60), channel_id=1, source_target_pairs={{0,20},{4,16},{8,28},{12,24},{16,4},{20,0},{24,12},{28,8},{1,21},{... | collective-permute-start | bytes 196616 | tf_op jit(solution)/shard_map/ppermute | solution.py:376
  106.1 1.6 %collective-permute-start.17 = (bf16[4,128,128]{2,1,0:T(8,128)(2,1)S(1)}, bf16[4,128,128]{2,1,0:T(8,128)(2,1)S(1)}, u32[]{:S(2)}, u32[]{:S(2)}) collective-permute-start(bf16[4,128,128]{2,1,0:T(8,128)(2,1)S(1)} %get-tuple-element.61), channel_id=1, source_target_pairs={{0,8},{4,12},{8,0},{12,4},{16,24},{20,28},{24,16},{28,20},{1,9},{5... | collective-permute-start | bytes 393224 | tf_op jit(solution)/shard_map/ppermute | solution.py:376
  107.8 2.7 %collective-permute-start.18 = (bf16[4,128,128]{2,1,0:T(8,128)(2,1)S(1)}, bf16[4,128,128]{2,1,0:T(8,128)(2,1)S(1)}, u32[]{:S(2)}, u32[]{:S(2)}) collective-permute-start(bf16[4,128,128]{2,1,0:T(8,128)(2,1)S(1)} %get-tuple-element.62), channel_id=1, source_target_pairs={{0,24},{4,28},{8,16},{12,20},{16,8},{20,12},{24,0},{28,4},{1,25},{... | collective-permute-start | bytes 393224 | tf_op jit(solution)/shard_map/ppermute | solution.py:376
  110.4 0.1 collective-permute-start.19
  110.5 5.4 %collective-permute-done.16.refs_2_ = bf16[2,128,128]{2,1,0:T(8,128)(2,1)S(1)} collective-permute-done((bf16[2,128,128]{2,1,0:T(8,128)(2,1)S(1)}, bf16[2,128,128]{2,1,0:T(8,128)(2,1)S(1)}, u32[]{:S(2)}, u32[]{:S(2)}) %collective-permute-start.16) | collective-permute-done | bytes 65568 | tf_op jit(solution)/shard_map/ppermute | solution.py:376
  115.9 3.3 %collective-permute-start.20 = (bf16[2,128,128]{2,1,0:T(8,128)(2,1)S(1)}, bf16[2,128,128]{2,1,0:T(8,128)(2,1)S(1)}, u32[]{:S(2)}, u32[]{:S(2)}) collective-permute-start(bf16[2,128,128]{2,1,0:T(8,128)(2,1)S(1)} %get-tuple-element.64), channel_id=1, source_target_pairs={{0,28},{4,24},{8,20},{12,16},{16,12},{20,8},{24,4},{28,0},{1,29},{... | collective-permute-start | bytes 196616 | tf_op jit(solution)/shard_map/ppermute | solution.py:376
  119.2 3.7 %collective-permute-done.20.refs_6_ = bf16[2,128,128]{2,1,0:T(8,128)(2,1)S(1)} collective-permute-done((bf16[2,128,128]{2,1,0:T(8,128)(2,1)S(1)}, bf16[2,128,128]{2,1,0:T(8,128)(2,1)S(1)}, u32[]{:S(2)}, u32[]{:S(2)}) %collective-permute-start.20) | collective-permute-done | bytes 65568 | tf_op jit(solution)/shard_map/ppermute | solution.py:376
  122.9 1.8 %shard_map.91 = (bf16[1,128,2560]{2,1,0:T(8,128)(2,1)}, bf16[1,128,2560]{2,1,0:T(8,128)(2,1)}) custom-call(s32[3]{0:T(128)S(1)} %copy-done.1, bf16[4,128,128]{2,1,0:T(8,128)(2,1)S(1)} %collective-permute-done.14.refs_0_, bf16[2,128,128]{2,1,0:T(8,128)(2,1)S(1)} %collective-permute-done.15.refs_1_, bf16[2,128,128]{2,1,0:T(8,128)(2,1)S(1)} %collective-permute-done.16.refs_2_, ...), custom_call_target="tpu_custom_call" | custom-call | bytes 2621440 | tf_op jit(solution)/shard_map/pallas_call | solution.py:361
  (46 shorter events, 0.1 us)
Async XLA Ops:
  5.2 13.8 %collective-permute-start.21 = (bf16[5,128,128]{2,1,0:T(8,128)(2,1)}, bf16[5,128,128]{2,1,0:T(8,128)(2,1)S(1)}, u32[]{:S(2)}, u32[]{:S(2)}) collective-permute-start(bf16[5,128,128]{2,1,0:T(8,128)(2,1)} %get-tuple-element.66), channel_id=1, source_target_pairs={{0,16},{4,20},{8,24},{12,28},{16,0},{20,4},{24,8},{28,12},{1,17},{... | collective-permute-start | bytes 491528 | tf_op jit(solution)/shard_map/ppermute | solution.py:376
  9.3 12.8 %collective-permute-start.22 = (bf16[5,128,128]{2,1,0:T(8,128)(2,1)}, bf16[5,128,128]{2,1,0:T(8,128)(2,1)S(1)}, u32[]{:S(2)}, u32[]{:S(2)}) collective-permute-start(bf16[5,128,128]{2,1,0:T(8,128)(2,1)} %get-tuple-element.67), channel_id=1, source_target_pairs={{0,8},{4,12},{8,0},{12,4},{16,24},{20,28},{24,16},{28,20},{1,9},{5... | collective-permute-start | bytes 491528 | tf_op jit(solution)/shard_map/ppermute | solution.py:376
  10.9 16.0 %collective-permute-start.23 = (bf16[5,128,128]{2,1,0:T(8,128)(2,1)}, bf16[5,128,128]{2,1,0:T(8,128)(2,1)S(1)}, u32[]{:S(2)}, u32[]{:S(2)}) collective-permute-start(bf16[5,128,128]{2,1,0:T(8,128)(2,1)} %get-tuple-element.68), channel_id=1, source_target_pairs={{0,20},{4,16},{8,28},{12,24},{16,4},{20,0},{24,12},{28,8},{1,21},{... | collective-permute-start | bytes 491528 | tf_op jit(solution)/shard_map/ppermute | solution.py:376
  12.2 15.6 %collective-permute-start.24 = (bf16[5,128,128]{2,1,0:T(8,128)(2,1)}, bf16[5,128,128]{2,1,0:T(8,128)(2,1)S(1)}, u32[]{:S(2)}, u32[]{:S(2)}) collective-permute-start(bf16[5,128,128]{2,1,0:T(8,128)(2,1)} %get-tuple-element.69), channel_id=1, source_target_pairs={{0,4},{4,0},{8,12},{12,8},{16,20},{20,16},{24,28},{28,24},{1,5},{5... | collective-permute-start | bytes 491528 | tf_op jit(solution)/shard_map/ppermute | solution.py:376
  12.7 6.3 %copy-start.12 = (bf16[5,128,128]{2,1,0:T(8,128)(2,1)S(1)}, bf16[5,128,128]{2,1,0:T(8,128)(2,1)}, u32[]{:S(2)}) copy-start(bf16[5,128,128]{2,1,0:T(8,128)(2,1)} %get-tuple-element.71) | copy-start | bytes 491524
  12.7 9.4 %copy-start.11 = (bf16[5,128,128]{2,1,0:T(8,128)(2,1)S(1)}, bf16[5,128,128]{2,1,0:T(8,128)(2,1)}, u32[]{:S(2)}) copy-start(bf16[5,128,128]{2,1,0:T(8,128)(2,1)} %get-tuple-element.72) | copy-start | bytes 491524
  12.7 22.5 %copy-start.10 = (bf16[5,128,128]{2,1,0:T(8,128)(2,1)S(1)}, bf16[5,128,128]{2,1,0:T(8,128)(2,1)}, u32[]{:S(2)}) copy-start(bf16[5,128,128]{2,1,0:T(8,128)(2,1)} %get-tuple-element.42) | copy-start | bytes 491524
  12.7 38.8 %copy-start.9 = (bf16[5,128,128]{2,1,0:T(8,128)(2,1)S(1)}, bf16[5,128,128]{2,1,0:T(8,128)(2,1)}, u32[]{:S(2)}) copy-start(bf16[5,128,128]{2,1,0:T(8,128)(2,1)} %get-tuple-element.43) | copy-start | bytes 491524
  12.7 40.2 %copy-start.8 = (bf16[5,128,128]{2,1,0:T(8,128)(2,1)S(1)}, bf16[5,128,128]{2,1,0:T(8,128)(2,1)}, u32[]{:S(2)}) copy-start(bf16[5,128,128]{2,1,0:T(8,128)(2,1)} %get-tuple-element.44) | copy-start | bytes 491524
  12.7 46.9 %copy-start.7 = (bf16[5,128,128]{2,1,0:T(8,128)(2,1)S(1)}, bf16[5,128,128]{2,1,0:T(8,128)(2,1)}, u32[]{:S(2)}) copy-start(bf16[5,128,128]{2,1,0:T(8,128)(2,1)} %get-tuple-element.45) | copy-start | bytes 491524
  12.7 54.8 %copy-start.6 = (bf16[5,128,128]{2,1,0:T(8,128)(2,1)S(1)}, bf16[5,128,128]{2,1,0:T(8,128)(2,1)}, u32[]{:S(2)}) copy-start(bf16[5,128,128]{2,1,0:T(8,128)(2,1)} %get-tuple-element.46) | copy-start | bytes 491524
  12.7 57.2 %copy-start.5 = (bf16[5,128,128]{2,1,0:T(8,128)(2,1)S(1)}, bf16[5,128,128]{2,1,0:T(8,128)(2,1)}, u32[]{:S(2)}) copy-start(bf16[5,128,128]{2,1,0:T(8,128)(2,1)} %get-tuple-element.47) | copy-start | bytes 491524
  12.8 64.2 %copy-start.4 = (bf16[5,128,128]{2,1,0:T(8,128)(2,1)S(1)}, bf16[5,128,128]{2,1,0:T(8,128)(2,1)}, u32[]{:S(2)}) copy-start(bf16[5,128,128]{2,1,0:T(8,128)(2,1)} %get-tuple-element.48) | copy-start | bytes 491524
  12.8 64.2 %copy-start.3 = (bf16[5,128,128]{2,1,0:T(8,128)(2,1)S(1)}, bf16[5,128,128]{2,1,0:T(8,128)(2,1)}, u32[]{:S(2)}) copy-start(bf16[5,128,128]{2,1,0:T(8,128)(2,1)} %get-tuple-element.73.refs_7_) | copy-start | bytes 491524
  12.8 18.1 %collective-permute-start.25 = (bf16[5,128,128]{2,1,0:T(8,128)(2,1)}, bf16[5,128,128]{2,1,0:T(8,128)(2,1)S(1)}, u32[]{:S(2)}, u32[]{:S(2)}) collective-permute-start(bf16[5,128,128]{2,1,0:T(8,128)(2,1)} %get-tuple-element.70), channel_id=1, source_target_pairs={{0,12},{4,8},{8,4},{12,0},{16,28},{20,24},{24,20},{28,16},{1,13},{... | collective-permute-start | bytes 491528 | tf_op jit(solution)/shard_map/ppermute | solution.py:376
  19.0 11.9 %collective-permute-start.26 = (bf16[5,128,128]{2,1,0:T(8,128)(2,1)S(1)}, bf16[5,128,128]{2,1,0:T(8,128)(2,1)S(1)}, u32[]{:S(2)}, u32[]{:S(2)}) collective-permute-start(bf16[5,128,128]{2,1,0:T(8,128)(2,1)S(1)} %copy-done.12), channel_id=1, source_target_pairs={{0,24},{4,28},{8,16},{12,20},{16,8},{20,12},{24,0},{28,4},{1,25},{... | collective-permute-start | bytes 491528 | tf_op jit(solution)/shard_map/ppermute | solution.py:376
  22.1 13.1 %collective-permute-start.27 = (bf16[5,128,128]{2,1,0:T(8,128)(2,1)S(1)}, bf16[5,128,128]{2,1,0:T(8,128)(2,1)S(1)}, u32[]{:S(2)}, u32[]{:S(2)}) collective-permute-start(bf16[5,128,128]{2,1,0:T(8,128)(2,1)S(1)} %copy-done.11), channel_id=1, source_target_pairs={{0,28},{4,24},{8,20},{12,16},{16,12},{20,8},{24,4},{28,0},{1,29},{... | collective-permute-start | bytes 491528 | tf_op jit(solution)/shard_map/ppermute | solution.py:376
  26.9 0.7 copy-start.13
  26.9 24.6 %collective-permute-start.7 = (bf16[5,128,128]{2,1,0:T(8,128)(2,1)}, bf16[5,128,128]{2,1,0:T(8,128)(2,1)S(1)}, u32[]{:S(2)}, u32[]{:S(2)}) collective-permute-start(bf16[5,128,128]{2,1,0:T(8,128)(2,1)} %get-tuple-element.50), channel_id=1, source_target_pairs={{0,16},{4,20},{8,24},{12,28},{16,0},{20,4},{24,8},{28,12},{1,17},{... | collective-permute-start | bytes 491528 | tf_op jit(solution)/shard_map/ppermute | solution.py:376
  27.8 25.2 %collective-permute-start.8 = (bf16[5,128,128]{2,1,0:T(8,128)(2,1)}, bf16[5,128,128]{2,1,0:T(8,128)(2,1)S(1)}, u32[]{:S(2)}, u32[]{:S(2)}) collective-permute-start(bf16[5,128,128]{2,1,0:T(8,128)(2,1)} %get-tuple-element.51), channel_id=1, source_target_pairs={{0,24},{4,28},{8,16},{12,20},{16,8},{20,12},{24,0},{28,4},{1,25},{... | collective-permute-start | bytes 491528 | tf_op jit(solution)/shard_map/ppermute | solution.py:376
  30.9 28.7 %collective-permute-start.9 = (bf16[5,128,128]{2,1,0:T(8,128)(2,1)}, bf16[5,128,128]{2,1,0:T(8,128)(2,1)S(1)}, u32[]{:S(2)}, u32[]{:S(2)}) collective-permute-start(bf16[5,128,128]{2,1,0:T(8,128)(2,1)} %get-tuple-element.52), channel_id=1, source_target_pairs={{0,8},{4,12},{8,0},{12,4},{16,24},{20,28},{24,16},{28,20},{1,9},{5... | collective-permute-start | bytes 491528 | tf_op jit(solution)/shard_map/ppermute | solution.py:376
  30.9 29.2 %collective-permute-start.13 = (bf16[5,128,128]{2,1,0:T(8,128)(2,1)}, bf16[5,128,128]{2,1,0:T(8,128)(2,1)S(1)}, u32[]{:S(2)}, u32[]{:S(2)}) collective-permute-start(bf16[5,128,128]{2,1,0:T(8,128)(2,1)} %get-tuple-element.53.refs_3_), channel_id=1, source_target_pairs={{0,4},{4,0},{8,12},{12,8},{16,20},{20,16},{24,28},{28,24},{1,5},{5... | collective-permute-start | bytes 491528 | tf_op jit(solution)/shard_map/ppermute | solution.py:376
  35.2 26.4 %collective-permute-start = (bf16[5,128,128]{2,1,0:T(8,128)(2,1)S(1)}, bf16[5,128,128]{2,1,0:T(8,128)(2,1)S(1)}, u32[]{:S(2)}, u32[]{:S(2)}) collective-permute-start(bf16[5,128,128]{2,1,0:T(8,128)(2,1)S(1)} %copy-done.10), channel_id=1, source_target_pairs={{0,16},{4,20},{8,24},{12,28},{16,0},{20,4},{24,8},{28,12},{1,17},{... | collective-permute-start | bytes 491528 | tf_op jit(solution)/shard_map/ppermute | solution.py:376
  51.5 10.7 %collective-permute-start.1 = (bf16[5,128,128]{2,1,0:T(8,128)(2,1)S(1)}, bf16[5,128,128]{2,1,0:T(8,128)(2,1)S(1)}, u32[]{:S(2)}, u32[]{:S(2)}) collective-permute-start(bf16[5,128,128]{2,1,0:T(8,128)(2,1)S(1)} %copy-done.9), channel_id=1, source_target_pairs={{0,8},{4,12},{8,0},{12,4},{16,24},{20,28},{24,16},{28,20},{1,9},{5... | collective-permute-start | bytes 491528 | tf_op jit(solution)/shard_map/ppermute | solution.py:376
  52.9 14.6 %collective-permute-start.2 = (bf16[5,128,128]{2,1,0:T(8,128)(2,1)S(1)}, bf16[5,128,128]{2,1,0:T(8,128)(2,1)S(1)}, u32[]{:S(2)}, u32[]{:S(2)}) collective-permute-start(bf16[5,128,128]{2,1,0:T(8,128)(2,1)S(1)} %copy-done.8), channel_id=1, source_target_pairs={{0,20},{4,16},{8,28},{12,24},{16,4},{20,0},{24,12},{28,8},{1,21},{... | collective-permute-start | bytes 491528 | tf_op jit(solution)/shard_map/ppermute | solution.py:376
  59.6 10.4 %collective-permute-start.3 = (bf16[5,128,128]{2,1,0:T(8,128)(2,1)S(1)}, bf16[5,128,128]{2,1,0:T(8,128)(2,1)S(1)}, u32[]{:S(2)}, u32[]{:S(2)}) collective-permute-start(bf16[5,128,128]{2,1,0:T(8,128)(2,1)S(1)} %copy-done.7), channel_id=1, source_target_pairs={{0,4},{4,0},{8,12},{12,8},{16,20},{20,16},{24,28},{28,24},{1,5},{5... | collective-permute-start | bytes 491528 | tf_op jit(solution)/shard_map/ppermute | solution.py:376
  60.1 16.9 %collective-permute-start.10 = (bf16[5,128,128]{2,1,0:T(8,128)(2,1)S(1)}, bf16[5,128,128]{2,1,0:T(8,128)(2,1)S(1)}, u32[]{:S(2)}, u32[]{:S(2)}) collective-permute-start(bf16[5,128,128]{2,1,0:T(8,128)(2,1)S(1)} %collective-permute-done.7.refs_0_), channel_id=1, source_target_pairs={{0,4},{4,0},{8,12},{12,8},{16,20},{20,16},{24,28},{28,24},{1,5},{5... | collective-permute-start | bytes 491528 | tf_op jit(solution)/shard_map/ppermute | solution.py:376
  61.6 20.6 %collective-permute-start.11 = (bf16[5,128,128]{2,1,0:T(8,128)(2,1)S(1)}, bf16[5,128,128]{2,1,0:T(8,128)(2,1)S(1)}, u32[]{:S(2)}, u32[]{:S(2)}) collective-permute-start(bf16[5,128,128]{2,1,0:T(8,128)(2,1)S(1)} %collective-permute-done.8.refs_1_), channel_id=1, source_target_pairs={{0,4},{4,0},{8,12},{12,8},{16,20},{20,16},{24,28},{28,24},{1,5},{5... | collective-permute-start | bytes 491528 | tf_op jit(solution)/shard_map/ppermute | solution.py:376
  62.2 24.3 %collective-permute-start.12 = (bf16[5,128,128]{2,1,0:T(8,128)(2,1)S(1)}, bf16[5,128,128]{2,1,0:T(8,128)(2,1)S(1)}, u32[]{:S(2)}, u32[]{:S(2)}) collective-permute-start(bf16[5,128,128]{2,1,0:T(8,128)(2,1)S(1)} %collective-permute-done.9.refs_2_), channel_id=1, source_target_pairs={{0,4},{4,0},{8,12},{12,8},{16,20},{20,16},{24,28},{28,24},{1,5},{5... | collective-permute-start | bytes 491528 | tf_op jit(solution)/shard_map/ppermute | solution.py:376
  67.6 22.5 %collective-permute-start.4 = (bf16[5,128,128]{2,1,0:T(8,128)(2,1)S(1)}, bf16[5,128,128]{2,1,0:T(8,128)(2,1)S(1)}, u32[]{:S(2)}, u32[]{:S(2)}) collective-permute-start(bf16[5,128,128]{2,1,0:T(8,128)(2,1)S(1)} %copy-done.6), channel_id=1, source_target_pairs={{0,12},{4,8},{8,4},{12,0},{16,28},{20,24},{24,20},{28,16},{1,13},{... | collective-permute-start | bytes 491528 | tf_op jit(solution)/shard_map/ppermute | solution.py:376
  70.0 20.3 %collective-permute-start.5 = (bf16[5,128,128]{2,1,0:T(8,128)(2,1)S(1)}, bf16[5,128,128]{2,1,0:T(8,128)(2,1)S(1)}, u32[]{:S(2)}, u32[]{:S(2)}) collective-permute-start(bf16[5,128,128]{2,1,0:T(8,128)(2,1)S(1)} %copy-done.5), channel_id=1, source_target_pairs={{0,24},{4,28},{8,16},{12,20},{16,8},{20,12},{24,0},{28,4},{1,25},{... | collective-permute-start | bytes 491528 | tf_op jit(solution)/shard_map/ppermute | solution.py:376
  77.0 0.6 copy-start.1
  77.0 16.4 %collective-permute-start.6 = (bf16[5,128,128]{2,1,0:T(8,128)(2,1)S(1)}, bf16[5,128,128]{2,1,0:T(8,128)(2,1)S(1)}, u32[]{:S(2)}, u32[]{:S(2)}) collective-permute-start(bf16[5,128,128]{2,1,0:T(8,128)(2,1)S(1)} %copy-done.4), channel_id=1, source_target_pairs={{0,28},{4,24},{8,20},{12,16},{16,12},{20,8},{24,4},{28,0},{1,29},{... | collective-permute-start | bytes 491528 | tf_op jit(solution)/shard_map/ppermute | solution.py:376
  77.6 8.9 %copy-start = (bf16[5,128,128]{2,1,0:T(8,128)(2,1)S(1)}, bf16[5,128,128]{2,1,0:T(8,128)(2,1)}, u32[]{:S(2)}) copy-start(bf16[5,128,128]{2,1,0:T(8,128)(2,1)} %get-tuple-element.53.refs_3_) | copy-start | bytes 491524
  82.3 13.8 %collective-permute-start.28 = (bf16[2,128,128]{2,1,0:T(8,128)(2,1)S(1)}, bf16[2,128,128]{2,1,0:T(8,128)(2,1)S(1)}, u32[]{:S(2)}, u32[]{:S(2)}) collective-permute-start(bf16[2,128,128]{2,1,0:T(8,128)(2,1)S(1)} %get-tuple-element.74), channel_id=1, source_target_pairs={{0,16},{4,20},{8,24},{12,28},{16,0},{20,4},{24,8},{28,12},{1,17},{... | collective-permute-start | bytes 196616 | tf_op jit(solution)/shard_map/ppermute | solution.py:376
  86.5 10.8 %copy-start.2 = (bf16[5,128,128]{2,1,0:T(8,128)(2,1)S(1)}, bf16[5,128,128]{2,1,0:T(8,128)(2,1)}, u32[]{:S(2)}) copy-start(bf16[5,128,128]{2,1,0:T(8,128)(2,1)} %get-tuple-element.49.refs_7_) | copy-start | bytes 491524
  86.5 9.5 %collective-permute-start.29 = (bf16[2,128,128]{2,1,0:T(8,128)(2,1)S(1)}, bf16[2,128,128]{2,1,0:T(8,128)(2,1)S(1)}, u32[]{:S(2)}, u32[]{:S(2)}) collective-permute-start(bf16[2,128,128]{2,1,0:T(8,128)(2,1)S(1)} %get-tuple-element.75), channel_id=1, source_target_pairs={{0,4},{4,0},{8,12},{12,8},{16,20},{20,16},{24,28},{28,24},{1,5},{5... | collective-permute-start | bytes 196616 | tf_op jit(solution)/shard_map/ppermute | solution.py:376
  90.1 11.2 %collective-permute-start.30 = (bf16[2,128,128]{2,1,0:T(8,128)(2,1)S(1)}, bf16[2,128,128]{2,1,0:T(8,128)(2,1)S(1)}, u32[]{:S(2)}, u32[]{:S(2)}) collective-permute-start(bf16[2,128,128]{2,1,0:T(8,128)(2,1)S(1)} %get-tuple-element.76), channel_id=1, source_target_pairs={{0,20},{4,16},{8,28},{12,24},{16,4},{20,0},{24,12},{28,8},{1,21},{... | collective-permute-start | bytes 196616 | tf_op jit(solution)/shard_map/ppermute | solution.py:376
  90.3 14.3 %collective-permute-start.31 = (bf16[2,128,128]{2,1,0:T(8,128)(2,1)S(1)}, bf16[2,128,128]{2,1,0:T(8,128)(2,1)S(1)}, u32[]{:S(2)}, u32[]{:S(2)}) collective-permute-start(bf16[2,128,128]{2,1,0:T(8,128)(2,1)S(1)} %get-tuple-element.77), channel_id=1, source_target_pairs={{0,8},{4,12},{8,0},{12,4},{16,24},{20,28},{24,16},{28,20},{1,9},{5... | collective-permute-start | bytes 196616 | tf_op jit(solution)/shard_map/ppermute | solution.py:376
  93.4 11.2 %collective-permute-start.32 = (bf16[2,128,128]{2,1,0:T(8,128)(2,1)S(1)}, bf16[2,128,128]{2,1,0:T(8,128)(2,1)S(1)}, u32[]{:S(2)}, u32[]{:S(2)}) collective-permute-start(bf16[2,128,128]{2,1,0:T(8,128)(2,1)S(1)} %get-tuple-element.78), channel_id=1, source_target_pairs={{0,24},{4,28},{8,16},{12,20},{16,8},{20,12},{24,0},{28,4},{1,25},{... | collective-permute-start | bytes 196616 | tf_op jit(solution)/shard_map/ppermute | solution.py:376
  96.0 10.1 %collective-permute-start.33 = (bf16[2,128,128]{2,1,0:T(8,128)(2,1)S(1)}, bf16[2,128,128]{2,1,0:T(8,128)(2,1)S(1)}, u32[]{:S(2)}, u32[]{:S(2)}) collective-permute-start(bf16[2,128,128]{2,1,0:T(8,128)(2,1)S(1)} %get-tuple-element.79), channel_id=1, source_target_pairs={{0,12},{4,8},{8,4},{12,0},{16,28},{20,24},{24,20},{28,16},{1,13},{... | collective-permute-start | bytes 196616 | tf_op jit(solution)/shard_map/ppermute | solution.py:376
  96.1 11.7 %collective-permute-start.34 = (bf16[2,128,128]{2,1,0:T(8,128)(2,1)S(1)}, bf16[2,128,128]{2,1,0:T(8,128)(2,1)S(1)}, u32[]{:S(2)}, u32[]{:S(2)}) collective-permute-start(bf16[2,128,128]{2,1,0:T(8,128)(2,1)S(1)} %get-tuple-element.80), channel_id=1, source_target_pairs={{0,28},{4,24},{8,20},{12,16},{16,12},{20,8},{24,4},{28,0},{1,29},{... | collective-permute-start | bytes 196616 | tf_op jit(solution)/shard_map/ppermute | solution.py:376
  101.3 21.6 %collective-permute-start.14 = (bf16[4,128,128]{2,1,0:T(8,128)(2,1)S(1)}, bf16[4,128,128]{2,1,0:T(8,128)(2,1)S(1)}, u32[]{:S(2)}, u32[]{:S(2)}) collective-permute-start(bf16[4,128,128]{2,1,0:T(8,128)(2,1)S(1)} %get-tuple-element.58), channel_id=1, source_target_pairs={{0,16},{4,20},{8,24},{12,28},{16,0},{20,4},{24,8},{28,12},{1,17},{... | collective-permute-start | bytes 393224 | tf_op jit(solution)/shard_map/ppermute | solution.py:376
  104.6 5.9 %collective-permute-start.15 = (bf16[2,128,128]{2,1,0:T(8,128)(2,1)S(1)}, bf16[2,128,128]{2,1,0:T(8,128)(2,1)S(1)}, u32[]{:S(2)}, u32[]{:S(2)}) collective-permute-start(bf16[2,128,128]{2,1,0:T(8,128)(2,1)S(1)} %get-tuple-element.59), channel_id=1, source_target_pairs={{0,4},{4,0},{8,12},{12,8},{16,20},{20,16},{24,28},{28,24},{1,5},{5... | collective-permute-start | bytes 196616 | tf_op jit(solution)/shard_map/ppermute | solution.py:376
  104.6 11.3 %collective-permute-start.16 = (bf16[2,128,128]{2,1,0:T(8,128)(2,1)S(1)}, bf16[2,128,128]{2,1,0:T(8,128)(2,1)S(1)}, u32[]{:S(2)}, u32[]{:S(2)}) collective-permute-start(bf16[2,128,128]{2,1,0:T(8,128)(2,1)S(1)} %get-tuple-element.60), channel_id=1, source_target_pairs={{0,20},{4,16},{8,28},{12,24},{16,4},{20,0},{24,12},{28,8},{1,21},{... | collective-permute-start | bytes 196616 | tf_op jit(solution)/shard_map/ppermute | solution.py:376
  106.1 16.8 %collective-permute-start.17 = (bf16[4,128,128]{2,1,0:T(8,128)(2,1)S(1)}, bf16[4,128,128]{2,1,0:T(8,128)(2,1)S(1)}, u32[]{:S(2)}, u32[]{:S(2)}) collective-permute-start(bf16[4,128,128]{2,1,0:T(8,128)(2,1)S(1)} %get-tuple-element.61), channel_id=1, source_target_pairs={{0,8},{4,12},{8,0},{12,4},{16,24},{20,28},{24,16},{28,20},{1,9},{5... | collective-permute-start | bytes 393224 | tf_op jit(solution)/shard_map/ppermute | solution.py:376
  107.8 15.1 %collective-permute-start.18 = (bf16[4,128,128]{2,1,0:T(8,128)(2,1)S(1)}, bf16[4,128,128]{2,1,0:T(8,128)(2,1)S(1)}, u32[]{:S(2)}, u32[]{:S(2)}) collective-permute-start(bf16[4,128,128]{2,1,0:T(8,128)(2,1)S(1)} %get-tuple-element.62), channel_id=1, source_target_pairs={{0,24},{4,28},{8,16},{12,20},{16,8},{20,12},{24,0},{28,4},{1,25},{... | collective-permute-start | bytes 393224 | tf_op jit(solution)/shard_map/ppermute | solution.py:376
  110.4 8.8 %collective-permute-start.19 = (bf16[2,128,128]{2,1,0:T(8,128)(2,1)S(1)}, bf16[2,128,128]{2,1,0:T(8,128)(2,1)S(1)}, u32[]{:S(2)}, u32[]{:S(2)}) collective-permute-start(bf16[2,128,128]{2,1,0:T(8,128)(2,1)S(1)} %get-tuple-element.63), channel_id=1, source_target_pairs={{0,12},{4,8},{8,4},{12,0},{16,28},{20,24},{24,20},{28,16},{1,13},{... | collective-permute-start | bytes 196616 | tf_op jit(solution)/shard_map/ppermute | solution.py:376
  115.9 7.0 %collective-permute-start.20 = (bf16[2,128,128]{2,1,0:T(8,128)(2,1)S(1)}, bf16[2,128,128]{2,1,0:T(8,128)(2,1)S(1)}, u32[]{:S(2)}, u32[]{:S(2)}) collective-permute-start(bf16[2,128,128]{2,1,0:T(8,128)(2,1)S(1)} %get-tuple-element.64), channel_id=1, source_target_pairs={{0,28},{4,24},{8,20},{12,16},{16,12},{20,8},{24,4},{28,0},{1,29},{... | collective-permute-start | bytes 196616 | tf_op jit(solution)/shard_map/ppermute | solution.py:376

commit v7 on v6

--- a/solution.py
+++ b/solution.py
@@ -385,13 +385,16 @@
     own = [swapped(pieces[s], 2 * s) for s in across]
     packed = slots_pack(full, there, where, tensors)
     arrived = [[swapped(x, d) for x, d in zip(xs, there)] for xs in packed]
+
+    def work(xs, pieces):
+        return slot_kernel(there, home, first, clips, where, xs, pieces)
+
+    results = [work(xs, ()) for xs in arrived[1:]]
+    results, own = lax.optimization_barrier((results, own))
     other = [swapped(x, 1) for x in own]
     pieces = rest_kernel(rest, across, first, clips, where, own, other)
-    slots = []
-    for xs in arrived:
-        results = slot_kernel(there, home, first, clips, where, xs, pieces)
-        slots += [swapped(x, d) for x, d in zip(results, home)]
-        pieces = ()
+    results = [work(arrived[0], pieces), *results]
+    slots = [swapped(x, d) for xs in results for x, d in zip(xs, home)]
     return tuple(join(full, home, rest, where, slots))
 
 

time: 125 us -> 133 us (1.064)
  starting transfers between devices: 66.4 us -> 76.9 us
    ppermute x35, starting transfers between devices: 66.4 us -> 76.9 us  [swapped(): lax.ppermute(x, 'tm', [(i, i ^ by) for i in range(peers)])]
    ppermute x35, waiting for transfers between devices: 33.7 us -> 32.4 us  [swapped(): lax.ppermute(x, 'tm', [(i, i ^ by) for i in range(peers)])]
  transfers between devices with their start and end apart: 35 -> 35, of which waited for: 11 -> 10; matrix products, arithmetic and copies ran while one was open for 1% -> 1% of each run, Pallas kernels for 11% -> 10%
where the time goes in v7:
time: 133 us
  starting transfers between devices  76.9 us (58%)
  waiting for transfers between devices  32.4 us (24%)
  Pallas kernels  19.7 us (15%)
  other arithmetic  1.65 us (1%)
  between operations  1.49 us (1%)
    ppermute x35, starting transfers between devices, swapped(): lax.ppermute(x, 'tm', [(i, i ^ by) for i in range(peers)])  76.9 us
    ppermute x35, waiting for transfers between devices, swapped(): lax.ppermute(x, 'tm', [(i, i ^ by) for i in range(peers)])  32.4 us
    pallas_call x2, Pallas kernels, slot_kernel(): pl.pallas_call(body, in_specs=[SMEM] * 3 + [VMEM] * (blocks + len(pieces)...  8.11 us
    pallas_call x1, Pallas kernels, slots_pack(): pl.pallas_call(body, in_specs=[SMEM] + [pl.BlockSpec(memory_space=pl.ANY)...  4 us
    pallas_call x1, Pallas kernels, rest_kernel(): pl.pallas_call(body, in_specs=[SMEM] * 3 + [VMEM] * (2 * columns), out_sp...  3.6 us
  transfers between devices with their start and end apart: 35, of which 10 were waited for; matrix products, arithmetic and copies ran while one was open for 1% of the time, Pallas kernels for 10%

profile of v7, /device:TPU:0, one launch (start us, length us, event | category | flops | bytes accessed | tf_op | source)
XLA Modules:
  0.0 132.8 jit_solution(1377975711158620203)
XLA Ops:
  0.6 0.7 pad_add_fusion.where_ref
  1.3 4.0 %shard_map.86 = (bf16[5,128,128]{2,1,0:T(8,128)(2,1)}, bf16[5,128,128]{2,1,0:T(8,128)(2,1)}, bf16[5,128,128]{2,1,0:T(8,128)(2,1)}, bf16[5,128,128]{2,1,0:T(8,128...) custom-call(s32[3]{0:T(128)} %pad_add_fusion.where_ref, ...), custom_call_target="tpu_custom_call" | custom-call | bytes 5242880 | tf_op jit(solution)/shard_map/pallas_call | solution.py:269
  5.3 4.1 %collective-permute-start.7 = (bf16[5,128,128]{2,1,0:T(8,128)(2,1)}, bf16[5,128,128]{2,1,0:T(8,128)(2,1)S(1)}, u32[]{:S(2)}, u32[]{:S(2)}) collective-permute-start(bf16[5,128,128]{2,1,0:T(8,128)(2,1)} %get-tuple-element.62), channel_id=1, source_target_pairs={{0,16},{4,20},{8,24},{12,28},{16,0},{20,4},{24,8},{28,12},{1,17},{... | collective-permute-start | bytes 491528 | tf_op jit(solution)/shard_map/ppermute | solution.py:376
  9.4 1.6 %collective-permute-start.8 = (bf16[5,128,128]{2,1,0:T(8,128)(2,1)}, bf16[5,128,128]{2,1,0:T(8,128)(2,1)S(1)}, u32[]{:S(2)}, u32[]{:S(2)}) collective-permute-start(bf16[5,128,128]{2,1,0:T(8,128)(2,1)} %get-tuple-element.63), channel_id=1, source_target_pairs={{0,8},{4,12},{8,0},{12,4},{16,24},{20,28},{24,16},{28,20},{1,9},{5... | collective-permute-start | bytes 491528 | tf_op jit(solution)/shard_map/ppermute | solution.py:376
  11.0 1.3 collective-permute-start.9
  12.3 0.5 collective-permute-start.10
  12.8 1.4 %collective-permute-start.11 = (bf16[5,128,128]{2,1,0:T(8,128)(2,1)}, bf16[5,128,128]{2,1,0:T(8,128)(2,1)S(1)}, u32[]{:S(2)}, u32[]{:S(2)}) collective-permute-start(bf16[5,128,128]{2,1,0:T(8,128)(2,1)} %get-tuple-element.66), channel_id=1, source_target_pairs={{0,12},{4,8},{8,4},{12,0},{16,28},{20,24},{24,20},{28,16},{1,13},{... | collective-permute-start | bytes 491528 | tf_op jit(solution)/shard_map/ppermute | solution.py:376
  14.2 0.2 reduce-window.8
  14.4 4.7 %collective-permute-done.7.refs_0_ = bf16[5,128,128]{2,1,0:T(8,128)(2,1)S(1)} collective-permute-done((bf16[5,128,128]{2,1,0:T(8,128)(2,1)}, bf16[5,128,128]{2,1,0:T(8,128)(2,1)S(1)}, u32[]{:S(2)}, u32[]{:S(2)}) %collective-permute-start.7) | collective-permute-done | bytes 163872 | tf_op jit(solution)/shard_map/ppermute | solution.py:376
  19.1 3.1 %collective-permute-start.12 = (bf16[5,128,128]{2,1,0:T(8,128)(2,1)}, bf16[5,128,128]{2,1,0:T(8,128)(2,1)S(1)}, u32[]{:S(2)}, u32[]{:S(2)}) collective-permute-start(bf16[5,128,128]{2,1,0:T(8,128)(2,1)} %get-tuple-element.67), channel_id=1, source_target_pairs={{0,24},{4,28},{8,16},{12,20},{16,8},{20,12},{24,0},{28,4},{1,25},{... | collective-permute-start | bytes 491528 | tf_op jit(solution)/shard_map/ppermute | solution.py:376
  22.2 0.6 fusion
  22.8 2.1 %shard_map.88 = (bf16[5,128,128]{2,1,0:T(8,128)(2,1)}, bf16[5,128,128]{2,1,0:T(8,128)(2,1)}, bf16[5,128,128]{2,1,0:T(8,128)(2,1)}, bf16[5,128,128]{2,1,0:T(8,128)(2,1)}) custom-call(s32[1]{0:T(128)} %bitcast.column_ref, bf16[1,128,2560]{2,1,0:T(8,128)(2,1)} %refs_0_.3, bf16[1,128,2560]{2,1,0:T(8,128)(2,1)} %refs_1_.3, bf16[1,128,2560]{2,1,0:T(8,128)(2,1)} %refs_2_.3, ...), custom_call_target="tpu_custom_call" | custom-call | bytes 1310720 | tf_op jit(solution)/shard_map/pallas_call | solution.py:298
  25.0 0.7 pad.2.clone
  25.7 0.1 select_reduce_fusion.1
  25.8 0.0 collective-permute-done.8.refs_1_
  25.8 0.1 collective-permute-start
  25.9 1.2 collective-permute-done.9.refs_2_
  27.0 3.1 %collective-permute-start.13 = (bf16[5,128,128]{2,1,0:T(8,128)(2,1)S(1)}, bf16[5,128,128]{2,1,0:T(8,128)(2,1)S(1)}, u32[]{:S(2)}, u32[]{:S(2)}) collective-permute-start(bf16[5,128,128]{2,1,0:T(8,128)(2,1)S(1)} %copy-done.11), channel_id=1, source_target_pairs={{0,28},{4,24},{8,20},{12,16},{16,12},{20,8},{24,4},{28,0},{1,29},{... | collective-permute-start | bytes 491528 | tf_op jit(solution)/shard_map/ppermute | solution.py:376
  30.1 0.0 collective-permute-done.10.refs_3_
  30.1 1.4 %collective-permute-start.14 = (bf16[5,128,128]{2,1,0:T(8,128)(2,1)}, bf16[5,128,128]{2,1,0:T(8,128)(2,1)S(1)}, u32[]{:S(2)}, u32[]{:S(2)}) collective-permute-start(bf16[5,128,128]{2,1,0:T(8,128)(2,1)} %get-tuple-element.78), channel_id=1, source_target_pairs={{0,16},{4,20},{8,24},{12,28},{16,0},{20,4},{24,8},{28,12},{1,17},{... | collective-permute-start | bytes 491528 | tf_op jit(solution)/shard_map/ppermute | solution.py:376
  31.5 0.0 collective-permute-done.11.refs_4_
  31.5 1.1 collective-permute-start.15
  32.6 0.0 collective-permute-done.12.refs_5_
  32.6 14.2 %collective-permute-start.16 = (bf16[5,128,128]{2,1,0:T(8,128)(2,1)}, bf16[5,128,128]{2,1,0:T(8,128)(2,1)S(1)}, u32[]{:S(2)}, u32[]{:S(2)}) collective-permute-start(bf16[5,128,128]{2,1,0:T(8,128)(2,1)} %get-tuple-element.80), channel_id=1, source_target_pairs={{0,8},{4,12},{8,0},{12,4},{16,24},{20,28},{24,16},{28,20},{1,9},{5... | collective-permute-start | bytes 491528 | tf_op jit(solution)/shard_map/ppermute | solution.py:376
  46.9 0.1 add_add_fusion.clip_ref
  47.6 7.6 %collective-permute-start.1 = (bf16[5,128,128]{2,1,0:T(8,128)(2,1)S(1)}, bf16[5,128,128]{2,1,0:T(8,128)(2,1)S(1)}, u32[]{:S(2)}, u32[]{:S(2)}) collective-permute-start(bf16[5,128,128]{2,1,0:T(8,128)(2,1)S(1)} %copy-done.9), channel_id=1, source_target_pairs={{0,8},{4,12},{8,0},{12,4},{16,24},{20,28},{24,16},{28,20},{1,9},{5... | collective-permute-start | bytes 491528 | tf_op jit(solution)/shard_map/ppermute | solution.py:376
  55.2 1.7 %collective-permute-done.14.refs_0_ = bf16[5,128,128]{2,1,0:T(8,128)(2,1)S(1)} collective-permute-done((bf16[5,128,128]{2,1,0:T(8,128)(2,1)}, bf16[5,128,128]{2,1,0:T(8,128)(2,1)S(1)}, u32[]{:S(2)}, u32[]{:S(2)}) %collective-permute-start.14) | collective-permute-done | bytes 163872 | tf_op jit(solution)/shard_map/ppermute | solution.py:376
  56.8 0.9 collective-permute-start.2
  57.8 4.1 %shard_map.87 = (bf16[2,128,128]{2,1,0:T(8,128)(2,1)S(1)}, bf16[2,128,128]{2,1,0:T(8,128)(2,1)S(1)}, bf16[2,128,128]{2,1,0:T(8,128)(2,1)S(1)}, bf16[2,128,128]{2...) custom-call(s32[1]{0:T(128)S(6)} %copy.9.first_ref, ...), custom_call_target="tpu_custom_call" | custom-call | flops 1073741824 | bytes 1835008 | tf_op jit(solution)/shard_map/pallas_call | solution.py:235
  61.9 1.6 %collective-permute-start.3 = (bf16[5,128,128]{2,1,0:T(8,128)(2,1)S(1)}, bf16[5,128,128]{2,1,0:T(8,128)(2,1)S(1)}, u32[]{:S(2)}, u32[]{:S(2)}) collective-permute-start(bf16[5,128,128]{2,1,0:T(8,128)(2,1)S(1)} %copy-done.7), channel_id=1, source_target_pairs={{0,4},{4,0},{8,12},{12,8},{16,20},{20,16},{24,28},{28,24},{1,5},{5... | collective-permute-start | bytes 491528 | tf_op jit(solution)/shard_map/ppermute | solution.py:376
  63.5 0.0 collective-permute-done.16.refs_2_
  63.5 0.5 collective-permute-start.17
  64.0 0.0 collective-permute-done.refs_0_
  64.0 1.6 %collective-permute-start.18 = (bf16[5,128,128]{2,1,0:T(8,128)(2,1)S(1)}, bf16[5,128,128]{2,1,0:T(8,128)(2,1)S(1)}, u32[]{:S(2)}, u32[]{:S(2)}) collective-permute-start(bf16[5,128,128]{2,1,0:T(8,128)(2,1)S(1)} %collective-permute-done.15.refs_1_), channel_id=1, source_target_pairs={{0,4},{4,0},{8,12},{12,8},{16,20},{20,16},{24,28},{28,24},{1,5},{5... | collective-permute-start | bytes 491528 | tf_op jit(solution)/shard_map/ppermute | solution.py:376
  65.6 0.5 collective-permute-start.19
  66.0 1.6 %collective-permute-done.2.refs_2_ = bf16[5,128,128]{2,1,0:T(8,128)(2,1)S(1)} collective-permute-done((bf16[5,128,128]{2,1,0:T(8,128)(2,1)S(1)}, bf16[5,128,128]{2,1,0:T(8,128)(2,1)S(1)}, u32[]{:S(2)}, u32[]{:S(2)}) %collective-permute-start.2) | collective-permute-done | bytes 163872 | tf_op jit(solution)/shard_map/ppermute | solution.py:376
  67.6 0.9 collective-permute-start.20
  68.5 4.4 %collective-permute-done.3.refs_3_ = bf16[5,128,128]{2,1,0:T(8,128)(2,1)S(1)} collective-permute-done((bf16[5,128,128]{2,1,0:T(8,128)(2,1)S(1)}, bf16[5,128,128]{2,1,0:T(8,128)(2,1)S(1)}, u32[]{:S(2)}, u32[]{:S(2)}) %collective-permute-start.3) | collective-permute-done | bytes 163872 | tf_op jit(solution)/shard_map/ppermute | solution.py:376
  72.9 0.0 collective-permute-start.4
  73.0 3.5 %collective-permute-done.17.refs_4_ = bf16[5,128,128]{2,1,0:T(8,128)(2,1)S(1)} collective-permute-done((bf16[5,128,128]{2,1,0:T(8,128)(2,1)S(1)}, bf16[5,128,128]{2,1,0:T(8,128)(2,1)S(1)}, u32[]{:S(2)}, u32[]{:S(2)}) %collective-permute-start.17) | collective-permute-done | bytes 163872 | tf_op jit(solution)/shard_map/ppermute | solution.py:376
  76.5 5.3 %collective-permute-start.5 = (bf16[5,128,128]{2,1,0:T(8,128)(2,1)S(1)}, bf16[5,128,128]{2,1,0:T(8,128)(2,1)S(1)}, u32[]{:S(2)}, u32[]{:S(2)}) collective-permute-start(bf16[5,128,128]{2,1,0:T(8,128)(2,1)S(1)} %copy-done.5), channel_id=1, source_target_pairs={{0,24},{4,28},{8,16},{12,20},{16,8},{20,12},{24,0},{28,4},{1,25},{... | collective-permute-start | bytes 491528 | tf_op jit(solution)/shard_map/ppermute | solution.py:376
  81.7 0.0 collective-permute-done.18.refs_5_
  81.7 3.4 %collective-permute-start.6 = (bf16[5,128,128]{2,1,0:T(8,128)(2,1)S(1)}, bf16[5,128,128]{2,1,0:T(8,128)(2,1)S(1)}, u32[]{:S(2)}, u32[]{:S(2)}) collective-permute-start(bf16[5,128,128]{2,1,0:T(8,128)(2,1)S(1)} %copy-done.4), channel_id=1, source_target_pairs={{0,28},{4,24},{8,20},{12,16},{16,12},{20,8},{24,4},{28,0},{1,29},{... | collective-permute-start | bytes 491528 | tf_op jit(solution)/shard_map/ppermute | solution.py:376
  85.2 0.0 collective-permute-done.19.refs_6_
  85.2 2.1 %collective-permute-start.28 = (bf16[2,128,128]{2,1,0:T(8,128)(2,1)S(1)}, bf16[2,128,128]{2,1,0:T(8,128)(2,1)S(1)}, u32[]{:S(2)}, u32[]{:S(2)}) collective-permute-start(bf16[2,128,128]{2,1,0:T(8,128)(2,1)S(1)} %get-tuple-element.98), channel_id=1, source_target_pairs={{0,16},{4,20},{8,24},{12,28},{16,0},{20,4},{24,8},{28,12},{1,17},{... | collective-permute-start | bytes 196616 | tf_op jit(solution)/shard_map/ppermute | solution.py:376
  87.2 0.6 collective-permute-done.20.refs_7_
  87.9 1.7 %collective-permute-start.29 = (bf16[2,128,128]{2,1,0:T(8,128)(2,1)S(1)}, bf16[2,128,128]{2,1,0:T(8,128)(2,1)S(1)}, u32[]{:S(2)}, u32[]{:S(2)}) collective-permute-start(bf16[2,128,128]{2,1,0:T(8,128)(2,1)S(1)} %get-tuple-element.99), channel_id=1, source_target_pairs={{0,4},{4,0},{8,12},{12,8},{16,20},{20,16},{24,28},{28,24},{1,5},{5... | collective-permute-start | bytes 196616 | tf_op jit(solution)/shard_map/ppermute | solution.py:376
  89.5 3.6 %shard_map.89 = (bf16[2,128,128]{2,1,0:T(8,128)(2,1)S(1)}, bf16[2,128,128]{2,1,0:T(8,128)(2,1)S(1)}, bf16[2,128,128]{2,1,0:T(8,128)(2,1)S(1)}, bf16[2,128,128]{2,1,0:T(8,128)(2,1)S(1)}) custom-call(s32[1]{0:T(128)S(6)} %copy.9.first_ref, s32[3,8]{1,0:T(4,128)S(1)} %add_add_fusion.clip_ref, s32[3]{0:T(128)S(1)} %copy-done.1, ...), custom_call_target="tpu_custom_call" | custom-call | bytes 32768 | tf_op jit(solution)/shard_map/pallas_call | solution.py:330
  93.1 0.0 collective-permute-done.4.refs_4_
  93.2 2.6 %collective-permute-start.30 = (bf16[2,128,128]{2,1,0:T(8,128)(2,1)S(1)}, bf16[2,128,128]{2,1,0:T(8,128)(2,1)S(1)}, u32[]{:S(2)}, u32[]{:S(2)}) collective-permute-start(bf16[2,128,128]{2,1,0:T(8,128)(2,1)S(1)} %get-tuple-element.100), channel_id=1, source_target_pairs={{0,20},{4,16},{8,28},{12,24},{16,4},{20,0},{24,12},{28,8},{1,21},{... | collective-permute-start | bytes 196616 | tf_op jit(solution)/shard_map/ppermute | solution.py:376
  95.7 5.1 %collective-permute-start.31 = (bf16[2,128,128]{2,1,0:T(8,128)(2,1)S(1)}, bf16[2,128,128]{2,1,0:T(8,128)(2,1)S(1)}, u32[]{:S(2)}, u32[]{:S(2)}) collective-permute-start(bf16[2,128,128]{2,1,0:T(8,128)(2,1)S(1)} %get-tuple-element.101), channel_id=1, source_target_pairs={{0,8},{4,12},{8,0},{12,4},{16,24},{20,28},{24,16},{28,20},{1,9},{5... | collective-permute-start | bytes 196616 | tf_op jit(solution)/shard_map/ppermute | solution.py:376
  100.9 0.6 collective-permute-start.33
  101.5 3.7 %collective-permute-start.34 = (bf16[2,128,128]{2,1,0:T(8,128)(2,1)S(1)}, bf16[2,128,128]{2,1,0:T(8,128)(2,1)S(1)}, u32[]{:S(2)}, u32[]{:S(2)}) collective-permute-start(bf16[2,128,128]{2,1,0:T(8,128)(2,1)S(1)} %get-tuple-element.104), channel_id=1, source_target_pairs={{0,28},{4,24},{8,20},{12,16},{16,12},{20,8},{24,4},{28,0},{1,29},{... | collective-permute-start | bytes 196616 | tf_op jit(solution)/shard_map/ppermute | solution.py:376
  105.2 4.0 %shard_map.90 = (bf16[4,128,128]{2,1,0:T(8,128)(2,1)S(1)}, bf16[2,128,128]{2,1,0:T(8,128)(2,1)S(1)}, bf16[2,128,128]{2,1,0:T(8,128)(2,1)S(1)}, bf16[4,128,128]{2...) custom-call(s32[1]{0:T(128)S(6)} %copy.9.first_ref, ...), custom_call_target="tpu_custom_call" | custom-call | flops 1073741824 | bytes 1835008 | tf_op jit(solution)/shard_map/pallas_call | solution.py:235
  109.3 0.6 collective-permute-start.21
  109.9 1.0 collective-permute-start.22
  110.9 2.8 %collective-permute-start.23 = (bf16[2,128,128]{2,1,0:T(8,128)(2,1)S(1)}, bf16[2,128,128]{2,1,0:T(8,128)(2,1)S(1)}, u32[]{:S(2)}, u32[]{:S(2)}) collective-permute-start(bf16[2,128,128]{2,1,0:T(8,128)(2,1)S(1)} %get-tuple-element.92), channel_id=1, source_target_pairs={{0,20},{4,16},{8,28},{12,24},{16,4},{20,0},{24,12},{28,8},{1,21},{... | collective-permute-start | bytes 196616 | tf_op jit(solution)/shard_map/ppermute | solution.py:376
  113.7 1.5 %collective-permute-start.24 = (bf16[4,128,128]{2,1,0:T(8,128)(2,1)S(1)}, bf16[4,128,128]{2,1,0:T(8,128)(2,1)S(1)}, u32[]{:S(2)}, u32[]{:S(2)}) collective-permute-start(bf16[4,128,128]{2,1,0:T(8,128)(2,1)S(1)} %get-tuple-element.93), channel_id=1, source_target_pairs={{0,8},{4,12},{8,0},{12,4},{16,24},{20,28},{24,16},{28,20},{1,9},{5... | collective-permute-start | bytes 393224 | tf_op jit(solution)/shard_map/ppermute | solution.py:376
  115.3 0.5 collective-permute-start.25
  115.7 0.6 collective-permute-start.26
  116.4 7.6 %collective-permute-done.23.refs_2_ = bf16[2,128,128]{2,1,0:T(8,128)(2,1)S(1)} collective-permute-done((bf16[2,128,128]{2,1,0:T(8,128)(2,1)S(1)}, bf16[2,128,128]{2,1,0:T(8,128)(2,1)S(1)}, u32[]{:S(2)}, u32[]{:S(2)}) %collective-permute-start.23) | collective-permute-done | bytes 65568 | tf_op jit(solution)/shard_map/ppermute | solution.py:376
  124.0 0.1 collective-permute-done.26.refs_5_
  124.1 6.8 %collective-permute-done.27.refs_6_ = bf16[2,128,128]{2,1,0:T(8,128)(2,1)S(1)} collective-permute-done((bf16[2,128,128]{2,1,0:T(8,128)(2,1)S(1)}, bf16[2,128,128]{2,1,0:T(8,128)(2,1)S(1)}, u32[]{:S(2)}, u32[]{:S(2)}) %collective-permute-start.27) | collective-permute-done | bytes 65568 | tf_op jit(solution)/shard_map/ppermute | solution.py:376
  130.9 1.8 %shard_map.91 = (bf16[1,128,2560]{2,1,0:T(8,128)(2,1)}, bf16[1,128,2560]{2,1,0:T(8,128)(2,1)}) custom-call(s32[3]{0:T(128)S(1)} %copy-done.1, bf16[4,128,128]{2,1,0:T(8,128)(2,1)S(1)} %collective-permute-done.21.refs_0_, bf16[2,128,128]{2,1,0:T(8,128)(2,1)S(1)} %collective-permute-done.22.refs_1_, bf16[2,128,128]{2,1,0:T(8,128)(2,1)S(1)} %collective-permute-done.23.refs_2_, ...), custom_call_target="tpu_custom_call" | custom-call | bytes 2621440 | tf_op jit(solution)/shard_map/pallas_call | solution.py:361
  (44 shorter events, 0.1 us)
Async XLA Ops:
  5.3 13.8 %collective-permute-start.7 = (bf16[5,128,128]{2,1,0:T(8,128)(2,1)}, bf16[5,128,128]{2,1,0:T(8,128)(2,1)S(1)}, u32[]{:S(2)}, u32[]{:S(2)}) collective-permute-start(bf16[5,128,128]{2,1,0:T(8,128)(2,1)} %get-tuple-element.62), channel_id=1, source_target_pairs={{0,16},{4,20},{8,24},{12,28},{16,0},{20,4},{24,8},{28,12},{1,17},{... | collective-permute-start | bytes 491528 | tf_op jit(solution)/shard_map/ppermute | solution.py:376
  9.4 16.3 %collective-permute-start.8 = (bf16[5,128,128]{2,1,0:T(8,128)(2,1)}, bf16[5,128,128]{2,1,0:T(8,128)(2,1)S(1)}, u32[]{:S(2)}, u32[]{:S(2)}) collective-permute-start(bf16[5,128,128]{2,1,0:T(8,128)(2,1)} %get-tuple-element.63), channel_id=1, source_target_pairs={{0,8},{4,12},{8,0},{12,4},{16,24},{20,28},{24,16},{28,20},{1,9},{5... | collective-permute-start | bytes 491528 | tf_op jit(solution)/shard_map/ppermute | solution.py:376
  11.0 16.0 %collective-permute-start.9 = (bf16[5,128,128]{2,1,0:T(8,128)(2,1)}, bf16[5,128,128]{2,1,0:T(8,128)(2,1)S(1)}, u32[]{:S(2)}, u32[]{:S(2)}) collective-permute-start(bf16[5,128,128]{2,1,0:T(8,128)(2,1)} %get-tuple-element.64), channel_id=1, source_target_pairs={{0,20},{4,16},{8,28},{12,24},{16,4},{20,0},{24,12},{28,8},{1,21},{... | collective-permute-start | bytes 491528 | tf_op jit(solution)/shard_map/ppermute | solution.py:376
  12.3 17.8 %collective-permute-start.10 = (bf16[5,128,128]{2,1,0:T(8,128)(2,1)}, bf16[5,128,128]{2,1,0:T(8,128)(2,1)S(1)}, u32[]{:S(2)}, u32[]{:S(2)}) collective-permute-start(bf16[5,128,128]{2,1,0:T(8,128)(2,1)} %get-tuple-element.65), channel_id=1, source_target_pairs={{0,4},{4,0},{8,12},{12,8},{16,20},{20,16},{24,28},{28,24},{1,5},{5... | collective-permute-start | bytes 491528 | tf_op jit(solution)/shard_map/ppermute | solution.py:376
  12.8 1.4 %copy-start.12 = (s32[1,3]{1,0:T(1,128)S(1)}, s32[1,3]{1,0:T(1,128)}, u32[]{:S(2)}) copy-start(s32[1,3]{1,0:T(1,128)} %param.13) | copy-start | bytes 40
  12.8 18.7 %collective-permute-start.11 = (bf16[5,128,128]{2,1,0:T(8,128)(2,1)}, bf16[5,128,128]{2,1,0:T(8,128)(2,1)S(1)}, u32[]{:S(2)}, u32[]{:S(2)}) collective-permute-start(bf16[5,128,128]{2,1,0:T(8,128)(2,1)} %get-tuple-element.66), channel_id=1, source_target_pairs={{0,12},{4,8},{8,4},{12,0},{16,28},{20,24},{24,20},{28,16},{1,13},{... | collective-permute-start | bytes 491528 | tf_op jit(solution)/shard_map/ppermute | solution.py:376
  19.1 13.6 %collective-permute-start.12 = (bf16[5,128,128]{2,1,0:T(8,128)(2,1)}, bf16[5,128,128]{2,1,0:T(8,128)(2,1)S(1)}, u32[]{:S(2)}, u32[]{:S(2)}) collective-permute-start(bf16[5,128,128]{2,1,0:T(8,128)(2,1)} %get-tuple-element.67), channel_id=1, source_target_pairs={{0,24},{4,28},{8,16},{12,20},{16,8},{20,12},{24,0},{28,4},{1,25},{... | collective-permute-start | bytes 491528 | tf_op jit(solution)/shard_map/ppermute | solution.py:376
  22.8 3.0 %copy-start.10 = (bf16[5,128,128]{2,1,0:T(8,128)(2,1)S(1)}, bf16[5,128,128]{2,1,0:T(8,128)(2,1)}, u32[]{:S(2)}) copy-start(bf16[5,128,128]{2,1,0:T(8,128)(2,1)} %get-tuple-element.54) | copy-start | bytes 491524
  22.8 4.2 %copy-start.11 = (bf16[5,128,128]{2,1,0:T(8,128)(2,1)S(1)}, bf16[5,128,128]{2,1,0:T(8,128)(2,1)}, u32[]{:S(2)}) copy-start(bf16[5,128,128]{2,1,0:T(8,128)(2,1)} %get-tuple-element.68) | copy-start | bytes 491524
  22.8 24.8 %copy-start.9 = (bf16[5,128,128]{2,1,0:T(8,128)(2,1)S(1)}, bf16[5,128,128]{2,1,0:T(8,128)(2,1)}, u32[]{:S(2)}) copy-start(bf16[5,128,128]{2,1,0:T(8,128)(2,1)} %get-tuple-element.55) | copy-start | bytes 491524
  22.8 34.0 %copy-start.8 = (bf16[5,128,128]{2,1,0:T(8,128)(2,1)S(1)}, bf16[5,128,128]{2,1,0:T(8,128)(2,1)}, u32[]{:S(2)}) copy-start(bf16[5,128,128]{2,1,0:T(8,128)(2,1)} %get-tuple-element.56) | copy-start | bytes 491524
  22.8 34.9 %copy-start.3 = (bf16[5,128,128]{2,1,0:T(8,128)(2,1)S(1)}, bf16[5,128,128]{2,1,0:T(8,128)(2,1)}, u32[]{:S(2)}) copy-start(bf16[5,128,128]{2,1,0:T(8,128)(2,1)} %get-tuple-element.69.refs_7_) | copy-start | bytes 491524
  25.8 38.2 %collective-permute-start = (bf16[5,128,128]{2,1,0:T(8,128)(2,1)S(1)}, bf16[5,128,128]{2,1,0:T(8,128)(2,1)S(1)}, u32[]{:S(2)}, u32[]{:S(2)}) collective-permute-start(bf16[5,128,128]{2,1,0:T(8,128)(2,1)S(1)} %copy-done.10), channel_id=1, source_target_pairs={{0,16},{4,20},{8,24},{12,28},{16,0},{20,4},{24,8},{28,12},{1,17},{... | collective-permute-start | bytes 491528 | tf_op jit(solution)/shard_map/ppermute | solution.py:376
  27.0 20.6 %collective-permute-start.13 = (bf16[5,128,128]{2,1,0:T(8,128)(2,1)S(1)}, bf16[5,128,128]{2,1,0:T(8,128)(2,1)S(1)}, u32[]{:S(2)}, u32[]{:S(2)}) collective-permute-start(bf16[5,128,128]{2,1,0:T(8,128)(2,1)S(1)} %copy-done.11), channel_id=1, source_target_pairs={{0,28},{4,24},{8,20},{12,16},{16,12},{20,8},{24,4},{28,0},{1,29},{... | collective-permute-start | bytes 491528 | tf_op jit(solution)/shard_map/ppermute | solution.py:376
  30.1 26.7 %collective-permute-start.14 = (bf16[5,128,128]{2,1,0:T(8,128)(2,1)}, bf16[5,128,128]{2,1,0:T(8,128)(2,1)S(1)}, u32[]{:S(2)}, u32[]{:S(2)}) collective-permute-start(bf16[5,128,128]{2,1,0:T(8,128)(2,1)} %get-tuple-element.78), channel_id=1, source_target_pairs={{0,16},{4,20},{8,24},{12,28},{16,0},{20,4},{24,8},{28,12},{1,17},{... | collective-permute-start | bytes 491528 | tf_op jit(solution)/shard_map/ppermute | solution.py:376
  31.5 30.4 %collective-permute-start.15 = (bf16[5,128,128]{2,1,0:T(8,128)(2,1)}, bf16[5,128,128]{2,1,0:T(8,128)(2,1)S(1)}, u32[]{:S(2)}, u32[]{:S(2)}) collective-permute-start(bf16[5,128,128]{2,1,0:T(8,128)(2,1)} %get-tuple-element.79), channel_id=1, source_target_pairs={{0,24},{4,28},{8,16},{12,20},{16,8},{20,12},{24,0},{28,4},{1,25},{... | collective-permute-start | bytes 491528 | tf_op jit(solution)/shard_map/ppermute | solution.py:376
  32.6 30.9 %collective-permute-start.16 = (bf16[5,128,128]{2,1,0:T(8,128)(2,1)}, bf16[5,128,128]{2,1,0:T(8,128)(2,1)S(1)}, u32[]{:S(2)}, u32[]{:S(2)}) collective-permute-start(bf16[5,128,128]{2,1,0:T(8,128)(2,1)} %get-tuple-element.80), channel_id=1, source_target_pairs={{0,8},{4,12},{8,0},{12,4},{16,24},{20,28},{24,16},{28,20},{1,9},{5... | collective-permute-start | bytes 491528 | tf_op jit(solution)/shard_map/ppermute | solution.py:376
  47.6 18.0 %collective-permute-start.1 = (bf16[5,128,128]{2,1,0:T(8,128)(2,1)S(1)}, bf16[5,128,128]{2,1,0:T(8,128)(2,1)S(1)}, u32[]{:S(2)}, u32[]{:S(2)}) collective-permute-start(bf16[5,128,128]{2,1,0:T(8,128)(2,1)S(1)} %copy-done.9), channel_id=1, source_target_pairs={{0,8},{4,12},{8,0},{12,4},{16,24},{20,28},{24,16},{28,20},{1,9},{5... | collective-permute-start | bytes 491528 | tf_op jit(solution)/shard_map/ppermute | solution.py:376
  56.8 0.9 copy-start.1
  56.8 10.8 %collective-permute-start.2 = (bf16[5,128,128]{2,1,0:T(8,128)(2,1)S(1)}, bf16[5,128,128]{2,1,0:T(8,128)(2,1)S(1)}, u32[]{:S(2)}, u32[]{:S(2)}) collective-permute-start(bf16[5,128,128]{2,1,0:T(8,128)(2,1)S(1)} %copy-done.8), channel_id=1, source_target_pairs={{0,20},{4,16},{8,28},{12,24},{16,4},{20,0},{24,12},{28,8},{1,21},{... | collective-permute-start | bytes 491528 | tf_op jit(solution)/shard_map/ppermute | solution.py:376
  57.8 4.1 %copy-start.7 = (bf16[5,128,128]{2,1,0:T(8,128)(2,1)S(1)}, bf16[5,128,128]{2,1,0:T(8,128)(2,1)}, u32[]{:S(2)}) copy-start(bf16[5,128,128]{2,1,0:T(8,128)(2,1)} %get-tuple-element.57) | copy-start | bytes 491524
  57.8 9.9 %copy-start = (bf16[5,128,128]{2,1,0:T(8,128)(2,1)S(1)}, bf16[5,128,128]{2,1,0:T(8,128)(2,1)}, u32[]{:S(2)}) copy-start(bf16[5,128,128]{2,1,0:T(8,128)(2,1)} %get-tuple-element.85.refs_3_) | copy-start | bytes 491524
  57.8 15.2 %copy-start.6 = (bf16[5,128,128]{2,1,0:T(8,128)(2,1)S(1)}, bf16[5,128,128]{2,1,0:T(8,128)(2,1)}, u32[]{:S(2)}) copy-start(bf16[5,128,128]{2,1,0:T(8,128)(2,1)} %get-tuple-element.58) | copy-start | bytes 491524
  57.8 18.7 %copy-start.5 = (bf16[5,128,128]{2,1,0:T(8,128)(2,1)S(1)}, bf16[5,128,128]{2,1,0:T(8,128)(2,1)}, u32[]{:S(2)}) copy-start(bf16[5,128,128]{2,1,0:T(8,128)(2,1)} %get-tuple-element.59) | copy-start | bytes 491524
  57.8 23.9 %copy-start.4 = (bf16[5,128,128]{2,1,0:T(8,128)(2,1)S(1)}, bf16[5,128,128]{2,1,0:T(8,128)(2,1)}, u32[]{:S(2)}) copy-start(bf16[5,128,128]{2,1,0:T(8,128)(2,1)} %get-tuple-element.60) | copy-start | bytes 491524
  61.9 11.0 %collective-permute-start.3 = (bf16[5,128,128]{2,1,0:T(8,128)(2,1)S(1)}, bf16[5,128,128]{2,1,0:T(8,128)(2,1)S(1)}, u32[]{:S(2)}, u32[]{:S(2)}) collective-permute-start(bf16[5,128,128]{2,1,0:T(8,128)(2,1)S(1)} %copy-done.7), channel_id=1, source_target_pairs={{0,4},{4,0},{8,12},{12,8},{16,20},{20,16},{24,28},{28,24},{1,5},{5... | collective-permute-start | bytes 491528 | tf_op jit(solution)/shard_map/ppermute | solution.py:376
  63.5 12.9 %collective-permute-start.17 = (bf16[5,128,128]{2,1,0:T(8,128)(2,1)S(1)}, bf16[5,128,128]{2,1,0:T(8,128)(2,1)S(1)}, u32[]{:S(2)}, u32[]{:S(2)}) collective-permute-start(bf16[5,128,128]{2,1,0:T(8,128)(2,1)S(1)} %collective-permute-done.14.refs_0_), channel_id=1, source_target_pairs={{0,4},{4,0},{8,12},{12,8},{16,20},{20,16},{24,28},{28,24},{1,5},{5... | collective-permute-start | bytes 491528 | tf_op jit(solution)/shard_map/ppermute | solution.py:376
  64.0 17.7 %collective-permute-start.18 = (bf16[5,128,128]{2,1,0:T(8,128)(2,1)S(1)}, bf16[5,128,128]{2,1,0:T(8,128)(2,1)S(1)}, u32[]{:S(2)}, u32[]{:S(2)}) collective-permute-start(bf16[5,128,128]{2,1,0:T(8,128)(2,1)S(1)} %collective-permute-done.15.refs_1_), channel_id=1, source_target_pairs={{0,4},{4,0},{8,12},{12,8},{16,20},{20,16},{24,28},{28,24},{1,5},{5... | collective-permute-start | bytes 491528 | tf_op jit(solution)/shard_map/ppermute | solution.py:376
  65.6 19.6 %collective-permute-start.19 = (bf16[5,128,128]{2,1,0:T(8,128)(2,1)S(1)}, bf16[5,128,128]{2,1,0:T(8,128)(2,1)S(1)}, u32[]{:S(2)}, u32[]{:S(2)}) collective-permute-start(bf16[5,128,128]{2,1,0:T(8,128)(2,1)S(1)} %collective-permute-done.16.refs_2_), channel_id=1, source_target_pairs={{0,4},{4,0},{8,12},{12,8},{16,20},{20,16},{24,28},{28,24},{1,5},{5... | collective-permute-start | bytes 491528 | tf_op jit(solution)/shard_map/ppermute | solution.py:376
  67.6 20.2 %collective-permute-start.20 = (bf16[5,128,128]{2,1,0:T(8,128)(2,1)S(1)}, bf16[5,128,128]{2,1,0:T(8,128)(2,1)S(1)}, u32[]{:S(2)}, u32[]{:S(2)}) collective-permute-start(bf16[5,128,128]{2,1,0:T(8,128)(2,1)S(1)} %copy-done), channel_id=1, source_target_pairs={{0,4},{4,0},{8,12},{12,8},{16,20},{20,16},{24,28},{28,24},{1,5},{5... | collective-permute-start | bytes 491528 | tf_op jit(solution)/shard_map/ppermute | solution.py:376
  72.9 20.2 %collective-permute-start.4 = (bf16[5,128,128]{2,1,0:T(8,128)(2,1)S(1)}, bf16[5,128,128]{2,1,0:T(8,128)(2,1)S(1)}, u32[]{:S(2)}, u32[]{:S(2)}) collective-permute-start(bf16[5,128,128]{2,1,0:T(8,128)(2,1)S(1)} %copy-done.6), channel_id=1, source_target_pairs={{0,12},{4,8},{8,4},{12,0},{16,28},{20,24},{24,20},{28,16},{1,13},{... | collective-permute-start | bytes 491528 | tf_op jit(solution)/shard_map/ppermute | solution.py:376
  76.5 19.3 %collective-permute-start.5 = (bf16[5,128,128]{2,1,0:T(8,128)(2,1)S(1)}, bf16[5,128,128]{2,1,0:T(8,128)(2,1)S(1)}, u32[]{:S(2)}, u32[]{:S(2)}) collective-permute-start(bf16[5,128,128]{2,1,0:T(8,128)(2,1)S(1)} %copy-done.5), channel_id=1, source_target_pairs={{0,24},{4,28},{8,16},{12,20},{16,8},{20,12},{24,0},{28,4},{1,25},{... | collective-permute-start | bytes 491528 | tf_op jit(solution)/shard_map/ppermute | solution.py:376
  81.7 23.5 %copy-start.2 = (bf16[5,128,128]{2,1,0:T(8,128)(2,1)S(1)}, bf16[5,128,128]{2,1,0:T(8,128)(2,1)}, u32[]{:S(2)}) copy-start(bf16[5,128,128]{2,1,0:T(8,128)(2,1)} %get-tuple-element.61.refs_7_) | copy-start | bytes 491524
  81.7 19.1 %collective-permute-start.6 = (bf16[5,128,128]{2,1,0:T(8,128)(2,1)S(1)}, bf16[5,128,128]{2,1,0:T(8,128)(2,1)S(1)}, u32[]{:S(2)}, u32[]{:S(2)}) collective-permute-start(bf16[5,128,128]{2,1,0:T(8,128)(2,1)S(1)} %copy-done.4), channel_id=1, source_target_pairs={{0,28},{4,24},{8,20},{12,16},{16,12},{20,8},{24,4},{28,0},{1,29},{... | collective-permute-start | bytes 491528 | tf_op jit(solution)/shard_map/ppermute | solution.py:376
  85.2 15.7 %collective-permute-start.28 = (bf16[2,128,128]{2,1,0:T(8,128)(2,1)S(1)}, bf16[2,128,128]{2,1,0:T(8,128)(2,1)S(1)}, u32[]{:S(2)}, u32[]{:S(2)}) collective-permute-start(bf16[2,128,128]{2,1,0:T(8,128)(2,1)S(1)} %get-tuple-element.98), channel_id=1, source_target_pairs={{0,16},{4,20},{8,24},{12,28},{16,0},{20,4},{24,8},{28,12},{1,17},{... | collective-permute-start | bytes 196616 | tf_op jit(solution)/shard_map/ppermute | solution.py:376
  87.9 13.7 %collective-permute-start.29 = (bf16[2,128,128]{2,1,0:T(8,128)(2,1)S(1)}, bf16[2,128,128]{2,1,0:T(8,128)(2,1)S(1)}, u32[]{:S(2)}, u32[]{:S(2)}) collective-permute-start(bf16[2,128,128]{2,1,0:T(8,128)(2,1)S(1)} %get-tuple-element.99), channel_id=1, source_target_pairs={{0,4},{4,0},{8,12},{12,8},{16,20},{20,16},{24,28},{28,24},{1,5},{5... | collective-permute-start | bytes 196616 | tf_op jit(solution)/shard_map/ppermute | solution.py:376
  93.2 16.1 %collective-permute-start.30 = (bf16[2,128,128]{2,1,0:T(8,128)(2,1)S(1)}, bf16[2,128,128]{2,1,0:T(8,128)(2,1)S(1)}, u32[]{:S(2)}, u32[]{:S(2)}) collective-permute-start(bf16[2,128,128]{2,1,0:T(8,128)(2,1)S(1)} %get-tuple-element.100), channel_id=1, source_target_pairs={{0,20},{4,16},{8,28},{12,24},{16,4},{20,0},{24,12},{28,8},{1,21},{... | collective-permute-start | bytes 196616 | tf_op jit(solution)/shard_map/ppermute | solution.py:376
  95.7 14.1 %collective-permute-start.31 = (bf16[2,128,128]{2,1,0:T(8,128)(2,1)S(1)}, bf16[2,128,128]{2,1,0:T(8,128)(2,1)S(1)}, u32[]{:S(2)}, u32[]{:S(2)}) collective-permute-start(bf16[2,128,128]{2,1,0:T(8,128)(2,1)S(1)} %get-tuple-element.101), channel_id=1, source_target_pairs={{0,8},{4,12},{8,0},{12,4},{16,24},{20,28},{24,16},{28,20},{1,9},{5... | collective-permute-start | bytes 196616 | tf_op jit(solution)/shard_map/ppermute | solution.py:376
  100.9 10.0 %collective-permute-start.32 = (bf16[2,128,128]{2,1,0:T(8,128)(2,1)S(1)}, bf16[2,128,128]{2,1,0:T(8,128)(2,1)S(1)}, u32[]{:S(2)}, u32[]{:S(2)}) collective-permute-start(bf16[2,128,128]{2,1,0:T(8,128)(2,1)S(1)} %get-tuple-element.102), channel_id=1, source_target_pairs={{0,24},{4,28},{8,16},{12,20},{16,8},{20,12},{24,0},{28,4},{1,25},{... | collective-permute-start | bytes 196616 | tf_op jit(solution)/shard_map/ppermute | solution.py:376
  100.9 12.9 %collective-permute-start.33 = (bf16[2,128,128]{2,1,0:T(8,128)(2,1)S(1)}, bf16[2,128,128]{2,1,0:T(8,128)(2,1)S(1)}, u32[]{:S(2)}, u32[]{:S(2)}) collective-permute-start(bf16[2,128,128]{2,1,0:T(8,128)(2,1)S(1)} %get-tuple-element.103), channel_id=1, source_target_pairs={{0,12},{4,8},{8,4},{12,0},{16,28},{20,24},{24,20},{28,16},{1,13},{... | collective-permute-start | bytes 196616 | tf_op jit(solution)/shard_map/ppermute | solution.py:376
  101.5 13.7 %collective-permute-start.34 = (bf16[2,128,128]{2,1,0:T(8,128)(2,1)S(1)}, bf16[2,128,128]{2,1,0:T(8,128)(2,1)S(1)}, u32[]{:S(2)}, u32[]{:S(2)}) collective-permute-start(bf16[2,128,128]{2,1,0:T(8,128)(2,1)S(1)} %get-tuple-element.104), channel_id=1, source_target_pairs={{0,28},{4,24},{8,20},{12,16},{16,12},{20,8},{24,4},{28,0},{1,29},{... | collective-permute-start | bytes 196616 | tf_op jit(solution)/shard_map/ppermute | solution.py:376
  109.3 21.7 %collective-permute-start.21 = (bf16[4,128,128]{2,1,0:T(8,128)(2,1)S(1)}, bf16[4,128,128]{2,1,0:T(8,128)(2,1)S(1)}, u32[]{:S(2)}, u32[]{:S(2)}) collective-permute-start(bf16[4,128,128]{2,1,0:T(8,128)(2,1)S(1)} %get-tuple-element.90), channel_id=1, source_target_pairs={{0,16},{4,20},{8,24},{12,28},{16,0},{20,4},{24,8},{28,12},{1,17},{... | collective-permute-start | bytes 393224 | tf_op jit(solution)/shard_map/ppermute | solution.py:376
  109.9 5.9 %collective-permute-start.22 = (bf16[2,128,128]{2,1,0:T(8,128)(2,1)S(1)}, bf16[2,128,128]{2,1,0:T(8,128)(2,1)S(1)}, u32[]{:S(2)}, u32[]{:S(2)}) collective-permute-start(bf16[2,128,128]{2,1,0:T(8,128)(2,1)S(1)} %get-tuple-element.91), channel_id=1, source_target_pairs={{0,4},{4,0},{8,12},{12,8},{16,20},{20,16},{24,28},{28,24},{1,5},{5... | collective-permute-start | bytes 196616 | tf_op jit(solution)/shard_map/ppermute | solution.py:376
  110.9 13.1 %collective-permute-start.23 = (bf16[2,128,128]{2,1,0:T(8,128)(2,1)S(1)}, bf16[2,128,128]{2,1,0:T(8,128)(2,1)S(1)}, u32[]{:S(2)}, u32[]{:S(2)}) collective-permute-start(bf16[2,128,128]{2,1,0:T(8,128)(2,1)S(1)} %get-tuple-element.92), channel_id=1, source_target_pairs={{0,20},{4,16},{8,28},{12,24},{16,4},{20,0},{24,12},{28,8},{1,21},{... | collective-permute-start | bytes 196616 | tf_op jit(solution)/shard_map/ppermute | solution.py:376
  113.7 17.2 %collective-permute-start.24 = (bf16[4,128,128]{2,1,0:T(8,128)(2,1)S(1)}, bf16[4,128,128]{2,1,0:T(8,128)(2,1)S(1)}, u32[]{:S(2)}, u32[]{:S(2)}) collective-permute-start(bf16[4,128,128]{2,1,0:T(8,128)(2,1)S(1)} %get-tuple-element.93), channel_id=1, source_target_pairs={{0,8},{4,12},{8,0},{12,4},{16,24},{20,28},{24,16},{28,20},{1,9},{5... | collective-permute-start | bytes 393224 | tf_op jit(solution)/shard_map/ppermute | solution.py:376
  115.3 15.7 %collective-permute-start.25 = (bf16[4,128,128]{2,1,0:T(8,128)(2,1)S(1)}, bf16[4,128,128]{2,1,0:T(8,128)(2,1)S(1)}, u32[]{:S(2)}, u32[]{:S(2)}) collective-permute-start(bf16[4,128,128]{2,1,0:T(8,128)(2,1)S(1)} %get-tuple-element.94), channel_id=1, source_target_pairs={{0,24},{4,28},{8,16},{12,20},{16,8},{20,12},{24,0},{28,4},{1,25},{... | collective-permute-start | bytes 393224 | tf_op jit(solution)/shard_map/ppermute | solution.py:376
  115.7 8.4 %collective-permute-start.26 = (bf16[2,128,128]{2,1,0:T(8,128)(2,1)S(1)}, bf16[2,128,128]{2,1,0:T(8,128)(2,1)S(1)}, u32[]{:S(2)}, u32[]{:S(2)}) collective-permute-start(bf16[2,128,128]{2,1,0:T(8,128)(2,1)S(1)} %get-tuple-element.95), channel_id=1, source_target_pairs={{0,12},{4,8},{8,4},{12,0},{16,28},{20,24},{24,20},{28,16},{1,13},{... | collective-permute-start | bytes 196616 | tf_op jit(solution)/shard_map/ppermute | solution.py:376
  124.0 7.0 %collective-permute-start.27 = (bf16[2,128,128]{2,1,0:T(8,128)(2,1)S(1)}, bf16[2,128,128]{2,1,0:T(8,128)(2,1)S(1)}, u32[]{:S(2)}, u32[]{:S(2)}) collective-permute-start(bf16[2,128,128]{2,1,0:T(8,128)(2,1)S(1)} %get-tuple-element.96), channel_id=1, source_target_pairs={{0,28},{4,24},{8,20},{12,16},{16,12},{20,8},{24,4},{28,0},{1,29},{... | collective-permute-start | bytes 196616 | tf_op jit(solution)/shard_map/ppermute | solution.py:376

commit v8 on v3

--- a/solution.py
+++ b/solution.py
@@ -221,13 +221,12 @@
         for i in range(blocks):
             x[at[i]] = x_refs[i][...]
 
-        def head(s, carry):
+        for s in range(full):
             sources = [(x, 5 * s + t) for t in range(5)]
             student_head(range(0, blocks, 2), first_ref[0], sources[:3], y, 2 * s)
-            gen = lambda at: y[at, 2 * s]
+            gen = functools.partial(lambda u, at: y[at, u], 2 * s)
             teacher_whole_head(blocks, clip_ref, sources[3:], gen, y, 2 * s + 1)
 
-        lax.fori_loop(0, full, head, None)
         for i, d in enumerate(home):
             o_refs[i][...] = y[where_ref[2] ^ d]
 

time: 118 us -> 117 us (level)
  no operation moved by 1% of the time
where the time goes in v8:
time: 117 us; the launch traced here: 116 us
  starting transfers between devices  63.3 us (54%)
  waiting for transfers between devices  29.2 us (25%)
  Pallas kernels  18.8 us (16%)
  local copies, waits for them, and re-layouts  1.85 us (2%)
  other arithmetic  1.57 us (1%)
  between operations  1.41 us (1%)
    ppermute x24, starting transfers between devices, swapped(): lax.ppermute(x, 'tm', [(i, i ^ by) for i in range(peers)])  63.3 us
    ppermute x24, waiting for transfers between devices, swapped(): lax.ppermute(x, 'tm', [(i, i ^ by) for i in range(peers)])  29.2 us
    pallas_call x1, Pallas kernels, slots_kernel(): pl.pallas_call(body, in_specs=[SMEM] * 3 + [VMEM] * blocks, out_specs=[VM...  7.2 us
    pallas_call x1, Pallas kernels, slots_pack(): pl.pallas_call(body, in_specs=[SMEM] + [pl.BlockSpec(memory_space=pl.ANY)...  4.14 us
    pallas_call x1, Pallas kernels, rest_kernel(): pl.pallas_call(body, in_specs=[SMEM] * 3 + [VMEM] * (2 * columns), out_sp...  3.58 us
  transfers between devices with their start and end apart: 24, of which 5 were waited for; matrix products, arithmetic and copies ran while one was open for 2% of the time, Pallas kernels for 13%

profile of v8, /device:TPU:0, one launch (start us, length us, event | category | flops | bytes accessed | tf_op | source)
XLA Modules:
  0.0 116.1 jit_solution(8937789086104079737)
XLA Ops:
  0.6 2.1 %shard_map.87 = (bf16[5,128,128]{2,1,0:T(8,128)(2,1)}, bf16[5,128,128]{2,1,0:T(8,128)(2,1)}, bf16[5,128,128]{2,1,0:T(8,128)(2,1)}, bf16[5,128,128]{2,1,0:T(8,128)(2,1)}) custom-call(s32[1]{0:T(128)} %bitcast.column_ref, bf16[1,128,2560]{2,1,0:T(8,128)(2,1)} %refs_0_.3, bf16[1,128,2560]{2,1,0:T(8,128)(2,1)} %refs_1_.3, bf16[1,128,2560]{2,1,0:T(8,128)(2,1)} %refs_2_.3, ...), custom_call_target="tpu_custom_call" | custom-call | bytes 1310720 | tf_op jit(solution)/shard_map/pallas_call | solution.py:292
  2.7 3.1 %collective-permute-start.7 = (bf16[5,128,128]{2,1,0:T(8,128)(2,1)}, bf16[5,128,128]{2,1,0:T(8,128)(2,1)S(1)}, u32[]{:S(2)}, u32[]{:S(2)}) collective-permute-start(bf16[5,128,128]{2,1,0:T(8,128)(2,1)} %get-tuple-element.59), channel_id=1, source_target_pairs={{0,8},{4,12},{8,0},{12,4},{16,24},{20,28},{24,16},{28,20},{1,9},{5... | collective-permute-start | bytes 491528 | tf_op jit(solution)/shard_map/ppermute | solution.py:369
  5.8 2.6 %collective-permute-start.8 = (bf16[5,128,128]{2,1,0:T(8,128)(2,1)}, bf16[5,128,128]{2,1,0:T(8,128)(2,1)S(1)}, u32[]{:S(2)}, u32[]{:S(2)}) collective-permute-start(bf16[5,128,128]{2,1,0:T(8,128)(2,1)} %get-tuple-element.60), channel_id=1, source_target_pairs={{0,16},{4,20},{8,24},{12,28},{16,0},{20,4},{24,8},{28,12},{1,17},{... | collective-permute-start | bytes 491528 | tf_op jit(solution)/shard_map/ppermute | solution.py:369
  8.4 0.0 collective-permute-start.9
  8.4 1.7 %collective-permute-start.10 = (bf16[5,128,128]{2,1,0:T(8,128)(2,1)}, bf16[5,128,128]{2,1,0:T(8,128)(2,1)S(1)}, u32[]{:S(2)}, u32[]{:S(2)}) collective-permute-start(bf16[5,128,128]{2,1,0:T(8,128)(2,1)} %get-tuple-element.58.refs_0_), channel_id=1, source_target_pairs={{0,4},{4,0},{8,12},{12,8},{16,20},{20,16},{24,28},{28,24},{1,5},{5... | collective-permute-start | bytes 491528 | tf_op jit(solution)/shard_map/ppermute | solution.py:369
  10.1 0.6 pad_add_fusion.where_ref
  10.7 4.1 %shard_map.86 = (bf16[10,128,128]{2,1,0:T(8,128)(2,1)}, bf16[10,128,128]{2,1,0:T(8,128)(2,1)}, bf16[10,128,128]{2,1,0:T(8,128)(2,1)}, bf16[10,128,128]{2,1,0:T(8...) custom-call(s32[3]{0:T(128)} %pad_add_fusion.where_ref, ...), custom_call_target="tpu_custom_call" | custom-call | bytes 5242880 | tf_op jit(solution)/shard_map/pallas_call | solution.py:264
  14.8 1.8 %collective-permute-start = (bf16[10,128,128]{2,1,0:T(8,128)(2,1)}, bf16[10,128,128]{2,1,0:T(8,128)(2,1)S(1)}, u32[]{:S(2)}, u32[]{:S(2)}) collective-permute-start(bf16[10,128,128]{2,1,0:T(8,128)(2,1)} %get-tuple-element.50), channel_id=1, source_target_pairs={{0,16},{4,20},{8,24},{12,28},{16,0},{20,4},{24,8},{28,12},{1,17},{... | collective-permute-start | bytes 983048 | tf_op jit(solution)/shard_map/ppermute | solution.py:369
  16.6 0.0 collective-permute-done.7.refs_1_
  16.6 2.5 %collective-permute-start.1 = (bf16[10,128,128]{2,1,0:T(8,128)(2,1)}, bf16[10,128,128]{2,1,0:T(8,128)(2,1)S(1)}, u32[]{:S(2)}, u32[]{:S(2)}) collective-permute-start(bf16[10,128,128]{2,1,0:T(8,128)(2,1)} %get-tuple-element.51), channel_id=1, source_target_pairs={{0,8},{4,12},{8,0},{12,4},{16,24},{20,28},{24,16},{28,20},{1,9},{5... | collective-permute-start | bytes 983048 | tf_op jit(solution)/shard_map/ppermute | solution.py:369
  19.1 9.0 %collective-permute-done.8.refs_2_ = bf16[5,128,128]{2,1,0:T(8,128)(2,1)S(1)} collective-permute-done((bf16[5,128,128]{2,1,0:T(8,128)(2,1)}, bf16[5,128,128]{2,1,0:T(8,128)(2,1)S(1)}, u32[]{:S(2)}, u32[]{:S(2)}) %collective-permute-start.8) | collective-permute-done | bytes 163872 | tf_op jit(solution)/shard_map/ppermute | solution.py:369
  28.1 1.5 %collective-permute-start.11 = (bf16[5,128,128]{2,1,0:T(8,128)(2,1)S(1)}, bf16[5,128,128]{2,1,0:T(8,128)(2,1)S(1)}, u32[]{:S(2)}, u32[]{:S(2)}) collective-permute-start(bf16[5,128,128]{2,1,0:T(8,128)(2,1)S(1)} %collective-permute-done.7.refs_1_), channel_id=1, source_target_pairs={{0,4},{4,0},{8,12},{12,8},{16,20},{20,16},{24,28},{28,24},{1,5},{5... | collective-permute-start | bytes 491528 | tf_op jit(solution)/shard_map/ppermute | solution.py:369
  29.6 0.0 collective-permute-done.9.refs_3_
  29.6 0.5 collective-permute-start.12
  30.1 0.0 collective-permute-done.10.refs_4_
  30.1 1.5 %collective-permute-start.13 = (bf16[5,128,128]{2,1,0:T(8,128)(2,1)S(1)}, bf16[5,128,128]{2,1,0:T(8,128)(2,1)S(1)}, u32[]{:S(2)}, u32[]{:S(2)}) collective-permute-start(bf16[5,128,128]{2,1,0:T(8,128)(2,1)S(1)} %collective-permute-done.9.refs_3_), channel_id=1, source_target_pairs={{0,4},{4,0},{8,12},{12,8},{16,20},{20,16},{24,28},{28,24},{1,5},{5... | collective-permute-start | bytes 491528 | tf_op jit(solution)/shard_map/ppermute | solution.py:369
  32.3 0.0 copy-start.3
  32.3 0.6 copy-done.3
  32.9 0.2 reduce-window.8
  33.1 0.7 fusion
  33.8 0.7 pad.2.clone
  34.5 0.0 collective-permute-done.11.refs_5_
  34.5 4.4 %collective-permute-start.2 = (bf16[10,128,128]{2,1,0:T(8,128)(2,1)}, bf16[10,128,128]{2,1,0:T(8,128)(2,1)S(1)}, u32[]{:S(2)}, u32[]{:S(2)}) collective-permute-start(bf16[10,128,128]{2,1,0:T(8,128)(2,1)} %get-tuple-element.52), channel_id=1, source_target_pairs={{0,20},{4,16},{8,28},{12,24},{16,4},{20,0},{24,12},{28,8},{1,21},{... | collective-permute-start | bytes 983048 | tf_op jit(solution)/shard_map/ppermute | solution.py:369
  38.9 0.0 collective-permute-done.12.refs_6_
  38.9 0.5 collective-permute-start.3
  39.4 0.0 collective-permute-done.13.refs_7_
  39.4 14.7 %collective-permute-start.4 = (bf16[10,128,128]{2,1,0:T(8,128)(2,1)}, bf16[10,128,128]{2,1,0:T(8,128)(2,1)S(1)}, u32[]{:S(2)}, u32[]{:S(2)}) collective-permute-start(bf16[10,128,128]{2,1,0:T(8,128)(2,1)} %get-tuple-element.54), channel_id=1, source_target_pairs={{0,12},{4,8},{8,4},{12,0},{16,28},{20,24},{24,20},{28,16},{1,13},{... | collective-permute-start | bytes 983048 | tf_op jit(solution)/shard_map/ppermute | solution.py:369
  54.1 0.0 collective-permute-done.refs_0_
  54.1 1.4 %collective-permute-start.5 = (bf16[10,128,128]{2,1,0:T(8,128)(2,1)}, bf16[10,128,128]{2,1,0:T(8,128)(2,1)S(1)}, u32[]{:S(2)}, u32[]{:S(2)}) collective-permute-start(bf16[10,128,128]{2,1,0:T(8,128)(2,1)} %get-tuple-element.55), channel_id=1, source_target_pairs={{0,24},{4,28},{8,16},{12,20},{16,8},{20,12},{24,0},{28,4},{1,25},{... | collective-permute-start | bytes 983048 | tf_op jit(solution)/shard_map/ppermute | solution.py:369
  55.5 0.0 collective-permute-done.1.refs_1_
  55.5 2.4 %collective-permute-start.6 = (bf16[10,128,128]{2,1,0:T(8,128)(2,1)}, bf16[10,128,128]{2,1,0:T(8,128)(2,1)S(1)}, u32[]{:S(2)}, u32[]{:S(2)}) collective-permute-start(bf16[10,128,128]{2,1,0:T(8,128)(2,1)} %get-tuple-element.56), channel_id=1, source_target_pairs={{0,28},{4,24},{8,20},{12,16},{16,12},{20,8},{24,4},{28,0},{1,29},{... | collective-permute-start | bytes 983048 | tf_op jit(solution)/shard_map/ppermute | solution.py:369
  57.9 0.1 select_reduce_fusion.1
  58.0 0.1 add_add_fusion.clip_ref
  58.0 0.0 copy-done
  58.0 0.5 copy-done.1
  58.5 3.6 %shard_map.88 = (bf16[2,128,128]{2,1,0:T(8,128)(2,1)S(1)}, bf16[2,128,128]{2,1,0:T(8,128)(2,1)S(1)}, bf16[2,128,128]{2,1,0:T(8,128)(2,1)S(1)}, bf16[2,128,128]{2,1,0:T(8,128)(2,1)S(1)}) custom-call(s32[1]{0:T(128)S(6)} %copy.9.first_ref, s32[3,8]{1,0:T(4,128)S(1)} %add_add_fusion.clip_ref, s32[3]{0:T(128)S(1)} %copy-done.1, ...), custom_call_target="tpu_custom_call" | custom-call | bytes 32768 | tf_op jit(solution)/shard_map/pallas_call | solution.py:324
  62.1 0.0 collective-permute-done.2.refs_2_
  62.1 0.0 collective-permute-done.3.refs_3_
  62.1 7.6 %collective-permute-done.4.refs_4_ = bf16[10,128,128]{2,1,0:T(8,128)(2,1)S(1)} collective-permute-done((bf16[10,128,128]{2,1,0:T(8,128)(2,1)}, bf16[10,128,128]{2,1,0:T(8,128)(2,1)S(1)}, u32[]{:S(2)}, u32[]{:S(2)}) %collective-permute-start.4) | collective-permute-done | bytes 327712 | tf_op jit(solution)/shard_map/ppermute | solution.py:369
  69.7 0.0 collective-permute-done.5.refs_5_
  69.7 0.0 collective-permute-done.6.refs_6_
  69.8 11.1 %collective-permute-start.14 = (bf16[2,128,128]{2,1,0:T(8,128)(2,1)S(1)}, bf16[2,128,128]{2,1,0:T(8,128)(2,1)S(1)}, u32[]{:S(2)}, u32[]{:S(2)}) collective-permute-start(bf16[2,128,128]{2,1,0:T(8,128)(2,1)S(1)} %get-tuple-element.83), channel_id=1, source_target_pairs={{0,8},{4,12},{8,0},{12,4},{16,24},{20,28},{24,16},{28,20},{1,9},{5... | collective-permute-start | bytes 196616 | tf_op jit(solution)/shard_map/ppermute | solution.py:369
  80.8 1.0 collective-permute-start.15
  81.9 1.5 %collective-permute-start.16 = (bf16[2,128,128]{2,1,0:T(8,128)(2,1)S(1)}, bf16[2,128,128]{2,1,0:T(8,128)(2,1)S(1)}, u32[]{:S(2)}, u32[]{:S(2)}) collective-permute-start(bf16[2,128,128]{2,1,0:T(8,128)(2,1)S(1)} %get-tuple-element.85), channel_id=1, source_target_pairs={{0,24},{4,28},{8,16},{12,20},{16,8},{20,12},{24,0},{28,4},{1,25},{... | collective-permute-start | bytes 196616 | tf_op jit(solution)/shard_map/ppermute | solution.py:369
  83.3 0.0 copy-done.2
  83.3 7.2 %shard_map.89 = (bf16[4,128,128]{2,1,0:T(8,128)(2,1)S(1)}, bf16[4,128,128]{2,1,0:T(8,128)(2,1)S(1)}, bf16[4,128,128]{2,1,0:T(8,128)(2,1)S(1)}, bf16[4,128,128]{2...) custom-call(s32[1]{0:T(128)S(6)} %copy.9.first_ref, ...), custom_call_target="tpu_custom_call" | custom-call | flops 2147483648 | bytes 3670016 | tf_op jit(solution)/shard_map/pallas_call | solution.py:233
  90.5 0.0 collective-permute-done.14.refs_9_
  90.5 0.0 collective-permute-done.15.refs_10_
  90.5 0.0 collective-permute-done.16.refs_11_
  90.6 0.6 collective-permute-start.17
  91.2 1.0 collective-permute-start.18
  92.2 1.9 %collective-permute-start.19 = (bf16[4,128,128]{2,1,0:T(8,128)(2,1)S(1)}, bf16[4,128,128]{2,1,0:T(8,128)(2,1)S(1)}, u32[]{:S(2)}, u32[]{:S(2)}) collective-permute-start(bf16[4,128,128]{2,1,0:T(8,128)(2,1)S(1)} %get-tuple-element.88), channel_id=1, source_target_pairs={{0,12},{4,8},{8,4},{12,0},{16,28},{20,24},{24,20},{28,16},{1,13},{... | collective-permute-start | bytes 393224 | tf_op jit(solution)/shard_map/ppermute | solution.py:369
  94.1 2.0 %collective-permute-start.20 = (bf16[4,128,128]{2,1,0:T(8,128)(2,1)S(1)}, bf16[4,128,128]{2,1,0:T(8,128)(2,1)S(1)}, u32[]{:S(2)}, u32[]{:S(2)}) collective-permute-start(bf16[4,128,128]{2,1,0:T(8,128)(2,1)S(1)} %get-tuple-element.89), channel_id=1, source_target_pairs={{0,16},{4,20},{8,24},{12,28},{16,0},{20,4},{24,8},{28,12},{1,17},{... | collective-permute-start | bytes 393224 | tf_op jit(solution)/shard_map/ppermute | solution.py:369
  96.1 0.9 collective-permute-start.21
  97.0 0.0 collective-permute-done.17.refs_0_
  97.0 2.4 %collective-permute-start.22 = (bf16[4,128,128]{2,1,0:T(8,128)(2,1)S(1)}, bf16[4,128,128]{2,1,0:T(8,128)(2,1)S(1)}, u32[]{:S(2)}, u32[]{:S(2)}) collective-permute-start(bf16[4,128,128]{2,1,0:T(8,128)(2,1)S(1)} %get-tuple-element.91), channel_id=1, source_target_pairs={{0,24},{4,28},{8,16},{12,20},{16,8},{20,12},{24,0},{28,4},{1,25},{... | collective-permute-start | bytes 393224 | tf_op jit(solution)/shard_map/ppermute | solution.py:369
  99.4 0.0 collective-permute-done.18.refs_1_
  99.4 2.4 %collective-permute-start.23 = (bf16[4,128,128]{2,1,0:T(8,128)(2,1)S(1)}, bf16[4,128,128]{2,1,0:T(8,128)(2,1)S(1)}, u32[]{:S(2)}, u32[]{:S(2)}) collective-permute-start(bf16[4,128,128]{2,1,0:T(8,128)(2,1)S(1)} %get-tuple-element.92), channel_id=1, source_target_pairs={{0,28},{4,24},{8,20},{12,16},{16,12},{20,8},{24,4},{28,0},{1,29},{... | collective-permute-start | bytes 393224 | tf_op jit(solution)/shard_map/ppermute | solution.py:369
  101.8 0.7 collective-permute-done.19.refs_2_
  102.5 9.0 %collective-permute-done.20.refs_3_ = bf16[4,128,128]{2,1,0:T(8,128)(2,1)S(1)} collective-permute-done((bf16[4,128,128]{2,1,0:T(8,128)(2,1)S(1)}, bf16[4,128,128]{2,1,0:T(8,128)(2,1)S(1)}, u32[]{:S(2)}, u32[]{:S(2)}) %collective-permute-start.20) | collective-permute-done | bytes 131104 | tf_op jit(solution)/shard_map/ppermute | solution.py:369
  111.5 2.7 %collective-permute-done.21.refs_4_ = bf16[4,128,128]{2,1,0:T(8,128)(2,1)S(1)} collective-permute-done((bf16[4,128,128]{2,1,0:T(8,128)(2,1)S(1)}, bf16[4,128,128]{2,1,0:T(8,128)(2,1)S(1)}, u32[]{:S(2)}, u32[]{:S(2)}) %collective-permute-start.21) | collective-permute-done | bytes 131104 | tf_op jit(solution)/shard_map/ppermute | solution.py:369
  114.2 0.0 collective-permute-done.22.refs_5_
  114.2 0.0 collective-permute-done.23.refs_6_
  114.2 1.8 %shard_map.90 = (bf16[1,128,2560]{2,1,0:T(8,128)(2,1)}, bf16[1,128,2560]{2,1,0:T(8,128)(2,1)}) custom-call(s32[3]{0:T(128)S(1)} %copy-done.1, bf16[4,128,128]{2,1,0:T(8,128)(2,1)S(1)} %collective-permute-done.17.refs_0_, bf16[4,128,128]{2,1,0:T(8,128)(2,1)S(1)} %collective-permute-done.18.refs_1_, bf16[4,128,128]{2,1,0:T(8,128)(2,1)S(1)} %collective-permute-done.19.refs_2_, ...), custom_call_target="tpu_custom_call" | custom-call | bytes 2621440 | tf_op jit(solution)/shard_map/pallas_call | solution.py:354
  (3 shorter events, 0.0 us)
Async XLA Ops:
  2.7 13.9 %collective-permute-start.7 = (bf16[5,128,128]{2,1,0:T(8,128)(2,1)}, bf16[5,128,128]{2,1,0:T(8,128)(2,1)S(1)}, u32[]{:S(2)}, u32[]{:S(2)}) collective-permute-start(bf16[5,128,128]{2,1,0:T(8,128)(2,1)} %get-tuple-element.59), channel_id=1, source_target_pairs={{0,8},{4,12},{8,0},{12,4},{16,24},{20,28},{24,16},{28,20},{1,9},{5... | collective-permute-start | bytes 491528 | tf_op jit(solution)/shard_map/ppermute | solution.py:369
  5.8 22.3 %collective-permute-start.8 = (bf16[5,128,128]{2,1,0:T(8,128)(2,1)}, bf16[5,128,128]{2,1,0:T(8,128)(2,1)S(1)}, u32[]{:S(2)}, u32[]{:S(2)}) collective-permute-start(bf16[5,128,128]{2,1,0:T(8,128)(2,1)} %get-tuple-element.60), channel_id=1, source_target_pairs={{0,16},{4,20},{8,24},{12,28},{16,0},{20,4},{24,8},{28,12},{1,17},{... | collective-permute-start | bytes 491528 | tf_op jit(solution)/shard_map/ppermute | solution.py:369
  8.4 21.2 %collective-permute-start.9 = (bf16[5,128,128]{2,1,0:T(8,128)(2,1)}, bf16[5,128,128]{2,1,0:T(8,128)(2,1)S(1)}, u32[]{:S(2)}, u32[]{:S(2)}) collective-permute-start(bf16[5,128,128]{2,1,0:T(8,128)(2,1)} %get-tuple-element.61), channel_id=1, source_target_pairs={{0,24},{4,28},{8,16},{12,20},{16,8},{20,12},{24,0},{28,4},{1,25},{... | collective-permute-start | bytes 491528 | tf_op jit(solution)/shard_map/ppermute | solution.py:369
  8.4 21.7 %collective-permute-start.10 = (bf16[5,128,128]{2,1,0:T(8,128)(2,1)}, bf16[5,128,128]{2,1,0:T(8,128)(2,1)S(1)}, u32[]{:S(2)}, u32[]{:S(2)}) collective-permute-start(bf16[5,128,128]{2,1,0:T(8,128)(2,1)} %get-tuple-element.58.refs_0_), channel_id=1, source_target_pairs={{0,4},{4,0},{8,12},{12,8},{16,20},{20,16},{24,28},{28,24},{1,5},{5... | collective-permute-start | bytes 491528 | tf_op jit(solution)/shard_map/ppermute | solution.py:369
  10.7 47.4 %copy-start = (bf16[5,128,128]{2,1,0:T(8,128)(2,1)S(1)}, bf16[5,128,128]{2,1,0:T(8,128)(2,1)}, u32[]{:S(2)}) copy-start(bf16[5,128,128]{2,1,0:T(8,128)(2,1)} %get-tuple-element.58.refs_0_) | copy-start | bytes 491524
  14.8 39.2 %collective-permute-start = (bf16[10,128,128]{2,1,0:T(8,128)(2,1)}, bf16[10,128,128]{2,1,0:T(8,128)(2,1)S(1)}, u32[]{:S(2)}, u32[]{:S(2)}) collective-permute-start(bf16[10,128,128]{2,1,0:T(8,128)(2,1)} %get-tuple-element.50), channel_id=1, source_target_pairs={{0,16},{4,20},{8,24},{12,28},{16,0},{20,4},{24,8},{28,12},{1,17},{... | collective-permute-start | bytes 983048 | tf_op jit(solution)/shard_map/ppermute | solution.py:369
  16.6 38.9 %collective-permute-start.1 = (bf16[10,128,128]{2,1,0:T(8,128)(2,1)}, bf16[10,128,128]{2,1,0:T(8,128)(2,1)S(1)}, u32[]{:S(2)}, u32[]{:S(2)}) collective-permute-start(bf16[10,128,128]{2,1,0:T(8,128)(2,1)} %get-tuple-element.51), channel_id=1, source_target_pairs={{0,8},{4,12},{8,0},{12,4},{16,24},{20,28},{24,16},{28,20},{1,9},{5... | collective-permute-start | bytes 983048 | tf_op jit(solution)/shard_map/ppermute | solution.py:369
  28.1 6.4 %collective-permute-start.11 = (bf16[5,128,128]{2,1,0:T(8,128)(2,1)S(1)}, bf16[5,128,128]{2,1,0:T(8,128)(2,1)S(1)}, u32[]{:S(2)}, u32[]{:S(2)}) collective-permute-start(bf16[5,128,128]{2,1,0:T(8,128)(2,1)S(1)} %collective-permute-done.7.refs_1_), channel_id=1, source_target_pairs={{0,4},{4,0},{8,12},{12,8},{16,20},{20,16},{24,28},{28,24},{1,5},{5... | collective-permute-start | bytes 491528 | tf_op jit(solution)/shard_map/ppermute | solution.py:369
  29.6 9.3 %collective-permute-start.12 = (bf16[5,128,128]{2,1,0:T(8,128)(2,1)S(1)}, bf16[5,128,128]{2,1,0:T(8,128)(2,1)S(1)}, u32[]{:S(2)}, u32[]{:S(2)}) collective-permute-start(bf16[5,128,128]{2,1,0:T(8,128)(2,1)S(1)} %collective-permute-done.8.refs_2_), channel_id=1, source_target_pairs={{0,4},{4,0},{8,12},{12,8},{16,20},{20,16},{24,28},{28,24},{1,5},{5... | collective-permute-start | bytes 491528 | tf_op jit(solution)/shard_map/ppermute | solution.py:369
  30.1 9.3 %collective-permute-start.13 = (bf16[5,128,128]{2,1,0:T(8,128)(2,1)S(1)}, bf16[5,128,128]{2,1,0:T(8,128)(2,1)S(1)}, u32[]{:S(2)}, u32[]{:S(2)}) collective-permute-start(bf16[5,128,128]{2,1,0:T(8,128)(2,1)S(1)} %collective-permute-done.9.refs_3_), channel_id=1, source_target_pairs={{0,4},{4,0},{8,12},{12,8},{16,20},{20,16},{24,28},{28,24},{1,5},{5... | collective-permute-start | bytes 491528 | tf_op jit(solution)/shard_map/ppermute | solution.py:369
  32.3 0.7 copy-start.3
  34.5 27.6 %collective-permute-start.2 = (bf16[10,128,128]{2,1,0:T(8,128)(2,1)}, bf16[10,128,128]{2,1,0:T(8,128)(2,1)S(1)}, u32[]{:S(2)}, u32[]{:S(2)}) collective-permute-start(bf16[10,128,128]{2,1,0:T(8,128)(2,1)} %get-tuple-element.52), channel_id=1, source_target_pairs={{0,20},{4,16},{8,28},{12,24},{16,4},{20,0},{24,12},{28,8},{1,21},{... | collective-permute-start | bytes 983048 | tf_op jit(solution)/shard_map/ppermute | solution.py:369
  38.9 23.3 %collective-permute-start.3 = (bf16[10,128,128]{2,1,0:T(8,128)(2,1)}, bf16[10,128,128]{2,1,0:T(8,128)(2,1)S(1)}, u32[]{:S(2)}, u32[]{:S(2)}) collective-permute-start(bf16[10,128,128]{2,1,0:T(8,128)(2,1)} %get-tuple-element.53), channel_id=1, source_target_pairs={{0,4},{4,0},{8,12},{12,8},{16,20},{20,16},{24,28},{28,24},{1,5},{5... | collective-permute-start | bytes 983048 | tf_op jit(solution)/shard_map/ppermute | solution.py:369
  39.4 30.3 %collective-permute-start.4 = (bf16[10,128,128]{2,1,0:T(8,128)(2,1)}, bf16[10,128,128]{2,1,0:T(8,128)(2,1)S(1)}, u32[]{:S(2)}, u32[]{:S(2)}) collective-permute-start(bf16[10,128,128]{2,1,0:T(8,128)(2,1)} %get-tuple-element.54), channel_id=1, source_target_pairs={{0,12},{4,8},{8,4},{12,0},{16,28},{20,24},{24,20},{28,16},{1,13},{... | collective-permute-start | bytes 983048 | tf_op jit(solution)/shard_map/ppermute | solution.py:369
  54.1 15.7 %collective-permute-start.5 = (bf16[10,128,128]{2,1,0:T(8,128)(2,1)}, bf16[10,128,128]{2,1,0:T(8,128)(2,1)S(1)}, u32[]{:S(2)}, u32[]{:S(2)}) collective-permute-start(bf16[10,128,128]{2,1,0:T(8,128)(2,1)} %get-tuple-element.55), channel_id=1, source_target_pairs={{0,24},{4,28},{8,16},{12,20},{16,8},{20,12},{24,0},{28,4},{1,25},{... | collective-permute-start | bytes 983048 | tf_op jit(solution)/shard_map/ppermute | solution.py:369
  55.5 14.2 %collective-permute-start.6 = (bf16[10,128,128]{2,1,0:T(8,128)(2,1)}, bf16[10,128,128]{2,1,0:T(8,128)(2,1)S(1)}, u32[]{:S(2)}, u32[]{:S(2)}) collective-permute-start(bf16[10,128,128]{2,1,0:T(8,128)(2,1)} %get-tuple-element.56), channel_id=1, source_target_pairs={{0,28},{4,24},{8,20},{12,16},{16,12},{20,8},{24,4},{28,0},{1,29},{... | collective-permute-start | bytes 983048 | tf_op jit(solution)/shard_map/ppermute | solution.py:369
  58.0 0.6 copy-start.1
  58.5 24.8 %copy-start.2 = (bf16[10,128,128]{2,1,0:T(8,128)(2,1)S(1)}, bf16[10,128,128]{2,1,0:T(8,128)(2,1)}, u32[]{:S(2)}) copy-start(bf16[10,128,128]{2,1,0:T(8,128)(2,1)} %get-tuple-element.73.refs_7_) | copy-start | bytes 983044
  69.8 20.8 %collective-permute-start.14 = (bf16[2,128,128]{2,1,0:T(8,128)(2,1)S(1)}, bf16[2,128,128]{2,1,0:T(8,128)(2,1)S(1)}, u32[]{:S(2)}, u32[]{:S(2)}) collective-permute-start(bf16[2,128,128]{2,1,0:T(8,128)(2,1)S(1)} %get-tuple-element.83), channel_id=1, source_target_pairs={{0,8},{4,12},{8,0},{12,4},{16,24},{20,28},{24,16},{28,20},{1,9},{5... | collective-permute-start | bytes 196616 | tf_op jit(solution)/shard_map/ppermute | solution.py:369
  80.8 9.7 %collective-permute-start.15 = (bf16[2,128,128]{2,1,0:T(8,128)(2,1)S(1)}, bf16[2,128,128]{2,1,0:T(8,128)(2,1)S(1)}, u32[]{:S(2)}, u32[]{:S(2)}) collective-permute-start(bf16[2,128,128]{2,1,0:T(8,128)(2,1)S(1)} %get-tuple-element.84), channel_id=1, source_target_pairs={{0,16},{4,20},{8,24},{12,28},{16,0},{20,4},{24,8},{28,12},{1,17},{... | collective-permute-start | bytes 196616 | tf_op jit(solution)/shard_map/ppermute | solution.py:369
  81.9 8.7 %collective-permute-start.16 = (bf16[2,128,128]{2,1,0:T(8,128)(2,1)S(1)}, bf16[2,128,128]{2,1,0:T(8,128)(2,1)S(1)}, u32[]{:S(2)}, u32[]{:S(2)}) collective-permute-start(bf16[2,128,128]{2,1,0:T(8,128)(2,1)S(1)} %get-tuple-element.85), channel_id=1, source_target_pairs={{0,24},{4,28},{8,16},{12,20},{16,8},{20,12},{24,0},{28,4},{1,25},{... | collective-permute-start | bytes 196616 | tf_op jit(solution)/shard_map/ppermute | solution.py:369
  90.6 6.5 %collective-permute-start.17 = (bf16[4,128,128]{2,1,0:T(8,128)(2,1)S(1)}, bf16[4,128,128]{2,1,0:T(8,128)(2,1)S(1)}, u32[]{:S(2)}, u32[]{:S(2)}) collective-permute-start(bf16[4,128,128]{2,1,0:T(8,128)(2,1)S(1)} %get-tuple-element.86), channel_id=1, source_target_pairs={{0,4},{4,0},{8,12},{12,8},{16,20},{20,16},{24,28},{28,24},{1,5},{5... | collective-permute-start | bytes 393224 | tf_op jit(solution)/shard_map/ppermute | solution.py:369
  91.2 8.2 %collective-permute-start.18 = (bf16[4,128,128]{2,1,0:T(8,128)(2,1)S(1)}, bf16[4,128,128]{2,1,0:T(8,128)(2,1)S(1)}, u32[]{:S(2)}, u32[]{:S(2)}) collective-permute-start(bf16[4,128,128]{2,1,0:T(8,128)(2,1)S(1)} %get-tuple-element.87), channel_id=1, source_target_pairs={{0,8},{4,12},{8,0},{12,4},{16,24},{20,28},{24,16},{28,20},{1,9},{5... | collective-permute-start | bytes 393224 | tf_op jit(solution)/shard_map/ppermute | solution.py:369
  92.2 10.3 %collective-permute-start.19 = (bf16[4,128,128]{2,1,0:T(8,128)(2,1)S(1)}, bf16[4,128,128]{2,1,0:T(8,128)(2,1)S(1)}, u32[]{:S(2)}, u32[]{:S(2)}) collective-permute-start(bf16[4,128,128]{2,1,0:T(8,128)(2,1)S(1)} %get-tuple-element.88), channel_id=1, source_target_pairs={{0,12},{4,8},{8,4},{12,0},{16,28},{20,24},{24,20},{28,16},{1,13},{... | collective-permute-start | bytes 393224 | tf_op jit(solution)/shard_map/ppermute | solution.py:369
  94.1 17.4 %collective-permute-start.20 = (bf16[4,128,128]{2,1,0:T(8,128)(2,1)S(1)}, bf16[4,128,128]{2,1,0:T(8,128)(2,1)S(1)}, u32[]{:S(2)}, u32[]{:S(2)}) collective-permute-start(bf16[4,128,128]{2,1,0:T(8,128)(2,1)S(1)} %get-tuple-element.89), channel_id=1, source_target_pairs={{0,16},{4,20},{8,24},{12,28},{16,0},{20,4},{24,8},{28,12},{1,17},{... | collective-permute-start | bytes 393224 | tf_op jit(solution)/shard_map/ppermute | solution.py:369
  96.1 18.1 %collective-permute-start.21 = (bf16[4,128,128]{2,1,0:T(8,128)(2,1)S(1)}, bf16[4,128,128]{2,1,0:T(8,128)(2,1)S(1)}, u32[]{:S(2)}, u32[]{:S(2)}) collective-permute-start(bf16[4,128,128]{2,1,0:T(8,128)(2,1)S(1)} %get-tuple-element.90), channel_id=1, source_target_pairs={{0,20},{4,16},{8,28},{12,24},{16,4},{20,0},{24,12},{28,8},{1,21},{... | collective-permute-start | bytes 393224 | tf_op jit(solution)/shard_map/ppermute | solution.py:369
  97.0 17.2 %collective-permute-start.22 = (bf16[4,128,128]{2,1,0:T(8,128)(2,1)S(1)}, bf16[4,128,128]{2,1,0:T(8,128)(2,1)S(1)}, u32[]{:S(2)}, u32[]{:S(2)}) collective-permute-start(bf16[4,128,128]{2,1,0:T(8,128)(2,1)S(1)} %get-tuple-element.91), channel_id=1, source_target_pairs={{0,24},{4,28},{8,16},{12,20},{16,8},{20,12},{24,0},{28,4},{1,25},{... | collective-permute-start | bytes 393224 | tf_op jit(solution)/shard_map/ppermute | solution.py:369
  99.4 14.9 %collective-permute-start.23 = (bf16[4,128,128]{2,1,0:T(8,128)(2,1)S(1)}, bf16[4,128,128]{2,1,0:T(8,128)(2,1)S(1)}, u32[]{:S(2)}, u32[]{:S(2)}) collective-permute-start(bf16[4,128,128]{2,1,0:T(8,128)(2,1)S(1)} %get-tuple-element.92), channel_id=1, source_target_pairs={{0,28},{4,24},{8,20},{12,16},{16,12},{20,8},{24,4},{28,0},{1,29},{... | collective-permute-start | bytes 393224 | tf_op jit(solution)/shard_map/ppermute | solution.py:369

commit v9 on v8

--- a/solution.py
+++ b/solution.py
@@ -287,7 +287,7 @@
             copies[t].wait()
             for s in range(columns):
                 at = pl.multiple_of((column_ref[0] ^ s) * HD, HD)
-                refs[5 + s][t] = rows[t, :, pl.ds(at, HD)]
+                refs[5 + s][(0, 1, 2, 4, 3)[t]] = rows[t, :, pl.ds(at, HD)]
 
     return pl.pallas_call(
         body,
@@ -312,8 +312,8 @@
         mine = [2 * (column ^ s) + side for s in range(columns)]
         for s in range(columns):
             x[mine[s]] = refs[s][...]
-            x[mine[s] ^ 1] = refs[columns + s][...]
-        sources = [(x, t) for t in range(5)]
+            x[mine[s] ^ 1, 0:4] = refs[columns + s][...]
+        sources = [(x, t) for t in (0, 1, 2, 4, 3)]
         student_head(range(0, blocks, 2), first_ref[0], sources[:3], gen, 0)
         at_gen = lambda at: gen[at, 0]
         for s in range(columns):
@@ -377,7 +377,7 @@
     own = [swapped(x, 2 * s) for s, x in enumerate(pieces)]
     packed = slots_pack(full, there, where, tensors)
     arrived = [swapped(x, d) for x, d in zip(packed, there)]
-    other = [swapped(x, 1) for x in own]
+    other = [swapped(x[:4], 1) for x in own]
     pieces = rest_kernel(rest, first, clips, where, own, other)
     arrived, pieces = lax.optimization_barrier((arrived, pieces))
     rests = [swapped(x, 2 * s) for s, x in enumerate(pieces)]

time: 117 us -> 128 us (1.094)
  waiting for transfers between devices: 29.2 us -> 50 us
  starting transfers between devices: 63.3 us -> 52.7 us
    ppermute x24, waiting for transfers between devices: 29.2 us -> 50 us  [swapped(): lax.ppermute(x, 'tm', [(i, i ^ by) for i in range(peers)])]
    ppermute x24, starting transfers between devices: 63.3 us -> 52.7 us  [swapped(): lax.ppermute(x, 'tm', [(i, i ^ by) for i in range(peers)])]
  transfers between devices with their start and end apart: 24 -> 24, of which waited for: 5 -> 9; matrix products, arithmetic and copies ran while one was open for 2% -> 2% of each run, Pallas kernels for 13% -> 12%
where the time goes in v9:
time: 128 us; the launch traced here: 127 us
  starting transfers between devices  52.7 us (41%)
  waiting for transfers between devices  50 us (39%)
  Pallas kernels  18.8 us (15%)
  local copies, waits for them, and re-layouts  1.95 us (2%)
  other arithmetic  1.63 us (1%)
  between operations  1.45 us (1%)
    ppermute x24, starting transfers between devices, swapped(): lax.ppermute(x, 'tm', [(i, i ^ by) for i in range(peers)])  52.7 us
    ppermute x24, waiting for transfers between devices, swapped(): lax.ppermute(x, 'tm', [(i, i ^ by) for i in range(peers)])  50 us
    pallas_call x1, Pallas kernels, slots_kernel(): pl.pallas_call(body, in_specs=[SMEM] * 3 + [VMEM] * blocks, out_specs=[VM...  7.2 us
    pallas_call x1, Pallas kernels, slots_pack(): pl.pallas_call(body, in_specs=[SMEM] + [pl.BlockSpec(memory_space=pl.ANY)...  4.12 us
    pallas_call x1, Pallas kernels, rest_kernel(): pl.pallas_call(body, in_specs=[SMEM] * 3 + [VMEM] * (2 * columns), out_sp...  3.59 us
  transfers between devices with their start and end apart: 24, of which 9 were waited for; matrix products, arithmetic and copies ran while one was open for 2% of the time, Pallas kernels for 12%

profile of v9, /device:TPU:0, one launch (start us, length us, event | category | flops | bytes accessed | tf_op | source)
XLA Modules:
  0.0 126.6 jit_solution(16090158413672969486)
XLA Ops:
  0.6 2.1 %shard_map.87 = (bf16[5,128,128]{2,1,0:T(8,128)(2,1)}, bf16[5,128,128]{2,1,0:T(8,128)(2,1)}, bf16[5,128,128]{2,1,0:T(8,128)(2,1)}, bf16[5,128,128]{2,1,0:T(8,128)(2,1)}) custom-call(s32[1]{0:T(128)} %bitcast.column_ref, bf16[1,128,2560]{2,1,0:T(8,128)(2,1)} %refs_0_.3, bf16[1,128,2560]{2,1,0:T(8,128)(2,1)} %refs_1_.3, bf16[1,128,2560]{2,1,0:T(8,128)(2,1)} %refs_2_.3, ...), custom_call_target="tpu_custom_call" | custom-call | bytes 1310720 | tf_op jit(solution)/shard_map/pallas_call | solution.py:292
  2.7 3.1 %collective-permute-start.7 = (bf16[5,128,128]{2,1,0:T(8,128)(2,1)}, bf16[5,128,128]{2,1,0:T(8,128)(2,1)S(1)}, u32[]{:S(2)}, u32[]{:S(2)}) collective-permute-start(bf16[5,128,128]{2,1,0:T(8,128)(2,1)} %get-tuple-element.59), channel_id=1, source_target_pairs={{0,8},{4,12},{8,0},{12,4},{16,24},{20,28},{24,16},{28,20},{1,9},{5... | collective-permute-start | bytes 491528 | tf_op jit(solution)/shard_map/ppermute | solution.py:369
  5.8 0.7 pad_add_fusion.where_ref
  6.5 4.1 %shard_map.86 = (bf16[10,128,128]{2,1,0:T(8,128)(2,1)}, bf16[10,128,128]{2,1,0:T(8,128)(2,1)}, bf16[10,128,128]{2,1,0:T(8,128)(2,1)}, bf16[10,128,128]{2,1,0:T(8...) custom-call(s32[3]{0:T(128)} %pad_add_fusion.where_ref, ...), custom_call_target="tpu_custom_call" | custom-call | bytes 5242880 | tf_op jit(solution)/shard_map/pallas_call | solution.py:264
  10.6 2.7 %collective-permute-start = (bf16[10,128,128]{2,1,0:T(8,128)(2,1)}, bf16[10,128,128]{2,1,0:T(8,128)(2,1)S(1)}, u32[]{:S(2)}, u32[]{:S(2)}) collective-permute-start(bf16[10,128,128]{2,1,0:T(8,128)(2,1)} %get-tuple-element.50), channel_id=1, source_target_pairs={{0,16},{4,20},{8,24},{12,28},{16,0},{20,4},{24,8},{28,12},{1,17},{... | collective-permute-start | bytes 983048 | tf_op jit(solution)/shard_map/ppermute | solution.py:369
  13.3 0.4 collective-permute-start.1
  13.7 0.1 collective-permute-start.8
  13.8 3.9 %collective-permute-start.9 = (bf16[5,128,128]{2,1,0:T(8,128)(2,1)S(1)}, bf16[5,128,128]{2,1,0:T(8,128)(2,1)S(1)}, u32[]{:S(2)}, u32[]{:S(2)}) collective-permute-start(bf16[5,128,128]{2,1,0:T(8,128)(2,1)S(1)} %copy-done.6), channel_id=1, source_target_pairs={{0,24},{4,28},{8,16},{12,20},{16,8},{20,12},{24,0},{28,4},{1,25},{... | collective-permute-start | bytes 491528 | tf_op jit(solution)/shard_map/ppermute | solution.py:369
  17.7 0.0 copy-done
  17.7 0.0 collective-permute-done.7.refs_1_
  17.7 1.6 %collective-permute-start.10 = (bf16[4,128,128]{2,1,0:T(8,128)(2,1)S(1)}, bf16[4,128,128]{2,1,0:T(8,128)(2,1)S(1)}, u32[]{:S(2)}, u32[]{:S(2)}) collective-permute-start(bf16[4,128,128]{2,1,0:T(8,128)(2,1)S(1)} %slice.12), channel_id=1, source_target_pairs={{0,4},{4,0},{8,12},{12,8},{16,20},{20,16},{24,28},{28,24},{1,5},{5... | collective-permute-start | bytes 393224 | tf_op jit(solution)/shard_map/ppermute | solution.py:369
  19.3 0.0 copy-start.3
  19.3 19.2 %collective-permute-done.8.refs_2_ = bf16[5,128,128]{2,1,0:T(8,128)(2,1)S(1)} collective-permute-done((bf16[5,128,128]{2,1,0:T(8,128)(2,1)S(1)}, bf16[5,128,128]{2,1,0:T(8,128)(2,1)S(1)}, u32[]{:S(2)}, u32[]{:S(2)}) %collective-permute-start.8) | collective-permute-done | bytes 163872 | tf_op jit(solution)/shard_map/ppermute | solution.py:369
  38.5 1.5 %collective-permute-start.11 = (bf16[4,128,128]{2,1,0:T(8,128)(2,1)S(1)}, bf16[4,128,128]{2,1,0:T(8,128)(2,1)S(1)}, u32[]{:S(2)}, u32[]{:S(2)}) collective-permute-start(bf16[4,128,128]{2,1,0:T(8,128)(2,1)S(1)} %slice.16), channel_id=1, source_target_pairs={{0,4},{4,0},{8,12},{12,8},{16,20},{20,16},{24,28},{28,24},{1,5},{5... | collective-permute-start | bytes 393224 | tf_op jit(solution)/shard_map/ppermute | solution.py:369
  40.1 0.0 collective-permute-done.9.refs_3_
  40.1 0.5 collective-permute-start.12
  40.6 0.0 collective-permute-done.10.refs_4_
  40.6 1.6 %collective-permute-start.13 = (bf16[4,128,128]{2,1,0:T(8,128)(2,1)S(1)}, bf16[4,128,128]{2,1,0:T(8,128)(2,1)S(1)}, u32[]{:S(2)}, u32[]{:S(2)}) collective-permute-start(bf16[4,128,128]{2,1,0:T(8,128)(2,1)S(1)} %slice.18), channel_id=1, source_target_pairs={{0,4},{4,0},{8,12},{12,8},{16,20},{20,16},{24,28},{28,24},{1,5},{5... | collective-permute-start | bytes 393224 | tf_op jit(solution)/shard_map/ppermute | solution.py:369
  42.9 0.0 copy-start.8
  42.9 0.6 copy-done.8
  43.6 0.2 reduce-window.8
  43.7 0.6 fusion
  44.4 0.6 pad.2.clone
  45.0 0.0 collective-permute-done.11.refs_5_
  45.0 4.5 %collective-permute-start.2 = (bf16[10,128,128]{2,1,0:T(8,128)(2,1)}, bf16[10,128,128]{2,1,0:T(8,128)(2,1)S(1)}, u32[]{:S(2)}, u32[]{:S(2)}) collective-permute-start(bf16[10,128,128]{2,1,0:T(8,128)(2,1)} %get-tuple-element.52), channel_id=1, source_target_pairs={{0,20},{4,16},{8,28},{12,24},{16,4},{20,0},{24,12},{28,8},{1,21},{... | collective-permute-start | bytes 983048 | tf_op jit(solution)/shard_map/ppermute | solution.py:369
  49.5 0.0 collective-permute-done.12.refs_6_
  49.5 0.5 collective-permute-start.3
  50.0 2.6 %collective-permute-done.13.refs_7_ = bf16[4,128,128]{2,1,0:T(8,128)(2,1)S(1)} collective-permute-done((bf16[4,128,128]{2,1,0:T(8,128)(2,1)S(1)}, bf16[4,128,128]{2,1,0:T(8,128)(2,1)S(1)}, u32[]{:S(2)}, u32[]{:S(2)}) %collective-permute-start.13) | collective-permute-done | bytes 131104 | tf_op jit(solution)/shard_map/ppermute | solution.py:369
  52.6 0.0 collective-permute-start.4
  52.6 0.0 collective-permute-done.refs_0_
  52.6 6.2 %collective-permute-start.5 = (bf16[10,128,128]{2,1,0:T(8,128)(2,1)S(1)}, bf16[10,128,128]{2,1,0:T(8,128)(2,1)S(1)}, u32[]{:S(2)}, u32[]{:S(2)}) collective-permute-start(bf16[10,128,128]{2,1,0:T(8,128)(2,1)S(1)} %copy-done.4), channel_id=1, source_target_pairs={{0,24},{4,28},{8,16},{12,20},{16,8},{20,12},{24,0},{28,4},{1,25},{... | collective-permute-start | bytes 983048 | tf_op jit(solution)/shard_map/ppermute | solution.py:369
  58.8 0.0 collective-permute-done.1.refs_1_
  58.8 0.4 collective-permute-start.6
  59.2 0.1 select_reduce_fusion.1
  59.3 0.1 add_add_fusion.clip_ref
  59.4 0.6 copy-done.1
  60.0 3.6 %shard_map.88 = (bf16[2,128,128]{2,1,0:T(8,128)(2,1)S(1)}, bf16[2,128,128]{2,1,0:T(8,128)(2,1)S(1)}, bf16[2,128,128]{2,1,0:T(8,128)(2,1)S(1)}, bf16[2,128,128]{2,1,0:T(8,128)(2,1)S(1)}) custom-call(s32[1]{0:T(128)S(6)} %copy.9.first_ref, s32[3,8]{1,0:T(4,128)S(1)} %add_add_fusion.clip_ref, s32[3]{0:T(128)S(1)} %copy-done.1, ...), custom_call_target="tpu_custom_call" | custom-call | bytes 32768 | tf_op jit(solution)/shard_map/pallas_call | solution.py:324
  63.6 3.9 %collective-permute-done.2.refs_2_ = bf16[10,128,128]{2,1,0:T(8,128)(2,1)S(1)} collective-permute-done((bf16[10,128,128]{2,1,0:T(8,128)(2,1)}, bf16[10,128,128]{2,1,0:T(8,128)(2,1)S(1)}, u32[]{:S(2)}, u32[]{:S(2)}) %collective-permute-start.2) | collective-permute-done | bytes 327712 | tf_op jit(solution)/shard_map/ppermute | solution.py:369
  67.5 3.7 %collective-permute-done.3.refs_3_ = bf16[10,128,128]{2,1,0:T(8,128)(2,1)S(1)} collective-permute-done((bf16[10,128,128]{2,1,0:T(8,128)(2,1)}, bf16[10,128,128]{2,1,0:T(8,128)(2,1)S(1)}, u32[]{:S(2)}, u32[]{:S(2)}) %collective-permute-start.3) | collective-permute-done | bytes 327712 | tf_op jit(solution)/shard_map/ppermute | solution.py:369
  71.1 0.0 collective-permute-done.4.refs_4_
  71.1 4.0 %collective-permute-done.5.refs_5_ = bf16[10,128,128]{2,1,0:T(8,128)(2,1)S(1)} collective-permute-done((bf16[10,128,128]{2,1,0:T(8,128)(2,1)S(1)}, bf16[10,128,128]{2,1,0:T(8,128)(2,1)S(1)}, u32[]{:S(2)}, u32[]{:S(2)}) %collective-permute-start.5) | collective-permute-done | bytes 327712 | tf_op jit(solution)/shard_map/ppermute | solution.py:369
  75.1 4.4 %collective-permute-done.6.refs_6_ = bf16[10,128,128]{2,1,0:T(8,128)(2,1)S(1)} collective-permute-done((bf16[10,128,128]{2,1,0:T(8,128)(2,1)S(1)}, bf16[10,128,128]{2,1,0:T(8,128)(2,1)S(1)}, u32[]{:S(2)}, u32[]{:S(2)}) %collective-permute-start.6) | collective-permute-done | bytes 327712 | tf_op jit(solution)/shard_map/ppermute | solution.py:369
  79.6 12.1 %collective-permute-start.14 = (bf16[2,128,128]{2,1,0:T(8,128)(2,1)S(1)}, bf16[2,128,128]{2,1,0:T(8,128)(2,1)S(1)}, u32[]{:S(2)}, u32[]{:S(2)}) collective-permute-start(bf16[2,128,128]{2,1,0:T(8,128)(2,1)S(1)} %get-tuple-element.83), channel_id=1, source_target_pairs={{0,8},{4,12},{8,0},{12,4},{16,24},{20,28},{24,16},{28,20},{1,9},{5... | collective-permute-start | bytes 196616 | tf_op jit(solution)/shard_map/ppermute | solution.py:369
  91.7 0.8 collective-permute-start.15
  92.5 1.6 %collective-permute-start.16 = (bf16[2,128,128]{2,1,0:T(8,128)(2,1)S(1)}, bf16[2,128,128]{2,1,0:T(8,128)(2,1)S(1)}, u32[]{:S(2)}, u32[]{:S(2)}) collective-permute-start(bf16[2,128,128]{2,1,0:T(8,128)(2,1)S(1)} %get-tuple-element.85), channel_id=1, source_target_pairs={{0,24},{4,28},{8,16},{12,20},{16,8},{20,12},{24,0},{28,4},{1,25},{... | collective-permute-start | bytes 196616 | tf_op jit(solution)/shard_map/ppermute | solution.py:369
  94.1 7.2 %shard_map.89 = (bf16[4,128,128]{2,1,0:T(8,128)(2,1)S(1)}, bf16[4,128,128]{2,1,0:T(8,128)(2,1)S(1)}, bf16[4,128,128]{2,1,0:T(8,128)(2,1)S(1)}, bf16[4,128,128]{2...) custom-call(s32[1]{0:T(128)S(6)} %copy.9.first_ref, ...), custom_call_target="tpu_custom_call" | custom-call | flops 2147483648 | bytes 3670016 | tf_op jit(solution)/shard_map/pallas_call | solution.py:233
  101.3 0.0 collective-permute-done.14.refs_9_
  101.3 0.0 collective-permute-done.15.refs_10_
  101.3 0.0 collective-permute-done.16.refs_11_
  101.3 0.5 collective-permute-start.17
  101.8 1.1 collective-permute-start.18
  103.0 1.9 %collective-permute-start.19 = (bf16[4,128,128]{2,1,0:T(8,128)(2,1)S(1)}, bf16[4,128,128]{2,1,0:T(8,128)(2,1)S(1)}, u32[]{:S(2)}, u32[]{:S(2)}) collective-permute-start(bf16[4,128,128]{2,1,0:T(8,128)(2,1)S(1)} %get-tuple-element.88), channel_id=1, source_target_pairs={{0,12},{4,8},{8,4},{12,0},{16,28},{20,24},{24,20},{28,16},{1,13},{... | collective-permute-start | bytes 393224 | tf_op jit(solution)/shard_map/ppermute | solution.py:369
  104.9 1.9 %collective-permute-start.20 = (bf16[4,128,128]{2,1,0:T(8,128)(2,1)S(1)}, bf16[4,128,128]{2,1,0:T(8,128)(2,1)S(1)}, u32[]{:S(2)}, u32[]{:S(2)}) collective-permute-start(bf16[4,128,128]{2,1,0:T(8,128)(2,1)S(1)} %get-tuple-element.89), channel_id=1, source_target_pairs={{0,16},{4,20},{8,24},{12,28},{16,0},{20,4},{24,8},{28,12},{1,17},{... | collective-permute-start | bytes 393224 | tf_op jit(solution)/shard_map/ppermute | solution.py:369
  106.8 0.9 collective-permute-start.21
  107.7 0.0 collective-permute-done.17.refs_0_
  107.7 2.2 %collective-permute-start.22 = (bf16[4,128,128]{2,1,0:T(8,128)(2,1)S(1)}, bf16[4,128,128]{2,1,0:T(8,128)(2,1)S(1)}, u32[]{:S(2)}, u32[]{:S(2)}) collective-permute-start(bf16[4,128,128]{2,1,0:T(8,128)(2,1)S(1)} %get-tuple-element.91), channel_id=1, source_target_pairs={{0,24},{4,28},{8,16},{12,20},{16,8},{20,12},{24,0},{28,4},{1,25},{... | collective-permute-start | bytes 393224 | tf_op jit(solution)/shard_map/ppermute | solution.py:369
  109.9 0.0 collective-permute-done.18.refs_1_
  109.9 2.6 %collective-permute-start.23 = (bf16[4,128,128]{2,1,0:T(8,128)(2,1)S(1)}, bf16[4,128,128]{2,1,0:T(8,128)(2,1)S(1)}, u32[]{:S(2)}, u32[]{:S(2)}) collective-permute-start(bf16[4,128,128]{2,1,0:T(8,128)(2,1)S(1)} %get-tuple-element.92), channel_id=1, source_target_pairs={{0,28},{4,24},{8,20},{12,16},{16,12},{20,8},{24,4},{28,0},{1,29},{... | collective-permute-start | bytes 393224 | tf_op jit(solution)/shard_map/ppermute | solution.py:369
  112.5 0.3 collective-permute-done.19.refs_2_
  112.9 9.2 %collective-permute-done.20.refs_3_ = bf16[4,128,128]{2,1,0:T(8,128)(2,1)S(1)} collective-permute-done((bf16[4,128,128]{2,1,0:T(8,128)(2,1)S(1)}, bf16[4,128,128]{2,1,0:T(8,128)(2,1)S(1)}, u32[]{:S(2)}, u32[]{:S(2)}) %collective-permute-start.20) | collective-permute-done | bytes 131104 | tf_op jit(solution)/shard_map/ppermute | solution.py:369
  122.0 2.7 %collective-permute-done.21.refs_4_ = bf16[4,128,128]{2,1,0:T(8,128)(2,1)S(1)} collective-permute-done((bf16[4,128,128]{2,1,0:T(8,128)(2,1)S(1)}, bf16[4,128,128]{2,1,0:T(8,128)(2,1)S(1)}, u32[]{:S(2)}, u32[]{:S(2)}) %collective-permute-start.21) | collective-permute-done | bytes 131104 | tf_op jit(solution)/shard_map/ppermute | solution.py:369
  124.8 0.0 collective-permute-done.22.refs_5_
  124.8 0.0 collective-permute-done.23.refs_6_
  124.8 1.8 %shard_map.90 = (bf16[1,128,2560]{2,1,0:T(8,128)(2,1)}, bf16[1,128,2560]{2,1,0:T(8,128)(2,1)}) custom-call(s32[3]{0:T(128)S(1)} %copy-done.1, bf16[4,128,128]{2,1,0:T(8,128)(2,1)S(1)} %collective-permute-done.17.refs_0_, bf16[4,128,128]{2,1,0:T(8,128)(2,1)S(1)} %collective-permute-done.18.refs_1_, bf16[4,128,128]{2,1,0:T(8,128)(2,1)S(1)} %collective-permute-done.19.refs_2_, ...), custom_call_target="tpu_custom_call" | custom-call | bytes 2621440 | tf_op jit(solution)/shard_map/pallas_call | solution.py:354
  (17 shorter events, 0.1 us)
Async XLA Ops:
  2.7 15.0 %collective-permute-start.7 = (bf16[5,128,128]{2,1,0:T(8,128)(2,1)}, bf16[5,128,128]{2,1,0:T(8,128)(2,1)S(1)}, u32[]{:S(2)}, u32[]{:S(2)}) collective-permute-start(bf16[5,128,128]{2,1,0:T(8,128)(2,1)} %get-tuple-element.59), channel_id=1, source_target_pairs={{0,8},{4,12},{8,0},{12,4},{16,24},{20,28},{24,16},{28,20},{1,9},{5... | collective-permute-start | bytes 491528 | tf_op jit(solution)/shard_map/ppermute | solution.py:369
  6.5 7.2 %copy-start.7 = (bf16[5,128,128]{2,1,0:T(8,128)(2,1)S(1)}, bf16[5,128,128]{2,1,0:T(8,128)(2,1)}, u32[]{:S(2)}) copy-start(bf16[5,128,128]{2,1,0:T(8,128)(2,1)} %get-tuple-element.60) | copy-start | bytes 491524
  6.5 7.3 %copy-start.6 = (bf16[5,128,128]{2,1,0:T(8,128)(2,1)S(1)}, bf16[5,128,128]{2,1,0:T(8,128)(2,1)}, u32[]{:S(2)}) copy-start(bf16[5,128,128]{2,1,0:T(8,128)(2,1)} %get-tuple-element.61) | copy-start | bytes 491524
  6.5 11.2 %copy-start = (bf16[5,128,128]{2,1,0:T(8,128)(2,1)S(1)}, bf16[5,128,128]{2,1,0:T(8,128)(2,1)}, u32[]{:S(2)}) copy-start(bf16[5,128,128]{2,1,0:T(8,128)(2,1)} %get-tuple-element.58.refs_0_) | copy-start | bytes 491524
  10.6 41.9 %collective-permute-start = (bf16[10,128,128]{2,1,0:T(8,128)(2,1)}, bf16[10,128,128]{2,1,0:T(8,128)(2,1)S(1)}, u32[]{:S(2)}, u32[]{:S(2)}) collective-permute-start(bf16[10,128,128]{2,1,0:T(8,128)(2,1)} %get-tuple-element.50), channel_id=1, source_target_pairs={{0,16},{4,20},{8,24},{12,28},{16,0},{20,4},{24,8},{28,12},{1,17},{... | collective-permute-start | bytes 983048 | tf_op jit(solution)/shard_map/ppermute | solution.py:369
  13.3 45.5 %collective-permute-start.1 = (bf16[10,128,128]{2,1,0:T(8,128)(2,1)}, bf16[10,128,128]{2,1,0:T(8,128)(2,1)S(1)}, u32[]{:S(2)}, u32[]{:S(2)}) collective-permute-start(bf16[10,128,128]{2,1,0:T(8,128)(2,1)} %get-tuple-element.51), channel_id=1, source_target_pairs={{0,8},{4,12},{8,0},{12,4},{16,24},{20,28},{24,16},{28,20},{1,9},{5... | collective-permute-start | bytes 983048 | tf_op jit(solution)/shard_map/ppermute | solution.py:369
  13.7 24.8 %collective-permute-start.8 = (bf16[5,128,128]{2,1,0:T(8,128)(2,1)S(1)}, bf16[5,128,128]{2,1,0:T(8,128)(2,1)S(1)}, u32[]{:S(2)}, u32[]{:S(2)}) collective-permute-start(bf16[5,128,128]{2,1,0:T(8,128)(2,1)S(1)} %copy-done.7), channel_id=1, source_target_pairs={{0,16},{4,20},{8,24},{12,28},{16,0},{20,4},{24,8},{28,12},{1,17},{... | collective-permute-start | bytes 491528 | tf_op jit(solution)/shard_map/ppermute | solution.py:369
  13.8 26.2 %collective-permute-start.9 = (bf16[5,128,128]{2,1,0:T(8,128)(2,1)S(1)}, bf16[5,128,128]{2,1,0:T(8,128)(2,1)S(1)}, u32[]{:S(2)}, u32[]{:S(2)}) collective-permute-start(bf16[5,128,128]{2,1,0:T(8,128)(2,1)S(1)} %copy-done.6), channel_id=1, source_target_pairs={{0,24},{4,28},{8,16},{12,20},{16,8},{20,12},{24,0},{28,4},{1,25},{... | collective-permute-start | bytes 491528 | tf_op jit(solution)/shard_map/ppermute | solution.py:369
  17.7 34.9 %copy-start.5 = (bf16[10,128,128]{2,1,0:T(8,128)(2,1)S(1)}, bf16[10,128,128]{2,1,0:T(8,128)(2,1)}, u32[]{:S(2)}) copy-start(bf16[10,128,128]{2,1,0:T(8,128)(2,1)} %get-tuple-element.54) | copy-start | bytes 983044
  17.7 22.9 %collective-permute-start.10 = (bf16[4,128,128]{2,1,0:T(8,128)(2,1)S(1)}, bf16[4,128,128]{2,1,0:T(8,128)(2,1)S(1)}, u32[]{:S(2)}, u32[]{:S(2)}) collective-permute-start(bf16[4,128,128]{2,1,0:T(8,128)(2,1)S(1)} %slice.12), channel_id=1, source_target_pairs={{0,4},{4,0},{8,12},{12,8},{16,20},{20,16},{24,28},{28,24},{1,5},{5... | collective-permute-start | bytes 393224 | tf_op jit(solution)/shard_map/ppermute | solution.py:369
  19.3 33.3 %copy-start.4 = (bf16[10,128,128]{2,1,0:T(8,128)(2,1)S(1)}, bf16[10,128,128]{2,1,0:T(8,128)(2,1)}, u32[]{:S(2)}) copy-start(bf16[10,128,128]{2,1,0:T(8,128)(2,1)} %get-tuple-element.55) | copy-start | bytes 983044
  19.3 39.5 %copy-start.3 = (bf16[10,128,128]{2,1,0:T(8,128)(2,1)S(1)}, bf16[10,128,128]{2,1,0:T(8,128)(2,1)}, u32[]{:S(2)}) copy-start(bf16[10,128,128]{2,1,0:T(8,128)(2,1)} %get-tuple-element.56) | copy-start | bytes 983044
  38.5 6.5 %collective-permute-start.11 = (bf16[4,128,128]{2,1,0:T(8,128)(2,1)S(1)}, bf16[4,128,128]{2,1,0:T(8,128)(2,1)S(1)}, u32[]{:S(2)}, u32[]{:S(2)}) collective-permute-start(bf16[4,128,128]{2,1,0:T(8,128)(2,1)S(1)} %slice.16), channel_id=1, source_target_pairs={{0,4},{4,0},{8,12},{12,8},{16,20},{20,16},{24,28},{28,24},{1,5},{5... | collective-permute-start | bytes 393224 | tf_op jit(solution)/shard_map/ppermute | solution.py:369
  40.1 9.4 %collective-permute-start.12 = (bf16[4,128,128]{2,1,0:T(8,128)(2,1)S(1)}, bf16[4,128,128]{2,1,0:T(8,128)(2,1)S(1)}, u32[]{:S(2)}, u32[]{:S(2)}) collective-permute-start(bf16[4,128,128]{2,1,0:T(8,128)(2,1)S(1)} %slice.17), channel_id=1, source_target_pairs={{0,4},{4,0},{8,12},{12,8},{16,20},{20,16},{24,28},{28,24},{1,5},{5... | collective-permute-start | bytes 393224 | tf_op jit(solution)/shard_map/ppermute | solution.py:369
  40.6 11.9 %collective-permute-start.13 = (bf16[4,128,128]{2,1,0:T(8,128)(2,1)S(1)}, bf16[4,128,128]{2,1,0:T(8,128)(2,1)S(1)}, u32[]{:S(2)}, u32[]{:S(2)}) collective-permute-start(bf16[4,128,128]{2,1,0:T(8,128)(2,1)S(1)} %slice.18), channel_id=1, source_target_pairs={{0,4},{4,0},{8,12},{12,8},{16,20},{20,16},{24,28},{28,24},{1,5},{5... | collective-permute-start | bytes 393224 | tf_op jit(solution)/shard_map/ppermute | solution.py:369
  42.9 0.7 copy-start.8
  45.0 22.5 %collective-permute-start.2 = (bf16[10,128,128]{2,1,0:T(8,128)(2,1)}, bf16[10,128,128]{2,1,0:T(8,128)(2,1)S(1)}, u32[]{:S(2)}, u32[]{:S(2)}) collective-permute-start(bf16[10,128,128]{2,1,0:T(8,128)(2,1)} %get-tuple-element.52), channel_id=1, source_target_pairs={{0,20},{4,16},{8,28},{12,24},{16,4},{20,0},{24,12},{28,8},{1,21},{... | collective-permute-start | bytes 983048 | tf_op jit(solution)/shard_map/ppermute | solution.py:369
  49.5 21.7 %collective-permute-start.3 = (bf16[10,128,128]{2,1,0:T(8,128)(2,1)}, bf16[10,128,128]{2,1,0:T(8,128)(2,1)S(1)}, u32[]{:S(2)}, u32[]{:S(2)}) collective-permute-start(bf16[10,128,128]{2,1,0:T(8,128)(2,1)} %get-tuple-element.53), channel_id=1, source_target_pairs={{0,4},{4,0},{8,12},{12,8},{16,20},{20,16},{24,28},{28,24},{1,5},{5... | collective-permute-start | bytes 983048 | tf_op jit(solution)/shard_map/ppermute | solution.py:369
  52.6 18.6 %collective-permute-start.4 = (bf16[10,128,128]{2,1,0:T(8,128)(2,1)S(1)}, bf16[10,128,128]{2,1,0:T(8,128)(2,1)S(1)}, u32[]{:S(2)}, u32[]{:S(2)}) collective-permute-start(bf16[10,128,128]{2,1,0:T(8,128)(2,1)S(1)} %copy-done.5), channel_id=1, source_target_pairs={{0,12},{4,8},{8,4},{12,0},{16,28},{20,24},{24,20},{28,16},{1,13},{... | collective-permute-start | bytes 983048 | tf_op jit(solution)/shard_map/ppermute | solution.py:369
  52.6 22.5 %collective-permute-start.5 = (bf16[10,128,128]{2,1,0:T(8,128)(2,1)S(1)}, bf16[10,128,128]{2,1,0:T(8,128)(2,1)S(1)}, u32[]{:S(2)}, u32[]{:S(2)}) collective-permute-start(bf16[10,128,128]{2,1,0:T(8,128)(2,1)S(1)} %copy-done.4), channel_id=1, source_target_pairs={{0,24},{4,28},{8,16},{12,20},{16,8},{20,12},{24,0},{28,4},{1,25},{... | collective-permute-start | bytes 983048 | tf_op jit(solution)/shard_map/ppermute | solution.py:369
  58.8 20.7 %collective-permute-start.6 = (bf16[10,128,128]{2,1,0:T(8,128)(2,1)S(1)}, bf16[10,128,128]{2,1,0:T(8,128)(2,1)S(1)}, u32[]{:S(2)}, u32[]{:S(2)}) collective-permute-start(bf16[10,128,128]{2,1,0:T(8,128)(2,1)S(1)} %copy-done.3), channel_id=1, source_target_pairs={{0,28},{4,24},{8,20},{12,16},{16,12},{20,8},{24,4},{28,0},{1,29},{... | collective-permute-start | bytes 983048 | tf_op jit(solution)/shard_map/ppermute | solution.py:369
  59.3 0.7 copy-start.1
  60.0 34.1 %copy-start.2 = (bf16[10,128,128]{2,1,0:T(8,128)(2,1)S(1)}, bf16[10,128,128]{2,1,0:T(8,128)(2,1)}, u32[]{:S(2)}) copy-start(bf16[10,128,128]{2,1,0:T(8,128)(2,1)} %get-tuple-element.73.refs_7_) | copy-start | bytes 983044
  79.6 21.7 %collective-permute-start.14 = (bf16[2,128,128]{2,1,0:T(8,128)(2,1)S(1)}, bf16[2,128,128]{2,1,0:T(8,128)(2,1)S(1)}, u32[]{:S(2)}, u32[]{:S(2)}) collective-permute-start(bf16[2,128,128]{2,1,0:T(8,128)(2,1)S(1)} %get-tuple-element.83), channel_id=1, source_target_pairs={{0,8},{4,12},{8,0},{12,4},{16,24},{20,28},{24,16},{28,20},{1,9},{5... | collective-permute-start | bytes 196616 | tf_op jit(solution)/shard_map/ppermute | solution.py:369
  91.7 9.6 %collective-permute-start.15 = (bf16[2,128,128]{2,1,0:T(8,128)(2,1)S(1)}, bf16[2,128,128]{2,1,0:T(8,128)(2,1)S(1)}, u32[]{:S(2)}, u32[]{:S(2)}) collective-permute-start(bf16[2,128,128]{2,1,0:T(8,128)(2,1)S(1)} %get-tuple-element.84), channel_id=1, source_target_pairs={{0,16},{4,20},{8,24},{12,28},{16,0},{20,4},{24,8},{28,12},{1,17},{... | collective-permute-start | bytes 196616 | tf_op jit(solution)/shard_map/ppermute | solution.py:369
  92.5 8.8 %collective-permute-start.16 = (bf16[2,128,128]{2,1,0:T(8,128)(2,1)S(1)}, bf16[2,128,128]{2,1,0:T(8,128)(2,1)S(1)}, u32[]{:S(2)}, u32[]{:S(2)}) collective-permute-start(bf16[2,128,128]{2,1,0:T(8,128)(2,1)S(1)} %get-tuple-element.85), channel_id=1, source_target_pairs={{0,24},{4,28},{8,16},{12,20},{16,8},{20,12},{24,0},{28,4},{1,25},{... | collective-permute-start | bytes 196616 | tf_op jit(solution)/shard_map/ppermute | solution.py:369
  101.3 6.4 %collective-permute-start.17 = (bf16[4,128,128]{2,1,0:T(8,128)(2,1)S(1)}, bf16[4,128,128]{2,1,0:T(8,128)(2,1)S(1)}, u32[]{:S(2)}, u32[]{:S(2)}) collective-permute-start(bf16[4,128,128]{2,1,0:T(8,128)(2,1)S(1)} %get-tuple-element.86), channel_id=1, source_target_pairs={{0,4},{4,0},{8,12},{12,8},{16,20},{20,16},{24,28},{28,24},{1,5},{5... | collective-permute-start | bytes 393224 | tf_op jit(solution)/shard_map/ppermute | solution.py:369
  101.8 8.1 %collective-permute-start.18 = (bf16[4,128,128]{2,1,0:T(8,128)(2,1)S(1)}, bf16[4,128,128]{2,1,0:T(8,128)(2,1)S(1)}, u32[]{:S(2)}, u32[]{:S(2)}) collective-permute-start(bf16[4,128,128]{2,1,0:T(8,128)(2,1)S(1)} %get-tuple-element.87), channel_id=1, source_target_pairs={{0,8},{4,12},{8,0},{12,4},{16,24},{20,28},{24,16},{28,20},{1,9},{5... | collective-permute-start | bytes 393224 | tf_op jit(solution)/shard_map/ppermute | solution.py:369
  103.0 9.9 %collective-permute-start.19 = (bf16[4,128,128]{2,1,0:T(8,128)(2,1)S(1)}, bf16[4,128,128]{2,1,0:T(8,128)(2,1)S(1)}, u32[]{:S(2)}, u32[]{:S(2)}) collective-permute-start(bf16[4,128,128]{2,1,0:T(8,128)(2,1)S(1)} %get-tuple-element.88), channel_id=1, source_target_pairs={{0,12},{4,8},{8,4},{12,0},{16,28},{20,24},{24,20},{28,16},{1,13},{... | collective-permute-start | bytes 393224 | tf_op jit(solution)/shard_map/ppermute | solution.py:369
  104.9 17.2 %collective-permute-start.20 = (bf16[4,128,128]{2,1,0:T(8,128)(2,1)S(1)}, bf16[4,128,128]{2,1,0:T(8,128)(2,1)S(1)}, u32[]{:S(2)}, u32[]{:S(2)}) collective-permute-start(bf16[4,128,128]{2,1,0:T(8,128)(2,1)S(1)} %get-tuple-element.89), channel_id=1, source_target_pairs={{0,16},{4,20},{8,24},{12,28},{16,0},{20,4},{24,8},{28,12},{1,17},{... | collective-permute-start | bytes 393224 | tf_op jit(solution)/shard_map/ppermute | solution.py:369
  106.8 18.0 %collective-permute-start.21 = (bf16[4,128,128]{2,1,0:T(8,128)(2,1)S(1)}, bf16[4,128,128]{2,1,0:T(8,128)(2,1)S(1)}, u32[]{:S(2)}, u32[]{:S(2)}) collective-permute-start(bf16[4,128,128]{2,1,0:T(8,128)(2,1)S(1)} %get-tuple-element.90), channel_id=1, source_target_pairs={{0,20},{4,16},{8,28},{12,24},{16,4},{20,0},{24,12},{28,8},{1,21},{... | collective-permute-start | bytes 393224 | tf_op jit(solution)/shard_map/ppermute | solution.py:369
  107.7 17.1 %collective-permute-start.22 = (bf16[4,128,128]{2,1,0:T(8,128)(2,1)S(1)}, bf16[4,128,128]{2,1,0:T(8,128)(2,1)S(1)}, u32[]{:S(2)}, u32[]{:S(2)}) collective-permute-start(bf16[4,128,128]{2,1,0:T(8,128)(2,1)S(1)} %get-tuple-element.91), channel_id=1, source_target_pairs={{0,24},{4,28},{8,16},{12,20},{16,8},{20,12},{24,0},{28,4},{1,25},{... | collective-permute-start | bytes 393224 | tf_op jit(solution)/shard_map/ppermute | solution.py:369
  109.9 14.9 %collective-permute-start.23 = (bf16[4,128,128]{2,1,0:T(8,128)(2,1)S(1)}, bf16[4,128,128]{2,1,0:T(8,128)(2,1)S(1)}, u32[]{:S(2)}, u32[]{:S(2)}) collective-permute-start(bf16[4,128,128]{2,1,0:T(8,128)(2,1)S(1)} %get-tuple-element.92), channel_id=1, source_target_pairs={{0,28},{4,24},{8,20},{12,16},{16,12},{20,8},{24,4},{28,0},{1,29},{... | collective-permute-start | bytes 393224 | tf_op jit(solution)/shard_map/ppermute | solution.py:369
